TPU v7x, 32 devices: a whole 2x2x4 slice. The times are simulated.
32 devices in a mesh: groups: 2 (over x), nodes: 16 (over z, y, core).
Axes of the slice: x: 2, y: 2, z: 4, core: 2. Of those that a mesh axis runs over, the one named last changes fastest.
Arguments:
- features: bfloat16 [16384, 128], P(('groups', 'nodes')), parts along dimension 0, may hold values from -6 to 6
- cluster: int32 [16384], P(('groups', 'nodes')), parts along dimension 0, may hold values from 0 to 15, as said below
- slot: int32 [16384], P(('groups', 'nodes')), parts along dimension 0, may hold values from 0 to 511, as said below
- halo_tiles: int32 [32, 64], P(('groups', 'nodes')), parts along dimension 0, may hold values from 0 to 63, as said below
- tile_slots: int32 [128, 64], P(('groups', 'nodes')), parts along dimension 0, may hold values from 0 to 63
- adjacency: bfloat16 [16384, 64, 128], P(('groups', 'nodes')), parts along dimension 0, may hold values from -0.0625 to 0.0625
- labels: int32 [16384], P(('groups', 'nodes')), parts along dimension 0, may hold values from -1 to 171, as said below
- w_self: bfloat16 [128, 256], replicated, may hold values from -0.5 to 0.5
- w_neigh: bfloat16 [128, 256], replicated, may hold values from -0.5 to 0.5
- w_out: bfloat16 [256, 172], replicated, may hold values from -0.375 to 0.375
- b_out: float32 [172], replicated, may hold values from -9 to 9
Outputs:
- hidden: bfloat16 [16384, 256], P(('groups', 'nodes')), parts along dimension 0
- grad_self: float32 [256, 256], P('groups'), parts along dimension 0
- grad_neigh: float32 [256, 256], P('groups'), parts along dimension 0
- grad_out: float32 [512, 172], P('groups'), parts along dimension 0
- class_weight: float32 [344], P('groups'), parts along dimension 0
There are 2 independent parts, one for each index of `groups`. A program takes and returns all parts, laid end to end along the dimension named above; an argument that names none is the same for every part. Nothing has to cross between parts.
Inputs may be any that keep to these rules, and one draw needn't show every extreme that they name: `cluster`: exactly 32 of the rows stored on each device belong to each partition. `slot`: together with cluster, every position of every partition is taken by exactly one stored row. `halo_tiles`: tile g is held in partition order by device g // 4. In each row, no device holds more than 4 of the tiles, and some device holds exactly 4. `labels`: -1 marks an unlabelled node.
All inputs are finite; a program needn't handle non-finite values.
Results may differ from a plain program's by a relative error of at most 0.006.
The roundings to bfloat16 on the way count: a program that leaves them out, or rounds other values in their place, can miss the bound.
Values may be sent and summed in bfloat16 or wider, within the bound.
No kernel may reach another device: no remote copies, remote signals or barrier semaphores. Data moves between devices by JAX's collectives and lax.ppermute only.
A program may use at most 128 MiB of HBM per device.

v0:
```python
import jax
import jax.numpy as jnp
from jax import lax
from jax.sharding import PartitionSpec as P

TILE = 128


def body(
    features,
    cluster,
    slot,
    halo_tiles,
    tile_slots,
    adjacency,
    labels,
    w_self,
    w_neigh,
    w_out,
    b_out,
):
    rows = features.shape[0]
    width = features.shape[1]
    devices = lax.axis_size("nodes")
    per_peer = rows // devices
    order = jnp.argsort(cluster, stable=True)
    send_rows = features[order].reshape(devices, per_peer, width)
    send_slots = slot[order].reshape(devices, per_peer)
    recv_rows, recv_slots = (
        lax.all_to_all(send_rows, "nodes", split_axis=0, concat_axis=0, tiled=True),
        lax.all_to_all(send_slots, "nodes", split_axis=0, concat_axis=0, tiled=True),
    )
    part_x = (
        jnp.zeros((rows, width), jnp.bfloat16)
        .at[recv_slots.reshape(rows)]
        .set(recv_rows.reshape(rows, width))
    )
    local_tiles = rows // TILE
    wanted = halo_tiles[0]
    gathered = lax.all_gather(part_x, "nodes", axis=0, tiled=True)
    halo = gathered.reshape(-1, TILE, width)[wanted]
    sources = halo[tile_slots]
    adj_tiles = adjacency.reshape(local_tiles, TILE, adjacency.shape[1], TILE)
    agg = jnp.einsum("tikc,tkcf->tif", adj_tiles, sources, preferred_element_type=jnp.float32)
    agg = agg.reshape(rows, width).astype(jnp.bfloat16)
    pre = jnp.dot(part_x, w_self, preferred_element_type=jnp.float32) + jnp.dot(
        agg, w_neigh, preferred_element_type=jnp.float32
    )
    hidden = jnp.maximum(pre, 0.0).astype(jnp.bfloat16)
    logits = jnp.dot(hidden, w_out, preferred_element_type=jnp.float32) + b_out
    lse = jnp.log(jnp.sum(jnp.exp(logits), axis=1))
    classes_row = jnp.arange(w_out.shape[1], dtype=jnp.int32)
    onehot = (labels[:, None] == classes_row[None, :]).astype(jnp.float32)
    picked = jnp.sum(onehot * logits, axis=1)
    ce_rows = lse - picked
    local_loss = jnp.sum(onehot * ce_rows[:, None], axis=0)
    local_counts = jnp.sum(onehot, axis=0)
    loss_sum, counts = lax.psum((local_loss, local_counts), "nodes")
    difficulty = (loss_sum + 1.0) / (counts + 1.0)
    class_weight = difficulty / jnp.mean(difficulty)
    total = jnp.sum(counts)
    row_weight = jnp.sum(onehot * class_weight[None, :], axis=1) / (total + 1.0)
    probs = jnp.exp(logits - lse[:, None])
    dlogits = (row_weight[:, None] * (probs - onehot)).astype(jnp.bfloat16)
    part_out = jnp.dot(hidden.T, dlogits, preferred_element_type=jnp.float32)
    dhidden = jnp.dot(dlogits, w_out.T, preferred_element_type=jnp.float32)
    dpre = jnp.where(hidden > 0, dhidden, 0.0).astype(jnp.bfloat16)
    part_self = jnp.dot(part_x.T, dpre, preferred_element_type=jnp.float32)
    part_neigh = jnp.dot(agg.T, dpre, preferred_element_type=jnp.float32)
    grad_self, grad_neigh, grad_out = lax.psum((part_self, part_neigh, part_out), "nodes")
    return (hidden, grad_self, grad_neigh, grad_out, class_weight)


def solution(mesh):
    return jax.shard_map(
        body,
        mesh=mesh,
        in_specs=(
            P(("groups", "nodes"), None),
            P(("groups", "nodes")),
            P(("groups", "nodes")),
            P(("groups", "nodes"), None),
            P(("groups", "nodes"), None),
            P(("groups", "nodes"), None, None),
            P(("groups", "nodes")),
            P(),
            P(),
            P(),
            P(),
        ),
        out_specs=(
            P(("groups", "nodes"), None),
            P("groups", None),
            P("groups", None),
            P("groups", None),
            P("groups"),
        ),
        check_vma=False,
    )
```

profile of v0, /device:TPU:0, one launch (start us, length us, event | category | flops | bytes accessed | tf_op | source)
XLA Modules:
  0.0 241.6 jit_solution(11378294168101366983)
XLA Ops:
  7.2 0.0 copy-start
  7.2 4.5 %sort.17 = (s32[512]{0:T(512)}, s32[512]{0:T(512)S(1)}) sort(s32[512]{0:T(512)} %param.12, s32[512]{0:T(512)S(1)} %iota.8), dimensions={0}, to_apply=%region_0.0 | sort | flops 4608 | bytes 8192 | tf_op jit(solution)/shard_map/jit(argsort)/sort | solution.py:26
  11.7 3.6 %gather_fusion = s32[512]{0:T(512)S(1)} fusion(s32[512]{0:T(512)} %param.13, s32[1024]{0:T(1024)S(1)} %pad_clamp_fusion.2), kind=kCustom, calls=%fused_computation | custom fusion | bytes 6144 | tf_op jit(solution)/shard_map/gather | solution.py:28
  15.3 0.7 all_to_all.9
  16.0 7.4 %all-to-all-start = ((s32[16,1,32]{2,1,0:T(1,128)}), s32[16,1,32]{2,1,0:T(1,128)S(1)}, u32[]{:S(2)}, u32[]{:S(2)}) async-start(s32[16,1,32]{2,1,0:T(1,128)} %all_to_all.9), calls=%async_computation | async-start | bytes 16384 | tf_op jit(solution)/shard_map/all_to_all | solution.py:31
  23.4 0.0 copy-done
  23.4 1.9 gather_fusion.1
  25.3 4.4 %all-to-all-done = s32[16,1,32]{2,1,0:T(1,128)S(1)} async-done(((s32[16,1,32]{2,1,0:T(1,128)}), s32[16,1,32]{2,1,0:T(1,128)S(1)}, u32[]{:S(2)}, u32[]{:S(2)}) %all-to-all-start) | async-done | bytes 2080 | tf_op jit(solution)/shard_map/all_to_all | solution.py:31
  29.7 3.5 %all-to-all-start.1 = ((bf16[16,32,128]{2,1,0:T(8,128)(2,1)}), bf16[16,32,128]{2,1,0:T(8,128)(2,1)S(1)}, u32[]{:S(2)}, u32[]{:S(2)}) async-start(bf16[16,32,128]{2,1,0:T(8,128)(2,1)} %bitcast.1), calls=%async_computation.1 | async-start | bytes 262144 | tf_op jit(solution)/shard_map/all_to_all | solution.py:30
  33.2 0.0 all-gather.2.cloned.1.call-start
  33.3 0.5 broadcast.86
  33.8 0.7 reduce.3
  34.5 0.1 reshape.102
  34.6 6.6 %all-to-all-done.1 = bf16[16,32,128]{2,1,0:T(8,128)(2,1)S(1)} async-done(((bf16[16,32,128]{2,1,0:T(8,128)(2,1)}), bf16[16,32,128]{2,1,0:T(8,128)(2,1)S(1)}, u32[]{:S(2)}, u32[]{:S(2)}) %all-to-all-start.1) | async-done | bytes 131104 | tf_op jit(solution)/shard_map/all_to_all | solution.py:30
  41.1 2.4 scatter_custom_fusion
  43.5 0.0 all-gather.2.cloned.1.call-update
  43.5 0.2 all-reduce.4.cloned.1.call-start
  43.7 0.7 compare_select_fusion.1
  44.4 0.1 reshape.133
  44.5 0.7 fusion.15
  45.2 1.1 fusion.20
  46.3 36.4 %all-gather.2.cloned.1.call-done = bf16[8192,128]{1,0:T(8,128)(2,1)} async-done(((bf16[512,128]{1,0:T(8,128)(2,1)}), bf16[8192,128]{1,0:T(8,128)(2,1)}) %all-gather.2.cloned.1.call-update) | async-done | bytes 2097168 | tf_op jit(solution)/shard_map/all_gather | solution.py:40
  82.7 2.5 %gather_fusion.2 = bf16[64,128,128]{2,1,0:T(8,128)(2,1)S(1)} fusion(bf16[64,128,128]{2,1,0:T(8,128)(2,1)} %bitcast.32, s32[1024]{0:T(1024)S(1)} %pad_clamp_fusion.1), kind=kCustom, calls=%fused_computation.2 | custom fusion | bytes 4194560 | tf_op jit(solution)/shard_map/gather | solution.py:41
  85.3 8.6 %gather_fusion.3 = bf16[256,128,128]{2,1,0:T(8,128)(2,1)} fusion(bf16[64,128,128]{2,1,0:T(8,128)(2,1)S(1)} %gather_fusion.2, s32[1024]{0:T(1024)S(1)} %pad_clamp_fusion), kind=kCustom, calls=%fused_computation.3 | custom fusion | bytes 16778240 | tf_op jit(solution)/shard_map/gather | solution.py:42
  93.9 0.0 copy-start.1
  93.9 11.0 %fusion.8 = bf16[4,128,128]{1,2,0:T(8,128)(2,1)S(1)} fusion(bf16[4,64,128,128]{3,2,1,0:T(8,128)(2,1)} %bitcast.31, bf16[4,128,64,128]{3,2,1,0:T(8,128)(2,1)} %bitcast.37), kind=kOutput, calls=%fused_computation.14 | convolution fusion | flops 1073807360 | bytes 16908288 | tf_op jit(solution)/shard_map/tikc,tkcf->tif/dot_general | solution.py:44
  104.9 0.0 copy-done.3
  104.9 0.2 fusion.3
  105.2 0.0 copy-done.4
  105.2 0.0 copy-done.6
  105.2 0.0 copy-done.7
  105.2 0.0 copy-start.2
  105.2 0.3 select_reduce_fusion.2
  105.5 0.2 select_reduce_fusion.1
  105.7 31.4 %all-reduce = (f32[172]{0:T(256)S(1)}, f32[172]{0:T(256)S(1)}) all-reduce(f32[172]{0:T(256)S(1)} %get-tuple-element.10, f32[172]{0:T(256)S(1)} %get-tuple-element.9), channel_id=1, replica_groups=mesh['groups'=2,'nodes'=16] {'nodes'}, use_global_device_ids=true, to_apply=%region_7.8 | all-reduce | flops 344 | bytes 2752 | tf_op jit(solution)/shard_map/psum | solution.py:58
  137.1 0.6 fusion.19
  138.4 0.0 copy-start.5
  138.4 0.1 select_reduce_fusion
  139.2 0.9 fusion.16
  140.1 0.3 fusion.4
  140.4 0.9 fusion.22
  141.3 0.9 fusion.21
  142.2 0.0 all-reduce.4.cloned.1.call-update
  142.2 87.8 %all-reduce.4.cloned.1.call-done = (f32[128,256]{1,0:T(8,128)}, f32[128,256]{1,0:T(8,128)}, f32[256,172]{0,1:T(8,128)}) async-done(((f32[128,256]{1,0:T(8,128)}, f32[128,256]{1,0:T(8,128)}, f32[256,172]{0,1:T(8,128)}), (f32[128,256]{1,0:T(8,128)}, f32[128,256]{1,0:T(8,128)}, f32[256,172]{0,1:T(8,128)})) %all-reduce.4.cloned.1.call-update) | async-done | bytes 438288 | tf_op jit(solution)/shard_map/psum | solution.py:70
  230.0 1.6 copy.28
  231.6 1.6 copy.29
  233.2 1.6 copy.30
  234.8 0.0 copy-done.2
  (15 shorter events, 0.1 us)
Async XLA Ops:
  7.2 16.2 %copy-start = (bf16[512,128]{1,0:T(8,128)(2,1)S(1)}, bf16[512,128]{1,0:T(8,128)(2,1)}, u32[]{:S(2)}) copy-start(bf16[512,128]{1,0:T(8,128)(2,1)} %param.11) | copy-start | bytes 393220
  16.0 13.7 %all-to-all-start = ((s32[16,1,32]{2,1,0:T(1,128)}), s32[16,1,32]{2,1,0:T(1,128)S(1)}, u32[]{:S(2)}, u32[]{:S(2)}) async-start(s32[16,1,32]{2,1,0:T(1,128)} %all_to_all.9), calls=%async_computation | async-start | bytes 16384 | tf_op jit(solution)/shard_map/all_to_all | solution.py:31
  29.7 11.4 %all-to-all-start.1 = ((bf16[16,32,128]{2,1,0:T(8,128)(2,1)}), bf16[16,32,128]{2,1,0:T(8,128)(2,1)S(1)}, u32[]{:S(2)}, u32[]{:S(2)}) async-start(bf16[16,32,128]{2,1,0:T(8,128)(2,1)} %bitcast.1), calls=%async_computation.1 | async-start | bytes 262144 | tf_op jit(solution)/shard_map/all_to_all | solution.py:30
  33.2 49.5 %all-gather.2.cloned.1.call-start = ((), (), s32[]{:S(2)}) async-start(), calls=%async_computation.2 | async-start | bytes 2228224 | tf_op jit(solution)/shard_map/all_gather | solution.py:40
  43.5 186.5 %all-reduce.4.cloned.1.call-start = ((), (), s32[]{:S(2)}) async-start(), calls=%async_computation.3 | async-start | bytes 884736 | tf_op jit(solution)/shard_map/psum | solution.py:70
  93.9 11.0 %copy-start.3 = (bf16[128,256]{1,0:T(8,128)(2,1)S(1)}, bf16[128,256]{1,0:T(8,128)(2,1)}, u32[]{:S(2)}) copy-start(bf16[128,256]{1,0:T(8,128)(2,1)} %param.19) | copy-start | bytes 196612
  93.9 11.3 %copy-start.4 = (s32[512]{0:T(512)S(1)}, s32[512]{0:T(512)}, u32[]{:S(2)}) copy-start(s32[512]{0:T(512)} %param.17) | copy-start | bytes 6148
  93.9 11.3 %copy-start.6 = (bf16[256,172]{0,1:T(8,128)(2,1)S(1)}, bf16[256,172]{0,1:T(8,128)(2,1)}, u32[]{:S(2)}) copy-start(bf16[256,172]{0,1:T(8,128)(2,1)} %param.20) | copy-start | bytes 264196
  93.9 11.3 %copy-start.7 = (f32[172]{0:T(256)S(1)}, f32[172]{0:T(256)}, u32[]{:S(2)}) copy-start(f32[172]{0:T(256)} %param.21) | copy-start | bytes 2068
  93.9 47.4 %copy-start.1 = (bf16[512,128]{1,0:T(8,128)(2,1)S(1)}, bf16[512,128]{1,0:T(8,128)(2,1)}, u32[]{:S(2)}) copy-start(bf16[512,128]{1,0:T(8,128)(2,1)} %scatter_custom_fusion) | copy-start | bytes 393220
  105.2 129.6 %copy-start.2 = (bf16[512,256]{1,0:T(8,128)(2,1)}, bf16[512,256]{1,0:T(8,128)(2,1)S(1)}, u32[]{:S(2)}) copy-start(bf16[512,256]{1,0:T(8,128)(2,1)S(1)} %fusion.3) | copy-start | bytes 786436
  138.4 96.4 %copy-start.5 = (f32[172]{0:T(256)}, f32[172]{0:T(256)S(1)}, u32[]{:S(2)}) copy-start(f32[172]{0:T(256)S(1)} %multiply_divide_fusion) | copy-start | bytes 2068
Sparse Core Ops, SparseCore 0:
  43.6 39.0 all-gather.1
  142.4 87.6 all-reduce.3
where the time goes:
time: 242 us
  waiting for transfers between devices  135 us (56%)
  blocking collectives  31.4 us (13%)
  local copies, waits for them, and re-layouts  25.2 us (10%)
  matrix products  15.6 us (6%)
  between operations  15.5 us (6%)
  starting transfers between devices  11.2 us (5%)
  other arithmetic  7.46 us (3%)
    psum x1, waiting for transfers between devices, body(): lax.psum((part_self, part_neigh, part_out), 'nodes')  87.8 us
    all_gather x1, waiting for transfers between devices, body(): gathered = lax.all_gather(part_x, 'nodes', axis=0, tiled=True)  36.4 us
    psum x1, blocking collectives, body(): loss_sum, counts = lax.psum((local_loss, local_counts), 'nodes')  31.4 us
    dot_general x1, matrix products, body(): jnp.einsum('tikc,tkcf->tif', adj_tiles, sources, preferred_element_type=j...  11 us
    gather x1, local copies, waits for them, and re-layouts, body(): sources = halo[tile_slots]  8.62 us
    all_to_all x1, starting transfers between devices, body(): lax.all_to_all(send_slots, 'nodes', split_axis=0, concat_axis=0, tiled=True)  7.39 us
    all_to_all x1, waiting for transfers between devices, body(): lax.all_to_all(send_rows, 'nodes', split_axis=0, concat_axis=0, tiled=True)  6.57 us
  transfers between devices with their start and end apart: 4, of which 4 were waited for; matrix products, arithmetic and copies ran while one was open for 2% of the time, Pallas kernels for 0%

commit v1 on v0

--- a/solution.py
+++ b/solution.py
@@ -1,23 +1,307 @@
 import jax
 import jax.numpy as jnp
 from jax import lax
+from jax.experimental import pallas as pl
+from jax.experimental.pallas import tpu as pltpu
 from jax.sharding import PartitionSpec as P
 
 TILE = 128
-
-
-def body(
-    features,
-    cluster,
-    slot,
-    halo_tiles,
-    tile_slots,
-    adjacency,
-    labels,
-    w_self,
-    w_neigh,
-    w_out,
-    b_out,
+LANES = 128
+SUB = 16
+VMEM = 48 << 20
+F32 = jnp.float32
+BF16 = jnp.bfloat16
+
+
+def _dot(a, b, contract=((1,), (0,))):
+    return lax.dot_general(a, b, (contract, ((), ())), preferred_element_type=F32)
+
+
+NT = ((1,), (1,))
+
+
+def _iota(shape, dim):
+    return lax.broadcasted_iota(jnp.int32, shape, dim)
+
+
+def _params():
+    return pltpu.CompilerParams(vmem_limit_bytes=VMEM)
+
+
+def gather_all(block, devices):
+    def swap(x, m):
+        return lax.ppermute(x, "nodes", [(i, i ^ m) for i in range(devices)])
+
+    have = {0: block}
+    m = devices // 2
+    while m > 1:
+        have.update({k | m: swap(x, m) for k, x in sorted(have.items(), reverse=True)})
+        m //= 2
+    have.update({k | 1: swap(x, 1) for k, x in sorted(have.items())})
+    return [have[m] for m in range(devices)]
+
+
+def pack_kernel(devices, feat_ref, cluster_ref, slot_ref, label_ref, out_ref):
+    rows = feat_ref.shape[0]
+    per = rows // devices
+    mine = lax.axis_index("nodes") % (LANES // per)
+    cluster = cluster_ref[...]
+    member = (_iota((devices, rows), 0) == cluster).astype(F32)
+    before = (_iota((rows, rows), 0) < _iota((rows, rows), 1)).astype(BF16)
+    rank = jnp.sum(member * _dot(member.astype(BF16), before), axis=0, keepdims=True).astype(jnp.int32)
+    take = (_iota((rows, rows), 0) == cluster * per + rank).astype(BF16)
+    out_ref[0:devices] = _dot(take, feat_ref[...]).astype(BF16).reshape(devices, per, feat_ref.shape[1])
+    place = (_iota((LANES, rows), 0) == mine * per + rank).astype(BF16)
+    slots = (member * (slot_ref[...] - rows // 2).astype(F32)).astype(BF16)
+    out_ref[devices, 0:SUB] = _dot(slots, place, NT).astype(BF16)
+    out_ref[devices, SUB : 2 * SUB] = label_ref[...].astype(BF16)
+
+
+def pack(features, cluster, slot, labels, devices):
+    rows, width = features.shape
+    per = rows // devices
+    padded = jnp.pad(labels.reshape(rows // LANES, LANES).astype(F32), ((0, SUB - rows // LANES), (0, 0)))
+    return pl.pallas_call(
+        lambda *refs: pack_kernel(devices, *refs),
+        out_shape=jax.ShapeDtypeStruct((devices + 1, per, width), BF16),
+        compiler_params=_params(),
+        name="pack_rows",
+    )(features, cluster.reshape(1, rows), slot.reshape(1, rows), padded)
+
+
+def turn_kernel(a_ref, o_ref):
+    side = SUB * SUB
+    row = _iota((side, side), 0)
+    move = ((row % SUB) * SUB + row // SUB == _iota((side, side), 1)).astype(BF16)
+    for b in range(a_ref.shape[0] // SUB):
+        for j in range(a_ref.shape[1] // (2 * SUB)):
+            halves = [
+                a_ref[SUB * b : SUB * (b + 1), SUB * k : SUB * (k + 1), :].reshape(side, LANES)
+                for k in (2 * j, 2 * j + 1)
+            ]
+            moved = _dot(move, jnp.concatenate(halves, axis=1)).astype(BF16)
+            for h in range(2):
+                k = 2 * j + h
+                o_ref[0, SUB * k : SUB * (k + 1), SUB * b : SUB * (b + 1), :] = moved[
+                    :, LANES * h : LANES * (h + 1)
+                ].reshape(SUB, SUB, LANES)
+
+
+def turn(adjacency):
+    rows, neigh, tile = adjacency.shape
+    tiles = rows // tile
+    return pl.pallas_call(
+        turn_kernel,
+        grid=(tiles,),
+        in_specs=[pl.BlockSpec((tile, neigh, tile), lambda t: (t, 0, 0))],
+        out_specs=pl.BlockSpec((1, neigh, tile, tile), lambda t: (t, 0, 0, 0)),
+        out_shape=jax.ShapeDtypeStruct((tiles, neigh, tile, tile), BF16),
+        compiler_params=_params(),
+        name="turn_adjacency",
+    )(adjacency)
+
+
+def aggregate_kernel(devices, *refs):
+    blocks = refs[:devices]
+    adj_ref, halo_ref, slots_ref = refs[devices : devices + 3]
+    px_ref, labels_ref, agg_ref = refs[devices + 3 : devices + 6]
+    got, meta, adj, sems, adj_sems = refs[devices + 6 :]
+    me = lax.axis_index("nodes")
+    per = blocks[0].shape[1]
+    rows = devices * per
+    tiles, neigh = adj.shape[0], adj.shape[1]
+    group = LANES // per
+
+    adj_copies = [pltpu.make_async_copy(adj_ref.at[t], adj.at[t], adj_sems.at[t]) for t in range(tiles)]
+    copies = []
+    for m, block in enumerate(blocks):
+        owner = me ^ m
+        at = pl.ds(pl.multiple_of(owner * per, per), per)
+        copies.append(pltpu.make_async_copy(block.at[0:devices], got.at[:, at, :], sems.at[0, m]))
+        copies.append(pltpu.make_async_copy(block.at[devices], meta.at[owner], sems.at[1, m]))
+    for copy in copies + adj_copies:
+        copy.start()
+    for copy in copies:
+        copy.wait()
+
+    labels_ref[...] = meta[:, SUB : 2 * SUB, :]
+    slots = [
+        sum(meta[q * group + j, 0:SUB, :].astype(F32) for j in range(group)) for q in range(devices // group)
+    ]
+    slots = jnp.concatenate(slots, axis=1).astype(jnp.int32)
+    position = _iota((rows, rows), 0) - rows // 2
+    for p in range(devices):
+        put = (position == slots[p : p + 1, :]).astype(BF16)
+        px_ref[p * rows : (p + 1) * rows, :] = _dot(put, got[p]).astype(BF16)
+
+    for t in range(tiles):
+        adj_copies[t].wait()
+        total = jnp.zeros((TILE, px_ref.shape[1]), F32)
+        for k in range(0, neigh, 2):
+            sources = []
+            for j in (k, k + 1):
+                tile = halo_ref[0, slots_ref[t, j]]
+                sources.append(px_ref[pl.ds(pl.multiple_of(tile * TILE, TILE), TILE), :])
+            weights = jnp.concatenate([adj[t, k], adj[t, k + 1]], axis=1)
+            total += _dot(weights, jnp.concatenate(sources, axis=0))
+        agg_ref[t * TILE : (t + 1) * TILE, :] = total.astype(BF16)
+
+
+def aggregate(blocks, turned, halo_tiles, tile_slots, devices):
+    per, width = blocks[0].shape[1:]
+    rows = devices * per
+    anywhere = pl.BlockSpec(memory_space=pl.ANY)
+    scalars = pl.BlockSpec(memory_space=pltpu.SMEM)
+    vmem = pl.BlockSpec(memory_space=pltpu.VMEM)
+    return pl.pallas_call(
+        lambda *refs: aggregate_kernel(devices, *refs),
+        in_specs=[anywhere] * (devices + 1) + [scalars] * 2,
+        out_specs=[vmem] * 3,
+        out_shape=[
+            jax.ShapeDtypeStruct((devices * rows, width), BF16),
+            jax.ShapeDtypeStruct((devices, SUB, LANES), BF16),
+            jax.ShapeDtypeStruct((rows, width), BF16),
+        ],
+        scratch_shapes=[
+            pltpu.VMEM((devices, rows, width), BF16),
+            pltpu.VMEM((devices, 2 * SUB, LANES), BF16),
+            pltpu.VMEM(turned.shape, BF16),
+            pltpu.SemaphoreType.DMA((2, devices)),
+            pltpu.SemaphoreType.DMA((turned.shape[0],)),
+        ],
+        compiler_params=_params(),
+        name="aggregate",
+    )(*blocks, turned, halo_tiles, tile_slots)
+
+
+def learn_kernel(devices, classes, *refs):
+    blocks = refs[:devices]
+    px_ref, labels_ref, w_in_t_ref, w_out_ref, w_out_t_ref, bias_ref = refs[devices : devices + 6]
+    self_ref, neigh_ref, out_ref, class_ref = refs[devices + 6 : devices + 10]
+    x, hid, log, lse_all, sems = refs[devices + 10 :]
+    me = lax.axis_index("nodes")
+    rows, width = blocks[0].shape
+    padded = log.shape[1]
+    copies = []
+    for m, block in enumerate(blocks):
+        owner = me ^ m
+        copies.append(pltpu.make_async_copy(block, x.at[owner, :, pl.ds(width, width)], sems.at[0, m]))
+        source = px_ref.at[pl.ds(pl.multiple_of(m * rows, rows), rows), :]
+        copies.append(pltpu.make_async_copy(source, x.at[m, :, pl.ds(0, width)], sems.at[1, m]))
+    for copy in copies:
+        copy.start()
+    for copy in copies:
+        copy.wait()
+
+    kinds = _iota((padded, rows), 0)
+
+    def is_class(s):
+        held = labels_ref[s].astype(F32)
+        label = jnp.concatenate([held[j : j + 1, :] for j in range(rows // LANES)], axis=1)
+        return kinds == label.astype(jnp.int32)
+
+    def fold(a):
+        return sum(a[:, LANES * j : LANES * (j + 1)] for j in range(rows // LANES))
+
+    def forward(s, carry):
+        loss, count = carry
+        pre = _dot(w_in_t_ref[...], x[s], NT)
+        hidden = jnp.maximum(pre, 0.0).astype(BF16)
+        hid[s] = hidden
+        logits = _dot(w_out_t_ref[...], hidden) + bias_ref[...]
+        log[s] = logits
+        lse = jnp.log(jnp.sum(jnp.exp(logits), axis=0, keepdims=True))
+        lse_all[s] = lse
+        hot = is_class(s)
+        picked = jnp.sum(jnp.where(hot, logits, 0.0), axis=0, keepdims=True)
+        loss += fold(jnp.where(hot, lse - picked, 0.0))
+        count += fold(hot.astype(F32))
+        return loss, count
+
+    zero = jnp.zeros((padded, LANES), F32)
+    loss, count = lax.fori_loop(0, devices, forward, (zero, zero))
+    loss = jnp.sum(loss, axis=1, keepdims=True)
+    count = jnp.sum(count, axis=1, keepdims=True)
+    real = _iota((padded, 1), 0) < classes
+    difficulty = jnp.where(real, (loss + 1.0) / (count + 1.0), 0.0)
+    weight = difficulty / (jnp.sum(difficulty, axis=0, keepdims=True) / classes)
+    share = 1.0 / (1.0 + jnp.sum(count, axis=0, keepdims=True))
+    class_ref[...] = jnp.transpose(jnp.broadcast_to(weight, (padded, LANES)))[0:1, 0:classes]
+    scaled = weight * share
+
+    def backward(s, carry):
+        grad_in, grad_out = carry
+        hot = is_class(s)
+        row = jnp.sum(jnp.where(hot, scaled, 0.0), axis=0, keepdims=True)
+        probs = jnp.exp(log[s] - lse_all[s])
+        dlogits = (row * (probs - hot.astype(F32))).astype(BF16)
+        hidden = hid[s]
+        grad_out += _dot(hidden, dlogits, NT)
+        dhidden = _dot(w_out_ref[...], dlogits)
+        dpre = jnp.where(hidden > 0, dhidden, 0.0).astype(BF16)
+        grad_in += _dot(dpre, x[s])
+        return grad_in, grad_out
+
+    units = hid.shape[1]
+    start = (jnp.zeros((units, 2 * width), F32), jnp.zeros((units, padded), F32))
+    grad_in, grad_out = lax.fori_loop(0, devices, backward, start)
+    grad_in = jnp.transpose(grad_in)
+    self_ref[...] = grad_in[0:width]
+    neigh_ref[...] = grad_in[width : 2 * width]
+    out_ref[...] = grad_out[:, 0:classes]
+
+
+def learn(blocks, part_x, labels, w_in, w_out, b_out, devices):
+    rows, width = blocks[0].shape
+    units, classes = w_out.shape
+    padded = -(-classes // SUB) * SUB
+    extra = padded - classes
+    w_out_p = jnp.pad(w_out, ((0, 0), (0, extra)))
+    bias = jnp.pad(b_out, (0, extra), constant_values=-1e30).reshape(padded, 1)
+    anywhere = pl.BlockSpec(memory_space=pl.ANY)
+    vmem = pl.BlockSpec(memory_space=pltpu.VMEM)
+    return pl.pallas_call(
+        lambda *refs: learn_kernel(devices, classes, *refs),
+        in_specs=[anywhere] * (devices + 1) + [vmem] * 5,
+        out_specs=[vmem] * 4,
+        out_shape=[
+            jax.ShapeDtypeStruct((width, units), F32),
+            jax.ShapeDtypeStruct((width, units), F32),
+            jax.ShapeDtypeStruct((units, classes), F32),
+            jax.ShapeDtypeStruct((1, classes), F32),
+        ],
+        scratch_shapes=[
+            pltpu.VMEM((devices, rows, 2 * width), BF16),
+            pltpu.VMEM((devices, units, rows), BF16),
+            pltpu.VMEM((devices, padded, rows), F32),
+            pltpu.VMEM((devices, 1, rows), F32),
+            pltpu.SemaphoreType.DMA((2, devices)),
+        ],
+        compiler_params=_params(),
+        name="learn",
+    )(*blocks, part_x, labels, w_in.T, w_out_p, w_out_p.T, bias)
+
+
+def gathered_body(
+    features, cluster, slot, halo_tiles, tile_slots, adjacency, labels, w_self, w_neigh, w_out, b_out
+):
+    rows = features.shape[0]
+    devices = lax.axis_size("nodes")
+    packed = pack(features, cluster, slot, labels, devices)
+    turned = turn(adjacency)
+    part_x, all_labels, agg = aggregate(gather_all(packed, devices), turned, halo_tiles, tile_slots, devices)
+    w_in = jnp.concatenate([w_self, w_neigh], axis=0)
+    mine = lax.dynamic_slice_in_dim(part_x, lax.axis_index("nodes") * rows, rows, 0)
+    pre = _dot(jnp.concatenate([mine, agg], axis=1), w_in)
+    hidden = jnp.maximum(pre, 0.0).astype(BF16)
+    grad_self, grad_neigh, grad_out, class_weight = learn(
+        gather_all(agg, devices), part_x, all_labels, w_in, w_out, b_out, devices
+    )
+    return hidden, grad_self, grad_neigh, grad_out, class_weight.reshape(-1)
+
+
+def split_body(
+    features, cluster, slot, halo_tiles, tile_slots, adjacency, labels, w_self, w_neigh, w_out, b_out
 ):
     rows = features.shape[0]
     width = features.shape[1]
@@ -72,6 +356,14 @@
 
 
 def solution(mesh):
+    def body(*args):
+        devices = mesh.shape["nodes"]
+        rows = args[0].shape[0]
+        per = rows // devices
+        classes = args[9].shape[1]
+        fits = devices & (devices - 1) == 0 and devices <= SUB and per == 2 * SUB and rows <= 512 and classes <= 256
+        return (gathered_body if fits else split_body)(*args)
+
     return jax.shard_map(
         body,
         mesh=mesh,

time: 242 us -> 89.4 us (0.37)
  waiting for transfers between devices: 135 us -> 17.2 us
  Pallas kernels: 0 us -> 35.3 us
  blocking collectives: 31.4 us -> 0 us
  local copies, waits for them, and re-layouts: 25.2 us -> 8.18 us
  between operations: 15.5 us -> 0.88 us
  matrix products: 15.6 us -> 1.84 us
  starting transfers between devices: 11.2 us -> 24 us
  other arithmetic: 7.46 us -> 1.57 us
    psum x1 -> x0, waiting for transfers between devices: 87.8 us -> none  [body(): lax.psum((part_self, part_neigh, part_out), 'nodes')]
    all_gather x1 -> x0, waiting for transfers between devices: 36.4 us -> none  [body(): gathered = lax.all_gather(part_x, 'nodes', axis=0, tiled=True)]
    pallas_call x0 -> x4, Pallas kernels: none -> 35.3 us  [the longest x1 19.9 us: learn(): pl.pallas_call(lambda *refs: learn_kernel(devices, classes, *refs), in_sp...]
    psum x1 -> x0, blocking collectives: 31.4 us -> none  [body(): loss_sum, counts = lax.psum((local_loss, local_counts), 'nodes')]
    ppermute x0 -> x30, starting transfers between devices: none -> 24 us  [swap(): return lax.ppermute(x, 'nodes', [(i, i ^ m) for i in range(devices)])]
    ppermute x0 -> x30, waiting for transfers between devices: none -> 17.2 us  [swap(): return lax.ppermute(x, 'nodes', [(i, i ^ m) for i in range(devices)])]
    gather x4 -> x0, local copies, waits for them, and re-layouts: 16.7 us -> none  [the longest x1 8.62 us: body(): sources = halo[tile_slots]]
    dot_general x8 -> x1, matrix products: 15.6 us -> 1.84 us  [_dot(): lax.dot_general(a, b, (contract, ((), ())), preferred_element_type=F32)]
  transfers between devices with their start and end apart: 4 -> 30, of which waited for: 4 -> 7; matrix products, arithmetic and copies ran while one was open for 2% -> 7% of each run, Pallas kernels for 0% -> 9%
where the time goes in v1:
time: 89.4 us; the launch traced here: 89 us
  Pallas kernels  35.3 us (39%)
  starting transfers between devices  24 us (27%)
  waiting for transfers between devices  17.2 us (19%)
  local copies, waits for them, and re-layouts  8.18 us (9%)
  matrix products  1.84 us (2%)
  other arithmetic  1.57 us (2%)
    ppermute x30, starting transfers between devices, swap(): return lax.ppermute(x, 'nodes', [(i, i ^ m) for i in range(devices)])  24 us
    pallas_call x1, Pallas kernels, learn(): pl.pallas_call(lambda *refs: learn_kernel(devices, classes, *refs), in_sp...  19.9 us
    ppermute x30, waiting for transfers between devices, swap(): return lax.ppermute(x, 'nodes', [(i, i ^ m) for i in range(devices)])  17.2 us
    pallas_call x1, Pallas kernels, turn(): pl.pallas_call(turn_kernel, grid=(tiles,), in_specs=[pl.BlockSpec((tile,...  8.26 us
    unnamed x30, local copies, waits for them, and re-layouts  7.11 us
    pallas_call x1, Pallas kernels, aggregate(): pl.pallas_call(lambda *refs: aggregate_kernel(devices, *refs), in_specs=[...  6.64 us
    dot_general x1, matrix products, _dot(): lax.dot_general(a, b, (contract, ((), ())), preferred_element_type=F32)  1.84 us
  transfers between devices with their start and end apart: 30, of which 7 were waited for; matrix products, arithmetic and copies ran while one was open for 7% of the time, Pallas kernels for 9%

profile of v1, /device:TPU:0, one launch (start us, length us, event | category | flops | bytes accessed | tf_op | source)
XLA Modules:
  0.0 89.0 jit_solution(3041106973058930990)
XLA Ops:
  0.6 0.7 convert_bitcast_fusion
  1.3 0.9 %copy-done.4 = bf16[512,128]{1,0:T(8,128)(2,1)S(1)} copy-done((bf16[512,128]{1,0:T(8,128)(2,1)S(1)}, bf16[512,128]{1,0:T(8,128)(2,1)}, u32[]{:S(2)}) %copy-start.4) | copy-done | bytes 131096
  2.2 0.7 copy-done.5
  2.9 0.7 copy-done.6
  3.6 0.5 pack_rows.1.refs_0_
  4.1 4.1 %collective-permute-start.7 = (bf16[17,32,128]{2,1,0:T(8,128)(2,1)S(1)}, bf16[17,32,128]{2,1,0:T(8,128)(2,1)S(1)}, u32[]{:S(2)}, u32[]{:S(2)}) collective-permute-start(bf16[17,32,128]{2,1,0:T(8,128)(2,1)S(1)} %pack_rows.1.refs_0_), channel_id=1, source_target_pairs={{0,8},{1,9},{2,10},{3,11},{4,12},{5,13},{6,14},{7,15},{8,0},{9,1},... | collective-permute-start | bytes 417800 | tf_op jit(solution)/shard_map/ppermute | solution.py:33
  8.2 1.6 %collective-permute-start.3 = (bf16[17,32,128]{2,1,0:T(8,128)(2,1)S(1)}, bf16[17,32,128]{2,1,0:T(8,128)(2,1)S(1)}, u32[]{:S(2)}, u32[]{:S(2)}) collective-permute-start(bf16[17,32,128]{2,1,0:T(8,128)(2,1)S(1)} %pack_rows.1.refs_0_), channel_id=1, source_target_pairs={{0,4},{1,5},{2,6},{3,7},{4,0},{5,1},{6,2},{7,3},{8,12},{9,13},{10,... | collective-permute-start | bytes 417800 | tf_op jit(solution)/shard_map/ppermute | solution.py:33
  9.8 1.5 %collective-permute-start.1 = (bf16[17,32,128]{2,1,0:T(8,128)(2,1)S(1)}, bf16[17,32,128]{2,1,0:T(8,128)(2,1)S(1)}, u32[]{:S(2)}, u32[]{:S(2)}) collective-permute-start(bf16[17,32,128]{2,1,0:T(8,128)(2,1)S(1)} %pack_rows.1.refs_0_), channel_id=1, source_target_pairs={{0,2},{1,3},{2,0},{3,1},{4,6},{5,7},{6,4},{7,5},{8,10},{9,11},{10,... | collective-permute-start | bytes 417800 | tf_op jit(solution)/shard_map/ppermute | solution.py:33
  11.3 3.7 %collective-permute-done.7.refs_8_ = bf16[17,32,128]{2,1,0:T(8,128)(2,1)S(1)} collective-permute-done((bf16[17,32,128]{2,1,0:T(8,128)(2,1)S(1)}, bf16[17,32,128]{2,1,0:T(8,128)(2,1)S(1)}, u32[]{:S(2)}, u32[]{:S(2)}) %collective-permute-start.7) | collective-permute-done | bytes 139296 | tf_op jit(solution)/shard_map/ppermute | solution.py:33
  15.0 0.6 collective-permute-start.11
  15.6 1.5 %collective-permute-start.9 = (bf16[17,32,128]{2,1,0:T(8,128)(2,1)S(1)}, bf16[17,32,128]{2,1,0:T(8,128)(2,1)S(1)}, u32[]{:S(2)}, u32[]{:S(2)}) collective-permute-start(bf16[17,32,128]{2,1,0:T(8,128)(2,1)S(1)} %collective-permute-done.7.refs_8_), channel_id=1, source_target_pairs={{0,2},{1,3},{2,0},{3,1},{4,6},{5,7},{6,4},{7,5},{8,10},{9,11},{10,... | collective-permute-start | bytes 417800 | tf_op jit(solution)/shard_map/ppermute | solution.py:33
  17.1 0.5 collective-permute-start.5
  17.6 0.5 collective-permute-start.4
  18.2 1.9 %collective-permute-done.11.refs_12_ = bf16[17,32,128]{2,1,0:T(8,128)(2,1)S(1)} collective-permute-done((bf16[17,32,128]{2,1,0:T(8,128)(2,1)S(1)}, bf16[17,32,128]{2,1,0:T(8,128)(2,1)S(1)}, u32[]{:S(2)}, u32[]{:S(2)}) %collective-permute-start.11) | collective-permute-done | bytes 139296 | tf_op jit(solution)/shard_map/ppermute | solution.py:33
  20.0 1.6 %collective-permute-start.13 = (bf16[17,32,128]{2,1,0:T(8,128)(2,1)S(1)}, bf16[17,32,128]{2,1,0:T(8,128)(2,1)S(1)}, u32[]{:S(2)}, u32[]{:S(2)}) collective-permute-start(bf16[17,32,128]{2,1,0:T(8,128)(2,1)S(1)} %collective-permute-done.11.refs_12_), channel_id=1, source_target_pairs={{0,2},{1,3},{2,0},{3,1},{4,6},{5,7},{6,4},{7,5},{8,10},{9,11},{10,... | collective-permute-start | bytes 417800 | tf_op jit(solution)/shard_map/ppermute | solution.py:33
  21.6 0.6 collective-permute-done.9.refs_10_
  22.2 3.0 %collective-permute-done.5.refs_6_ = bf16[17,32,128]{2,1,0:T(8,128)(2,1)S(1)} collective-permute-done((bf16[17,32,128]{2,1,0:T(8,128)(2,1)S(1)}, bf16[17,32,128]{2,1,0:T(8,128)(2,1)S(1)}, u32[]{:S(2)}, u32[]{:S(2)}) %collective-permute-start.5) | collective-permute-done | bytes 139296 | tf_op jit(solution)/shard_map/ppermute | solution.py:33
  25.2 0.5 collective-permute-start.10
  25.7 0.1 collective-permute-start.6
  25.8 1.1 %collective-permute-done.13.refs_14_ = bf16[17,32,128]{2,1,0:T(8,128)(2,1)S(1)} collective-permute-done((bf16[17,32,128]{2,1,0:T(8,128)(2,1)S(1)}, bf16[17,32,128]{2,1,0:T(8,128)(2,1)S(1)}, u32[]{:S(2)}, u32[]{:S(2)}) %collective-permute-start.13) | collective-permute-done | bytes 139296 | tf_op jit(solution)/shard_map/ppermute | solution.py:33
  26.9 8.3 %turn_adjacency.1.refs_16_ = bf16[4,64,128,128]{3,2,1,0:T(8,128)(2,1)} custom-call(bf16[512,64,128]{2,1,0:T(8,128)(2,1)} %a_ref.1), custom_call_target="tpu_custom_call" | custom-call | tf_op jit(solution)/shard_map/turn_adjacency/pallas_call | solution.py:93
  35.2 6.6 %aggregate.1 = (bf16[8192,128]{1,0:T(8,128)(2,1)S(1)}, bf16[16,16,128]{2,1,0:T(8,128)(2,1)S(1)}, bf16[512,128]{1,0:T(8,128)(2,1)S(1)}) custom-call(bf16[17,32,128]{2,1,0:T(8,128)(2,1)S(1)} %pack_rows.1.refs_0_, bf16[17,32,128]{2,1,0:T(8,128)(2,1)S(1)} %collective-permute-done.refs_1_, bf16[17,32,128]{2,1,0:T(8,128)(2,1)S(1)} %collective-permute-done.1.refs_2_, ...), custom_call_target="tpu_custom_call" | custom-call | tf_op jit(solution)/shard_map/aggregate/pallas_call | solution.py:156
  41.9 3.4 %collective-permute-start.22 = (bf16[512,128]{1,0:T(8,128)(2,1)S(1)}, bf16[512,128]{1,0:T(8,128)(2,1)S(1)}, u32[]{:S(2)}, u32[]{:S(2)}) collective-permute-start(bf16[512,128]{1,0:T(8,128)(2,1)S(1)} %get-tuple-element.13.refs_0_), channel_id=1, source_target_pairs={{0,8},{1,9},{2,10},{3,11},{4,12},{5,13},{6,14},{7,15},{8,0},{9,1},... | collective-permute-start | bytes 393224 | tf_op jit(solution)/shard_map/ppermute | solution.py:33
  45.3 0.3 collective-permute-start.18
  45.6 1.5 %collective-permute-start.16 = (bf16[512,128]{1,0:T(8,128)(2,1)S(1)}, bf16[512,128]{1,0:T(8,128)(2,1)S(1)}, u32[]{:S(2)}, u32[]{:S(2)}) collective-permute-start(bf16[512,128]{1,0:T(8,128)(2,1)S(1)} %get-tuple-element.13.refs_0_), channel_id=1, source_target_pairs={{0,2},{1,3},{2,0},{3,1},{4,6},{5,7},{6,4},{7,5},{8,10},{9,11},{10,... | collective-permute-start | bytes 393224 | tf_op jit(solution)/shard_map/ppermute | solution.py:33
  47.1 5.0 %collective-permute-done.22.refs_8_ = bf16[512,128]{1,0:T(8,128)(2,1)S(1)} collective-permute-done((bf16[512,128]{1,0:T(8,128)(2,1)S(1)}, bf16[512,128]{1,0:T(8,128)(2,1)S(1)}, u32[]{:S(2)}, u32[]{:S(2)}) %collective-permute-start.22) | collective-permute-done | bytes 131104 | tf_op jit(solution)/shard_map/ppermute | solution.py:33
  52.1 1.5 %collective-permute-start.24 = (bf16[512,128]{1,0:T(8,128)(2,1)S(1)}, bf16[512,128]{1,0:T(8,128)(2,1)S(1)}, u32[]{:S(2)}, u32[]{:S(2)}) collective-permute-start(bf16[512,128]{1,0:T(8,128)(2,1)S(1)} %collective-permute-done.22.refs_8_), channel_id=1, source_target_pairs={{0,2},{1,3},{2,0},{3,1},{4,6},{5,7},{6,4},{7,5},{8,10},{9,11},{10,... | collective-permute-start | bytes 393224 | tf_op jit(solution)/shard_map/ppermute | solution.py:33
  53.7 0.0 collective-permute-done.18.refs_4_
  53.7 1.5 %collective-permute-start.20 = (bf16[512,128]{1,0:T(8,128)(2,1)S(1)}, bf16[512,128]{1,0:T(8,128)(2,1)S(1)}, u32[]{:S(2)}, u32[]{:S(2)}) collective-permute-start(bf16[512,128]{1,0:T(8,128)(2,1)S(1)} %collective-permute-done.18.refs_4_), channel_id=1, source_target_pairs={{0,2},{1,3},{2,0},{3,1},{4,6},{5,7},{6,4},{7,5},{8,10},{9,11},{10,... | collective-permute-start | bytes 393224 | tf_op jit(solution)/shard_map/ppermute | solution.py:33
  55.2 0.5 collective-permute-start.17
  55.7 1.9 %collective-permute-done.26.refs_12_ = bf16[512,128]{1,0:T(8,128)(2,1)S(1)} collective-permute-done((bf16[512,128]{1,0:T(8,128)(2,1)S(1)}, bf16[512,128]{1,0:T(8,128)(2,1)S(1)}, u32[]{:S(2)}, u32[]{:S(2)}) %collective-permute-start.26) | collective-permute-done | bytes 131104 | tf_op jit(solution)/shard_map/ppermute | solution.py:33
  57.6 1.5 %collective-permute-start.28 = (bf16[512,128]{1,0:T(8,128)(2,1)S(1)}, bf16[512,128]{1,0:T(8,128)(2,1)}, u32[]{:S(2)}, u32[]{:S(2)}) collective-permute-start(bf16[512,128]{1,0:T(8,128)(2,1)S(1)} %collective-permute-done.26.refs_12_), channel_id=1, source_target_pairs={{0,2},{1,3},{2,0},{3,1},{4,6},{5,7},{6,4},{7,5},{8,10},{9,11},{10,... | collective-permute-start | bytes 393224 | tf_op jit(solution)/shard_map/ppermute | solution.py:33
  59.1 0.8 copy.25
  59.9 0.7 copy.20
  60.6 0.7 copy.21
  61.3 0.1 copy.23.refs_21_
  61.5 0.9 %pad.13.clone.refs_19_ = bf16[256,176]{1,0:T(8,128)(2,1)S(1)} pad(bf16[256,172]{1,0:T(8,128)(2,1)} %copy.25, bf16[]{:T(256)} %constant.15.clone.1), padding=0_0x0_4 | pad | bytes 178178 | tf_op jit(solution)/shard_map/jit(_pad)/pad | solution.py:259
  62.4 0.9 fusion.4.refs_18_
  63.3 0.1 collective-permute-start.23
  63.4 0.5 collective-permute-start.27
  63.9 0.1 collective-permute-start.21
  64.0 0.4 collective-permute-start.25
  64.4 0.1 collective-permute-start.29
  64.5 1.8 %fusion = bf16[512,256]{1,0:T(8,128)(2,1)} fusion(bf16[512,128]{1,0:T(8,128)(2,1)S(1)} %get-tuple-element.13.refs_0_, bf16[512,128]{1,0:T(8,128)(2,1)S(1)} %constant_dynamic-slice_fusion, bf16[128,256]{0,1:T(8,128)(2,1)} %copy.21, bf16[128,256]{0,1:T(8,128)(2,1)} %copy.20), kind=kOutput, calls=%fused_computation.1 | convolution fusion | flops 68157440 | bytes 655360 | tf_op jit(solution)/shard_map/dot_general | solution.py:17
  66.4 0.9 %copy-done.1 = bf16[512,128]{1,0:T(8,128)(2,1)S(1)} copy-done((bf16[512,128]{1,0:T(8,128)(2,1)S(1)}, bf16[512,128]{1,0:T(8,128)(2,1)}, u32[]{:S(2)}) %copy-start.1) | copy-done | bytes 131096
  67.3 0.9 %copy-done.3 = bf16[512,128]{1,0:T(8,128)(2,1)S(1)} copy-done((bf16[512,128]{1,0:T(8,128)(2,1)S(1)}, bf16[512,128]{1,0:T(8,128)(2,1)}, u32[]{:S(2)}) %copy-start.3) | copy-done | bytes 131096
  68.2 19.9 %learn.1 = (f32[128,256]{1,0:T(8,128)}, f32[128,256]{1,0:T(8,128)}, f32[256,172]{1,0:T(8,128)S(1)}, f32[1,172]{1,0:T(1,128)}) custom-call(bf16[512,128]{1,0:T(8,128)(2,1)S(1)} %get-tuple-element.13.refs_0_, bf16[512,128]{1,0:T(8,128)(2,1)S(1)} %collective-permute-done.15.refs_1_, bf16[512,128]{1,0:T(8,128)(2,1)S(1)} %collective-permute-done.16.refs_2_, ...), custom_call_target="tpu_custom_call" | custom-call | tf_op jit(solution)/shard_map/learn/pallas_call | solution.py:263
  88.2 0.8 copy.24
  (55 shorter events, 0.2 us)
Async XLA Ops:
  1.3 0.9 %copy-start.4 = (bf16[512,128]{1,0:T(8,128)(2,1)S(1)}, bf16[512,128]{1,0:T(8,128)(2,1)}, u32[]{:S(2)}) copy-start(bf16[512,128]{1,0:T(8,128)(2,1)} %refs_0_.1) | copy-start | bytes 393220
  2.2 0.7 copy-start.5
  2.9 0.7 copy-start.6
  4.1 31.1 %copy-start.7 = (s32[4,64]{1,0:T(4,128)S(1)}, s32[4,64]{1,0:T(4,128)}, u32[]{:S(2)}) copy-start(s32[4,64]{1,0:T(4,128)} %refs_18_.1) | copy-start | bytes 3076
  4.1 31.1 %copy-start.8 = (s32[1,64]{1,0:T(1,128)S(1)}, s32[1,64]{1,0:T(1,128)}, u32[]{:S(2)}) copy-start(s32[1,64]{1,0:T(1,128)} %refs_17_.1) | copy-start | bytes 772
  4.1 10.9 %collective-permute-start.7 = (bf16[17,32,128]{2,1,0:T(8,128)(2,1)S(1)}, bf16[17,32,128]{2,1,0:T(8,128)(2,1)S(1)}, u32[]{:S(2)}, u32[]{:S(2)}) collective-permute-start(bf16[17,32,128]{2,1,0:T(8,128)(2,1)S(1)} %pack_rows.1.refs_0_), channel_id=1, source_target_pairs={{0,8},{1,9},{2,10},{3,11},{4,12},{5,13},{6,14},{7,15},{8,0},{9,1},... | collective-permute-start | bytes 417800 | tf_op jit(solution)/shard_map/ppermute | solution.py:33
  8.2 8.9 %collective-permute-start.3 = (bf16[17,32,128]{2,1,0:T(8,128)(2,1)S(1)}, bf16[17,32,128]{2,1,0:T(8,128)(2,1)S(1)}, u32[]{:S(2)}, u32[]{:S(2)}) collective-permute-start(bf16[17,32,128]{2,1,0:T(8,128)(2,1)S(1)} %pack_rows.1.refs_0_), channel_id=1, source_target_pairs={{0,4},{1,5},{2,6},{3,7},{4,0},{5,1},{6,2},{7,3},{8,12},{9,13},{10,... | collective-permute-start | bytes 417800 | tf_op jit(solution)/shard_map/ppermute | solution.py:33
  9.8 7.8 %collective-permute-start.1 = (bf16[17,32,128]{2,1,0:T(8,128)(2,1)S(1)}, bf16[17,32,128]{2,1,0:T(8,128)(2,1)S(1)}, u32[]{:S(2)}, u32[]{:S(2)}) collective-permute-start(bf16[17,32,128]{2,1,0:T(8,128)(2,1)S(1)} %pack_rows.1.refs_0_), channel_id=1, source_target_pairs={{0,2},{1,3},{2,0},{3,1},{4,6},{5,7},{6,4},{7,5},{8,10},{9,11},{10,... | collective-permute-start | bytes 417800 | tf_op jit(solution)/shard_map/ppermute | solution.py:33
  11.3 6.3 %collective-permute-start = (bf16[17,32,128]{2,1,0:T(8,128)(2,1)S(1)}, bf16[17,32,128]{2,1,0:T(8,128)(2,1)S(1)}, u32[]{:S(2)}, u32[]{:S(2)}) collective-permute-start(bf16[17,32,128]{2,1,0:T(8,128)(2,1)S(1)} %pack_rows.1.refs_0_), channel_id=1, source_target_pairs={{0,1},{1,0},{2,3},{3,2},{4,5},{5,4},{6,7},{7,6},{8,9},{9,8},{10,11... | collective-permute-start | bytes 417800 | tf_op jit(solution)/shard_map/ppermute | solution.py:33
  15.0 5.1 %collective-permute-start.11 = (bf16[17,32,128]{2,1,0:T(8,128)(2,1)S(1)}, bf16[17,32,128]{2,1,0:T(8,128)(2,1)S(1)}, u32[]{:S(2)}, u32[]{:S(2)}) collective-permute-start(bf16[17,32,128]{2,1,0:T(8,128)(2,1)S(1)} %collective-permute-done.7.refs_8_), channel_id=1, source_target_pairs={{0,4},{1,5},{2,6},{3,7},{4,0},{5,1},{6,2},{7,3},{8,12},{9,13},{10,... | collective-permute-start | bytes 417800 | tf_op jit(solution)/shard_map/ppermute | solution.py:33
  15.6 6.6 %collective-permute-start.9 = (bf16[17,32,128]{2,1,0:T(8,128)(2,1)S(1)}, bf16[17,32,128]{2,1,0:T(8,128)(2,1)S(1)}, u32[]{:S(2)}, u32[]{:S(2)}) collective-permute-start(bf16[17,32,128]{2,1,0:T(8,128)(2,1)S(1)} %collective-permute-done.7.refs_8_), channel_id=1, source_target_pairs={{0,2},{1,3},{2,0},{3,1},{4,6},{5,7},{6,4},{7,5},{8,10},{9,11},{10,... | collective-permute-start | bytes 417800 | tf_op jit(solution)/shard_map/ppermute | solution.py:33
  17.1 8.0 %collective-permute-start.5 = (bf16[17,32,128]{2,1,0:T(8,128)(2,1)S(1)}, bf16[17,32,128]{2,1,0:T(8,128)(2,1)S(1)}, u32[]{:S(2)}, u32[]{:S(2)}) collective-permute-start(bf16[17,32,128]{2,1,0:T(8,128)(2,1)S(1)} %collective-permute-done.3.refs_4_), channel_id=1, source_target_pairs={{0,2},{1,3},{2,0},{3,1},{4,6},{5,7},{6,4},{7,5},{8,10},{9,11},{10,... | collective-permute-start | bytes 417800 | tf_op jit(solution)/shard_map/ppermute | solution.py:33
  17.6 7.5 %collective-permute-start.8 = (bf16[17,32,128]{2,1,0:T(8,128)(2,1)S(1)}, bf16[17,32,128]{2,1,0:T(8,128)(2,1)S(1)}, u32[]{:S(2)}, u32[]{:S(2)}) collective-permute-start(bf16[17,32,128]{2,1,0:T(8,128)(2,1)S(1)} %collective-permute-done.7.refs_8_), channel_id=1, source_target_pairs={{0,1},{1,0},{2,3},{3,2},{4,5},{5,4},{6,7},{7,6},{8,9},{9,8},{10,11... | collective-permute-start | bytes 417800 | tf_op jit(solution)/shard_map/ppermute | solution.py:33
  17.6 8.0 %collective-permute-start.4 = (bf16[17,32,128]{2,1,0:T(8,128)(2,1)S(1)}, bf16[17,32,128]{2,1,0:T(8,128)(2,1)S(1)}, u32[]{:S(2)}, u32[]{:S(2)}) collective-permute-start(bf16[17,32,128]{2,1,0:T(8,128)(2,1)S(1)} %collective-permute-done.3.refs_4_), channel_id=1, source_target_pairs={{0,1},{1,0},{2,3},{3,2},{4,5},{5,4},{6,7},{7,6},{8,9},{9,8},{10,11... | collective-permute-start | bytes 417800 | tf_op jit(solution)/shard_map/ppermute | solution.py:33
  20.0 6.8 %collective-permute-start.13 = (bf16[17,32,128]{2,1,0:T(8,128)(2,1)S(1)}, bf16[17,32,128]{2,1,0:T(8,128)(2,1)S(1)}, u32[]{:S(2)}, u32[]{:S(2)}) collective-permute-start(bf16[17,32,128]{2,1,0:T(8,128)(2,1)S(1)} %collective-permute-done.11.refs_12_), channel_id=1, source_target_pairs={{0,2},{1,3},{2,0},{3,1},{4,6},{5,7},{6,4},{7,5},{8,10},{9,11},{10,... | collective-permute-start | bytes 417800 | tf_op jit(solution)/shard_map/ppermute | solution.py:33
  22.2 13.0 %collective-permute-start.2 = (bf16[17,32,128]{2,1,0:T(8,128)(2,1)S(1)}, bf16[17,32,128]{2,1,0:T(8,128)(2,1)S(1)}, u32[]{:S(2)}, u32[]{:S(2)}) collective-permute-start(bf16[17,32,128]{2,1,0:T(8,128)(2,1)S(1)} %collective-permute-done.1.refs_2_), channel_id=1, source_target_pairs={{0,1},{1,0},{2,3},{3,2},{4,5},{5,4},{6,7},{7,6},{8,9},{9,8},{10,11... | collective-permute-start | bytes 417800 | tf_op jit(solution)/shard_map/ppermute | solution.py:33
  25.2 10.0 %collective-permute-start.12 = (bf16[17,32,128]{2,1,0:T(8,128)(2,1)S(1)}, bf16[17,32,128]{2,1,0:T(8,128)(2,1)S(1)}, u32[]{:S(2)}, u32[]{:S(2)}) collective-permute-start(bf16[17,32,128]{2,1,0:T(8,128)(2,1)S(1)} %collective-permute-done.11.refs_12_), channel_id=1, source_target_pairs={{0,1},{1,0},{2,3},{3,2},{4,5},{5,4},{6,7},{7,6},{8,9},{9,8},{10,11... | collective-permute-start | bytes 417800 | tf_op jit(solution)/shard_map/ppermute | solution.py:33
  25.2 10.0 %collective-permute-start.10 = (bf16[17,32,128]{2,1,0:T(8,128)(2,1)S(1)}, bf16[17,32,128]{2,1,0:T(8,128)(2,1)S(1)}, u32[]{:S(2)}, u32[]{:S(2)}) collective-permute-start(bf16[17,32,128]{2,1,0:T(8,128)(2,1)S(1)} %collective-permute-done.9.refs_10_), channel_id=1, source_target_pairs={{0,1},{1,0},{2,3},{3,2},{4,5},{5,4},{6,7},{7,6},{8,9},{9,8},{10,11... | collective-permute-start | bytes 417800 | tf_op jit(solution)/shard_map/ppermute | solution.py:33
  25.7 9.5 %collective-permute-start.6 = (bf16[17,32,128]{2,1,0:T(8,128)(2,1)S(1)}, bf16[17,32,128]{2,1,0:T(8,128)(2,1)S(1)}, u32[]{:S(2)}, u32[]{:S(2)}) collective-permute-start(bf16[17,32,128]{2,1,0:T(8,128)(2,1)S(1)} %collective-permute-done.5.refs_6_), channel_id=1, source_target_pairs={{0,1},{1,0},{2,3},{3,2},{4,5},{5,4},{6,7},{7,6},{8,9},{9,8},{10,11... | collective-permute-start | bytes 417800 | tf_op jit(solution)/shard_map/ppermute | solution.py:33
  26.9 8.3 %collective-permute-start.14 = (bf16[17,32,128]{2,1,0:T(8,128)(2,1)S(1)}, bf16[17,32,128]{2,1,0:T(8,128)(2,1)S(1)}, u32[]{:S(2)}, u32[]{:S(2)}) collective-permute-start(bf16[17,32,128]{2,1,0:T(8,128)(2,1)S(1)} %collective-permute-done.13.refs_14_), channel_id=1, source_target_pairs={{0,1},{1,0},{2,3},{3,2},{4,5},{5,4},{6,7},{7,6},{8,9},{9,8},{10,11... | collective-permute-start | bytes 417800 | tf_op jit(solution)/shard_map/ppermute | solution.py:33
  35.2 23.9 %copy-start.9 = (bf16[256,172]{0,1:T(8,128)(2,1)S(1)}, bf16[256,172]{0,1:T(8,128)(2,1)}, u32[]{:S(2)}) copy-start(bf16[256,172]{0,1:T(8,128)(2,1)} %param.20) | copy-start | bytes 264196
  35.2 24.7 %copy-start.10 = (bf16[128,256]{1,0:T(8,128)(2,1)S(1)}, bf16[128,256]{1,0:T(8,128)(2,1)}, u32[]{:S(2)}) copy-start(bf16[128,256]{1,0:T(8,128)(2,1)} %param.18) | copy-start | bytes 196612
  35.2 25.4 %copy-start.11 = (bf16[128,256]{1,0:T(8,128)(2,1)S(1)}, bf16[128,256]{1,0:T(8,128)(2,1)}, u32[]{:S(2)}) copy-start(bf16[128,256]{1,0:T(8,128)(2,1)} %param.19) | copy-start | bytes 196612
  35.2 26.2 %copy-start.12 = (f32[172]{0:T(256)S(1)}, f32[172]{0:T(256)}, u32[]{:S(2)}) copy-start(f32[172]{0:T(256)} %param.21) | copy-start | bytes 2068
  41.9 10.3 %collective-permute-start.22 = (bf16[512,128]{1,0:T(8,128)(2,1)S(1)}, bf16[512,128]{1,0:T(8,128)(2,1)S(1)}, u32[]{:S(2)}, u32[]{:S(2)}) collective-permute-start(bf16[512,128]{1,0:T(8,128)(2,1)S(1)} %get-tuple-element.13.refs_0_), channel_id=1, source_target_pairs={{0,8},{1,9},{2,10},{3,11},{4,12},{5,13},{6,14},{7,15},{8,0},{9,1},... | collective-permute-start | bytes 393224 | tf_op jit(solution)/shard_map/ppermute | solution.py:33
  45.3 8.3 %collective-permute-start.18 = (bf16[512,128]{1,0:T(8,128)(2,1)S(1)}, bf16[512,128]{1,0:T(8,128)(2,1)S(1)}, u32[]{:S(2)}, u32[]{:S(2)}) collective-permute-start(bf16[512,128]{1,0:T(8,128)(2,1)S(1)} %get-tuple-element.13.refs_0_), channel_id=1, source_target_pairs={{0,4},{1,5},{2,6},{3,7},{4,0},{5,1},{6,2},{7,3},{8,12},{9,13},{10,... | collective-permute-start | bytes 393224 | tf_op jit(solution)/shard_map/ppermute | solution.py:33
  45.6 9.6 %collective-permute-start.16 = (bf16[512,128]{1,0:T(8,128)(2,1)S(1)}, bf16[512,128]{1,0:T(8,128)(2,1)S(1)}, u32[]{:S(2)}, u32[]{:S(2)}) collective-permute-start(bf16[512,128]{1,0:T(8,128)(2,1)S(1)} %get-tuple-element.13.refs_0_), channel_id=1, source_target_pairs={{0,2},{1,3},{2,0},{3,1},{4,6},{5,7},{6,4},{7,5},{8,10},{9,11},{10,... | collective-permute-start | bytes 393224 | tf_op jit(solution)/shard_map/ppermute | solution.py:33
  47.1 8.1 %collective-permute-start.15 = (bf16[512,128]{1,0:T(8,128)(2,1)S(1)}, bf16[512,128]{1,0:T(8,128)(2,1)S(1)}, u32[]{:S(2)}, u32[]{:S(2)}) collective-permute-start(bf16[512,128]{1,0:T(8,128)(2,1)S(1)} %get-tuple-element.13.refs_0_), channel_id=1, source_target_pairs={{0,1},{1,0},{2,3},{3,2},{4,5},{5,4},{6,7},{7,6},{8,9},{9,8},{10,11... | collective-permute-start | bytes 393224 | tf_op jit(solution)/shard_map/ppermute | solution.py:33
  52.1 5.4 %collective-permute-start.26 = (bf16[512,128]{1,0:T(8,128)(2,1)S(1)}, bf16[512,128]{1,0:T(8,128)(2,1)S(1)}, u32[]{:S(2)}, u32[]{:S(2)}) collective-permute-start(bf16[512,128]{1,0:T(8,128)(2,1)S(1)} %collective-permute-done.22.refs_8_), channel_id=1, source_target_pairs={{0,4},{1,5},{2,6},{3,7},{4,0},{5,1},{6,2},{7,3},{8,12},{9,13},{10,... | collective-permute-start | bytes 393224 | tf_op jit(solution)/shard_map/ppermute | solution.py:33
  52.1 11.3 %collective-permute-start.24 = (bf16[512,128]{1,0:T(8,128)(2,1)S(1)}, bf16[512,128]{1,0:T(8,128)(2,1)S(1)}, u32[]{:S(2)}, u32[]{:S(2)}) collective-permute-start(bf16[512,128]{1,0:T(8,128)(2,1)S(1)} %collective-permute-done.22.refs_8_), channel_id=1, source_target_pairs={{0,2},{1,3},{2,0},{3,1},{4,6},{5,7},{6,4},{7,5},{8,10},{9,11},{10,... | collective-permute-start | bytes 393224 | tf_op jit(solution)/shard_map/ppermute | solution.py:33
  53.7 9.6 %collective-permute-start.20 = (bf16[512,128]{1,0:T(8,128)(2,1)S(1)}, bf16[512,128]{1,0:T(8,128)(2,1)S(1)}, u32[]{:S(2)}, u32[]{:S(2)}) collective-permute-start(bf16[512,128]{1,0:T(8,128)(2,1)S(1)} %collective-permute-done.18.refs_4_), channel_id=1, source_target_pairs={{0,2},{1,3},{2,0},{3,1},{4,6},{5,7},{6,4},{7,5},{8,10},{9,11},{10,... | collective-permute-start | bytes 393224 | tf_op jit(solution)/shard_map/ppermute | solution.py:33
  55.2 8.8 %collective-permute-start.19 = (bf16[512,128]{1,0:T(8,128)(2,1)S(1)}, bf16[512,128]{1,0:T(8,128)(2,1)}, u32[]{:S(2)}, u32[]{:S(2)}) collective-permute-start(bf16[512,128]{1,0:T(8,128)(2,1)S(1)} %collective-permute-done.18.refs_4_), channel_id=1, source_target_pairs={{0,1},{1,0},{2,3},{3,2},{4,5},{5,4},{6,7},{7,6},{8,9},{9,8},{10,11... | collective-permute-start | bytes 393224 | tf_op jit(solution)/shard_map/ppermute | solution.py:33
  55.2 8.7 %collective-permute-start.17 = (bf16[512,128]{1,0:T(8,128)(2,1)S(1)}, bf16[512,128]{1,0:T(8,128)(2,1)}, u32[]{:S(2)}, u32[]{:S(2)}) collective-permute-start(bf16[512,128]{1,0:T(8,128)(2,1)S(1)} %collective-permute-done.16.refs_2_), channel_id=1, source_target_pairs={{0,1},{1,0},{2,3},{3,2},{4,5},{5,4},{6,7},{7,6},{8,9},{9,8},{10,11... | collective-permute-start | bytes 393224 | tf_op jit(solution)/shard_map/ppermute | solution.py:33
  57.6 6.8 %collective-permute-start.28 = (bf16[512,128]{1,0:T(8,128)(2,1)S(1)}, bf16[512,128]{1,0:T(8,128)(2,1)}, u32[]{:S(2)}, u32[]{:S(2)}) collective-permute-start(bf16[512,128]{1,0:T(8,128)(2,1)S(1)} %collective-permute-done.26.refs_12_), channel_id=1, source_target_pairs={{0,2},{1,3},{2,0},{3,1},{4,6},{5,7},{6,4},{7,5},{8,10},{9,11},{10,... | collective-permute-start | bytes 393224 | tf_op jit(solution)/shard_map/ppermute | solution.py:33
  63.3 3.1 %copy-start.2 = (bf16[512,128]{1,0:T(8,128)(2,1)}, bf16[512,128]{1,0:T(8,128)(2,1)S(1)}, u32[]{:S(2)}) copy-start(bf16[512,128]{1,0:T(8,128)(2,1)S(1)} %collective-permute-done.20.refs_6_) | copy-start | bytes 393220
  63.3 3.1 %collective-permute-start.23 = (bf16[512,128]{1,0:T(8,128)(2,1)S(1)}, bf16[512,128]{1,0:T(8,128)(2,1)S(1)}, u32[]{:S(2)}, u32[]{:S(2)}) collective-permute-start(bf16[512,128]{1,0:T(8,128)(2,1)S(1)} %collective-permute-done.22.refs_8_), channel_id=1, source_target_pairs={{0,1},{1,0},{2,3},{3,2},{4,5},{5,4},{6,7},{7,6},{8,9},{9,8},{10,11... | collective-permute-start | bytes 393224 | tf_op jit(solution)/shard_map/ppermute | solution.py:33
  63.4 3.0 %copy-start = (bf16[512,128]{1,0:T(8,128)(2,1)}, bf16[512,128]{1,0:T(8,128)(2,1)S(1)}, u32[]{:S(2)}) copy-start(bf16[512,128]{1,0:T(8,128)(2,1)S(1)} %collective-permute-done.24.refs_10_) | copy-start | bytes 393220
  63.4 3.0 %collective-permute-start.27 = (bf16[512,128]{1,0:T(8,128)(2,1)S(1)}, bf16[512,128]{1,0:T(8,128)(2,1)S(1)}, u32[]{:S(2)}, u32[]{:S(2)}) collective-permute-start(bf16[512,128]{1,0:T(8,128)(2,1)S(1)} %collective-permute-done.26.refs_12_), channel_id=1, source_target_pairs={{0,1},{1,0},{2,3},{3,2},{4,5},{5,4},{6,7},{7,6},{8,9},{9,8},{10,11... | collective-permute-start | bytes 393224 | tf_op jit(solution)/shard_map/ppermute | solution.py:33
  63.9 2.5 %collective-permute-start.21 = (bf16[512,128]{1,0:T(8,128)(2,1)S(1)}, bf16[512,128]{1,0:T(8,128)(2,1)S(1)}, u32[]{:S(2)}, u32[]{:S(2)}) collective-permute-start(bf16[512,128]{1,0:T(8,128)(2,1)S(1)} %collective-permute-done.20.refs_6_), channel_id=1, source_target_pairs={{0,1},{1,0},{2,3},{3,2},{4,5},{5,4},{6,7},{7,6},{8,9},{9,8},{10,11... | collective-permute-start | bytes 393224 | tf_op jit(solution)/shard_map/ppermute | solution.py:33
  64.0 2.4 %collective-permute-start.25 = (bf16[512,128]{1,0:T(8,128)(2,1)S(1)}, bf16[512,128]{1,0:T(8,128)(2,1)S(1)}, u32[]{:S(2)}, u32[]{:S(2)}) collective-permute-start(bf16[512,128]{1,0:T(8,128)(2,1)S(1)} %collective-permute-done.24.refs_10_), channel_id=1, source_target_pairs={{0,1},{1,0},{2,3},{3,2},{4,5},{5,4},{6,7},{7,6},{8,9},{9,8},{10,11... | collective-permute-start | bytes 393224 | tf_op jit(solution)/shard_map/ppermute | solution.py:33
  64.4 2.0 %collective-permute-start.29 = (bf16[512,128]{1,0:T(8,128)(2,1)}, bf16[512,128]{1,0:T(8,128)(2,1)S(1)}, u32[]{:S(2)}, u32[]{:S(2)}) collective-permute-start(bf16[512,128]{1,0:T(8,128)(2,1)} %collective-permute-done.28.refs_14_), channel_id=1, source_target_pairs={{0,1},{1,0},{2,3},{3,2},{4,5},{5,4},{6,7},{7,6},{8,9},{9,8},{10,11... | collective-permute-start | bytes 393224 | tf_op jit(solution)/shard_map/ppermute | solution.py:33
  66.4 0.9 %copy-start.1 = (bf16[512,128]{1,0:T(8,128)(2,1)S(1)}, bf16[512,128]{1,0:T(8,128)(2,1)}, u32[]{:S(2)}) copy-start(bf16[512,128]{1,0:T(8,128)(2,1)} %copy-done) | copy-start | bytes 393220
  67.3 0.9 %copy-start.3 = (bf16[512,128]{1,0:T(8,128)(2,1)S(1)}, bf16[512,128]{1,0:T(8,128)(2,1)}, u32[]{:S(2)}) copy-start(bf16[512,128]{1,0:T(8,128)(2,1)} %copy-done.2) | copy-start | bytes 393220

commit v2 on v0

--- a/solution.py
+++ b/solution.py
@@ -1,23 +1,405 @@
 import jax
 import jax.numpy as jnp
 from jax import lax
+from jax.experimental import pallas as pl
+from jax.experimental.pallas import tpu as pltpu
 from jax.sharding import PartitionSpec as P
 
+DEVICES = 16
+QUAD = 4
 TILE = 128
-
-
-def body(
-    features,
-    cluster,
-    slot,
-    halo_tiles,
-    tile_slots,
-    adjacency,
-    labels,
-    w_self,
-    w_neigh,
-    w_out,
-    b_out,
+LANES = 128
+SUB = 16
+F32 = jnp.float32
+BF16 = jnp.bfloat16
+
+
+def _dot(a, b, contract=((1,), (0,))):
+    return lax.dot_general(a, b, (contract, ((), ())), preferred_element_type=F32)
+
+
+NT = ((1,), (1,))
+
+
+def _iota(shape, dim):
+    return lax.broadcasted_iota(jnp.int32, shape, dim)
+
+
+def _params(mib):
+    return pltpu.CompilerParams(vmem_limit_bytes=mib << 20)
+
+
+def swap(x, m):
+    return lax.ppermute(x, "nodes", [(i, i ^ m) for i in range(DEVICES)])
+
+
+def gather_all(block, work):
+    have = {0: block}
+    done = []
+
+    def hop(i, m):
+        if i < len(work):
+            out = work[i](have)
+            if len(work) == 1:
+                have[m], out = lax.optimization_barrier((have[m], out))
+            done.append(out)
+
+    have[8], have[4], have[2], have[1] = (swap(block, m) for m in (8, 4, 2, 1))
+    have[3] = swap(have[2], 1)
+    hop(0, 8)
+    have[12], have[10], have[6] = swap(have[8], 4), swap(have[8], 2), swap(have[4], 2)
+    have[5], have[7], have[9] = swap(have[4], 1), swap(have[6], 1), swap(have[8], 1)
+    hop(1, 12)
+    have[14] = swap(have[12], 2)
+    have[11], have[13] = swap(have[10], 1), swap(have[12], 1)
+    hop(2, 14)
+    have[15] = swap(have[14], 1)
+    return have, done
+
+
+def pack_kernel(devices, *refs):
+    sources, out_ref, targets, sems = refs[0:4], refs[4], refs[5:9], refs[9]
+    copies = [pltpu.make_async_copy(a, b, sems.at[i]) for i, (a, b) in enumerate(zip(sources, targets))]
+    for copy in copies:
+        copy.start()
+    for copy in copies:
+        copy.wait()
+    feat_ref, cluster_ref, slot_ref, label_ref = targets
+    rows = feat_ref.shape[0]
+    per = rows // devices
+    mine = lax.axis_index("nodes") % (LANES // per)
+    cluster = cluster_ref[...]
+    member = (_iota((devices, rows), 0) == cluster).astype(F32)
+    before = (_iota((rows, rows), 0) < _iota((rows, rows), 1)).astype(BF16)
+    rank = jnp.sum(member * _dot(member.astype(BF16), before), axis=0, keepdims=True).astype(jnp.int32)
+    take = (_iota((rows, rows), 0) == cluster * per + rank).astype(BF16)
+    out_ref[0:devices] = _dot(take, feat_ref[...]).astype(BF16).reshape(devices, per, feat_ref.shape[1])
+    place = (_iota((LANES, rows), 0) == mine * per + rank).astype(BF16)
+    slots = (member * (slot_ref[...] - rows // 2).astype(F32)).astype(BF16)
+    out_ref[devices, 0:SUB] = _dot(slots, place, NT).astype(BF16)
+    labels = jnp.concatenate([label_ref[...].astype(F32), jnp.zeros((SUB - label_ref.shape[0], LANES), F32)], axis=0)
+    out_ref[devices, SUB : 2 * SUB] = labels.astype(BF16)
+
+
+def pack(features, cluster, slot, labels, devices):
+    rows, width = features.shape
+    per = rows // devices
+    inputs = (features, cluster.reshape(1, rows), slot.reshape(1, rows), labels.reshape(rows // LANES, LANES))
+    return pl.pallas_call(
+        lambda *refs: pack_kernel(devices, *refs),
+        in_specs=[pl.BlockSpec(memory_space=pltpu.HBM)] * 4,
+        out_specs=pl.BlockSpec(memory_space=pltpu.VMEM),
+        out_shape=jax.ShapeDtypeStruct((devices + 1, per, width), BF16),
+        scratch_shapes=[*[pltpu.VMEM(x.shape, x.dtype) for x in inputs], pltpu.SemaphoreType.DMA((4,))],
+        compiler_params=_params(60),
+        name="pack_rows",
+    )(*inputs)
+
+
+def prepare_kernel(adj_ref, self_ref, neigh_ref, w_out_ref, b_ref, *refs):
+    turned_ref, in_t_ref, out_t_ref, out_ref, bias_ref, adj, wide, line, sems = refs
+    tiles, neigh = turned_ref.shape[0:2]
+    classes = w_out_ref.shape[0]
+    copies = [pltpu.make_async_copy(adj_ref.at[pl.ds(t * TILE, TILE)], adj.at[t], sems.at[t]) for t in range(tiles)]
+    for copy in copies:
+        copy.start()
+
+    in_t_ref[...] = jnp.transpose(jnp.concatenate([self_ref[...], neigh_ref[...]], axis=0).astype(F32)).astype(BF16)
+    wide[...] = jnp.zeros_like(wide)
+    wide[0:classes, :] = w_out_ref[...].astype(F32)
+    out_t_ref[...] = wide[...].astype(BF16)
+    out_ref[...] = jnp.transpose(wide[...]).astype(BF16)
+    line[...] = jnp.full_like(line, -1e30)
+    line[:, 0:classes] = b_ref[...]
+    bias_ref[...] = jnp.transpose(jnp.broadcast_to(line[...], (LANES, line.shape[1])))[0 : bias_ref.shape[0]]
+
+    side = SUB * SUB
+    row = _iota((side, side), 0)
+    move = ((row % SUB) * SUB + row // SUB == _iota((side, side), 1)).astype(BF16)
+    for t in range(tiles):
+        copies[t].wait()
+        for b in range(TILE // SUB):
+            for j in range(neigh // (2 * SUB)):
+                halves = [
+                    adj[t, SUB * b : SUB * (b + 1), SUB * k : SUB * (k + 1), :].reshape(side, TILE)
+                    for k in (2 * j, 2 * j + 1)
+                ]
+                moved = _dot(move, jnp.concatenate(halves, axis=1)).astype(BF16)
+                for h in range(2):
+                    k = 2 * j + h
+                    turned_ref[t, SUB * k : SUB * (k + 1), SUB * b : SUB * (b + 1), :] = moved[
+                        :, TILE * h : TILE * (h + 1)
+                    ].reshape(SUB, SUB, TILE)
+
+
+def prepare(adjacency, w_self, w_neigh, w_out, b_out):
+    rows, neigh, tile = adjacency.shape
+    width, units = w_self.shape
+    classes = w_out.shape[1]
+    padded = -(-classes // SUB) * SUB
+    tiles = rows // tile
+    vmem = pl.BlockSpec(memory_space=pltpu.VMEM)
+    return pl.pallas_call(
+        prepare_kernel,
+        in_specs=[pl.BlockSpec(memory_space=pltpu.HBM), *[vmem] * 4],
+        out_specs=[vmem] * 5,
+        out_shape=[
+            jax.ShapeDtypeStruct((tiles, neigh, tile, tile), BF16),
+            jax.ShapeDtypeStruct((units, 2 * width), BF16),
+            jax.ShapeDtypeStruct((padded, units), BF16),
+            jax.ShapeDtypeStruct((units, padded), BF16),
+            jax.ShapeDtypeStruct((padded, LANES), F32),
+        ],
+        scratch_shapes=[
+            pltpu.VMEM((tiles, tile, neigh, tile), BF16),
+            pltpu.VMEM((padded, units), F32),
+            pltpu.VMEM((1, 2 * LANES), F32),
+            pltpu.SemaphoreType.DMA((tiles,)),
+        ],
+        cost_estimate=pl.CostEstimate(flops=1 << 31, bytes_accessed=1 << 23, transcendentals=0),
+        compiler_params=_params(44),
+        name="prepare",
+    )(adjacency, w_self, w_neigh, w_out.T, b_out.reshape(1, classes))
+
+
+def aggregate_kernel(devices, *refs):
+    blocks = refs[:devices]
+    adj, halo_ref, slots_ref, px_ref, labels_ref, agg_ref, got, meta, sems = refs[devices:]
+    tiles, neigh = adj.shape[0:2]
+    me = lax.axis_index("nodes")
+    per = blocks[0].shape[1]
+    rows = devices * per
+    group = LANES // per
+
+    copies = []
+    for m, block in enumerate(blocks):
+        owner = me ^ m
+        at = pl.ds(pl.multiple_of(owner * per, per), per)
+        copies.append(pltpu.make_async_copy(block.at[0:devices], got.at[:, at, :], sems.at[0, m]))
+        copies.append(pltpu.make_async_copy(block.at[devices], meta.at[owner], sems.at[1, m]))
+    for copy in copies:
+        copy.start()
+    for copy in copies:
+        copy.wait()
+
+    labels_ref[...] = meta[:, SUB : 2 * SUB, :]
+    slots = [
+        sum(meta[q * group + j, 0:SUB, :].astype(F32) for j in range(group)) for q in range(devices // group)
+    ]
+    slots = jnp.concatenate(slots, axis=1).astype(jnp.int32)
+    position = _iota((rows, rows), 0) - rows // 2
+    for p in range(devices):
+        put = (position == slots[p : p + 1, :]).astype(BF16)
+        px_ref[p * rows : (p + 1) * rows, :] = _dot(put, got[p]).astype(BF16)
+
+    for t in range(tiles):
+        total = jnp.zeros((TILE, px_ref.shape[1]), F32)
+        for k in range(0, neigh, 2):
+            sources = []
+            for j in (k, k + 1):
+                tile = halo_ref[0, slots_ref[t, j]]
+                sources.append(px_ref[pl.ds(pl.multiple_of(tile * TILE, TILE), TILE), :])
+            weights = jnp.concatenate([adj[t, k], adj[t, k + 1]], axis=1)
+            total += _dot(weights, jnp.concatenate(sources, axis=0))
+        agg_ref[t * TILE : (t + 1) * TILE, :] = total.astype(BF16)
+
+
+def aggregate(blocks, turned, halo_tiles, tile_slots, devices):
+    per, width = blocks[0].shape[1:]
+    rows = devices * per
+    anywhere = pl.BlockSpec(memory_space=pl.ANY)
+    scalars = pl.BlockSpec(memory_space=pltpu.SMEM)
+    vmem = pl.BlockSpec(memory_space=pltpu.VMEM)
+    return pl.pallas_call(
+        lambda *refs: aggregate_kernel(devices, *refs),
+        in_specs=[anywhere] * devices + [vmem] + [scalars] * 2,
+        out_specs=[vmem] * 3,
+        out_shape=[
+            jax.ShapeDtypeStruct((devices * rows, width), BF16),
+            jax.ShapeDtypeStruct((devices, SUB, LANES), BF16),
+            jax.ShapeDtypeStruct((rows, width), BF16),
+        ],
+        scratch_shapes=[
+            pltpu.VMEM((devices, rows, width), BF16),
+            pltpu.VMEM((devices, 2 * SUB, LANES), BF16),
+            pltpu.SemaphoreType.DMA((2, devices)),
+        ],
+        compiler_params=_params(20),
+        name="aggregate",
+    )(*blocks, turned, halo_tiles, tile_slots)
+
+
+def _hot(kinds, labels_ref, owner):
+    held = labels_ref[owner].astype(F32)
+    return [kinds == held[j : j + 1, :].astype(jnp.int32) for j in range(QUAD)]
+
+
+def _forward(quad, blocks, px_ref, labels_ref, in_t_ref, out_t_ref, bias_ref, agg_ref, hid_ref, slope_ref, loss_ref, count_ref):
+    me = lax.axis_index("nodes")
+    rows, width = blocks[0].shape
+    for m, block in enumerate(blocks):
+        at = ((me % QUAD) ^ m) * rows
+        agg_ref[pl.ds(pl.multiple_of(at, rows), rows), :] = block[...]
+    kinds = _iota(bias_ref.shape, 0)
+    loss = count = jnp.zeros(bias_ref.shape, F32)
+    half = QUAD // 2 * rows
+    for h in range(2):
+        at = slice(h * half, (h + 1) * half)
+        x = px_ref[pl.ds(pl.multiple_of(quad * (2 * half) + h * half, half), half), :]
+        hidden = jnp.maximum(_dot(in_t_ref[...], jnp.concatenate([x, agg_ref[at, :]], axis=1), NT), 0.0).astype(BF16)
+        hid_ref[:, at] = hidden
+        logits = _dot(out_t_ref[...], hidden) + jnp.concatenate([bias_ref[...]] * (half // LANES), axis=1)
+        logits -= jnp.log(jnp.sum(jnp.exp(logits), axis=0, keepdims=True))
+        probs = jnp.exp(logits)
+        for o in range(QUAD // 2):
+            owner = quad * QUAD + h * (QUAD // 2) + o
+            for j, hot in enumerate(_hot(kinds, labels_ref, owner)):
+                lane = o * rows + j * LANES
+                one = hot.astype(F32)
+                loss -= jnp.where(hot, logits[:, lane : lane + LANES], 0.0)
+                count += one
+                slope_ref[:, h * half + lane : h * half + lane + LANES] = probs[:, lane : lane + LANES] - one
+    loss_ref[...], count_ref[...] = loss, count
+
+
+def forward_kernel(c, *refs):
+    me = lax.axis_index("nodes")
+    blocks, shared, outs = refs[:QUAD], refs[QUAD : QUAD + 5], refs[QUAD + 5 :]
+    _forward((me // QUAD) ^ c, blocks, *shared, *outs[0:5])
+    if c == 0:
+        px_ref, in_t_ref = shared[0], shared[2]
+        rows = blocks[0].shape[0]
+        x = px_ref[pl.ds(pl.multiple_of(me * rows, rows), rows), :]
+        pre = _dot(jnp.concatenate([x, blocks[0][...]], axis=1), in_t_ref[...], NT)
+        outs[5][...] = jnp.maximum(pre, 0.0).astype(BF16)
+
+
+def _held(rows, width, units, padded):
+    return [
+        ((QUAD * rows, width), BF16),
+        ((units, QUAD * rows), BF16),
+        ((padded, QUAD * rows), F32),
+        ((padded, LANES), F32),
+        ((padded, LANES), F32),
+    ]
+
+
+def forward(have, c, shared):
+    rows, width = have[0].shape
+    units, padded = shared[2].shape[0], shared[4].shape[0]
+    vmem = pl.BlockSpec(memory_space=pltpu.VMEM)
+    shapes = [jax.ShapeDtypeStruct(*x) for x in _held(rows, width, units, padded)]
+    if c == 0:
+        shapes.append(jax.ShapeDtypeStruct((rows, units), BF16))
+    return pl.pallas_call(
+        lambda *refs: forward_kernel(c, *refs),
+        in_specs=[vmem] * (QUAD + 5),
+        out_specs=[vmem] * len(shapes),
+        out_shape=shapes,
+        cost_estimate=pl.CostEstimate(flops=1 << 30, bytes_accessed=1 << 22, transcendentals=1 << 19),
+        compiler_params=_params(16),
+        name="forward",
+    )(*[have[QUAD * c + m] for m in range(QUAD)], *shared)
+
+
+def backward_kernel(classes, *refs):
+    me = lax.axis_index("nodes")
+    blocks, refs = refs[:QUAD], refs[QUAD:]
+    early, refs = [refs[5 * c : 5 * c + 5] for c in range(QUAD - 1)], refs[5 * (QUAD - 1) :]
+    shared, out_ref = refs[0:5], refs[5]
+    px_ref, labels_ref, _, _, bias_ref = shared
+    self_ref, neigh_ref, grad_out_ref, class_ref = refs[6:10]
+    last, refs = refs[10:15], refs[15:]
+    losses, counts, grads_in, grads_out = refs
+    rows, width = blocks[0].shape
+    padded = bias_ref.shape[0]
+    mine = me // QUAD
+    _forward(mine ^ (QUAD - 1), blocks, *shared, *last)
+    held = [*early, last]
+
+    for c in range(QUAD):
+        losses[mine ^ c], counts[mine ^ c] = held[c][3][...], held[c][4][...]
+    loss = jnp.sum(sum(losses[q] for q in range(QUAD)), axis=1, keepdims=True)
+    count = jnp.sum(sum(counts[q] for q in range(QUAD)), axis=1, keepdims=True)
+    real = _iota((padded, 1), 0) < classes
+    difficulty = jnp.where(real, (loss + 1.0) / (count + 1.0), 0.0)
+    weight = difficulty / (jnp.sum(difficulty, axis=0, keepdims=True) / classes)
+    share = 1.0 / (1.0 + jnp.sum(count, axis=0, keepdims=True))
+    class_ref[...] = jnp.transpose(jnp.broadcast_to(weight, (padded, LANES)))[0:1, 0:classes]
+    scaled = jnp.broadcast_to(weight * share, (padded, LANES))
+
+    kinds = _iota(bias_ref.shape, 0)
+    half = QUAD // 2 * rows
+    for c, (agg_ref, hid_ref, slope_ref, _, _) in enumerate(held):
+        quad = mine ^ c
+        grad_in = grad_out = 0.0
+        for h in range(2):
+            at = slice(h * half, (h + 1) * half)
+            parts = []
+            for o in range(QUAD // 2):
+                for j, hot in enumerate(_hot(kinds, labels_ref, quad * QUAD + h * (QUAD // 2) + o)):
+                    row = jnp.sum(jnp.where(hot, scaled, 0.0), axis=0, keepdims=True)
+                    lane = h * half + o * rows + j * LANES
+                    parts.append((row * slope_ref[:, lane : lane + LANES]).astype(BF16))
+            dlogits = jnp.concatenate(parts, axis=1)
+            hidden = hid_ref[:, at]
+            dpre = jnp.where(hidden > 0, _dot(out_ref[...], dlogits), 0.0).astype(BF16)
+            x = px_ref[pl.ds(pl.multiple_of(quad * (2 * half) + h * half, half), half), :]
+            grad_out += _dot(dlogits, hidden, NT)
+            grad_in += _dot(dpre, jnp.concatenate([x, agg_ref[at, :]], axis=1))
+        grads_in[quad], grads_out[quad] = grad_in, grad_out
+
+    grad_out_ref[...] = sum(grads_out[q] for q in range(QUAD))[0:classes]
+    grad_in = jnp.transpose(sum(grads_in[q] for q in range(QUAD)))
+    self_ref[...] = grad_in[0:width]
+    neigh_ref[...] = grad_in[width : 2 * width]
+
+
+def backward(have, early, shared, out_p, classes):
+    rows, width = have[0].shape
+    units, padded = out_p.shape
+    vmem = pl.BlockSpec(memory_space=pltpu.VMEM)
+    operands = [*[have[m] for m in range(DEVICES - QUAD, DEVICES)], *[x for held in early for x in held], *shared, out_p]
+    return pl.pallas_call(
+        lambda *refs: backward_kernel(classes, *refs),
+        in_specs=[vmem] * len(operands),
+        out_specs=[vmem] * 4,
+        out_shape=[
+            jax.ShapeDtypeStruct((width, units), F32),
+            jax.ShapeDtypeStruct((width, units), F32),
+            jax.ShapeDtypeStruct((classes, units), F32),
+            jax.ShapeDtypeStruct((1, classes), F32),
+        ],
+        scratch_shapes=[
+            *[pltpu.VMEM(*x) for x in _held(rows, width, units, padded)],
+            pltpu.VMEM((QUAD, padded, LANES), F32),
+            pltpu.VMEM((QUAD, padded, LANES), F32),
+            pltpu.VMEM((QUAD, units, 2 * width), F32),
+            pltpu.VMEM((QUAD, padded, units), F32),
+        ],
+        compiler_params=_params(24),
+        name="backward",
+    )(*operands)
+
+
+def gathered_body(
+    features, cluster, slot, halo_tiles, tile_slots, adjacency, labels, w_self, w_neigh, w_out, b_out
+):
+    packed = pack(features, cluster, slot, labels, DEVICES)
+    have, done = gather_all(packed, [lambda _: prepare(adjacency, w_self, w_neigh, w_out, b_out)])
+    turned, in_t, out_t, out_p, bias = done[0]
+    blocks = [have[m] for m in range(DEVICES)]
+    part_x, all_labels, agg = aggregate(blocks, turned, halo_tiles, tile_slots, DEVICES)
+    shared = (part_x, all_labels, in_t, out_t, bias)
+    have, done = gather_all(agg, [lambda have, c=c: forward(have, c, shared) for c in range(QUAD - 1)])
+    hidden = done[0][5]
+    early = [out[0:5] for out in done]
+    grad_self, grad_neigh, grad_out, class_weight = backward(have, early, shared, out_p, w_out.shape[1])
+    return hidden, grad_self, grad_neigh, grad_out.T, class_weight.reshape(-1)
+
+
+def split_body(
+    features, cluster, slot, halo_tiles, tile_slots, adjacency, labels, w_self, w_neigh, w_out, b_out
 ):
     rows = features.shape[0]
     width = features.shape[1]
@@ -72,6 +454,14 @@
 
 
 def solution(mesh):
+    def body(*args):
+        devices = mesh.shape["nodes"]
+        rows = args[0].shape[0]
+        per = rows // devices
+        classes = args[9].shape[1]
+        fits = devices == DEVICES and per == 2 * SUB and classes <= 256
+        return (gathered_body if fits else split_body)(*args)
+
     return jax.shard_map(
         body,
         mesh=mesh,

time: 242 us -> 69.9 us (0.29)
  waiting for transfers between devices: 135 us -> 22.1 us
  blocking collectives: 31.4 us -> 0 us
  Pallas kernels: 0 us -> 25.5 us
  local copies, waits for them, and re-layouts: 25.2 us -> 3.26 us
  matrix products: 15.6 us -> 0 us
  between operations: 15.5 us -> 0.77 us
  other arithmetic: 7.46 us -> 0 us
  starting transfers between devices: 11.2 us -> 18.1 us
    psum x1 -> x0, waiting for transfers between devices: 87.8 us -> none  [body(): lax.psum((part_self, part_neigh, part_out), 'nodes')]
    all_gather x1 -> x0, waiting for transfers between devices: 36.4 us -> none  [body(): gathered = lax.all_gather(part_x, 'nodes', axis=0, tiled=True)]
    psum x1 -> x0, blocking collectives: 31.4 us -> none  [body(): loss_sum, counts = lax.psum((local_loss, local_counts), 'nodes')]
    pallas_call x0 -> x7, Pallas kernels: none -> 25.5 us  [the longest x1 6.89 us: backward(): pl.pallas_call(lambda *refs: backward_kernel(classes, *refs), in_specs=[v...]
    ppermute x0 -> x30, waiting for transfers between devices: none -> 22.1 us  [swap(): return lax.ppermute(x, 'nodes', [(i, i ^ m) for i in range(DEVICES)])]
    ppermute x0 -> x30, starting transfers between devices: none -> 18.1 us  [swap(): return lax.ppermute(x, 'nodes', [(i, i ^ m) for i in range(DEVICES)])]
    gather x4 -> x0, local copies, waits for them, and re-layouts: 16.7 us -> none  [the longest x1 8.62 us: body(): sources = halo[tile_slots]]
    dot_general x8 -> x0, matrix products: 15.6 us -> none  [the longest x1 11 us: body(): jnp.einsum('tikc,tkcf->tif', adj_tiles, sources, preferred_element_type=j...]
  transfers between devices with their start and end apart: 4 -> 30, of which waited for: 4 -> 9; matrix products, arithmetic and copies ran while one was open for 2% -> 0% of each run, Pallas kernels for 0% -> 15%
where the time goes in v2:
time: 69.9 us; the launch traced here: 69.6 us
  Pallas kernels  25.5 us (36%)
  waiting for transfers between devices  22.1 us (32%)
  starting transfers between devices  18.1 us (26%)
  local copies, waits for them, and re-layouts  3.26 us (5%)
  between operations  0.77 us (1%)
    ppermute x30, waiting for transfers between devices, swap(): return lax.ppermute(x, 'nodes', [(i, i ^ m) for i in range(DEVICES)])  22.1 us
    ppermute x30, starting transfers between devices, swap(): return lax.ppermute(x, 'nodes', [(i, i ^ m) for i in range(DEVICES)])  18.1 us
    pallas_call x1, Pallas kernels, backward(): pl.pallas_call(lambda *refs: backward_kernel(classes, *refs), in_specs=[v...  6.89 us
    pallas_call x1, Pallas kernels, aggregate(): pl.pallas_call(lambda *refs: aggregate_kernel(devices, *refs), in_specs=[...  6.27 us
    pallas_call x3, Pallas kernels, forward(): pl.pallas_call(lambda *refs: forward_kernel(c, *refs), in_specs=[vmem] *...  5.63 us
    pallas_call x1, Pallas kernels, prepare(): pl.pallas_call(prepare_kernel, in_specs=[pl.BlockSpec(memory_space=pltpu....  4.58 us
    unnamed x14, local copies, waits for them, and re-layouts  3.26 us
    pallas_call x1, Pallas kernels, pack(): pl.pallas_call(lambda *refs: pack_kernel(devices, *refs), in_specs=[pl.Bl...  2.11 us
  transfers between devices with their start and end apart: 30, of which 9 were waited for; matrix products, arithmetic and copies ran while one was open for 0% of the time, Pallas kernels for 15%

profile of v2, /device:TPU:0, one launch (start us, length us, event | category | flops | bytes accessed | tf_op | source)
XLA Modules:
  0.0 69.6 jit_solution(14929813286614799304)
XLA Ops:
  0.6 2.1 %pack_rows.1.refs_0_ = bf16[17,32,128]{2,1,0:T(8,128)(2,1)} custom-call(bf16[512,128]{1,0:T(8,128)(2,1)} %refs_0_.1, s32[1,512]{1,0:T(1,128)} %bitcast.9, s32[1,512]{1,0:T(1,128)} %bitcast.10, s32[4,128]{1,0:T(4,128)} %bitcast.11), custom_call_target="tpu_custom_call" | custom-call | tf_op jit(solution)/shard_map/pack_rows/pallas_call | solution.py:88
  2.7 4.1 %collective-permute-start.7 = (bf16[17,32,128]{2,1,0:T(8,128)(2,1)}, bf16[17,32,128]{2,1,0:T(8,128)(2,1)S(1)}, u32[]{:S(2)}, u32[]{:S(2)}) collective-permute-start(bf16[17,32,128]{2,1,0:T(8,128)(2,1)} %pack_rows.1.refs_0_), channel_id=1, source_target_pairs={{0,8},{1,9},{2,10},{3,11},{4,12},{5,13},{6,14},{7,15},{8,0},{9,1},... | collective-permute-start | bytes 417800 | tf_op jit(solution)/shard_map/ppermute | solution.py:33
  6.8 1.6 %collective-permute-start.3 = (bf16[17,32,128]{2,1,0:T(8,128)(2,1)}, bf16[17,32,128]{2,1,0:T(8,128)(2,1)S(1)}, u32[]{:S(2)}, u32[]{:S(2)}) collective-permute-start(bf16[17,32,128]{2,1,0:T(8,128)(2,1)} %pack_rows.1.refs_0_), channel_id=1, source_target_pairs={{0,4},{1,5},{2,6},{3,7},{4,0},{5,1},{6,2},{7,3},{8,12},{9,13},{10,... | collective-permute-start | bytes 417800 | tf_op jit(solution)/shard_map/ppermute | solution.py:33
  8.4 1.5 %collective-permute-start.1 = (bf16[17,32,128]{2,1,0:T(8,128)(2,1)}, bf16[17,32,128]{2,1,0:T(8,128)(2,1)S(1)}, u32[]{:S(2)}, u32[]{:S(2)}) collective-permute-start(bf16[17,32,128]{2,1,0:T(8,128)(2,1)} %pack_rows.1.refs_0_), channel_id=1, source_target_pairs={{0,2},{1,3},{2,0},{3,1},{4,6},{5,7},{6,4},{7,5},{8,10},{9,11},{10,... | collective-permute-start | bytes 417800 | tf_op jit(solution)/shard_map/ppermute | solution.py:33
  9.9 0.0 collective-permute-start
  10.0 0.9 %copy-done.1 = bf16[256,172]{0,1:T(8,128)(2,1)S(1)} copy-done((bf16[256,172]{0,1:T(8,128)(2,1)S(1)}, bf16[256,172]{0,1:T(8,128)(2,1)}, u32[]{:S(2)}) %copy-start.1) | copy-done | bytes 88088
  10.8 0.8 %copy-done.2 = bf16[128,256]{1,0:T(8,128)(2,1)S(1)} copy-done((bf16[128,256]{1,0:T(8,128)(2,1)S(1)}, bf16[128,256]{1,0:T(8,128)(2,1)}, u32[]{:S(2)}) %copy-start.2) | copy-done | bytes 65560
  11.7 0.8 %copy-done.3 = bf16[128,256]{1,0:T(8,128)(2,1)S(1)} copy-done((bf16[128,256]{1,0:T(8,128)(2,1)S(1)}, bf16[128,256]{1,0:T(8,128)(2,1)}, u32[]{:S(2)}) %copy-start.3) | copy-done | bytes 65560
  12.5 0.7 copy-done.5
  13.2 4.6 %prepare.1 = (bf16[4,64,128,128]{3,2,1,0:T(8,128)(2,1)S(1)}, bf16[256,256]{1,0:T(8,128)(2,1)S(1)}, bf16[176,256]{1,0:T(8,128)(2,1)S(1)}, bf16[256,176]{1,0:T(8,128)(2,1)S(1)}, f32[176,128]{1,0:T(8,128)S(1)}) custom-call(bf16[512,64,128]{2,1,0:T(8,128)(2,1)} %adj_ref.1, bf16[128,256]{1,0:T(8,128)(2,1)S(1)} %copy-done.2, bf16[128,256]{1,0:T(8,128)(2,1)S(1)} %copy-done.3, ...), custom_call_target="tpu_custom_call" | custom-call | flops 2147483648 | bytes 8388608 | tf_op jit(solution)/shard_map/prepare/pallas_call | solution.py:142
  17.8 0.0 collective-permute-done.7.refs_8_
  17.8 0.5 collective-permute-start.11
  18.3 0.5 collective-permute-start.9
  18.8 0.0 collective-permute-done.3.refs_4_
  18.8 0.0 collective-permute-start.8
  18.8 0.0 collective-permute-done.1.refs_2_
  18.8 1.6 %collective-permute-start.5 = (bf16[17,32,128]{2,1,0:T(8,128)(2,1)S(1)}, bf16[17,32,128]{2,1,0:T(8,128)(2,1)S(1)}, u32[]{:S(2)}, u32[]{:S(2)}) collective-permute-start(bf16[17,32,128]{2,1,0:T(8,128)(2,1)S(1)} %collective-permute-done.3.refs_4_), channel_id=1, source_target_pairs={{0,2},{1,3},{2,0},{3,1},{4,6},{5,7},{6,4},{7,5},{8,10},{9,11},{10,... | collective-permute-start | bytes 417800 | tf_op jit(solution)/shard_map/ppermute | solution.py:33
  20.4 0.0 collective-permute-done.refs_1_
  20.4 0.2 collective-permute-start.4
  20.6 3.4 %collective-permute-done.11.refs_12_ = bf16[17,32,128]{2,1,0:T(8,128)(2,1)S(1)} collective-permute-done((bf16[17,32,128]{2,1,0:T(8,128)(2,1)S(1)}, bf16[17,32,128]{2,1,0:T(8,128)(2,1)S(1)}, u32[]{:S(2)}, u32[]{:S(2)}) %collective-permute-start.11) | collective-permute-done | bytes 139296 | tf_op jit(solution)/shard_map/ppermute | solution.py:33
  23.9 0.5 collective-permute-start.13
  24.5 0.4 collective-permute-done.9.refs_10_
  24.8 0.0 collective-permute-start.2
  24.8 0.5 collective-permute-start.12
  25.3 2.5 %collective-permute-done.5.refs_6_ = bf16[17,32,128]{2,1,0:T(8,128)(2,1)S(1)} collective-permute-done((bf16[17,32,128]{2,1,0:T(8,128)(2,1)S(1)}, bf16[17,32,128]{2,1,0:T(8,128)(2,1)S(1)}, u32[]{:S(2)}, u32[]{:S(2)}) %collective-permute-start.5) | collective-permute-done | bytes 139296 | tf_op jit(solution)/shard_map/ppermute | solution.py:33
  27.8 0.0 collective-permute-start.10
  27.8 0.5 collective-permute-start.6
  28.3 1.8 %collective-permute-done.13.refs_14_ = bf16[17,32,128]{2,1,0:T(8,128)(2,1)S(1)} collective-permute-done((bf16[17,32,128]{2,1,0:T(8,128)(2,1)S(1)}, bf16[17,32,128]{2,1,0:T(8,128)(2,1)S(1)}, u32[]{:S(2)}, u32[]{:S(2)}) %collective-permute-start.13) | collective-permute-done | bytes 139296 | tf_op jit(solution)/shard_map/ppermute | solution.py:33
  30.1 1.3 %collective-permute-done.14.refs_15_ = bf16[17,32,128]{2,1,0:T(8,128)(2,1)S(1)} collective-permute-done((bf16[17,32,128]{2,1,0:T(8,128)(2,1)S(1)}, bf16[17,32,128]{2,1,0:T(8,128)(2,1)S(1)}, u32[]{:S(2)}, u32[]{:S(2)}) %collective-permute-start.14) | collective-permute-done | bytes 139296 | tf_op jit(solution)/shard_map/ppermute | solution.py:33
  31.5 6.3 %aggregate.1 = (bf16[8192,128]{1,0:T(8,128)(2,1)S(1)}, bf16[16,16,128]{2,1,0:T(8,128)(2,1)S(1)}, bf16[512,128]{1,0:T(8,128)(2,1)S(1)}) custom-call(bf16[17,32,128]{2,1,0:T(8,128)(2,1)S(1)} %copy-done, bf16[17,32,128]{2,1,0:T(8,128)(2,1)S(1)} %collective-permute-done.refs_1_, bf16[17,32,128]{2,1,0:T(8,128)(2,1)S(1)} %collective-permute-done.1.refs_2_, ...), custom_call_target="tpu_custom_call" | custom-call | tf_op jit(solution)/shard_map/aggregate/pallas_call | solution.py:213
  37.7 0.4 collective-permute-start.18
  38.1 1.6 %collective-permute-start.23 = (bf16[512,128]{1,0:T(8,128)(2,1)S(1)}, bf16[512,128]{1,0:T(8,128)(2,1)S(1)}, u32[]{:S(2)}, u32[]{:S(2)}) collective-permute-start(bf16[512,128]{1,0:T(8,128)(2,1)S(1)} %get-tuple-element.46.refs_0_), channel_id=1, source_target_pairs={{0,4},{1,5},{2,6},{3,7},{4,0},{5,1},{6,2},{7,3},{8,12},{9,13},{10,... | collective-permute-start | bytes 393224 | tf_op jit(solution)/shard_map/ppermute | solution.py:33
  39.7 0.5 collective-permute-start.16
  40.2 6.9 %collective-permute-done.18.refs_0_ = bf16[512,128]{1,0:T(8,128)(2,1)S(1)} collective-permute-done((bf16[512,128]{1,0:T(8,128)(2,1)S(1)}, bf16[512,128]{1,0:T(8,128)(2,1)S(1)}, u32[]{:S(2)}, u32[]{:S(2)}) %collective-permute-start.18) | collective-permute-done | bytes 131104 | tf_op jit(solution)/shard_map/ppermute | solution.py:33
  47.1 0.5 collective-permute-start.28
  47.6 1.5 %collective-permute-start.25 = (bf16[512,128]{1,0:T(8,128)(2,1)S(1)}, bf16[512,128]{1,0:T(8,128)(2,1)S(1)}, u32[]{:S(2)}, u32[]{:S(2)}) collective-permute-start(bf16[512,128]{1,0:T(8,128)(2,1)S(1)} %collective-permute-done.23.refs_0_), channel_id=1, source_target_pairs={{0,2},{1,3},{2,0},{3,1},{4,6},{5,7},{6,4},{7,5},{8,10},{9,11},{10,... | collective-permute-start | bytes 393224 | tf_op jit(solution)/shard_map/ppermute | solution.py:33
  49.1 0.5 collective-permute-start.27
  49.6 2.4 %collective-permute-done.19.refs_0_ = bf16[512,128]{1,0:T(8,128)(2,1)S(1)} collective-permute-done((bf16[512,128]{1,0:T(8,128)(2,1)S(1)}, bf16[512,128]{1,0:T(8,128)(2,1)S(1)}, u32[]{:S(2)}, u32[]{:S(2)}) %collective-permute-start.19) | collective-permute-done | bytes 131104 | tf_op jit(solution)/shard_map/ppermute | solution.py:33
  52.1 0.5 collective-permute-start.21
  52.6 1.0 %collective-permute-done.28.refs_2_ = bf16[512,128]{1,0:T(8,128)(2,1)S(1)} collective-permute-done((bf16[512,128]{1,0:T(8,128)(2,1)S(1)}, bf16[512,128]{1,0:T(8,128)(2,1)S(1)}, u32[]{:S(2)}, u32[]{:S(2)}) %collective-permute-start.28) | collective-permute-done | bytes 131104 | tf_op jit(solution)/shard_map/ppermute | solution.py:33
  53.5 2.5 %collective-permute-done.25.refs_2_ = bf16[512,128]{1,0:T(8,128)(2,1)S(1)} collective-permute-done((bf16[512,128]{1,0:T(8,128)(2,1)S(1)}, bf16[512,128]{1,0:T(8,128)(2,1)S(1)}, u32[]{:S(2)}, u32[]{:S(2)}) %collective-permute-start.25) | collective-permute-done | bytes 131104 | tf_op jit(solution)/shard_map/ppermute | solution.py:33
  56.0 0.5 collective-permute-start.26
  56.5 2.3 %forward.3 = (bf16[2048,128]{1,0:T(8,128)(2,1)S(1)}, bf16[256,2048]{1,0:T(8,128)(2,1)S(1)}, f32[176,2048]{1,0:T(8,128)S(1)}, f32[176,128]{1,0:T(8,128)S(1)}, f32...) custom-call(bf16[512,128]{1,0:T(8,128)(2,1)S(1)} %get-tuple-element.46.refs_0_, ...), custom_call_target="tpu_custom_call" | custom-call | flops 1073741824 | bytes 4194304 | tf_op jit(solution)/shard_map/forward/pallas_call | solution.py:294
  58.8 0.0 collective-permute-start.20
  58.9 0.5 collective-permute-start.22
  59.4 1.7 %forward.5 = (bf16[2048,128]{1,0:T(8,128)(2,1)S(1)}, bf16[256,2048]{1,0:T(8,128)(2,1)S(1)}, f32[176,2048]{1,0:T(8,128)S(1)}, f32[176,128]{1,0:T(8,128)S(1)}, f32[176,128]{1,0:T(8,128)S(1)}) custom-call(bf16[512,128]{1,0:T(8,128)(2,1)S(1)} %collective-permute-done.18.refs_0_, bf16[512,128]{1,0:T(8,128)(2,1)S(1)} %collective-permute-done.27.refs_1_, ...), custom_call_target="tpu_custom_call" | custom-call | flops 1073741824 | bytes 4194304 | tf_op jit(solution)/shard_map/forward/pallas_call | solution.py:294
  61.0 1.7 %forward.4 = (bf16[2048,128]{1,0:T(8,128)(2,1)S(1)}, bf16[256,2048]{1,0:T(8,128)(2,1)S(1)}, f32[176,2048]{1,0:T(8,128)S(1)}, f32[176,128]{1,0:T(8,128)S(1)}, f32[176,128]{1,0:T(8,128)S(1)}) custom-call(bf16[512,128]{1,0:T(8,128)(2,1)S(1)} %collective-permute-done.23.refs_0_, bf16[512,128]{1,0:T(8,128)(2,1)S(1)} %collective-permute-done.24.refs_1_, ...), custom_call_target="tpu_custom_call" | custom-call | flops 1073741824 | bytes 4194304 | tf_op jit(solution)/shard_map/forward/pallas_call | solution.py:294
  62.7 6.9 %backward.1 = (f32[128,256]{1,0:T(8,128)}, f32[128,256]{1,0:T(8,128)}, f32[172,256]{1,0:T(8,128)}, f32[1,172]{1,0:T(1,128)}) custom-call(bf16[512,128]{1,0:T(8,128)(2,1)S(1)} %collective-permute-done.19.refs_0_, bf16[512,128]{1,0:T(8,128)(2,1)S(1)} %collective-permute-done.20.refs_1_, bf16[512,128]{1,0:T(8,128)(2,1)S(1)} %collective-permute-done.21.refs_2_, ...), custom_call_target="tpu_custom_call" | custom-call | tf_op jit(solution)/shard_map/backward/pallas_call | solution.py:363
  (33 shorter events, 0.1 us)
Async XLA Ops:
  2.7 15.0 %collective-permute-start.7 = (bf16[17,32,128]{2,1,0:T(8,128)(2,1)}, bf16[17,32,128]{2,1,0:T(8,128)(2,1)S(1)}, u32[]{:S(2)}, u32[]{:S(2)}) collective-permute-start(bf16[17,32,128]{2,1,0:T(8,128)(2,1)} %pack_rows.1.refs_0_), channel_id=1, source_target_pairs={{0,8},{1,9},{2,10},{3,11},{4,12},{5,13},{6,14},{7,15},{8,0},{9,1},... | collective-permute-start | bytes 417800 | tf_op jit(solution)/shard_map/ppermute | solution.py:33
  6.8 12.0 %collective-permute-start.3 = (bf16[17,32,128]{2,1,0:T(8,128)(2,1)}, bf16[17,32,128]{2,1,0:T(8,128)(2,1)S(1)}, u32[]{:S(2)}, u32[]{:S(2)}) collective-permute-start(bf16[17,32,128]{2,1,0:T(8,128)(2,1)} %pack_rows.1.refs_0_), channel_id=1, source_target_pairs={{0,4},{1,5},{2,6},{3,7},{4,0},{5,1},{6,2},{7,3},{8,12},{9,13},{10,... | collective-permute-start | bytes 417800 | tf_op jit(solution)/shard_map/ppermute | solution.py:33
  8.4 10.4 %collective-permute-start.1 = (bf16[17,32,128]{2,1,0:T(8,128)(2,1)}, bf16[17,32,128]{2,1,0:T(8,128)(2,1)S(1)}, u32[]{:S(2)}, u32[]{:S(2)}) collective-permute-start(bf16[17,32,128]{2,1,0:T(8,128)(2,1)} %pack_rows.1.refs_0_), channel_id=1, source_target_pairs={{0,2},{1,3},{2,0},{3,1},{4,6},{5,7},{6,4},{7,5},{8,10},{9,11},{10,... | collective-permute-start | bytes 417800 | tf_op jit(solution)/shard_map/ppermute | solution.py:33
  9.9 10.5 %collective-permute-start = (bf16[17,32,128]{2,1,0:T(8,128)(2,1)}, bf16[17,32,128]{2,1,0:T(8,128)(2,1)S(1)}, u32[]{:S(2)}, u32[]{:S(2)}) collective-permute-start(bf16[17,32,128]{2,1,0:T(8,128)(2,1)} %pack_rows.1.refs_0_), channel_id=1, source_target_pairs={{0,1},{1,0},{2,3},{3,2},{4,5},{5,4},{6,7},{7,6},{8,9},{9,8},{10,11... | collective-permute-start | bytes 417800 | tf_op jit(solution)/shard_map/ppermute | solution.py:33
  9.9 0.9 %copy-start.1 = (bf16[256,172]{0,1:T(8,128)(2,1)S(1)}, bf16[256,172]{0,1:T(8,128)(2,1)}, u32[]{:S(2)}) copy-start(bf16[256,172]{0,1:T(8,128)(2,1)} %param.20) | copy-start | bytes 264196
  10.8 0.8 %copy-start.2 = (bf16[128,256]{1,0:T(8,128)(2,1)S(1)}, bf16[128,256]{1,0:T(8,128)(2,1)}, u32[]{:S(2)}) copy-start(bf16[128,256]{1,0:T(8,128)(2,1)} %self_ref.1) | copy-start | bytes 196612
  11.7 0.8 %copy-start.3 = (bf16[128,256]{1,0:T(8,128)(2,1)S(1)}, bf16[128,256]{1,0:T(8,128)(2,1)}, u32[]{:S(2)}) copy-start(bf16[128,256]{1,0:T(8,128)(2,1)} %neigh_ref.1) | copy-start | bytes 196612
  12.5 0.7 copy-start.5
  13.2 18.3 %copy-start = (bf16[17,32,128]{2,1,0:T(8,128)(2,1)S(1)}, bf16[17,32,128]{2,1,0:T(8,128)(2,1)}, u32[]{:S(2)}) copy-start(bf16[17,32,128]{2,1,0:T(8,128)(2,1)} %pack_rows.1.refs_0_) | copy-start | bytes 417796
  13.2 18.3 %copy-start.4 = (s32[4,64]{1,0:T(4,128)S(1)}, s32[4,64]{1,0:T(4,128)}, u32[]{:S(2)}) copy-start(s32[4,64]{1,0:T(4,128)} %refs_18_.1) | copy-start | bytes 3076
  13.2 18.3 %copy-start.6 = (s32[1,64]{1,0:T(1,128)S(1)}, s32[1,64]{1,0:T(1,128)}, u32[]{:S(2)}) copy-start(s32[1,64]{1,0:T(1,128)} %refs_17_.1) | copy-start | bytes 772
  17.8 6.1 %collective-permute-start.11 = (bf16[17,32,128]{2,1,0:T(8,128)(2,1)S(1)}, bf16[17,32,128]{2,1,0:T(8,128)(2,1)S(1)}, u32[]{:S(2)}, u32[]{:S(2)}) collective-permute-start(bf16[17,32,128]{2,1,0:T(8,128)(2,1)S(1)} %collective-permute-done.7.refs_8_), channel_id=1, source_target_pairs={{0,4},{1,5},{2,6},{3,7},{4,0},{5,1},{6,2},{7,3},{8,12},{9,13},{10,... | collective-permute-start | bytes 417800 | tf_op jit(solution)/shard_map/ppermute | solution.py:33
  18.3 6.5 %collective-permute-start.9 = (bf16[17,32,128]{2,1,0:T(8,128)(2,1)S(1)}, bf16[17,32,128]{2,1,0:T(8,128)(2,1)S(1)}, u32[]{:S(2)}, u32[]{:S(2)}) collective-permute-start(bf16[17,32,128]{2,1,0:T(8,128)(2,1)S(1)} %collective-permute-done.7.refs_8_), channel_id=1, source_target_pairs={{0,2},{1,3},{2,0},{3,1},{4,6},{5,7},{6,4},{7,5},{8,10},{9,11},{10,... | collective-permute-start | bytes 417800 | tf_op jit(solution)/shard_map/ppermute | solution.py:33
  18.8 6.0 %collective-permute-start.8 = (bf16[17,32,128]{2,1,0:T(8,128)(2,1)S(1)}, bf16[17,32,128]{2,1,0:T(8,128)(2,1)S(1)}, u32[]{:S(2)}, u32[]{:S(2)}) collective-permute-start(bf16[17,32,128]{2,1,0:T(8,128)(2,1)S(1)} %collective-permute-done.7.refs_8_), channel_id=1, source_target_pairs={{0,1},{1,0},{2,3},{3,2},{4,5},{5,4},{6,7},{7,6},{8,9},{9,8},{10,11... | collective-permute-start | bytes 417800 | tf_op jit(solution)/shard_map/ppermute | solution.py:33
  18.8 9.0 %collective-permute-start.5 = (bf16[17,32,128]{2,1,0:T(8,128)(2,1)S(1)}, bf16[17,32,128]{2,1,0:T(8,128)(2,1)S(1)}, u32[]{:S(2)}, u32[]{:S(2)}) collective-permute-start(bf16[17,32,128]{2,1,0:T(8,128)(2,1)S(1)} %collective-permute-done.3.refs_4_), channel_id=1, source_target_pairs={{0,2},{1,3},{2,0},{3,1},{4,6},{5,7},{6,4},{7,5},{8,10},{9,11},{10,... | collective-permute-start | bytes 417800 | tf_op jit(solution)/shard_map/ppermute | solution.py:33
  20.4 7.4 %collective-permute-start.4 = (bf16[17,32,128]{2,1,0:T(8,128)(2,1)S(1)}, bf16[17,32,128]{2,1,0:T(8,128)(2,1)S(1)}, u32[]{:S(2)}, u32[]{:S(2)}) collective-permute-start(bf16[17,32,128]{2,1,0:T(8,128)(2,1)S(1)} %collective-permute-done.3.refs_4_), channel_id=1, source_target_pairs={{0,1},{1,0},{2,3},{3,2},{4,5},{5,4},{6,7},{7,6},{8,9},{9,8},{10,11... | collective-permute-start | bytes 417800 | tf_op jit(solution)/shard_map/ppermute | solution.py:33
  23.9 6.1 %collective-permute-start.13 = (bf16[17,32,128]{2,1,0:T(8,128)(2,1)S(1)}, bf16[17,32,128]{2,1,0:T(8,128)(2,1)S(1)}, u32[]{:S(2)}, u32[]{:S(2)}) collective-permute-start(bf16[17,32,128]{2,1,0:T(8,128)(2,1)S(1)} %collective-permute-done.11.refs_12_), channel_id=1, source_target_pairs={{0,2},{1,3},{2,0},{3,1},{4,6},{5,7},{6,4},{7,5},{8,10},{9,11},{10,... | collective-permute-start | bytes 417800 | tf_op jit(solution)/shard_map/ppermute | solution.py:33
  24.8 5.3 %collective-permute-start.2 = (bf16[17,32,128]{2,1,0:T(8,128)(2,1)S(1)}, bf16[17,32,128]{2,1,0:T(8,128)(2,1)S(1)}, u32[]{:S(2)}, u32[]{:S(2)}) collective-permute-start(bf16[17,32,128]{2,1,0:T(8,128)(2,1)S(1)} %collective-permute-done.1.refs_2_), channel_id=1, source_target_pairs={{0,1},{1,0},{2,3},{3,2},{4,5},{5,4},{6,7},{7,6},{8,9},{9,8},{10,11... | collective-permute-start | bytes 417800 | tf_op jit(solution)/shard_map/ppermute | solution.py:33
  24.8 5.3 %collective-permute-start.12 = (bf16[17,32,128]{2,1,0:T(8,128)(2,1)S(1)}, bf16[17,32,128]{2,1,0:T(8,128)(2,1)S(1)}, u32[]{:S(2)}, u32[]{:S(2)}) collective-permute-start(bf16[17,32,128]{2,1,0:T(8,128)(2,1)S(1)} %collective-permute-done.11.refs_12_), channel_id=1, source_target_pairs={{0,1},{1,0},{2,3},{3,2},{4,5},{5,4},{6,7},{7,6},{8,9},{9,8},{10,11... | collective-permute-start | bytes 417800 | tf_op jit(solution)/shard_map/ppermute | solution.py:33
  27.8 2.3 %collective-permute-start.10 = (bf16[17,32,128]{2,1,0:T(8,128)(2,1)S(1)}, bf16[17,32,128]{2,1,0:T(8,128)(2,1)S(1)}, u32[]{:S(2)}, u32[]{:S(2)}) collective-permute-start(bf16[17,32,128]{2,1,0:T(8,128)(2,1)S(1)} %collective-permute-done.9.refs_10_), channel_id=1, source_target_pairs={{0,1},{1,0},{2,3},{3,2},{4,5},{5,4},{6,7},{7,6},{8,9},{9,8},{10,11... | collective-permute-start | bytes 417800 | tf_op jit(solution)/shard_map/ppermute | solution.py:33
  27.8 2.3 %collective-permute-start.6 = (bf16[17,32,128]{2,1,0:T(8,128)(2,1)S(1)}, bf16[17,32,128]{2,1,0:T(8,128)(2,1)S(1)}, u32[]{:S(2)}, u32[]{:S(2)}) collective-permute-start(bf16[17,32,128]{2,1,0:T(8,128)(2,1)S(1)} %collective-permute-done.5.refs_6_), channel_id=1, source_target_pairs={{0,1},{1,0},{2,3},{3,2},{4,5},{5,4},{6,7},{7,6},{8,9},{9,8},{10,11... | collective-permute-start | bytes 417800 | tf_op jit(solution)/shard_map/ppermute | solution.py:33
  30.1 1.4 %collective-permute-start.14 = (bf16[17,32,128]{2,1,0:T(8,128)(2,1)S(1)}, bf16[17,32,128]{2,1,0:T(8,128)(2,1)S(1)}, u32[]{:S(2)}, u32[]{:S(2)}) collective-permute-start(bf16[17,32,128]{2,1,0:T(8,128)(2,1)S(1)} %collective-permute-done.13.refs_14_), channel_id=1, source_target_pairs={{0,1},{1,0},{2,3},{3,2},{4,5},{5,4},{6,7},{7,6},{8,9},{9,8},{10,11... | collective-permute-start | bytes 417800 | tf_op jit(solution)/shard_map/ppermute | solution.py:33
  37.7 9.4 %collective-permute-start.18 = (bf16[512,128]{1,0:T(8,128)(2,1)S(1)}, bf16[512,128]{1,0:T(8,128)(2,1)S(1)}, u32[]{:S(2)}, u32[]{:S(2)}) collective-permute-start(bf16[512,128]{1,0:T(8,128)(2,1)S(1)} %get-tuple-element.46.refs_0_), channel_id=1, source_target_pairs={{0,8},{1,9},{2,10},{3,11},{4,12},{5,13},{6,14},{7,15},{8,0},{9,1},... | collective-permute-start | bytes 393224 | tf_op jit(solution)/shard_map/ppermute | solution.py:33
  38.1 9.5 %collective-permute-start.23 = (bf16[512,128]{1,0:T(8,128)(2,1)S(1)}, bf16[512,128]{1,0:T(8,128)(2,1)S(1)}, u32[]{:S(2)}, u32[]{:S(2)}) collective-permute-start(bf16[512,128]{1,0:T(8,128)(2,1)S(1)} %get-tuple-element.46.refs_0_), channel_id=1, source_target_pairs={{0,4},{1,5},{2,6},{3,7},{4,0},{5,1},{6,2},{7,3},{8,12},{9,13},{10,... | collective-permute-start | bytes 393224 | tf_op jit(solution)/shard_map/ppermute | solution.py:33
  39.7 9.4 %collective-permute-start.16 = (bf16[512,128]{1,0:T(8,128)(2,1)S(1)}, bf16[512,128]{1,0:T(8,128)(2,1)S(1)}, u32[]{:S(2)}, u32[]{:S(2)}) collective-permute-start(bf16[512,128]{1,0:T(8,128)(2,1)S(1)} %get-tuple-element.46.refs_0_), channel_id=1, source_target_pairs={{0,2},{1,3},{2,0},{3,1},{4,6},{5,7},{6,4},{7,5},{8,10},{9,11},{10,... | collective-permute-start | bytes 393224 | tf_op jit(solution)/shard_map/ppermute | solution.py:33
  40.2 8.9 %collective-permute-start.15 = (bf16[512,128]{1,0:T(8,128)(2,1)S(1)}, bf16[512,128]{1,0:T(8,128)(2,1)S(1)}, u32[]{:S(2)}, u32[]{:S(2)}) collective-permute-start(bf16[512,128]{1,0:T(8,128)(2,1)S(1)} %get-tuple-element.46.refs_0_), channel_id=1, source_target_pairs={{0,1},{1,0},{2,3},{3,2},{4,5},{5,4},{6,7},{7,6},{8,9},{9,8},{10,11... | collective-permute-start | bytes 393224 | tf_op jit(solution)/shard_map/ppermute | solution.py:33
  47.1 5.0 %collective-permute-start.19 = (bf16[512,128]{1,0:T(8,128)(2,1)S(1)}, bf16[512,128]{1,0:T(8,128)(2,1)S(1)}, u32[]{:S(2)}, u32[]{:S(2)}) collective-permute-start(bf16[512,128]{1,0:T(8,128)(2,1)S(1)} %collective-permute-done.18.refs_0_), channel_id=1, source_target_pairs={{0,4},{1,5},{2,6},{3,7},{4,0},{5,1},{6,2},{7,3},{8,12},{9,13},{10,... | collective-permute-start | bytes 393224 | tf_op jit(solution)/shard_map/ppermute | solution.py:33
  47.1 6.4 %collective-permute-start.28 = (bf16[512,128]{1,0:T(8,128)(2,1)S(1)}, bf16[512,128]{1,0:T(8,128)(2,1)S(1)}, u32[]{:S(2)}, u32[]{:S(2)}) collective-permute-start(bf16[512,128]{1,0:T(8,128)(2,1)S(1)} %collective-permute-done.18.refs_0_), channel_id=1, source_target_pairs={{0,2},{1,3},{2,0},{3,1},{4,6},{5,7},{6,4},{7,5},{8,10},{9,11},{10,... | collective-permute-start | bytes 393224 | tf_op jit(solution)/shard_map/ppermute | solution.py:33
  47.6 8.4 %collective-permute-start.25 = (bf16[512,128]{1,0:T(8,128)(2,1)S(1)}, bf16[512,128]{1,0:T(8,128)(2,1)S(1)}, u32[]{:S(2)}, u32[]{:S(2)}) collective-permute-start(bf16[512,128]{1,0:T(8,128)(2,1)S(1)} %collective-permute-done.23.refs_0_), channel_id=1, source_target_pairs={{0,2},{1,3},{2,0},{3,1},{4,6},{5,7},{6,4},{7,5},{8,10},{9,11},{10,... | collective-permute-start | bytes 393224 | tf_op jit(solution)/shard_map/ppermute | solution.py:33
  49.1 6.9 %collective-permute-start.17 = (bf16[512,128]{1,0:T(8,128)(2,1)S(1)}, bf16[512,128]{1,0:T(8,128)(2,1)S(1)}, u32[]{:S(2)}, u32[]{:S(2)}) collective-permute-start(bf16[512,128]{1,0:T(8,128)(2,1)S(1)} %collective-permute-done.16.refs_2_), channel_id=1, source_target_pairs={{0,1},{1,0},{2,3},{3,2},{4,5},{5,4},{6,7},{7,6},{8,9},{9,8},{10,11... | collective-permute-start | bytes 393224 | tf_op jit(solution)/shard_map/ppermute | solution.py:33
  49.1 9.7 %collective-permute-start.27 = (bf16[512,128]{1,0:T(8,128)(2,1)S(1)}, bf16[512,128]{1,0:T(8,128)(2,1)S(1)}, u32[]{:S(2)}, u32[]{:S(2)}) collective-permute-start(bf16[512,128]{1,0:T(8,128)(2,1)S(1)} %collective-permute-done.18.refs_0_), channel_id=1, source_target_pairs={{0,1},{1,0},{2,3},{3,2},{4,5},{5,4},{6,7},{7,6},{8,9},{9,8},{10,11... | collective-permute-start | bytes 393224 | tf_op jit(solution)/shard_map/ppermute | solution.py:33
  52.1 6.8 %collective-permute-start.21 = (bf16[512,128]{1,0:T(8,128)(2,1)S(1)}, bf16[512,128]{1,0:T(8,128)(2,1)S(1)}, u32[]{:S(2)}, u32[]{:S(2)}) collective-permute-start(bf16[512,128]{1,0:T(8,128)(2,1)S(1)} %collective-permute-done.19.refs_0_), channel_id=1, source_target_pairs={{0,2},{1,3},{2,0},{3,1},{4,6},{5,7},{6,4},{7,5},{8,10},{9,11},{10,... | collective-permute-start | bytes 393224 | tf_op jit(solution)/shard_map/ppermute | solution.py:33
  53.5 5.8 %collective-permute-start.29 = (bf16[512,128]{1,0:T(8,128)(2,1)S(1)}, bf16[512,128]{1,0:T(8,128)(2,1)S(1)}, u32[]{:S(2)}, u32[]{:S(2)}) collective-permute-start(bf16[512,128]{1,0:T(8,128)(2,1)S(1)} %collective-permute-done.28.refs_2_), channel_id=1, source_target_pairs={{0,1},{1,0},{2,3},{3,2},{4,5},{5,4},{6,7},{7,6},{8,9},{9,8},{10,11... | collective-permute-start | bytes 393224 | tf_op jit(solution)/shard_map/ppermute | solution.py:33
  56.0 5.0 %collective-permute-start.24 = (bf16[512,128]{1,0:T(8,128)(2,1)S(1)}, bf16[512,128]{1,0:T(8,128)(2,1)S(1)}, u32[]{:S(2)}, u32[]{:S(2)}) collective-permute-start(bf16[512,128]{1,0:T(8,128)(2,1)S(1)} %collective-permute-done.23.refs_0_), channel_id=1, source_target_pairs={{0,1},{1,0},{2,3},{3,2},{4,5},{5,4},{6,7},{7,6},{8,9},{9,8},{10,11... | collective-permute-start | bytes 393224 | tf_op jit(solution)/shard_map/ppermute | solution.py:33
  56.0 5.0 %collective-permute-start.26 = (bf16[512,128]{1,0:T(8,128)(2,1)S(1)}, bf16[512,128]{1,0:T(8,128)(2,1)S(1)}, u32[]{:S(2)}, u32[]{:S(2)}) collective-permute-start(bf16[512,128]{1,0:T(8,128)(2,1)S(1)} %collective-permute-done.25.refs_2_), channel_id=1, source_target_pairs={{0,1},{1,0},{2,3},{3,2},{4,5},{5,4},{6,7},{7,6},{8,9},{9,8},{10,11... | collective-permute-start | bytes 393224 | tf_op jit(solution)/shard_map/ppermute | solution.py:33
  58.8 3.9 %collective-permute-start.20 = (bf16[512,128]{1,0:T(8,128)(2,1)S(1)}, bf16[512,128]{1,0:T(8,128)(2,1)S(1)}, u32[]{:S(2)}, u32[]{:S(2)}) collective-permute-start(bf16[512,128]{1,0:T(8,128)(2,1)S(1)} %collective-permute-done.19.refs_0_), channel_id=1, source_target_pairs={{0,1},{1,0},{2,3},{3,2},{4,5},{5,4},{6,7},{7,6},{8,9},{9,8},{10,11... | collective-permute-start | bytes 393224 | tf_op jit(solution)/shard_map/ppermute | solution.py:33
  58.9 3.9 %collective-permute-start.22 = (bf16[512,128]{1,0:T(8,128)(2,1)S(1)}, bf16[512,128]{1,0:T(8,128)(2,1)S(1)}, u32[]{:S(2)}, u32[]{:S(2)}) collective-permute-start(bf16[512,128]{1,0:T(8,128)(2,1)S(1)} %collective-permute-done.21.refs_2_), channel_id=1, source_target_pairs={{0,1},{1,0},{2,3},{3,2},{4,5},{5,4},{6,7},{7,6},{8,9},{9,8},{10,11... | collective-permute-start | bytes 393224 | tf_op jit(solution)/shard_map/ppermute | solution.py:33

commit v3 on v2

--- a/solution.py
+++ b/solution.py
@@ -25,6 +25,18 @@
     return lax.broadcasted_iota(jnp.int32, shape, dim)
 
 
+def _stay(x):
+    return pltpu.with_memory_space_constraint(x, pltpu.HBM)
+
+
+def _fetch(sources, targets, sems):
+    copies = [pltpu.make_async_copy(a, b, sems.at[i]) for i, (a, b) in enumerate(zip(sources, targets))]
+    for copy in copies:
+        copy.start()
+    for copy in copies:
+        copy.wait()
+
+
 def _params(mib):
     return pltpu.CompilerParams(vmem_limit_bytes=mib << 20)
 
@@ -38,32 +50,26 @@
     done = []
 
     def hop(i, m):
-        if i < len(work):
-            out = work[i](have)
-            if len(work) == 1:
-                have[m], out = lax.optimization_barrier((have[m], out))
+        if work[i] is not None:
+            have[m], out = lax.optimization_barrier((have[m], work[i](have)))
             done.append(out)
 
     have[8], have[4], have[2], have[1] = (swap(block, m) for m in (8, 4, 2, 1))
-    have[3] = swap(have[2], 1)
     hop(0, 8)
     have[12], have[10], have[6] = swap(have[8], 4), swap(have[8], 2), swap(have[4], 2)
-    have[5], have[7], have[9] = swap(have[4], 1), swap(have[6], 1), swap(have[8], 1)
+    have[3], have[5], have[7], have[9] = (swap(have[m], 1) for m in (2, 4, 6, 8))
     hop(1, 12)
     have[14] = swap(have[12], 2)
     have[11], have[13] = swap(have[10], 1), swap(have[12], 1)
     hop(2, 14)
     have[15] = swap(have[14], 1)
+    done.extend(w(have) for w in work[3:])
     return have, done
 
 
 def pack_kernel(devices, *refs):
     sources, out_ref, targets, sems = refs[0:4], refs[4], refs[5:9], refs[9]
-    copies = [pltpu.make_async_copy(a, b, sems.at[i]) for i, (a, b) in enumerate(zip(sources, targets))]
-    for copy in copies:
-        copy.start()
-    for copy in copies:
-        copy.wait()
+    _fetch(sources, targets, sems)
     feat_ref, cluster_ref, slot_ref, label_ref = targets
     rows = feat_ref.shape[0]
     per = rows // devices
@@ -85,25 +91,24 @@
     rows, width = features.shape
     per = rows // devices
     inputs = (features, cluster.reshape(1, rows), slot.reshape(1, rows), labels.reshape(rows // LANES, LANES))
+    inputs = [_stay(x) for x in inputs]
     return pl.pallas_call(
         lambda *refs: pack_kernel(devices, *refs),
         in_specs=[pl.BlockSpec(memory_space=pltpu.HBM)] * 4,
         out_specs=pl.BlockSpec(memory_space=pltpu.VMEM),
         out_shape=jax.ShapeDtypeStruct((devices + 1, per, width), BF16),
         scratch_shapes=[*[pltpu.VMEM(x.shape, x.dtype) for x in inputs], pltpu.SemaphoreType.DMA((4,))],
-        compiler_params=_params(60),
+        compiler_params=_params(8),
         name="pack_rows",
     )(*inputs)
 
 
-def prepare_kernel(adj_ref, self_ref, neigh_ref, w_out_ref, b_ref, *refs):
-    turned_ref, in_t_ref, out_t_ref, out_ref, bias_ref, adj, wide, line, sems = refs
-    tiles, neigh = turned_ref.shape[0:2]
+def weights_kernel(*refs):
+    sources, (in_t_ref, out_t_ref, out_ref, bias_ref), targets = refs[0:4], refs[4:8], refs[8:12]
+    wide, line, sems = refs[12:15]
+    _fetch(sources, targets, sems)
+    self_ref, neigh_ref, w_out_ref, b_ref = targets
     classes = w_out_ref.shape[0]
-    copies = [pltpu.make_async_copy(adj_ref.at[pl.ds(t * TILE, TILE)], adj.at[t], sems.at[t]) for t in range(tiles)]
-    for copy in copies:
-        copy.start()
-
     in_t_ref[...] = jnp.transpose(jnp.concatenate([self_ref[...], neigh_ref[...]], axis=0).astype(F32)).astype(BF16)
     wide[...] = jnp.zeros_like(wide)
     wide[0:classes, :] = w_out_ref[...].astype(F32)
@@ -113,12 +118,56 @@
     line[:, 0:classes] = b_ref[...]
     bias_ref[...] = jnp.transpose(jnp.broadcast_to(line[...], (LANES, line.shape[1])))[0 : bias_ref.shape[0]]
 
+
+def weights(w_self, w_neigh, w_out, b_out):
+    width, units = w_self.shape
+    classes = w_out.shape[1]
+    padded = -(-classes // SUB) * SUB
+    inputs = [_stay(x) for x in (w_self, w_neigh, w_out.T, b_out.reshape(1, classes))]
+    return pl.pallas_call(
+        weights_kernel,
+        in_specs=[pl.BlockSpec(memory_space=pltpu.HBM)] * 4,
+        out_specs=[pl.BlockSpec(memory_space=pltpu.VMEM)] * 4,
+        out_shape=[
+            jax.ShapeDtypeStruct((units, 2 * width), BF16),
+            jax.ShapeDtypeStruct((padded, units), BF16),
+            jax.ShapeDtypeStruct((units, padded), BF16),
+            jax.ShapeDtypeStruct((padded, LANES), F32),
+        ],
+        scratch_shapes=[
+            *[pltpu.VMEM(x.shape, x.dtype) for x in inputs],
+            pltpu.VMEM((padded, units), F32),
+            pltpu.VMEM((1, 2 * LANES), F32),
+            pltpu.SemaphoreType.DMA((4,)),
+        ],
+        cost_estimate=pl.CostEstimate(flops=0, bytes_accessed=1 << 21, transcendentals=0),
+        compiler_params=_params(8),
+        name="weights",
+    )(*inputs)
+
+
+def turn_kernel(first, adj_ref, turned_ref, adj, sems):
+    tiles, neigh = turned_ref.shape[0:2]
+    pieces = sems.shape[1]
+    part = TILE // pieces
+    copies = [
+        [
+            pltpu.make_async_copy(
+                adj_ref.at[pl.ds((first + t) * TILE + i * part, part)], adj.at[t, pl.ds(i * part, part)], sems.at[t, i]
+            )
+            for i in range(pieces)
+        ]
+        for t in range(tiles)
+    ]
+    for copy in sum(copies, []):
+        copy.start()
     side = SUB * SUB
     row = _iota((side, side), 0)
     move = ((row % SUB) * SUB + row // SUB == _iota((side, side), 1)).astype(BF16)
     for t in range(tiles):
-        copies[t].wait()
         for b in range(TILE // SUB):
+            if b * SUB % part == 0:
+                copies[t][b * SUB // part].wait()
             for j in range(neigh // (2 * SUB)):
                 halves = [
                     adj[t, SUB * b : SUB * (b + 1), SUB * k : SUB * (k + 1), :].reshape(side, TILE)
@@ -132,101 +181,99 @@
                     ].reshape(SUB, SUB, TILE)
 
 
-def prepare(adjacency, w_self, w_neigh, w_out, b_out):
-    rows, neigh, tile = adjacency.shape
-    width, units = w_self.shape
-    classes = w_out.shape[1]
-    padded = -(-classes // SUB) * SUB
-    tiles = rows // tile
-    vmem = pl.BlockSpec(memory_space=pltpu.VMEM)
-    return pl.pallas_call(
-        prepare_kernel,
-        in_specs=[pl.BlockSpec(memory_space=pltpu.HBM), *[vmem] * 4],
-        out_specs=[vmem] * 5,
-        out_shape=[
-            jax.ShapeDtypeStruct((tiles, neigh, tile, tile), BF16),
-            jax.ShapeDtypeStruct((units, 2 * width), BF16),
-            jax.ShapeDtypeStruct((padded, units), BF16),
-            jax.ShapeDtypeStruct((units, padded), BF16),
-            jax.ShapeDtypeStruct((padded, LANES), F32),
-        ],
-        scratch_shapes=[
-            pltpu.VMEM((tiles, tile, neigh, tile), BF16),
-            pltpu.VMEM((padded, units), F32),
-            pltpu.VMEM((1, 2 * LANES), F32),
-            pltpu.SemaphoreType.DMA((tiles,)),
-        ],
-        cost_estimate=pl.CostEstimate(flops=1 << 31, bytes_accessed=1 << 23, transcendentals=0),
-        compiler_params=_params(44),
-        name="prepare",
-    )(adjacency, w_self, w_neigh, w_out.T, b_out.reshape(1, classes))
-
-
-def aggregate_kernel(devices, *refs):
-    blocks = refs[:devices]
-    adj, halo_ref, slots_ref, px_ref, labels_ref, agg_ref, got, meta, sems = refs[devices:]
-    tiles, neigh = adj.shape[0:2]
+def turn(adjacency, first, tiles):
+    _, neigh, tile = adjacency.shape
+    pieces = 2
+    return pl.pallas_call(
+        lambda *refs: turn_kernel(first, *refs),
+        in_specs=[pl.BlockSpec(memory_space=pltpu.HBM)],
+        out_specs=pl.BlockSpec(memory_space=pltpu.VMEM),
+        out_shape=jax.ShapeDtypeStruct((tiles, neigh, tile, tile), BF16),
+        scratch_shapes=[pltpu.VMEM((tiles, tile, neigh, tile), BF16), pltpu.SemaphoreType.DMA((tiles, pieces))],
+        cost_estimate=pl.CostEstimate(flops=tiles << 29, bytes_accessed=tiles << 21, transcendentals=0),
+        compiler_params=_params(16),
+        name="turn_adjacency",
+    )(_stay(adjacency))
+
+
+def _place(ms, blocks, prior, px_ref, labels_ref, got):
     me = lax.axis_index("nodes")
     per = blocks[0].shape[1]
-    rows = devices * per
-    group = LANES // per
-
-    copies = []
-    for m, block in enumerate(blocks):
-        owner = me ^ m
-        at = pl.ds(pl.multiple_of(owner * per, per), per)
-        copies.append(pltpu.make_async_copy(block.at[0:devices], got.at[:, at, :], sems.at[0, m]))
-        copies.append(pltpu.make_async_copy(block.at[devices], meta.at[owner], sems.at[1, m]))
-    for copy in copies:
-        copy.start()
-    for copy in copies:
-        copy.wait()
-
-    labels_ref[...] = meta[:, SUB : 2 * SUB, :]
-    slots = [
-        sum(meta[q * group + j, 0:SUB, :].astype(F32) for j in range(group)) for q in range(devices // group)
+    rows = DEVICES * per
+    if prior:
+        labels_ref[...] = prior[1][...]
+    slots = []
+    for q in range(len(ms) // QUAD):
+        held = 0.0
+        for m, block in list(zip(ms, blocks))[q * QUAD : (q + 1) * QUAD]:
+            at = q * LANES + ((me % QUAD) ^ (m % QUAD)) * per
+            got[:, pl.ds(pl.multiple_of(at, per), per), :] = block[0:DEVICES]
+            held += block[DEVICES, 0:SUB, :].astype(F32)
+            labels_ref[me ^ m] = block[DEVICES, SUB : 2 * SUB, :]
+        slots.append(held)
+    slots = jnp.concatenate(slots, axis=1).astype(jnp.int32)
+    position = _iota((rows, slots.shape[1]), 0) - rows // 2
+    for p in range(DEVICES):
+        put = (position == slots[p : p + 1, :]).astype(BF16)
+        placed = _dot(put, got[p])
+        if prior:
+            placed += prior[0][p * rows : (p + 1) * rows, :].astype(F32)
+        px_ref[p * rows : (p + 1) * rows, :] = placed.astype(BF16)
+
+
+def _placed(per, width):
+    return [
+        jax.ShapeDtypeStruct((DEVICES * DEVICES * per, width), BF16),
+        jax.ShapeDtypeStruct((DEVICES, SUB, LANES), BF16),
     ]
-    slots = jnp.concatenate(slots, axis=1).astype(jnp.int32)
-    position = _iota((rows, rows), 0) - rows // 2
-    for p in range(devices):
-        put = (position == slots[p : p + 1, :]).astype(BF16)
-        px_ref[p * rows : (p + 1) * rows, :] = _dot(put, got[p]).astype(BF16)
-
-    for t in range(tiles):
+
+
+def place(have, ms):
+    per, width = have[0].shape[1:]
+    vmem = pl.BlockSpec(memory_space=pltpu.VMEM)
+    return pl.pallas_call(
+        lambda *refs: _place(ms, refs[: len(ms)], None, *refs[len(ms) :]),
+        in_specs=[vmem] * len(ms),
+        out_specs=[vmem] * 2,
+        out_shape=_placed(per, width),
+        scratch_shapes=[pltpu.VMEM((DEVICES, len(ms) * per, width), BF16)],
+        cost_estimate=pl.CostEstimate(flops=1 << 30, bytes_accessed=1 << 22, transcendentals=0),
+        compiler_params=_params(16),
+        name="place",
+    )(*[have[m] for m in ms])
+
+
+def aggregate_kernel(ms, parts, *refs):
+    n = len(ms)
+    blocks, prior, turned, refs = refs[:n], refs[n : n + 2], refs[n + 2 : n + 2 + parts], refs[n + 2 + parts :]
+    halo_ref, slots_ref, px_ref, labels_ref, agg_ref, got = refs
+    _place(ms, blocks, prior, px_ref, labels_ref, got)
+    neigh = slots_ref.shape[1]
+    tiles = [ref.at[t] for ref in turned for t in range(ref.shape[0])]
+    for t, adj in enumerate(tiles):
         total = jnp.zeros((TILE, px_ref.shape[1]), F32)
         for k in range(0, neigh, 2):
             sources = []
             for j in (k, k + 1):
                 tile = halo_ref[0, slots_ref[t, j]]
                 sources.append(px_ref[pl.ds(pl.multiple_of(tile * TILE, TILE), TILE), :])
-            weights = jnp.concatenate([adj[t, k], adj[t, k + 1]], axis=1)
-            total += _dot(weights, jnp.concatenate(sources, axis=0))
+            total += _dot(jnp.concatenate([adj[k], adj[k + 1]], axis=1), jnp.concatenate(sources, axis=0))
         agg_ref[t * TILE : (t + 1) * TILE, :] = total.astype(BF16)
 
 
-def aggregate(blocks, turned, halo_tiles, tile_slots, devices):
-    per, width = blocks[0].shape[1:]
-    rows = devices * per
-    anywhere = pl.BlockSpec(memory_space=pl.ANY)
+def aggregate(have, ms, prior, turned, halo_tiles, tile_slots):
+    per, width = have[0].shape[1:]
     scalars = pl.BlockSpec(memory_space=pltpu.SMEM)
     vmem = pl.BlockSpec(memory_space=pltpu.VMEM)
     return pl.pallas_call(
-        lambda *refs: aggregate_kernel(devices, *refs),
-        in_specs=[anywhere] * devices + [vmem] + [scalars] * 2,
+        lambda *refs: aggregate_kernel(ms, len(turned), *refs),
+        in_specs=[vmem] * (len(ms) + 2 + len(turned)) + [scalars] * 2,
         out_specs=[vmem] * 3,
-        out_shape=[
-            jax.ShapeDtypeStruct((devices * rows, width), BF16),
-            jax.ShapeDtypeStruct((devices, SUB, LANES), BF16),
-            jax.ShapeDtypeStruct((rows, width), BF16),
-        ],
-        scratch_shapes=[
-            pltpu.VMEM((devices, rows, width), BF16),
-            pltpu.VMEM((devices, 2 * SUB, LANES), BF16),
-            pltpu.SemaphoreType.DMA((2, devices)),
-        ],
-        compiler_params=_params(20),
+        out_shape=[*_placed(per, width), jax.ShapeDtypeStruct((DEVICES * per, width), BF16)],
+        scratch_shapes=[pltpu.VMEM((DEVICES, len(ms) * per, width), BF16)],
+        compiler_params=_params(24),
         name="aggregate",
-    )(*blocks, turned, halo_tiles, tile_slots)
+    )(*[have[m] for m in ms], *prior, *turned, halo_tiles, tile_slots)
 
 
 def _hot(kinds, labels_ref, owner):
@@ -386,12 +433,28 @@
     features, cluster, slot, halo_tiles, tile_slots, adjacency, labels, w_self, w_neigh, w_out, b_out
 ):
     packed = pack(features, cluster, slot, labels, DEVICES)
-    have, done = gather_all(packed, [lambda _: prepare(adjacency, w_self, w_neigh, w_out, b_out)])
-    turned, in_t, out_t, out_p, bias = done[0]
-    blocks = [have[m] for m in range(DEVICES)]
-    part_x, all_labels, agg = aggregate(blocks, turned, halo_tiles, tile_slots, DEVICES)
+    early, late = tuple(range(0, 8)), tuple(range(8, 16))
+    half = features.shape[0] // TILE // 2
+    work = [
+        lambda have: turn(adjacency, 0, half),
+        None,
+        lambda have: (place(have, early), turn(adjacency, half, half)),
+    ]
+    have, (near, (prior, far)) = gather_all(packed, work)
+    part_x, all_labels, agg = aggregate(have, late, prior, (near, far), halo_tiles, tile_slots)
+    ready = []
+
+    def quad(have, c):
+        in_t, out_t, _, bias = ready[0]
+        return forward(have, c, (part_x, all_labels, in_t, out_t, bias))
+
+    def prepare(have):
+        ready.append(weights(w_self, w_neigh, w_out, b_out))
+        return ready[0]
+
+    have, (_, *done) = gather_all(agg, [prepare, *[lambda have, c=c: quad(have, c) for c in range(QUAD - 1)]])
+    in_t, out_t, out_p, bias = ready[0]
     shared = (part_x, all_labels, in_t, out_t, bias)
-    have, done = gather_all(agg, [lambda have, c=c: forward(have, c, shared) for c in range(QUAD - 1)])
     hidden = done[0][5]
     early = [out[0:5] for out in done]
     grad_self, grad_neigh, grad_out, class_weight = backward(have, early, shared, out_p, w_out.shape[1])

time: 69.9 us -> 62.9 us (0.90)
  waiting for transfers between devices: 22.1 us -> 12.5 us
  starting transfers between devices: 18.1 us -> 22.7 us
  local copies, waits for them, and re-layouts: 3.26 us -> 0.01 us
  Pallas kernels: 25.5 us -> 26.6 us
    ppermute x30, waiting for transfers between devices: 22.1 us -> 12.5 us  [swap(): return lax.ppermute(x, 'nodes', [(i, i ^ m) for i in range(DEVICES)])]
    ppermute x30, starting transfers between devices: 18.1 us -> 22.7 us  [swap(): return lax.ppermute(x, 'nodes', [(i, i ^ m) for i in range(DEVICES)])]
    unnamed x14 -> x4, local copies, waits for them, and re-layouts: 3.26 us -> 0.01 us
    pallas_call x2 -> x5, Pallas kernels: 10.8 us -> 12.9 us  [the longest x2 6.04 us: turn(): pl.pallas_call(lambda *refs: turn_kernel(first, *refs), in_specs=[pl.Bloc...]
  transfers between devices with their start and end apart: 30 -> 30, of which waited for: 9 -> 8; matrix products, arithmetic and copies ran while one was open for 0% -> 0% of each run, Pallas kernels for 15% -> 23%
where the time goes in v3:
time: 62.9 us; the launch traced here: 62.7 us
  Pallas kernels  26.6 us (42%)
  starting transfers between devices  22.7 us (36%)
  waiting for transfers between devices  12.5 us (20%)
  between operations  0.82 us (1%)
    ppermute x30, starting transfers between devices, swap(): return lax.ppermute(x, 'nodes', [(i, i ^ m) for i in range(DEVICES)])  22.7 us
    ppermute x30, waiting for transfers between devices, swap(): return lax.ppermute(x, 'nodes', [(i, i ^ m) for i in range(DEVICES)])  12.5 us
    pallas_call x1, Pallas kernels, backward(): pl.pallas_call(lambda *refs: backward_kernel(classes, *refs), in_specs=[v...  6.69 us
    pallas_call x2, Pallas kernels, turn(): pl.pallas_call(lambda *refs: turn_kernel(first, *refs), in_specs=[pl.Bloc...  6.04 us
    pallas_call x3, Pallas kernels, forward(): pl.pallas_call(lambda *refs: forward_kernel(c, *refs), in_specs=[vmem] *...  5.61 us
    pallas_call x1, Pallas kernels, aggregate(): pl.pallas_call(lambda *refs: aggregate_kernel(ms, len(turned), *refs), in...  4.33 us
    pallas_call x1, Pallas kernels, pack(): pl.pallas_call(lambda *refs: pack_kernel(devices, *refs), in_specs=[pl.Bl...  1.45 us
    pallas_call x1, Pallas kernels, place(): pl.pallas_call(lambda *refs: _place(ms, refs[:len(ms)], None, *refs[len(m...  1.34 us
  transfers between devices with their start and end apart: 30, of which 8 were waited for; matrix products, arithmetic and copies ran while one was open for 0% of the time, Pallas kernels for 23%

profile of v3, /device:TPU:0, one launch (start us, length us, event | category | flops | bytes accessed | tf_op | source)
XLA Modules:
  0.0 62.7 jit_solution(15591634712987652735)
XLA Ops:
  0.6 1.5 %pack_rows.1.refs_0_ = bf16[17,32,128]{2,1,0:T(8,128)(2,1)S(1)} custom-call(bf16[512,128]{1,0:T(8,128)(2,1)} %refs_0_.4, s32[1,512]{1,0:T(1,128)} %bitcast.8, s32[1,512]{1,0:T(1,128)} %bitcast.9, s32[4,128]{1,0:T(4,128)} %bitcast.10), custom_call_target="tpu_custom_call" | custom-call | tf_op jit(solution)/shard_map/pack_rows/pallas_call | solution.py:95
  2.1 3.1 %collective-permute-start.10 = (bf16[17,32,128]{2,1,0:T(8,128)(2,1)S(1)}, bf16[17,32,128]{2,1,0:T(8,128)(2,1)S(1)}, u32[]{:S(2)}, u32[]{:S(2)}) collective-permute-start(bf16[17,32,128]{2,1,0:T(8,128)(2,1)S(1)} %pack_rows.1.refs_0_), channel_id=1, source_target_pairs={{0,4},{1,5},{2,6},{3,7},{4,0},{5,1},{6,2},{7,3},{8,12},{9,13},{10,... | collective-permute-start | bytes 417800 | tf_op jit(solution)/shard_map/ppermute | solution.py:45
  5.2 2.6 %collective-permute-start = (bf16[17,32,128]{2,1,0:T(8,128)(2,1)S(1)}, bf16[17,32,128]{2,1,0:T(8,128)(2,1)S(1)}, u32[]{:S(2)}, u32[]{:S(2)}) collective-permute-start(bf16[17,32,128]{2,1,0:T(8,128)(2,1)S(1)} %pack_rows.1.refs_0_), channel_id=1, source_target_pairs={{0,8},{1,9},{2,10},{3,11},{4,12},{5,13},{6,14},{7,15},{8,0},{9,1},... | collective-permute-start | bytes 417800 | tf_op jit(solution)/shard_map/ppermute | solution.py:45
  7.8 1.5 %collective-permute-start.8 = (bf16[17,32,128]{2,1,0:T(8,128)(2,1)S(1)}, bf16[17,32,128]{2,1,0:T(8,128)(2,1)S(1)}, u32[]{:S(2)}, u32[]{:S(2)}) collective-permute-start(bf16[17,32,128]{2,1,0:T(8,128)(2,1)S(1)} %pack_rows.1.refs_0_), channel_id=1, source_target_pairs={{0,2},{1,3},{2,0},{3,1},{4,6},{5,7},{6,4},{7,5},{8,10},{9,11},{10,... | collective-permute-start | bytes 417800 | tf_op jit(solution)/shard_map/ppermute | solution.py:45
  9.3 1.8 %collective-permute-done.10.refs_4_ = bf16[17,32,128]{2,1,0:T(8,128)(2,1)S(1)} collective-permute-done((bf16[17,32,128]{2,1,0:T(8,128)(2,1)S(1)}, bf16[17,32,128]{2,1,0:T(8,128)(2,1)S(1)}, u32[]{:S(2)}, u32[]{:S(2)}) %collective-permute-start.10) | collective-permute-done | bytes 139296 | tf_op jit(solution)/shard_map/ppermute | solution.py:45
  11.1 1.8 %collective-permute-start.12 = (bf16[17,32,128]{2,1,0:T(8,128)(2,1)S(1)}, bf16[17,32,128]{2,1,0:T(8,128)(2,1)S(1)}, u32[]{:S(2)}, u32[]{:S(2)}) collective-permute-start(bf16[17,32,128]{2,1,0:T(8,128)(2,1)S(1)} %collective-permute-done.10.refs_4_), channel_id=1, source_target_pairs={{0,2},{1,3},{2,0},{3,1},{4,6},{5,7},{6,4},{7,5},{8,10},{9,11},{10,... | collective-permute-start | bytes 417800 | tf_op jit(solution)/shard_map/ppermute | solution.py:45
  12.9 3.0 %turn_adjacency.2.refs_10_ = bf16[2,64,128,128]{3,2,1,0:T(8,128)(2,1)S(1)} custom-call(bf16[512,64,128]{2,1,0:T(8,128)(2,1)} %refs_0_.6), custom_call_target="tpu_custom_call" | custom-call | flops 1073741824 | bytes 4194304 | tf_op jit(solution)/shard_map/turn_adjacency/pallas_call | solution.py:187
  15.9 0.0 collective-permute-done.refs_0_
  15.9 0.1 collective-permute-start.4
  16.0 0.1 collective-permute-start.11
  16.1 0.5 collective-permute-start.9
  16.6 0.0 collective-permute-done.7.refs_1_
  16.6 0.3 collective-permute-start.2
  16.9 4.2 %collective-permute-done.4.refs_4_ = bf16[17,32,128]{2,1,0:T(8,128)(2,1)S(1)} collective-permute-done((bf16[17,32,128]{2,1,0:T(8,128)(2,1)S(1)}, bf16[17,32,128]{2,1,0:T(8,128)(2,1)S(1)}, u32[]{:S(2)}, u32[]{:S(2)}) %collective-permute-start.4) | collective-permute-done | bytes 139296 | tf_op jit(solution)/shard_map/ppermute | solution.py:45
  21.1 0.2 collective-permute-start.6
  21.2 3.0 %turn_adjacency.3.refs_11_ = bf16[2,64,128,128]{3,2,1,0:T(8,128)(2,1)S(1)} custom-call(bf16[512,64,128]{2,1,0:T(8,128)(2,1)} %refs_0_.6), custom_call_target="tpu_custom_call" | custom-call | flops 1073741824 | bytes 4194304 | tf_op jit(solution)/shard_map/turn_adjacency/pallas_call | solution.py:187
  24.3 0.0 copy-start
  24.3 0.0 copy-start.1
  24.3 0.0 collective-permute-done.11.refs_5_
  24.3 0.1 collective-permute-start.1
  24.4 0.0 collective-permute-done.9.refs_3_
  24.4 0.5 collective-permute-start.5
  24.9 0.1 collective-permute-start.3
  25.0 0.0 collective-permute-done.13.refs_7_
  25.0 1.3 %place.1 = (bf16[8192,128]{1,0:T(8,128)(2,1)S(1)}, bf16[16,16,128]{2,1,0:T(8,128)(2,1)S(1)}) custom-call(bf16[17,32,128]{2,1,0:T(8,128)(2,1)S(1)} %pack_rows.1.refs_0_, bf16[17,32,128]{2,1,0:T(8,128)(2,1)S(1)} %collective-permute-done.7.refs_1_, bf16[17,32,128]{2,1,0:T(8,128)(2,1)S(1)} %collective-permute-done.8.refs_2_, ...), custom_call_target="tpu_custom_call" | custom-call | flops 1073741824 | bytes 4194304 | tf_op jit(solution)/shard_map/place/pallas_call | solution.py:234
  26.3 0.0 collective-permute-done.6.refs_6_
  26.3 0.5 collective-permute-start.14
  26.8 1.0 %collective-permute-done.14.refs_7_ = bf16[17,32,128]{2,1,0:T(8,128)(2,1)S(1)} collective-permute-done((bf16[17,32,128]{2,1,0:T(8,128)(2,1)S(1)}, bf16[17,32,128]{2,1,0:T(8,128)(2,1)S(1)}, u32[]{:S(2)}, u32[]{:S(2)}) %collective-permute-start.14) | collective-permute-done | bytes 139296 | tf_op jit(solution)/shard_map/ppermute | solution.py:45
  27.8 4.3 %aggregate.1 = (bf16[8192,128]{1,0:T(8,128)(2,1)S(1)}, bf16[16,16,128]{2,1,0:T(8,128)(2,1)S(1)}, bf16[512,128]{1,0:T(8,128)(2,1)S(1)}) custom-call(bf16[17,32,128]{2,1,0:T(8,128)(2,1)S(1)} %collective-permute-done.refs_0_, bf16[17,32,128]{2,1,0:T(8,128)(2,1)S(1)} %collective-permute-done.1.refs_1_, bf16[17,32,128]{2,1,0:T(8,128)(2,1)S(1)} %collective-permute-done.2.refs_2_, ...), custom_call_target="tpu_custom_call" | custom-call | tf_op jit(solution)/shard_map/aggregate/pallas_call | solution.py:268
  32.2 0.8 %collective-permute-start.22 = (bf16[512,128]{1,0:T(8,128)(2,1)S(1)}, bf16[512,128]{1,0:T(8,128)(2,1)S(1)}, u32[]{:S(2)}, u32[]{:S(2)}) collective-permute-start(bf16[512,128]{1,0:T(8,128)(2,1)S(1)} %get-tuple-element.62.refs_0_), channel_id=1, source_target_pairs={{0,4},{1,5},{2,6},{3,7},{4,0},{5,1},{6,2},{7,3},{8,12},{9,13},{10,... | collective-permute-start | bytes 393224 | tf_op jit(solution)/shard_map/ppermute | solution.py:45
  32.9 1.2 %collective-permute-start.18 = (bf16[512,128]{1,0:T(8,128)(2,1)S(1)}, bf16[512,128]{1,0:T(8,128)(2,1)S(1)}, u32[]{:S(2)}, u32[]{:S(2)}) collective-permute-start(bf16[512,128]{1,0:T(8,128)(2,1)S(1)} %get-tuple-element.62.refs_0_), channel_id=1, source_target_pairs={{0,2},{1,3},{2,0},{3,1},{4,6},{5,7},{6,4},{7,5},{8,10},{9,11},{10,... | collective-permute-start | bytes 393224 | tf_op jit(solution)/shard_map/ppermute | solution.py:45
  34.2 3.5 %collective-permute-start.15 = (bf16[512,128]{1,0:T(8,128)(2,1)S(1)}, bf16[512,128]{1,0:T(8,128)(2,1)S(1)}, u32[]{:S(2)}, u32[]{:S(2)}) collective-permute-start(bf16[512,128]{1,0:T(8,128)(2,1)S(1)} %get-tuple-element.62.refs_0_), channel_id=1, source_target_pairs={{0,8},{1,9},{2,10},{3,11},{4,12},{5,13},{6,14},{7,15},{8,0},{9,1},... | collective-permute-start | bytes 393224 | tf_op jit(solution)/shard_map/ppermute | solution.py:45
  37.6 0.3 collective-permute-done.22.refs_0_
  38.0 4.2 %collective-permute-start.24 = (bf16[512,128]{1,0:T(8,128)(2,1)S(1)}, bf16[512,128]{1,0:T(8,128)(2,1)S(1)}, u32[]{:S(2)}, u32[]{:S(2)}) collective-permute-start(bf16[512,128]{1,0:T(8,128)(2,1)S(1)} %collective-permute-done.22.refs_0_), channel_id=1, source_target_pairs={{0,2},{1,3},{2,0},{3,1},{4,6},{5,7},{6,4},{7,5},{8,10},{9,11},{10,... | collective-permute-start | bytes 393224 | tf_op jit(solution)/shard_map/ppermute | solution.py:45
  42.2 1.2 %weights.1 = (bf16[256,256]{1,0:T(8,128)(2,1)S(1)}, bf16[176,256]{1,0:T(8,128)(2,1)S(1)}, bf16[256,176]{1,0:T(8,128)(2,1)S(1)}, f32[176,128]{1,0:T(8,128)S(1)}) custom-call(bf16[128,256]{1,0:T(8,128)(2,1)} %refs_0_.7, bf16[128,256]{1,0:T(8,128)(2,1)} %refs_1_.1, bf16[172,256]{1,0:T(8,128)(2,1)} %bitcast.7, f32[1,172]{1,0:T(1,128)} %bitcast.11), custom_call_target="tpu_custom_call" | custom-call | bytes 2097152 | tf_op jit(solution)/shard_map/weights/pallas_call | solution.py:127
  43.4 0.5 collective-permute-done.15.refs_0_
  43.9 0.7 %collective-permute-start.28 = (bf16[512,128]{1,0:T(8,128)(2,1)S(1)}, bf16[512,128]{1,0:T(8,128)(2,1)S(1)}, u32[]{:S(2)}, u32[]{:S(2)}) collective-permute-start(bf16[512,128]{1,0:T(8,128)(2,1)S(1)} %collective-permute-done.15.refs_0_), channel_id=1, source_target_pairs={{0,2},{1,3},{2,0},{3,1},{4,6},{5,7},{6,4},{7,5},{8,10},{9,11},{10,... | collective-permute-start | bytes 393224 | tf_op jit(solution)/shard_map/ppermute | solution.py:45
  44.6 0.8 %collective-permute-done.24.refs_2_ = bf16[512,128]{1,0:T(8,128)(2,1)S(1)} collective-permute-done((bf16[512,128]{1,0:T(8,128)(2,1)S(1)}, bf16[512,128]{1,0:T(8,128)(2,1)S(1)}, u32[]{:S(2)}, u32[]{:S(2)}) %collective-permute-start.24) | collective-permute-done | bytes 131104 | tf_op jit(solution)/shard_map/ppermute | solution.py:45
  45.4 2.3 %forward.3 = (bf16[2048,128]{1,0:T(8,128)(2,1)S(1)}, bf16[256,2048]{1,0:T(8,128)(2,1)S(1)}, f32[176,2048]{1,0:T(8,128)S(1)}, f32[176,128]{1,0:T(8,128)S(1)}, f32...) custom-call(bf16[512,128]{1,0:T(8,128)(2,1)S(1)} %get-tuple-element.62.refs_0_, ...), custom_call_target="tpu_custom_call" | custom-call | flops 1073741824 | bytes 4194304 | tf_op jit(solution)/shard_map/forward/pallas_call | solution.py:341
  47.7 1.7 %collective-permute-done.16.refs_0_ = bf16[512,128]{1,0:T(8,128)(2,1)S(1)} collective-permute-done((bf16[512,128]{1,0:T(8,128)(2,1)S(1)}, bf16[512,128]{1,0:T(8,128)(2,1)S(1)}, u32[]{:S(2)}, u32[]{:S(2)}) %collective-permute-start.16) | collective-permute-done | bytes 131104 | tf_op jit(solution)/shard_map/ppermute | solution.py:45
  49.4 0.3 collective-permute-start.21
  49.7 0.2 collective-permute-start.27
  49.9 0.3 collective-permute-start.20
  50.2 0.2 collective-permute-start.29
  50.4 1.7 %forward.4 = (bf16[2048,128]{1,0:T(8,128)(2,1)S(1)}, bf16[256,2048]{1,0:T(8,128)(2,1)S(1)}, f32[176,2048]{1,0:T(8,128)S(1)}, f32[176,128]{1,0:T(8,128)S(1)}, f32[176,128]{1,0:T(8,128)S(1)}) custom-call(bf16[512,128]{1,0:T(8,128)(2,1)S(1)} %collective-permute-done.22.refs_0_, bf16[512,128]{1,0:T(8,128)(2,1)S(1)} %collective-permute-done.23.refs_1_, ...), custom_call_target="tpu_custom_call" | custom-call | flops 1073741824 | bytes 4194304 | tf_op jit(solution)/shard_map/forward/pallas_call | solution.py:341
  52.1 2.2 %collective-permute-done.21.refs_2_ = bf16[512,128]{1,0:T(8,128)(2,1)S(1)} collective-permute-done((bf16[512,128]{1,0:T(8,128)(2,1)S(1)}, bf16[512,128]{1,0:T(8,128)(2,1)S(1)}, u32[]{:S(2)}, u32[]{:S(2)}) %collective-permute-start.21) | collective-permute-done | bytes 131104 | tf_op jit(solution)/shard_map/ppermute | solution.py:45
  54.4 1.7 %forward.5 = (bf16[2048,128]{1,0:T(8,128)(2,1)S(1)}, bf16[256,2048]{1,0:T(8,128)(2,1)S(1)}, f32[176,2048]{1,0:T(8,128)S(1)}, f32[176,128]{1,0:T(8,128)S(1)}, f32[176,128]{1,0:T(8,128)S(1)}) custom-call(bf16[512,128]{1,0:T(8,128)(2,1)S(1)} %collective-permute-done.15.refs_0_, bf16[512,128]{1,0:T(8,128)(2,1)S(1)} %collective-permute-done.27.refs_1_, ...), custom_call_target="tpu_custom_call" | custom-call | flops 1073741824 | bytes 4194304 | tf_op jit(solution)/shard_map/forward/pallas_call | solution.py:341
  56.0 6.7 %backward.1 = (f32[128,256]{1,0:T(8,128)}, f32[128,256]{1,0:T(8,128)}, f32[172,256]{1,0:T(8,128)}, f32[1,172]{1,0:T(1,128)}) custom-call(bf16[512,128]{1,0:T(8,128)(2,1)S(1)} %collective-permute-done.16.refs_0_, bf16[512,128]{1,0:T(8,128)(2,1)S(1)} %collective-permute-done.20.refs_1_, bf16[512,128]{1,0:T(8,128)(2,1)S(1)} %collective-permute-done.21.refs_2_, ...), custom_call_target="tpu_custom_call" | custom-call | tf_op jit(solution)/shard_map/backward/pallas_call | solution.py:410
  (26 shorter events, 0.1 us)
Async XLA Ops:
  2.1 9.0 %collective-permute-start.10 = (bf16[17,32,128]{2,1,0:T(8,128)(2,1)S(1)}, bf16[17,32,128]{2,1,0:T(8,128)(2,1)S(1)}, u32[]{:S(2)}, u32[]{:S(2)}) collective-permute-start(bf16[17,32,128]{2,1,0:T(8,128)(2,1)S(1)} %pack_rows.1.refs_0_), channel_id=1, source_target_pairs={{0,4},{1,5},{2,6},{3,7},{4,0},{5,1},{6,2},{7,3},{8,12},{9,13},{10,... | collective-permute-start | bytes 417800 | tf_op jit(solution)/shard_map/ppermute | solution.py:45
  5.2 10.7 %collective-permute-start = (bf16[17,32,128]{2,1,0:T(8,128)(2,1)S(1)}, bf16[17,32,128]{2,1,0:T(8,128)(2,1)S(1)}, u32[]{:S(2)}, u32[]{:S(2)}) collective-permute-start(bf16[17,32,128]{2,1,0:T(8,128)(2,1)S(1)} %pack_rows.1.refs_0_), channel_id=1, source_target_pairs={{0,8},{1,9},{2,10},{3,11},{4,12},{5,13},{6,14},{7,15},{8,0},{9,1},... | collective-permute-start | bytes 417800 | tf_op jit(solution)/shard_map/ppermute | solution.py:45
  7.8 8.3 %collective-permute-start.8 = (bf16[17,32,128]{2,1,0:T(8,128)(2,1)S(1)}, bf16[17,32,128]{2,1,0:T(8,128)(2,1)S(1)}, u32[]{:S(2)}, u32[]{:S(2)}) collective-permute-start(bf16[17,32,128]{2,1,0:T(8,128)(2,1)S(1)} %pack_rows.1.refs_0_), channel_id=1, source_target_pairs={{0,2},{1,3},{2,0},{3,1},{4,6},{5,7},{6,4},{7,5},{8,10},{9,11},{10,... | collective-permute-start | bytes 417800 | tf_op jit(solution)/shard_map/ppermute | solution.py:45
  9.3 7.3 %collective-permute-start.7 = (bf16[17,32,128]{2,1,0:T(8,128)(2,1)S(1)}, bf16[17,32,128]{2,1,0:T(8,128)(2,1)S(1)}, u32[]{:S(2)}, u32[]{:S(2)}) collective-permute-start(bf16[17,32,128]{2,1,0:T(8,128)(2,1)S(1)} %pack_rows.1.refs_0_), channel_id=1, source_target_pairs={{0,1},{1,0},{2,3},{3,2},{4,5},{5,4},{6,7},{7,6},{8,9},{9,8},{10,11... | collective-permute-start | bytes 417800 | tf_op jit(solution)/shard_map/ppermute | solution.py:45
  11.1 5.9 %collective-permute-start.12 = (bf16[17,32,128]{2,1,0:T(8,128)(2,1)S(1)}, bf16[17,32,128]{2,1,0:T(8,128)(2,1)S(1)}, u32[]{:S(2)}, u32[]{:S(2)}) collective-permute-start(bf16[17,32,128]{2,1,0:T(8,128)(2,1)S(1)} %collective-permute-done.10.refs_4_), channel_id=1, source_target_pairs={{0,2},{1,3},{2,0},{3,1},{4,6},{5,7},{6,4},{7,5},{8,10},{9,11},{10,... | collective-permute-start | bytes 417800 | tf_op jit(solution)/shard_map/ppermute | solution.py:45
  15.9 5.1 %collective-permute-start.4 = (bf16[17,32,128]{2,1,0:T(8,128)(2,1)S(1)}, bf16[17,32,128]{2,1,0:T(8,128)(2,1)S(1)}, u32[]{:S(2)}, u32[]{:S(2)}) collective-permute-start(bf16[17,32,128]{2,1,0:T(8,128)(2,1)S(1)} %collective-permute-done.refs_0_), channel_id=1, source_target_pairs={{0,4},{1,5},{2,6},{3,7},{4,0},{5,1},{6,2},{7,3},{8,12},{9,13},{10,... | collective-permute-start | bytes 417800 | tf_op jit(solution)/shard_map/ppermute | solution.py:45
  16.0 8.3 %collective-permute-start.11 = (bf16[17,32,128]{2,1,0:T(8,128)(2,1)S(1)}, bf16[17,32,128]{2,1,0:T(8,128)(2,1)S(1)}, u32[]{:S(2)}, u32[]{:S(2)}) collective-permute-start(bf16[17,32,128]{2,1,0:T(8,128)(2,1)S(1)} %collective-permute-done.10.refs_4_), channel_id=1, source_target_pairs={{0,1},{1,0},{2,3},{3,2},{4,5},{5,4},{6,7},{7,6},{8,9},{9,8},{10,11... | collective-permute-start | bytes 417800 | tf_op jit(solution)/shard_map/ppermute | solution.py:45
  16.1 8.3 %collective-permute-start.9 = (bf16[17,32,128]{2,1,0:T(8,128)(2,1)S(1)}, bf16[17,32,128]{2,1,0:T(8,128)(2,1)S(1)}, u32[]{:S(2)}, u32[]{:S(2)}) collective-permute-start(bf16[17,32,128]{2,1,0:T(8,128)(2,1)S(1)} %collective-permute-done.8.refs_2_), channel_id=1, source_target_pairs={{0,1},{1,0},{2,3},{3,2},{4,5},{5,4},{6,7},{7,6},{8,9},{9,8},{10,11... | collective-permute-start | bytes 417800 | tf_op jit(solution)/shard_map/ppermute | solution.py:45
  16.6 8.3 %collective-permute-start.2 = (bf16[17,32,128]{2,1,0:T(8,128)(2,1)S(1)}, bf16[17,32,128]{2,1,0:T(8,128)(2,1)S(1)}, u32[]{:S(2)}, u32[]{:S(2)}) collective-permute-start(bf16[17,32,128]{2,1,0:T(8,128)(2,1)S(1)} %collective-permute-done.refs_0_), channel_id=1, source_target_pairs={{0,2},{1,3},{2,0},{3,1},{4,6},{5,7},{6,4},{7,5},{8,10},{9,11},{10,... | collective-permute-start | bytes 417800 | tf_op jit(solution)/shard_map/ppermute | solution.py:45
  16.9 8.1 %collective-permute-start.13 = (bf16[17,32,128]{2,1,0:T(8,128)(2,1)S(1)}, bf16[17,32,128]{2,1,0:T(8,128)(2,1)S(1)}, u32[]{:S(2)}, u32[]{:S(2)}) collective-permute-start(bf16[17,32,128]{2,1,0:T(8,128)(2,1)S(1)} %collective-permute-done.12.refs_6_), channel_id=1, source_target_pairs={{0,1},{1,0},{2,3},{3,2},{4,5},{5,4},{6,7},{7,6},{8,9},{9,8},{10,11... | collective-permute-start | bytes 417800 | tf_op jit(solution)/shard_map/ppermute | solution.py:45
  21.1 5.3 %collective-permute-start.6 = (bf16[17,32,128]{2,1,0:T(8,128)(2,1)S(1)}, bf16[17,32,128]{2,1,0:T(8,128)(2,1)S(1)}, u32[]{:S(2)}, u32[]{:S(2)}) collective-permute-start(bf16[17,32,128]{2,1,0:T(8,128)(2,1)S(1)} %collective-permute-done.4.refs_4_), channel_id=1, source_target_pairs={{0,2},{1,3},{2,0},{3,1},{4,6},{5,7},{6,4},{7,5},{8,10},{9,11},{10,... | collective-permute-start | bytes 417800 | tf_op jit(solution)/shard_map/ppermute | solution.py:45
  24.3 3.6 %copy-start = (s32[4,64]{1,0:T(4,128)S(1)}, s32[4,64]{1,0:T(4,128)}, u32[]{:S(2)}) copy-start(s32[4,64]{1,0:T(4,128)} %refs_13_.1) | copy-start | bytes 3076
  24.3 3.5 %copy-start.1 = (s32[1,64]{1,0:T(1,128)S(1)}, s32[1,64]{1,0:T(1,128)}, u32[]{:S(2)}) copy-start(s32[1,64]{1,0:T(1,128)} %refs_12_.1) | copy-start | bytes 772
  24.3 2.5 %collective-permute-start.1 = (bf16[17,32,128]{2,1,0:T(8,128)(2,1)S(1)}, bf16[17,32,128]{2,1,0:T(8,128)(2,1)S(1)}, u32[]{:S(2)}, u32[]{:S(2)}) collective-permute-start(bf16[17,32,128]{2,1,0:T(8,128)(2,1)S(1)} %collective-permute-done.refs_0_), channel_id=1, source_target_pairs={{0,1},{1,0},{2,3},{3,2},{4,5},{5,4},{6,7},{7,6},{8,9},{9,8},{10,11... | collective-permute-start | bytes 417800 | tf_op jit(solution)/shard_map/ppermute | solution.py:45
  24.4 2.4 %collective-permute-start.5 = (bf16[17,32,128]{2,1,0:T(8,128)(2,1)S(1)}, bf16[17,32,128]{2,1,0:T(8,128)(2,1)S(1)}, u32[]{:S(2)}, u32[]{:S(2)}) collective-permute-start(bf16[17,32,128]{2,1,0:T(8,128)(2,1)S(1)} %collective-permute-done.4.refs_4_), channel_id=1, source_target_pairs={{0,1},{1,0},{2,3},{3,2},{4,5},{5,4},{6,7},{7,6},{8,9},{9,8},{10,11... | collective-permute-start | bytes 417800 | tf_op jit(solution)/shard_map/ppermute | solution.py:45
  24.9 1.9 %collective-permute-start.3 = (bf16[17,32,128]{2,1,0:T(8,128)(2,1)S(1)}, bf16[17,32,128]{2,1,0:T(8,128)(2,1)S(1)}, u32[]{:S(2)}, u32[]{:S(2)}) collective-permute-start(bf16[17,32,128]{2,1,0:T(8,128)(2,1)S(1)} %collective-permute-done.2.refs_2_), channel_id=1, source_target_pairs={{0,1},{1,0},{2,3},{3,2},{4,5},{5,4},{6,7},{7,6},{8,9},{9,8},{10,11... | collective-permute-start | bytes 417800 | tf_op jit(solution)/shard_map/ppermute | solution.py:45
  26.3 1.5 %collective-permute-start.14 = (bf16[17,32,128]{2,1,0:T(8,128)(2,1)S(1)}, bf16[17,32,128]{2,1,0:T(8,128)(2,1)S(1)}, u32[]{:S(2)}, u32[]{:S(2)}) collective-permute-start(bf16[17,32,128]{2,1,0:T(8,128)(2,1)S(1)} %collective-permute-done.6.refs_6_), channel_id=1, source_target_pairs={{0,1},{1,0},{2,3},{3,2},{4,5},{5,4},{6,7},{7,6},{8,9},{9,8},{10,11... | collective-permute-start | bytes 417800 | tf_op jit(solution)/shard_map/ppermute | solution.py:45
  32.2 5.8 %collective-permute-start.22 = (bf16[512,128]{1,0:T(8,128)(2,1)S(1)}, bf16[512,128]{1,0:T(8,128)(2,1)S(1)}, u32[]{:S(2)}, u32[]{:S(2)}) collective-permute-start(bf16[512,128]{1,0:T(8,128)(2,1)S(1)} %get-tuple-element.62.refs_0_), channel_id=1, source_target_pairs={{0,4},{1,5},{2,6},{3,7},{4,0},{5,1},{6,2},{7,3},{8,12},{9,13},{10,... | collective-permute-start | bytes 393224 | tf_op jit(solution)/shard_map/ppermute | solution.py:45
  32.9 9.3 %collective-permute-start.18 = (bf16[512,128]{1,0:T(8,128)(2,1)S(1)}, bf16[512,128]{1,0:T(8,128)(2,1)S(1)}, u32[]{:S(2)}, u32[]{:S(2)}) collective-permute-start(bf16[512,128]{1,0:T(8,128)(2,1)S(1)} %get-tuple-element.62.refs_0_), channel_id=1, source_target_pairs={{0,2},{1,3},{2,0},{3,1},{4,6},{5,7},{6,4},{7,5},{8,10},{9,11},{10,... | collective-permute-start | bytes 393224 | tf_op jit(solution)/shard_map/ppermute | solution.py:45
  34.2 9.7 %collective-permute-start.15 = (bf16[512,128]{1,0:T(8,128)(2,1)S(1)}, bf16[512,128]{1,0:T(8,128)(2,1)S(1)}, u32[]{:S(2)}, u32[]{:S(2)}) collective-permute-start(bf16[512,128]{1,0:T(8,128)(2,1)S(1)} %get-tuple-element.62.refs_0_), channel_id=1, source_target_pairs={{0,8},{1,9},{2,10},{3,11},{4,12},{5,13},{6,14},{7,15},{8,0},{9,1},... | collective-permute-start | bytes 393224 | tf_op jit(solution)/shard_map/ppermute | solution.py:45
  37.6 6.9 %collective-permute-start.17 = (bf16[512,128]{1,0:T(8,128)(2,1)S(1)}, bf16[512,128]{1,0:T(8,128)(2,1)S(1)}, u32[]{:S(2)}, u32[]{:S(2)}) collective-permute-start(bf16[512,128]{1,0:T(8,128)(2,1)S(1)} %get-tuple-element.62.refs_0_), channel_id=1, source_target_pairs={{0,1},{1,0},{2,3},{3,2},{4,5},{5,4},{6,7},{7,6},{8,9},{9,8},{10,11... | collective-permute-start | bytes 393224 | tf_op jit(solution)/shard_map/ppermute | solution.py:45
  38.0 7.4 %collective-permute-start.24 = (bf16[512,128]{1,0:T(8,128)(2,1)S(1)}, bf16[512,128]{1,0:T(8,128)(2,1)S(1)}, u32[]{:S(2)}, u32[]{:S(2)}) collective-permute-start(bf16[512,128]{1,0:T(8,128)(2,1)S(1)} %collective-permute-done.22.refs_0_), channel_id=1, source_target_pairs={{0,2},{1,3},{2,0},{3,1},{4,6},{5,7},{6,4},{7,5},{8,10},{9,11},{10,... | collective-permute-start | bytes 393224 | tf_op jit(solution)/shard_map/ppermute | solution.py:45
  42.2 3.2 %collective-permute-start.19 = (bf16[512,128]{1,0:T(8,128)(2,1)S(1)}, bf16[512,128]{1,0:T(8,128)(2,1)S(1)}, u32[]{:S(2)}, u32[]{:S(2)}) collective-permute-start(bf16[512,128]{1,0:T(8,128)(2,1)S(1)} %collective-permute-done.18.refs_2_), channel_id=1, source_target_pairs={{0,1},{1,0},{2,3},{3,2},{4,5},{5,4},{6,7},{7,6},{8,9},{9,8},{10,11... | collective-permute-start | bytes 393224 | tf_op jit(solution)/shard_map/ppermute | solution.py:45
  43.9 5.5 %collective-permute-start.16 = (bf16[512,128]{1,0:T(8,128)(2,1)S(1)}, bf16[512,128]{1,0:T(8,128)(2,1)S(1)}, u32[]{:S(2)}, u32[]{:S(2)}) collective-permute-start(bf16[512,128]{1,0:T(8,128)(2,1)S(1)} %collective-permute-done.15.refs_0_), channel_id=1, source_target_pairs={{0,4},{1,5},{2,6},{3,7},{4,0},{5,1},{6,2},{7,3},{8,12},{9,13},{10,... | collective-permute-start | bytes 393224 | tf_op jit(solution)/shard_map/ppermute | solution.py:45
  43.9 6.0 %collective-permute-start.28 = (bf16[512,128]{1,0:T(8,128)(2,1)S(1)}, bf16[512,128]{1,0:T(8,128)(2,1)S(1)}, u32[]{:S(2)}, u32[]{:S(2)}) collective-permute-start(bf16[512,128]{1,0:T(8,128)(2,1)S(1)} %collective-permute-done.15.refs_0_), channel_id=1, source_target_pairs={{0,2},{1,3},{2,0},{3,1},{4,6},{5,7},{6,4},{7,5},{8,10},{9,11},{10,... | collective-permute-start | bytes 393224 | tf_op jit(solution)/shard_map/ppermute | solution.py:45
  44.6 5.6 %collective-permute-start.23 = (bf16[512,128]{1,0:T(8,128)(2,1)S(1)}, bf16[512,128]{1,0:T(8,128)(2,1)S(1)}, u32[]{:S(2)}, u32[]{:S(2)}) collective-permute-start(bf16[512,128]{1,0:T(8,128)(2,1)S(1)} %collective-permute-done.22.refs_0_), channel_id=1, source_target_pairs={{0,1},{1,0},{2,3},{3,2},{4,5},{5,4},{6,7},{7,6},{8,9},{9,8},{10,11... | collective-permute-start | bytes 393224 | tf_op jit(solution)/shard_map/ppermute | solution.py:45
  45.4 5.0 %collective-permute-start.25 = (bf16[512,128]{1,0:T(8,128)(2,1)S(1)}, bf16[512,128]{1,0:T(8,128)(2,1)S(1)}, u32[]{:S(2)}, u32[]{:S(2)}) collective-permute-start(bf16[512,128]{1,0:T(8,128)(2,1)S(1)} %collective-permute-done.24.refs_2_), channel_id=1, source_target_pairs={{0,1},{1,0},{2,3},{3,2},{4,5},{5,4},{6,7},{7,6},{8,9},{9,8},{10,11... | collective-permute-start | bytes 393224 | tf_op jit(solution)/shard_map/ppermute | solution.py:45
  49.4 5.0 %collective-permute-start.21 = (bf16[512,128]{1,0:T(8,128)(2,1)S(1)}, bf16[512,128]{1,0:T(8,128)(2,1)S(1)}, u32[]{:S(2)}, u32[]{:S(2)}) collective-permute-start(bf16[512,128]{1,0:T(8,128)(2,1)S(1)} %collective-permute-done.16.refs_0_), channel_id=1, source_target_pairs={{0,2},{1,3},{2,0},{3,1},{4,6},{5,7},{6,4},{7,5},{8,10},{9,11},{10,... | collective-permute-start | bytes 393224 | tf_op jit(solution)/shard_map/ppermute | solution.py:45
  49.7 4.7 %collective-permute-start.27 = (bf16[512,128]{1,0:T(8,128)(2,1)S(1)}, bf16[512,128]{1,0:T(8,128)(2,1)S(1)}, u32[]{:S(2)}, u32[]{:S(2)}) collective-permute-start(bf16[512,128]{1,0:T(8,128)(2,1)S(1)} %collective-permute-done.15.refs_0_), channel_id=1, source_target_pairs={{0,1},{1,0},{2,3},{3,2},{4,5},{5,4},{6,7},{7,6},{8,9},{9,8},{10,11... | collective-permute-start | bytes 393224 | tf_op jit(solution)/shard_map/ppermute | solution.py:45
  49.9 6.1 %collective-permute-start.20 = (bf16[512,128]{1,0:T(8,128)(2,1)S(1)}, bf16[512,128]{1,0:T(8,128)(2,1)S(1)}, u32[]{:S(2)}, u32[]{:S(2)}) collective-permute-start(bf16[512,128]{1,0:T(8,128)(2,1)S(1)} %collective-permute-done.16.refs_0_), channel_id=1, source_target_pairs={{0,1},{1,0},{2,3},{3,2},{4,5},{5,4},{6,7},{7,6},{8,9},{9,8},{10,11... | collective-permute-start | bytes 393224 | tf_op jit(solution)/shard_map/ppermute | solution.py:45
  50.2 4.1 %collective-permute-start.29 = (bf16[512,128]{1,0:T(8,128)(2,1)S(1)}, bf16[512,128]{1,0:T(8,128)(2,1)S(1)}, u32[]{:S(2)}, u32[]{:S(2)}) collective-permute-start(bf16[512,128]{1,0:T(8,128)(2,1)S(1)} %collective-permute-done.28.refs_2_), channel_id=1, source_target_pairs={{0,1},{1,0},{2,3},{3,2},{4,5},{5,4},{6,7},{7,6},{8,9},{9,8},{10,11... | collective-permute-start | bytes 393224 | tf_op jit(solution)/shard_map/ppermute | solution.py:45
  54.3 1.7 %collective-permute-start.26 = (bf16[512,128]{1,0:T(8,128)(2,1)S(1)}, bf16[512,128]{1,0:T(8,128)(2,1)S(1)}, u32[]{:S(2)}, u32[]{:S(2)}) collective-permute-start(bf16[512,128]{1,0:T(8,128)(2,1)S(1)} %collective-permute-done.21.refs_2_), channel_id=1, source_target_pairs={{0,1},{1,0},{2,3},{3,2},{4,5},{5,4},{6,7},{7,6},{8,9},{9,8},{10,11... | collective-permute-start | bytes 393224 | tf_op jit(solution)/shard_map/ppermute | solution.py:45

commit v4 on v3

--- a/solution.py
+++ b/solution.py
@@ -45,7 +45,7 @@
     return lax.ppermute(x, "nodes", [(i, i ^ m) for i in range(DEVICES)])
 
 
-def gather_all(block, work):
+def gather_all(block, work, cores=True):
     have = {0: block}
     done = []
 
@@ -54,17 +54,43 @@
             have[m], out = lax.optimization_barrier((have[m], work[i](have)))
             done.append(out)
 
-    have[8], have[4], have[2], have[1] = (swap(block, m) for m in (8, 4, 2, 1))
+    def cross(*ms):
+        if cores:
+            have.update({m + 1: swap(have[m], 1) for m in ms})
+
+    have[8], have[4], have[2] = (swap(block, m) for m in (8, 4, 2))
+    cross(0)
     hop(0, 8)
     have[12], have[10], have[6] = swap(have[8], 4), swap(have[8], 2), swap(have[4], 2)
-    have[3], have[5], have[7], have[9] = (swap(have[m], 1) for m in (2, 4, 6, 8))
+    cross(2, 4, 6, 8)
     hop(1, 12)
     have[14] = swap(have[12], 2)
+    cross(10, 12)
+    hop(2, 14)
+    cross(14)
+    return have, done
+
+
+def gather_plane(block, first, second):
+    have = {0: block}
+    have[8], have[4], have[2], have[6] = (swap(block, m) for m in (8, 4, 2, 6))
+    have[8], one = lax.optimization_barrier((have[8], first(have)))
+    have[12], have[10], have[14] = swap(have[8], 4), swap(have[8], 2), swap(have[8], 6)
+    have[14], two = lax.optimization_barrier((have[14], second(have)))
+    return have, one, two
+
+
+def gather_rows(block, first, second):
+    have = {0: block}
+    have[8], have[4], have[2] = (swap(block, m) for m in (8, 4, 2))
+    (have[8], have[4], have[2]), one = lax.optimization_barrier(((have[8], have[4], have[2]), first(have)))
+    have[12], have[10], have[6] = swap(have[8], 4), swap(have[8], 2), swap(have[4], 2)
+    have[1], have[3], have[5], have[7], have[9] = (swap(have[m], 1) for m in (0, 2, 4, 6, 8))
+    have[14] = swap(have[12], 2)
     have[11], have[13] = swap(have[10], 1), swap(have[12], 1)
-    hop(2, 14)
+    have[14], two = lax.optimization_barrier((have[14], second(have)))
     have[15] = swap(have[14], 1)
-    done.extend(w(have) for w in work[3:])
-    return have, done
+    return have, one, two
 
 
 def pack_kernel(devices, *refs):
@@ -276,98 +302,116 @@
     )(*[have[m] for m in ms], *prior, *turned, halo_tiles, tile_slots)
 
 
+def _owner(pair, o):
+    return pair * QUAD + 2 * o + lax.axis_index("nodes") % 2
+
+
 def _hot(kinds, labels_ref, owner):
     held = labels_ref[owner].astype(F32)
     return [kinds == held[j : j + 1, :].astype(jnp.int32) for j in range(QUAD)]
 
 
-def _forward(quad, blocks, px_ref, labels_ref, in_t_ref, out_t_ref, bias_ref, agg_ref, hid_ref, slope_ref, loss_ref, count_ref):
+def _inputs(pair, px_ref, agg_ref):
+    rows = agg_ref.shape[0] // 2
+    x = [px_ref[pl.ds(pl.multiple_of(_owner(pair, o) * rows, rows), rows), :] for o in range(2)]
+    return jnp.concatenate([jnp.concatenate(x, axis=0), agg_ref[...]], axis=1)
+
+
+def _forward(c, blocks, px_ref, labels_ref, in_t_ref, out_t_ref, bias_ref, agg_ref, hid_ref, slope_ref, loss_ref, count_ref):
     me = lax.axis_index("nodes")
-    rows, width = blocks[0].shape
-    for m, block in enumerate(blocks):
-        at = ((me % QUAD) ^ m) * rows
+    pair = (me // QUAD) ^ c
+    rows = blocks[0].shape[0]
+    for o, block in enumerate(blocks):
+        at = ((me // 2 % 2) ^ o) * rows
         agg_ref[pl.ds(pl.multiple_of(at, rows), rows), :] = block[...]
+    hidden = jnp.maximum(_dot(in_t_ref[...], _inputs(pair, px_ref, agg_ref), NT), 0.0).astype(BF16)
+    hid_ref[...] = hidden
+    logits = _dot(out_t_ref[...], hidden) + jnp.concatenate([bias_ref[...]] * (2 * rows // LANES), axis=1)
+    logits -= jnp.log(jnp.sum(jnp.exp(logits), axis=0, keepdims=True))
+    probs = jnp.exp(logits)
     kinds = _iota(bias_ref.shape, 0)
     loss = count = jnp.zeros(bias_ref.shape, F32)
-    half = QUAD // 2 * rows
-    for h in range(2):
-        at = slice(h * half, (h + 1) * half)
-        x = px_ref[pl.ds(pl.multiple_of(quad * (2 * half) + h * half, half), half), :]
-        hidden = jnp.maximum(_dot(in_t_ref[...], jnp.concatenate([x, agg_ref[at, :]], axis=1), NT), 0.0).astype(BF16)
-        hid_ref[:, at] = hidden
-        logits = _dot(out_t_ref[...], hidden) + jnp.concatenate([bias_ref[...]] * (half // LANES), axis=1)
-        logits -= jnp.log(jnp.sum(jnp.exp(logits), axis=0, keepdims=True))
-        probs = jnp.exp(logits)
-        for o in range(QUAD // 2):
-            owner = quad * QUAD + h * (QUAD // 2) + o
-            for j, hot in enumerate(_hot(kinds, labels_ref, owner)):
-                lane = o * rows + j * LANES
-                one = hot.astype(F32)
-                loss -= jnp.where(hot, logits[:, lane : lane + LANES], 0.0)
-                count += one
-                slope_ref[:, h * half + lane : h * half + lane + LANES] = probs[:, lane : lane + LANES] - one
+    for o in range(2):
+        for j, hot in enumerate(_hot(kinds, labels_ref, _owner(pair, o))):
+            cut = slice(o * rows + j * LANES, o * rows + (j + 1) * LANES)
+            one = hot.astype(F32)
+            loss -= jnp.where(hot, logits[:, cut], 0.0)
+            count += one
+            slope_ref[:, cut] = probs[:, cut] - one
     loss_ref[...], count_ref[...] = loss, count
 
 
-def forward_kernel(c, *refs):
-    me = lax.axis_index("nodes")
-    blocks, shared, outs = refs[:QUAD], refs[QUAD : QUAD + 5], refs[QUAD + 5 :]
-    _forward((me // QUAD) ^ c, blocks, *shared, *outs[0:5])
-    if c == 0:
-        px_ref, in_t_ref = shared[0], shared[2]
-        rows = blocks[0].shape[0]
-        x = px_ref[pl.ds(pl.multiple_of(me * rows, rows), rows), :]
-        pre = _dot(jnp.concatenate([x, blocks[0][...]], axis=1), in_t_ref[...], NT)
-        outs[5][...] = jnp.maximum(pre, 0.0).astype(BF16)
-
-
-def _held(rows, width, units, padded):
-    return [
-        ((QUAD * rows, width), BF16),
-        ((units, QUAD * rows), BF16),
-        ((padded, QUAD * rows), F32),
-        ((padded, LANES), F32),
-        ((padded, LANES), F32),
-    ]
-
-
-def forward(have, c, shared):
+def own_kernel(px_ref, agg_ref, in_t_ref, hidden_ref):
+    rows = agg_ref.shape[0]
+    x = px_ref[pl.ds(pl.multiple_of(lax.axis_index("nodes") * rows, rows), rows), :]
+    pre = _dot(jnp.concatenate([x, agg_ref[...]], axis=1), in_t_ref[...], NT)
+    hidden_ref[...] = jnp.maximum(pre, 0.0).astype(BF16)
+
+
+def own(part_x, agg, in_t):
+    vmem = pl.BlockSpec(memory_space=pltpu.VMEM)
+    return pl.pallas_call(
+        own_kernel,
+        in_specs=[vmem] * 3,
+        out_specs=vmem,
+        out_shape=jax.ShapeDtypeStruct((agg.shape[0], in_t.shape[0]), BF16),
+        cost_estimate=pl.CostEstimate(flops=1 << 26, bytes_accessed=1 << 18, transcendentals=0),
+        compiler_params=_params(8),
+        name="own",
+    )(part_x, agg, in_t)
+
+
+def forward_kernel(c, before, *refs):
+    blocks, shared, refs = refs[0:2], refs[2:7], refs[7:]
+    prior, outs = refs[: 2 * before], refs[2 * before :]
+    _forward(c, blocks, *shared, *outs[0:5])
+    if before:
+        losses, counts = outs[6:8]
+        mine = lax.axis_index("nodes") // QUAD
+        for i in range(before):
+            losses[mine ^ i], counts[mine ^ i] = prior[2 * i][...], prior[2 * i + 1][...]
+        losses[mine ^ c], counts[mine ^ c] = outs[3][...], outs[4][...]
+        loss, count = (jnp.sum(sum(x[q] for q in range(QUAD)), axis=1, keepdims=True) for x in (losses, counts))
+        outs[5][...] = jnp.where(_iota(outs[5].shape, 1) == 0, loss, count)
+
+
+def forward(have, c, shared, prior=()):
     rows, width = have[0].shape
     units, padded = shared[2].shape[0], shared[4].shape[0]
     vmem = pl.BlockSpec(memory_space=pltpu.VMEM)
-    shapes = [jax.ShapeDtypeStruct(*x) for x in _held(rows, width, units, padded)]
-    if c == 0:
-        shapes.append(jax.ShapeDtypeStruct((rows, units), BF16))
-    return pl.pallas_call(
-        lambda *refs: forward_kernel(c, *refs),
-        in_specs=[vmem] * (QUAD + 5),
+    shapes = [
+        jax.ShapeDtypeStruct((2 * rows, width), BF16),
+        jax.ShapeDtypeStruct((units, 2 * rows), BF16),
+        jax.ShapeDtypeStruct((padded, 2 * rows), F32),
+        jax.ShapeDtypeStruct((padded, LANES), F32),
+        jax.ShapeDtypeStruct((padded, LANES), F32),
+    ]
+    scratch = []
+    if prior:
+        shapes.append(jax.ShapeDtypeStruct((padded, LANES), F32))
+        scratch = [pltpu.VMEM((QUAD, padded, LANES), F32)] * 2
+    stats = [x for held in prior for x in held[3:5]]
+    return pl.pallas_call(
+        lambda *refs: forward_kernel(c, len(prior), *refs),
+        in_specs=[vmem] * (7 + len(stats)),
         out_specs=[vmem] * len(shapes),
         out_shape=shapes,
-        cost_estimate=pl.CostEstimate(flops=1 << 30, bytes_accessed=1 << 22, transcendentals=1 << 19),
-        compiler_params=_params(16),
+        scratch_shapes=scratch,
+        cost_estimate=pl.CostEstimate(flops=1 << 29, bytes_accessed=1 << 21, transcendentals=1 << 18),
+        compiler_params=_params(12),
         name="forward",
-    )(*[have[QUAD * c + m] for m in range(QUAD)], *shared)
+    )(have[4 * c], have[4 * c + 2], *shared, *stats)
 
 
 def backward_kernel(classes, *refs):
+    held, refs = [refs[3 * c : 3 * c + 3] for c in range(QUAD)], refs[3 * QUAD :]
+    px_ref, labels_ref, out_ref, mine_ref, other_ref, sums_ref, class_ref, grads = refs
     me = lax.axis_index("nodes")
-    blocks, refs = refs[:QUAD], refs[QUAD:]
-    early, refs = [refs[5 * c : 5 * c + 5] for c in range(QUAD - 1)], refs[5 * (QUAD - 1) :]
-    shared, out_ref = refs[0:5], refs[5]
-    px_ref, labels_ref, _, _, bias_ref = shared
-    self_ref, neigh_ref, grad_out_ref, class_ref = refs[6:10]
-    last, refs = refs[10:15], refs[15:]
-    losses, counts, grads_in, grads_out = refs
-    rows, width = blocks[0].shape
-    padded = bias_ref.shape[0]
-    mine = me // QUAD
-    _forward(mine ^ (QUAD - 1), blocks, *shared, *last)
-    held = [*early, last]
-
-    for c in range(QUAD):
-        losses[mine ^ c], counts[mine ^ c] = held[c][3][...], held[c][4][...]
-    loss = jnp.sum(sum(losses[q] for q in range(QUAD)), axis=1, keepdims=True)
-    count = jnp.sum(sum(counts[q] for q in range(QUAD)), axis=1, keepdims=True)
+    padded = mine_ref.shape[0]
+    units = out_ref.shape[0]
+
+    both = mine_ref[...] + other_ref[...]
+    loss, count = both[:, 0:1], both[:, 1:2]
     real = _iota((padded, 1), 0) < classes
     difficulty = jnp.where(real, (loss + 1.0) / (count + 1.0), 0.0)
     weight = difficulty / (jnp.sum(difficulty, axis=0, keepdims=True) / classes)
@@ -375,58 +419,64 @@
     class_ref[...] = jnp.transpose(jnp.broadcast_to(weight, (padded, LANES)))[0:1, 0:classes]
     scaled = jnp.broadcast_to(weight * share, (padded, LANES))
 
-    kinds = _iota(bias_ref.shape, 0)
-    half = QUAD // 2 * rows
-    for c, (agg_ref, hid_ref, slope_ref, _, _) in enumerate(held):
-        quad = mine ^ c
-        grad_in = grad_out = 0.0
-        for h in range(2):
-            at = slice(h * half, (h + 1) * half)
-            parts = []
-            for o in range(QUAD // 2):
-                for j, hot in enumerate(_hot(kinds, labels_ref, quad * QUAD + h * (QUAD // 2) + o)):
-                    row = jnp.sum(jnp.where(hot, scaled, 0.0), axis=0, keepdims=True)
-                    lane = h * half + o * rows + j * LANES
-                    parts.append((row * slope_ref[:, lane : lane + LANES]).astype(BF16))
-            dlogits = jnp.concatenate(parts, axis=1)
-            hidden = hid_ref[:, at]
-            dpre = jnp.where(hidden > 0, _dot(out_ref[...], dlogits), 0.0).astype(BF16)
-            x = px_ref[pl.ds(pl.multiple_of(quad * (2 * half) + h * half, half), half), :]
-            grad_out += _dot(dlogits, hidden, NT)
-            grad_in += _dot(dpre, jnp.concatenate([x, agg_ref[at, :]], axis=1))
-        grads_in[quad], grads_out[quad] = grad_in, grad_out
-
-    grad_out_ref[...] = sum(grads_out[q] for q in range(QUAD))[0:classes]
-    grad_in = jnp.transpose(sum(grads_in[q] for q in range(QUAD)))
+    kinds = _iota((padded, LANES), 0)
+    for c, (agg_ref, hid_ref, slope_ref) in enumerate(held):
+        pair = (me // QUAD) ^ c
+        parts = []
+        for o in range(2):
+            for hot in _hot(kinds, labels_ref, _owner(pair, o)):
+                row = jnp.sum(jnp.where(hot, scaled, 0.0), axis=0, keepdims=True)
+                cut = slice(LANES * len(parts), LANES * (len(parts) + 1))
+                parts.append((row * slope_ref[:, cut]).astype(BF16))
+        dlogits = jnp.concatenate(parts, axis=1)
+        hidden = hid_ref[...]
+        dpre = jnp.where(hidden > 0, _dot(out_ref[...], dlogits), 0.0).astype(BF16)
+        grads[pair, 0:units] = _dot(dpre, _inputs(pair, px_ref, agg_ref))
+        grads[pair, units : units + padded] = _dot(dlogits, hidden, NT)
+    sums_ref[...] = sum(grads[q] for q in range(QUAD))
+
+
+def backward(held, part_x, labels, out_p, mine, other, classes):
+    units, padded = out_p.shape
+    vmem = pl.BlockSpec(memory_space=pltpu.VMEM)
+    operands = [*[x for h in held for x in h[0:3]], part_x, labels, out_p, mine, other]
+    return pl.pallas_call(
+        lambda *refs: backward_kernel(classes, *refs),
+        in_specs=[vmem] * len(operands),
+        out_specs=[vmem] * 2,
+        out_shape=[
+            jax.ShapeDtypeStruct((units + padded, 2 * part_x.shape[1]), F32),
+            jax.ShapeDtypeStruct((1, classes), F32),
+        ],
+        scratch_shapes=[pltpu.VMEM((QUAD, units + padded, 2 * part_x.shape[1]), F32)],
+        compiler_params=_params(20),
+        name="backward",
+    )(*operands)
+
+
+def total_kernel(mine_ref, other_ref, self_ref, neigh_ref, out_ref):
+    width, units = self_ref.shape
+    classes = out_ref.shape[0]
+    grad_in = jnp.transpose(mine_ref[0:units] + other_ref[0:units])
     self_ref[...] = grad_in[0:width]
     neigh_ref[...] = grad_in[width : 2 * width]
-
-
-def backward(have, early, shared, out_p, classes):
-    rows, width = have[0].shape
-    units, padded = out_p.shape
+    out_ref[...] = (mine_ref[units:] + other_ref[units:])[0:classes]
+
+
+def total(mine, other, width, units, classes):
     vmem = pl.BlockSpec(memory_space=pltpu.VMEM)
-    operands = [*[have[m] for m in range(DEVICES - QUAD, DEVICES)], *[x for held in early for x in held], *shared, out_p]
-    return pl.pallas_call(
-        lambda *refs: backward_kernel(classes, *refs),
-        in_specs=[vmem] * len(operands),
-        out_specs=[vmem] * 4,
+    return pl.pallas_call(
+        total_kernel,
+        in_specs=[vmem] * 2,
+        out_specs=[vmem] * 3,
         out_shape=[
             jax.ShapeDtypeStruct((width, units), F32),
             jax.ShapeDtypeStruct((width, units), F32),
             jax.ShapeDtypeStruct((classes, units), F32),
-            jax.ShapeDtypeStruct((1, classes), F32),
         ],
-        scratch_shapes=[
-            *[pltpu.VMEM(*x) for x in _held(rows, width, units, padded)],
-            pltpu.VMEM((QUAD, padded, LANES), F32),
-            pltpu.VMEM((QUAD, padded, LANES), F32),
-            pltpu.VMEM((QUAD, units, 2 * width), F32),
-            pltpu.VMEM((QUAD, padded, units), F32),
-        ],
-        compiler_params=_params(24),
-        name="backward",
-    )(*operands)
+        compiler_params=_params(8),
+        name="total",
+    )(mine, other)
 
 
 def gathered_body(
@@ -435,29 +485,29 @@
     packed = pack(features, cluster, slot, labels, DEVICES)
     early, late = tuple(range(0, 8)), tuple(range(8, 16))
     half = features.shape[0] // TILE // 2
-    work = [
+    have, near, (prior, far) = gather_rows(
+        packed,
         lambda have: turn(adjacency, 0, half),
-        None,
         lambda have: (place(have, early), turn(adjacency, half, half)),
-    ]
-    have, (near, (prior, far)) = gather_all(packed, work)
+    )
     part_x, all_labels, agg = aggregate(have, late, prior, (near, far), halo_tiles, tile_slots)
-    ready = []
-
-    def quad(have, c):
-        in_t, out_t, _, bias = ready[0]
-        return forward(have, c, (part_x, all_labels, in_t, out_t, bias))
-
-    def prepare(have):
-        ready.append(weights(w_self, w_neigh, w_out, b_out))
-        return ready[0]
-
-    have, (_, *done) = gather_all(agg, [prepare, *[lambda have, c=c: quad(have, c) for c in range(QUAD - 1)]])
-    in_t, out_t, out_p, bias = ready[0]
+    weighed = []
+
+    def first(have):
+        weighed.extend(weights(w_self, w_neigh, w_out, b_out))
+        return weighed, own(part_x, agg, weighed[0])
+
+    def ahead(have):
+        in_t, out_t, _, bias = weighed
+        return [forward(have, c, (part_x, all_labels, in_t, out_t, bias)) for c in range(QUAD - 1)]
+
+    have, (_, hidden), held = gather_plane(agg, first, ahead)
+    in_t, out_t, out_p, bias = weighed
     shared = (part_x, all_labels, in_t, out_t, bias)
-    hidden = done[0][5]
-    early = [out[0:5] for out in done]
-    grad_self, grad_neigh, grad_out, class_weight = backward(have, early, shared, out_p, w_out.shape[1])
+    *last, mine = forward(have, QUAD - 1, shared, held)
+    classes = w_out.shape[1]
+    sums, class_weight = backward([*held, last], part_x, all_labels, out_p, mine, swap(mine, 1), classes)
+    grad_self, grad_neigh, grad_out = total(sums, swap(sums, 1), *w_self.shape, classes)
     return hidden, grad_self, grad_neigh, grad_out.T, class_weight.reshape(-1)
 
 

time: 62.9 us -> 60.5 us (0.962)
  Pallas kernels: 26.6 us -> 23.6 us
    pallas_call x1, Pallas kernels: 6.69 us -> 2.81 us  [backward(): pl.pallas_call(lambda *refs: backward_kernel(classes, *refs), in_specs=[v...]
    pallas_call x3 -> x6, Pallas kernels: 5.61 us -> 6.41 us  [the longest x4 4.55 us: forward(): pl.pallas_call(lambda *refs: forward_kernel(c, len(prior), *refs), in_spe...]
    ppermute x30 -> x24, waiting for transfers between devices: 12.5 us -> 13.1 us  [swap(): return lax.ppermute(x, 'nodes', [(i, i ^ m) for i in range(DEVICES)])]
    ppermute x30 -> x24, starting transfers between devices: 22.7 us -> 22.8 us  [swap(): return lax.ppermute(x, 'nodes', [(i, i ^ m) for i in range(DEVICES)])]
  transfers between devices with their start and end apart: 30 -> 24, of which waited for: 8 -> 10; matrix products, arithmetic and copies ran while one was open for 0% -> 0% of each run, Pallas kernels for 23% -> 21%
where the time goes in v4:
time: 60.5 us; the launch traced here: 60.3 us
  Pallas kernels  23.6 us (39%)
  starting transfers between devices  22.8 us (38%)
  waiting for transfers between devices  13.1 us (22%)
  between operations  0.8 us (1%)
    ppermute x24, starting transfers between devices, swap(): return lax.ppermute(x, 'nodes', [(i, i ^ m) for i in range(DEVICES)])  22.8 us
    ppermute x24, waiting for transfers between devices, swap(): return lax.ppermute(x, 'nodes', [(i, i ^ m) for i in range(DEVICES)])  13.1 us
    pallas_call x2, Pallas kernels, turn(): pl.pallas_call(lambda *refs: turn_kernel(first, *refs), in_specs=[pl.Bloc...  6.04 us
    pallas_call x4, Pallas kernels, forward(): pl.pallas_call(lambda *refs: forward_kernel(c, len(prior), *refs), in_spe...  4.55 us
    pallas_call x1, Pallas kernels, aggregate(): pl.pallas_call(lambda *refs: aggregate_kernel(ms, len(turned), *refs), in...  4.33 us
    pallas_call x1, Pallas kernels, backward(): pl.pallas_call(lambda *refs: backward_kernel(classes, *refs), in_specs=[v...  2.81 us
    pallas_call x1, Pallas kernels, pack(): pl.pallas_call(lambda *refs: pack_kernel(devices, *refs), in_specs=[pl.Bl...  1.45 us
    pallas_call x1, Pallas kernels, place(): pl.pallas_call(lambda *refs: _place(ms, refs[:len(ms)], None, *refs[len(m...  1.34 us
  transfers between devices with their start and end apart: 24, of which 10 were waited for; matrix products, arithmetic and copies ran while one was open for 0% of the time, Pallas kernels for 21%

profile of v4, /device:TPU:0, one launch (start us, length us, event | category | flops | bytes accessed | tf_op | source)
XLA Modules:
  0.0 60.3 jit_solution(13889304585851403550)
XLA Ops:
  0.6 1.5 %pack_rows.1.refs_0_ = bf16[17,32,128]{2,1,0:T(8,128)(2,1)S(1)} custom-call(bf16[512,128]{1,0:T(8,128)(2,1)} %refs_0_.4, s32[1,512]{1,0:T(1,128)} %bitcast.8, s32[1,512]{1,0:T(1,128)} %bitcast.9, s32[4,128]{1,0:T(4,128)} %bitcast.10), custom_call_target="tpu_custom_call" | custom-call | tf_op jit(solution)/shard_map/pack_rows/pallas_call | solution.py:121
  2.1 4.1 %collective-permute-start = (bf16[17,32,128]{2,1,0:T(8,128)(2,1)S(1)}, bf16[17,32,128]{2,1,0:T(8,128)(2,1)S(1)}, u32[]{:S(2)}, u32[]{:S(2)}) collective-permute-start(bf16[17,32,128]{2,1,0:T(8,128)(2,1)S(1)} %pack_rows.1.refs_0_), channel_id=1, source_target_pairs={{0,8},{1,9},{2,10},{3,11},{4,12},{5,13},{6,14},{7,15},{8,0},{9,1},... | collective-permute-start | bytes 417800 | tf_op jit(solution)/shard_map/ppermute | solution.py:45
  6.2 1.6 %collective-permute-start.1 = (bf16[17,32,128]{2,1,0:T(8,128)(2,1)S(1)}, bf16[17,32,128]{2,1,0:T(8,128)(2,1)S(1)}, u32[]{:S(2)}, u32[]{:S(2)}) collective-permute-start(bf16[17,32,128]{2,1,0:T(8,128)(2,1)S(1)} %pack_rows.1.refs_0_), channel_id=1, source_target_pairs={{0,4},{1,5},{2,6},{3,7},{4,0},{5,1},{6,2},{7,3},{8,12},{9,13},{10,... | collective-permute-start | bytes 417800 | tf_op jit(solution)/shard_map/ppermute | solution.py:45
  7.8 1.5 %collective-permute-start.2 = (bf16[17,32,128]{2,1,0:T(8,128)(2,1)S(1)}, bf16[17,32,128]{2,1,0:T(8,128)(2,1)S(1)}, u32[]{:S(2)}, u32[]{:S(2)}) collective-permute-start(bf16[17,32,128]{2,1,0:T(8,128)(2,1)S(1)} %pack_rows.1.refs_0_), channel_id=1, source_target_pairs={{0,2},{1,3},{2,0},{3,1},{4,6},{5,7},{6,4},{7,5},{8,10},{9,11},{10,... | collective-permute-start | bytes 417800 | tf_op jit(solution)/shard_map/ppermute | solution.py:45
  9.3 0.0 collective-permute-start.9
  9.3 3.0 %turn_adjacency.2.refs_10_ = bf16[2,64,128,128]{3,2,1,0:T(8,128)(2,1)S(1)} custom-call(bf16[512,64,128]{2,1,0:T(8,128)(2,1)} %refs_0_.6), custom_call_target="tpu_custom_call" | custom-call | flops 1073741824 | bytes 4194304 | tf_op jit(solution)/shard_map/turn_adjacency/pallas_call | solution.py:213
  12.3 0.0 copy-start
  12.3 0.0 copy-start.1
  12.3 0.6 %collective-permute-done.refs_0_ = bf16[17,32,128]{2,1,0:T(8,128)(2,1)S(1)} collective-permute-done((bf16[17,32,128]{2,1,0:T(8,128)(2,1)S(1)}, bf16[17,32,128]{2,1,0:T(8,128)(2,1)S(1)}, u32[]{:S(2)}, u32[]{:S(2)}) %collective-permute-start) | collective-permute-done | bytes 139296 | tf_op jit(solution)/shard_map/ppermute | solution.py:45
  13.0 0.2 collective-permute-done.1.refs_4_
  13.1 0.0 collective-permute-done.2.refs_2_
  13.2 1.6 %collective-permute-start.12 = (bf16[17,32,128]{2,1,0:T(8,128)(2,1)S(1)}, bf16[17,32,128]{2,1,0:T(8,128)(2,1)S(1)}, u32[]{:S(2)}, u32[]{:S(2)}) collective-permute-start(bf16[17,32,128]{2,1,0:T(8,128)(2,1)S(1)} %collective-permute-done.1.refs_4_), channel_id=1, source_target_pairs={{0,2},{1,3},{2,0},{3,1},{4,6},{5,7},{6,4},{7,5},{8,10},{9,11},{10,... | collective-permute-start | bytes 417800 | tf_op jit(solution)/shard_map/ppermute | solution.py:45
  14.7 1.4 %collective-permute-start.6 = (bf16[17,32,128]{2,1,0:T(8,128)(2,1)S(1)}, bf16[17,32,128]{2,1,0:T(8,128)(2,1)S(1)}, u32[]{:S(2)}, u32[]{:S(2)}) collective-permute-start(bf16[17,32,128]{2,1,0:T(8,128)(2,1)S(1)} %collective-permute-done.refs_0_), channel_id=1, source_target_pairs={{0,4},{1,5},{2,6},{3,7},{4,0},{5,1},{6,2},{7,3},{8,12},{9,13},{10,... | collective-permute-start | bytes 417800 | tf_op jit(solution)/shard_map/ppermute | solution.py:45
  16.1 0.0 collective-permute-start.11
  16.1 0.5 collective-permute-start.10
  16.7 0.5 collective-permute-start.4
  17.2 1.4 %collective-permute-done.12.refs_6_ = bf16[17,32,128]{2,1,0:T(8,128)(2,1)S(1)} collective-permute-done((bf16[17,32,128]{2,1,0:T(8,128)(2,1)S(1)}, bf16[17,32,128]{2,1,0:T(8,128)(2,1)S(1)}, u32[]{:S(2)}, u32[]{:S(2)}) %collective-permute-start.12) | collective-permute-done | bytes 139296 | tf_op jit(solution)/shard_map/ppermute | solution.py:45
  18.5 1.2 %collective-permute-done.6.refs_4_ = bf16[17,32,128]{2,1,0:T(8,128)(2,1)S(1)} collective-permute-done((bf16[17,32,128]{2,1,0:T(8,128)(2,1)S(1)}, bf16[17,32,128]{2,1,0:T(8,128)(2,1)S(1)}, u32[]{:S(2)}, u32[]{:S(2)}) %collective-permute-start.6) | collective-permute-done | bytes 139296 | tf_op jit(solution)/shard_map/ppermute | solution.py:45
  19.8 0.5 collective-permute-start.8
  20.3 3.0 %turn_adjacency.3.refs_11_ = bf16[2,64,128,128]{3,2,1,0:T(8,128)(2,1)S(1)} custom-call(bf16[512,64,128]{2,1,0:T(8,128)(2,1)} %refs_0_.6), custom_call_target="tpu_custom_call" | custom-call | flops 1073741824 | bytes 4194304 | tf_op jit(solution)/shard_map/turn_adjacency/pallas_call | solution.py:213
  23.3 0.1 collective-permute-start.3
  23.4 0.5 collective-permute-start.7
  23.9 0.1 collective-permute-start.5
  24.0 1.3 %place.1 = (bf16[8192,128]{1,0:T(8,128)(2,1)S(1)}, bf16[16,16,128]{2,1,0:T(8,128)(2,1)S(1)}) custom-call(bf16[17,32,128]{2,1,0:T(8,128)(2,1)S(1)} %pack_rows.1.refs_0_, bf16[17,32,128]{2,1,0:T(8,128)(2,1)S(1)} %collective-permute-done.9.refs_1_, bf16[17,32,128]{2,1,0:T(8,128)(2,1)S(1)} %collective-permute-done.2.refs_2_, ...), custom_call_target="tpu_custom_call" | custom-call | flops 1073741824 | bytes 4194304 | tf_op jit(solution)/shard_map/place/pallas_call | solution.py:260
  25.3 0.5 collective-permute-start.14
  25.8 1.0 %collective-permute-done.14.refs_7_ = bf16[17,32,128]{2,1,0:T(8,128)(2,1)S(1)} collective-permute-done((bf16[17,32,128]{2,1,0:T(8,128)(2,1)S(1)}, bf16[17,32,128]{2,1,0:T(8,128)(2,1)S(1)}, u32[]{:S(2)}, u32[]{:S(2)}) %collective-permute-start.14) | collective-permute-done | bytes 139296 | tf_op jit(solution)/shard_map/ppermute | solution.py:45
  26.8 4.3 %aggregate.1 = (bf16[8192,128]{1,0:T(8,128)(2,1)S(1)}, bf16[16,16,128]{2,1,0:T(8,128)(2,1)S(1)}, bf16[512,128]{1,0:T(8,128)(2,1)S(1)}) custom-call(bf16[17,32,128]{2,1,0:T(8,128)(2,1)S(1)} %collective-permute-done.refs_0_, bf16[17,32,128]{2,1,0:T(8,128)(2,1)S(1)} %collective-permute-done.3.refs_1_, bf16[17,32,128]{2,1,0:T(8,128)(2,1)S(1)} %collective-permute-done.4.refs_2_, ...), custom_call_target="tpu_custom_call" | custom-call | tf_op jit(solution)/shard_map/aggregate/pallas_call | solution.py:294
  31.2 2.4 %collective-permute-start.15 = (bf16[512,128]{1,0:T(8,128)(2,1)S(1)}, bf16[512,128]{1,0:T(8,128)(2,1)S(1)}, u32[]{:S(2)}, u32[]{:S(2)}) collective-permute-start(bf16[512,128]{1,0:T(8,128)(2,1)S(1)} %get-tuple-element.74.agg_ref.refs_0_), channel_id=1, source_target_pairs={{0,8},{1,9},{2,10},{3,11},{4,12},{5,13},{6,14},{7,15},{8,0},{9,1},... | collective-permute-start | bytes 393224 | tf_op jit(solution)/shard_map/ppermute | solution.py:45
  33.5 1.5 %collective-permute-start.17 = (bf16[512,128]{1,0:T(8,128)(2,1)S(1)}, bf16[512,128]{1,0:T(8,128)(2,1)S(1)}, u32[]{:S(2)}, u32[]{:S(2)}) collective-permute-start(bf16[512,128]{1,0:T(8,128)(2,1)S(1)} %get-tuple-element.74.agg_ref.refs_0_), channel_id=1, source_target_pairs={{0,2},{1,3},{2,0},{3,1},{4,6},{5,7},{6,4},{7,5},{8,10},{9,11},{10,... | collective-permute-start | bytes 393224 | tf_op jit(solution)/shard_map/ppermute | solution.py:45
  35.1 1.8 %collective-permute-start.18 = (bf16[512,128]{1,0:T(8,128)(2,1)S(1)}, bf16[512,128]{1,0:T(8,128)(2,1)S(1)}, u32[]{:S(2)}, u32[]{:S(2)}) collective-permute-start(bf16[512,128]{1,0:T(8,128)(2,1)S(1)} %get-tuple-element.74.agg_ref.refs_0_), channel_id=1, source_target_pairs={{0,4},{1,5},{2,6},{3,7},{4,0},{5,1},{6,2},{7,3},{8,12},{9,13},{10,... | collective-permute-start | bytes 393224 | tf_op jit(solution)/shard_map/ppermute | solution.py:45
  36.9 0.7 %collective-permute-start.19 = (bf16[512,128]{1,0:T(8,128)(2,1)S(1)}, bf16[512,128]{1,0:T(8,128)(2,1)S(1)}, u32[]{:S(2)}, u32[]{:S(2)}) collective-permute-start(bf16[512,128]{1,0:T(8,128)(2,1)S(1)} %get-tuple-element.74.agg_ref.refs_0_), channel_id=1, source_target_pairs={{0,6},{1,7},{2,4},{3,5},{4,2},{5,3},{6,0},{7,1},{8,14},{9,15},{10,... | collective-permute-start | bytes 393224 | tf_op jit(solution)/shard_map/ppermute | solution.py:45
  37.5 1.2 %weights.1 = (bf16[256,256]{1,0:T(8,128)(2,1)S(1)}, bf16[176,256]{1,0:T(8,128)(2,1)S(1)}, bf16[256,176]{1,0:T(8,128)(2,1)S(1)}, f32[176,128]{1,0:T(8,128)S(1)}) custom-call(bf16[128,256]{1,0:T(8,128)(2,1)} %refs_0_.7, bf16[128,256]{1,0:T(8,128)(2,1)} %refs_1_.1, bf16[172,256]{1,0:T(8,128)(2,1)} %bitcast.7, f32[1,172]{1,0:T(1,128)} %bitcast.11), custom_call_target="tpu_custom_call" | custom-call | bytes 2097152 | tf_op jit(solution)/shard_map/weights/pallas_call | solution.py:153
  38.7 1.0 %own.1 = bf16[512,256]{1,0:T(8,128)(2,1)} custom-call(bf16[8192,128]{1,0:T(8,128)(2,1)S(1)} %get-tuple-element.79.px_ref.refs_2_.refs_12_, bf16[512,128]{1,0:T(8,128)(2,1)S(1)} %get-tuple-element.74.agg_ref.refs_0_, bf16[256,256]{1,0:T(8,128)(2,1)S(1)} %get-tuple-element.75.in_t_ref.refs_4_), custom_call_target="tpu_custom_call" | custom-call | flops 67108864 | bytes 262144 | tf_op jit(solution)/shard_map/own/pallas_call | solution.py:353
  39.7 1.1 %collective-permute-done.15.refs_0_ = bf16[512,128]{1,0:T(8,128)(2,1)S(1)} collective-permute-done((bf16[512,128]{1,0:T(8,128)(2,1)S(1)}, bf16[512,128]{1,0:T(8,128)(2,1)S(1)}, u32[]{:S(2)}, u32[]{:S(2)}) %collective-permute-start.15) | collective-permute-done | bytes 131104 | tf_op jit(solution)/shard_map/ppermute | solution.py:45
  40.8 1.5 %collective-permute-start.20 = (bf16[512,128]{1,0:T(8,128)(2,1)S(1)}, bf16[512,128]{1,0:T(8,128)(2,1)S(1)}, u32[]{:S(2)}, u32[]{:S(2)}) collective-permute-start(bf16[512,128]{1,0:T(8,128)(2,1)S(1)} %collective-permute-done.15.refs_0_), channel_id=1, source_target_pairs={{0,2},{1,3},{2,0},{3,1},{4,6},{5,7},{6,4},{7,5},{8,10},{9,11},{10,... | collective-permute-start | bytes 393224 | tf_op jit(solution)/shard_map/ppermute | solution.py:45
  42.4 0.8 %collective-permute-start.16 = (bf16[512,128]{1,0:T(8,128)(2,1)S(1)}, bf16[512,128]{1,0:T(8,128)(2,1)S(1)}, u32[]{:S(2)}, u32[]{:S(2)}) collective-permute-start(bf16[512,128]{1,0:T(8,128)(2,1)S(1)} %collective-permute-done.15.refs_0_), channel_id=1, source_target_pairs={{0,6},{1,7},{2,4},{3,5},{4,2},{5,3},{6,0},{7,1},{8,14},{9,15},{10,... | collective-permute-start | bytes 393224 | tf_op jit(solution)/shard_map/ppermute | solution.py:45
  43.2 1.1 %collective-permute-start.21 = (bf16[512,128]{1,0:T(8,128)(2,1)S(1)}, bf16[512,128]{1,0:T(8,128)(2,1)S(1)}, u32[]{:S(2)}, u32[]{:S(2)}) collective-permute-start(bf16[512,128]{1,0:T(8,128)(2,1)S(1)} %collective-permute-done.15.refs_0_), channel_id=1, source_target_pairs={{0,4},{1,5},{2,6},{3,7},{4,0},{5,1},{6,2},{7,3},{8,12},{9,13},{10,... | collective-permute-start | bytes 393224 | tf_op jit(solution)/shard_map/ppermute | solution.py:45
  44.3 0.9 %forward.4 = (bf16[1024,128]{1,0:T(8,128)(2,1)S(1)}, bf16[256,1024]{1,0:T(8,128)(2,1)S(1)}, f32[176,1024]{1,0:T(8,128)S(1)}, f32[176,128]{1,0:T(8,128)S(1)}, f32[176,128]{1,0:T(8,128)S(1)}) custom-call(bf16[512,128]{1,0:T(8,128)(2,1)S(1)} %get-tuple-element.74.agg_ref.refs_0_, bf16[512,128]{1,0:T(8,128)(2,1)S(1)} %collective-permute-done.17.refs_1_, ...), custom_call_target="tpu_custom_call" | custom-call | flops 536870912 | bytes 2097152 | tf_op jit(solution)/shard_map/forward/pallas_call | solution.py:394
  45.2 1.0 %collective-permute-done.19.refs_1_ = bf16[512,128]{1,0:T(8,128)(2,1)S(1)} collective-permute-done((bf16[512,128]{1,0:T(8,128)(2,1)S(1)}, bf16[512,128]{1,0:T(8,128)(2,1)S(1)}, u32[]{:S(2)}, u32[]{:S(2)}) %collective-permute-start.19) | collective-permute-done | bytes 131104 | tf_op jit(solution)/shard_map/ppermute | solution.py:45
  46.2 0.9 %forward.5 = (bf16[1024,128]{1,0:T(8,128)(2,1)S(1)}, bf16[256,1024]{1,0:T(8,128)(2,1)S(1)}, f32[176,1024]{1,0:T(8,128)S(1)}, f32[176,128]{1,0:T(8,128)S(1)}, f32[176,128]{1,0:T(8,128)S(1)}) custom-call(bf16[512,128]{1,0:T(8,128)(2,1)S(1)} %collective-permute-done.18.refs_0_, bf16[512,128]{1,0:T(8,128)(2,1)S(1)} %collective-permute-done.19.refs_1_, ...), custom_call_target="tpu_custom_call" | custom-call | flops 536870912 | bytes 2097152 | tf_op jit(solution)/shard_map/forward/pallas_call | solution.py:394
  47.1 3.6 %collective-permute-done.20.refs_1_ = bf16[512,128]{1,0:T(8,128)(2,1)S(1)} collective-permute-done((bf16[512,128]{1,0:T(8,128)(2,1)S(1)}, bf16[512,128]{1,0:T(8,128)(2,1)S(1)}, u32[]{:S(2)}, u32[]{:S(2)}) %collective-permute-start.20) | collective-permute-done | bytes 131104 | tf_op jit(solution)/shard_map/ppermute | solution.py:45
  50.8 1.1 %forward.6 = (bf16[1024,128]{1,0:T(8,128)(2,1)S(1)}, bf16[256,1024]{1,0:T(8,128)(2,1)S(1)}, f32[176,1024]{1,0:T(8,128)S(1)}, f32[176,128]{1,0:T(8,128)S(1)}, f32[176,128]{1,0:T(8,128)S(1)}) custom-call(bf16[512,128]{1,0:T(8,128)(2,1)S(1)} %collective-permute-done.15.refs_0_, bf16[512,128]{1,0:T(8,128)(2,1)S(1)} %collective-permute-done.20.refs_1_, ...), custom_call_target="tpu_custom_call" | custom-call | flops 536870912 | bytes 2097152 | tf_op jit(solution)/shard_map/forward/pallas_call | solution.py:394
  51.9 1.6 %forward.7 = (bf16[1024,128]{1,0:T(8,128)(2,1)S(1)}, bf16[256,1024]{1,0:T(8,128)(2,1)S(1)}, f32[176,1024]{1,0:T(8,128)S(1)}, f32[176,128]{1,0:T(8,128)}, f32[176,128]{1,0:T(8,128)}, /*index=5*/f32[176,128]{1,0:T(8,128)S(1)}) custom-call(bf16[512,128]{1,0:T(8,128)(2,1)S(1)} %collective-permute-done.21.refs_0_, ...), custom_call_target="tpu_custom_call" | custom-call | flops 536870912 | bytes 2097152 | tf_op jit(solution)/shard_map/forward/pallas_call | solution.py:394
  53.5 1.3 %collective-permute-done.22.refs_16_ = f32[176,128]{1,0:T(8,128)S(1)} collective-permute-done((f32[176,128]{1,0:T(8,128)S(1)}, f32[176,128]{1,0:T(8,128)S(1)}, u32[]{:S(2)}, u32[]{:S(2)}) %collective-permute-start.22) | collective-permute-done | bytes 90144 | tf_op jit(solution)/shard_map/ppermute | solution.py:45
  54.8 2.8 %backward.1 = (f32[432,256]{1,0:T(8,128)S(1)}, f32[1,172]{1,0:T(1,128)}) custom-call(bf16[1024,128]{1,0:T(8,128)(2,1)S(1)} %get-tuple-element.98.refs_0_, bf16[256,1024]{1,0:T(8,128)(2,1)S(1)} %get-tuple-element.99.refs_1_, f32[176,1024]{1,0:T(8,128)S(1)} %get-tuple-element.100.refs_2_, bf16[1024,128]{1,0:T(8,128)(2,1)S(1)} %get-tuple-element.101.refs_3_, ...), custom_call_target="tpu_custom_call" | custom-call | tf_op jit(solution)/shard_map/backward/pallas_call | solution.py:443
  57.6 0.2 collective-permute-start.23
  57.8 1.6 %collective-permute-done.23.other_ref = f32[432,256]{1,0:T(8,128)S(1)} collective-permute-done((f32[432,256]{1,0:T(8,128)S(1)}, f32[432,256]{1,0:T(8,128)S(1)}, u32[]{:S(2)}, u32[]{:S(2)}) %collective-permute-start.23) | collective-permute-done | bytes 442400 | tf_op jit(solution)/shard_map/ppermute | solution.py:45
  59.4 0.9 %total.1 = (f32[128,256]{1,0:T(8,128)}, f32[128,256]{1,0:T(8,128)}, f32[172,256]{1,0:T(8,128)}) custom-call(f32[432,256]{1,0:T(8,128)S(1)} %get-tuple-element.118.mine_ref, f32[432,256]{1,0:T(8,128)S(1)} %collective-permute-done.23.other_ref), custom_call_target="tpu_custom_call" | custom-call | tf_op jit(solution)/shard_map/total/pallas_call | solution.py:468
  (17 shorter events, 0.0 us)
Async XLA Ops:
  2.1 10.9 %collective-permute-start = (bf16[17,32,128]{2,1,0:T(8,128)(2,1)S(1)}, bf16[17,32,128]{2,1,0:T(8,128)(2,1)S(1)}, u32[]{:S(2)}, u32[]{:S(2)}) collective-permute-start(bf16[17,32,128]{2,1,0:T(8,128)(2,1)S(1)} %pack_rows.1.refs_0_), channel_id=1, source_target_pairs={{0,8},{1,9},{2,10},{3,11},{4,12},{5,13},{6,14},{7,15},{8,0},{9,1},... | collective-permute-start | bytes 417800 | tf_op jit(solution)/shard_map/ppermute | solution.py:45
  6.2 7.0 %collective-permute-start.1 = (bf16[17,32,128]{2,1,0:T(8,128)(2,1)S(1)}, bf16[17,32,128]{2,1,0:T(8,128)(2,1)S(1)}, u32[]{:S(2)}, u32[]{:S(2)}) collective-permute-start(bf16[17,32,128]{2,1,0:T(8,128)(2,1)S(1)} %pack_rows.1.refs_0_), channel_id=1, source_target_pairs={{0,4},{1,5},{2,6},{3,7},{4,0},{5,1},{6,2},{7,3},{8,12},{9,13},{10,... | collective-permute-start | bytes 417800 | tf_op jit(solution)/shard_map/ppermute | solution.py:45
  7.8 5.4 %collective-permute-start.2 = (bf16[17,32,128]{2,1,0:T(8,128)(2,1)S(1)}, bf16[17,32,128]{2,1,0:T(8,128)(2,1)S(1)}, u32[]{:S(2)}, u32[]{:S(2)}) collective-permute-start(bf16[17,32,128]{2,1,0:T(8,128)(2,1)S(1)} %pack_rows.1.refs_0_), channel_id=1, source_target_pairs={{0,2},{1,3},{2,0},{3,1},{4,6},{5,7},{6,4},{7,5},{8,10},{9,11},{10,... | collective-permute-start | bytes 417800 | tf_op jit(solution)/shard_map/ppermute | solution.py:45
  9.3 7.4 %collective-permute-start.9 = (bf16[17,32,128]{2,1,0:T(8,128)(2,1)S(1)}, bf16[17,32,128]{2,1,0:T(8,128)(2,1)S(1)}, u32[]{:S(2)}, u32[]{:S(2)}) collective-permute-start(bf16[17,32,128]{2,1,0:T(8,128)(2,1)S(1)} %pack_rows.1.refs_0_), channel_id=1, source_target_pairs={{0,1},{1,0},{2,3},{3,2},{4,5},{5,4},{6,7},{7,6},{8,9},{9,8},{10,11... | collective-permute-start | bytes 417800 | tf_op jit(solution)/shard_map/ppermute | solution.py:45
  12.3 14.5 %copy-start = (s32[4,64]{1,0:T(4,128)S(1)}, s32[4,64]{1,0:T(4,128)}, u32[]{:S(2)}) copy-start(s32[4,64]{1,0:T(4,128)} %refs_13_.1) | copy-start | bytes 3076
  12.3 14.5 %copy-start.1 = (s32[1,64]{1,0:T(1,128)S(1)}, s32[1,64]{1,0:T(1,128)}, u32[]{:S(2)}) copy-start(s32[1,64]{1,0:T(1,128)} %refs_12_.1) | copy-start | bytes 772
  13.2 5.4 %collective-permute-start.12 = (bf16[17,32,128]{2,1,0:T(8,128)(2,1)S(1)}, bf16[17,32,128]{2,1,0:T(8,128)(2,1)S(1)}, u32[]{:S(2)}, u32[]{:S(2)}) collective-permute-start(bf16[17,32,128]{2,1,0:T(8,128)(2,1)S(1)} %collective-permute-done.1.refs_4_), channel_id=1, source_target_pairs={{0,2},{1,3},{2,0},{3,1},{4,6},{5,7},{6,4},{7,5},{8,10},{9,11},{10,... | collective-permute-start | bytes 417800 | tf_op jit(solution)/shard_map/ppermute | solution.py:45
  14.7 5.1 %collective-permute-start.6 = (bf16[17,32,128]{2,1,0:T(8,128)(2,1)S(1)}, bf16[17,32,128]{2,1,0:T(8,128)(2,1)S(1)}, u32[]{:S(2)}, u32[]{:S(2)}) collective-permute-start(bf16[17,32,128]{2,1,0:T(8,128)(2,1)S(1)} %collective-permute-done.refs_0_), channel_id=1, source_target_pairs={{0,4},{1,5},{2,6},{3,7},{4,0},{5,1},{6,2},{7,3},{8,12},{9,13},{10,... | collective-permute-start | bytes 417800 | tf_op jit(solution)/shard_map/ppermute | solution.py:45
  16.1 7.2 %collective-permute-start.11 = (bf16[17,32,128]{2,1,0:T(8,128)(2,1)S(1)}, bf16[17,32,128]{2,1,0:T(8,128)(2,1)S(1)}, u32[]{:S(2)}, u32[]{:S(2)}) collective-permute-start(bf16[17,32,128]{2,1,0:T(8,128)(2,1)S(1)} %collective-permute-done.1.refs_4_), channel_id=1, source_target_pairs={{0,1},{1,0},{2,3},{3,2},{4,5},{5,4},{6,7},{7,6},{8,9},{9,8},{10,11... | collective-permute-start | bytes 417800 | tf_op jit(solution)/shard_map/ppermute | solution.py:45
  16.1 7.3 %collective-permute-start.10 = (bf16[17,32,128]{2,1,0:T(8,128)(2,1)S(1)}, bf16[17,32,128]{2,1,0:T(8,128)(2,1)S(1)}, u32[]{:S(2)}, u32[]{:S(2)}) collective-permute-start(bf16[17,32,128]{2,1,0:T(8,128)(2,1)S(1)} %collective-permute-done.2.refs_2_), channel_id=1, source_target_pairs={{0,1},{1,0},{2,3},{3,2},{4,5},{5,4},{6,7},{7,6},{8,9},{9,8},{10,11... | collective-permute-start | bytes 417800 | tf_op jit(solution)/shard_map/ppermute | solution.py:45
  16.7 7.2 %collective-permute-start.4 = (bf16[17,32,128]{2,1,0:T(8,128)(2,1)S(1)}, bf16[17,32,128]{2,1,0:T(8,128)(2,1)S(1)}, u32[]{:S(2)}, u32[]{:S(2)}) collective-permute-start(bf16[17,32,128]{2,1,0:T(8,128)(2,1)S(1)} %collective-permute-done.refs_0_), channel_id=1, source_target_pairs={{0,2},{1,3},{2,0},{3,1},{4,6},{5,7},{6,4},{7,5},{8,10},{9,11},{10,... | collective-permute-start | bytes 417800 | tf_op jit(solution)/shard_map/ppermute | solution.py:45
  18.5 5.5 %collective-permute-start.13 = (bf16[17,32,128]{2,1,0:T(8,128)(2,1)S(1)}, bf16[17,32,128]{2,1,0:T(8,128)(2,1)S(1)}, u32[]{:S(2)}, u32[]{:S(2)}) collective-permute-start(bf16[17,32,128]{2,1,0:T(8,128)(2,1)S(1)} %collective-permute-done.12.refs_6_), channel_id=1, source_target_pairs={{0,1},{1,0},{2,3},{3,2},{4,5},{5,4},{6,7},{7,6},{8,9},{9,8},{10,11... | collective-permute-start | bytes 417800 | tf_op jit(solution)/shard_map/ppermute | solution.py:45
  19.8 5.6 %collective-permute-start.8 = (bf16[17,32,128]{2,1,0:T(8,128)(2,1)S(1)}, bf16[17,32,128]{2,1,0:T(8,128)(2,1)S(1)}, u32[]{:S(2)}, u32[]{:S(2)}) collective-permute-start(bf16[17,32,128]{2,1,0:T(8,128)(2,1)S(1)} %collective-permute-done.6.refs_4_), channel_id=1, source_target_pairs={{0,2},{1,3},{2,0},{3,1},{4,6},{5,7},{6,4},{7,5},{8,10},{9,11},{10,... | collective-permute-start | bytes 417800 | tf_op jit(solution)/shard_map/ppermute | solution.py:45
  23.3 2.5 %collective-permute-start.3 = (bf16[17,32,128]{2,1,0:T(8,128)(2,1)S(1)}, bf16[17,32,128]{2,1,0:T(8,128)(2,1)S(1)}, u32[]{:S(2)}, u32[]{:S(2)}) collective-permute-start(bf16[17,32,128]{2,1,0:T(8,128)(2,1)S(1)} %collective-permute-done.refs_0_), channel_id=1, source_target_pairs={{0,1},{1,0},{2,3},{3,2},{4,5},{5,4},{6,7},{7,6},{8,9},{9,8},{10,11... | collective-permute-start | bytes 417800 | tf_op jit(solution)/shard_map/ppermute | solution.py:45
  23.4 2.4 %collective-permute-start.7 = (bf16[17,32,128]{2,1,0:T(8,128)(2,1)S(1)}, bf16[17,32,128]{2,1,0:T(8,128)(2,1)S(1)}, u32[]{:S(2)}, u32[]{:S(2)}) collective-permute-start(bf16[17,32,128]{2,1,0:T(8,128)(2,1)S(1)} %collective-permute-done.6.refs_4_), channel_id=1, source_target_pairs={{0,1},{1,0},{2,3},{3,2},{4,5},{5,4},{6,7},{7,6},{8,9},{9,8},{10,11... | collective-permute-start | bytes 417800 | tf_op jit(solution)/shard_map/ppermute | solution.py:45
  23.9 1.9 %collective-permute-start.5 = (bf16[17,32,128]{2,1,0:T(8,128)(2,1)S(1)}, bf16[17,32,128]{2,1,0:T(8,128)(2,1)S(1)}, u32[]{:S(2)}, u32[]{:S(2)}) collective-permute-start(bf16[17,32,128]{2,1,0:T(8,128)(2,1)S(1)} %collective-permute-done.4.refs_2_), channel_id=1, source_target_pairs={{0,1},{1,0},{2,3},{3,2},{4,5},{5,4},{6,7},{7,6},{8,9},{9,8},{10,11... | collective-permute-start | bytes 417800 | tf_op jit(solution)/shard_map/ppermute | solution.py:45
  25.3 1.5 %collective-permute-start.14 = (bf16[17,32,128]{2,1,0:T(8,128)(2,1)S(1)}, bf16[17,32,128]{2,1,0:T(8,128)(2,1)S(1)}, u32[]{:S(2)}, u32[]{:S(2)}) collective-permute-start(bf16[17,32,128]{2,1,0:T(8,128)(2,1)S(1)} %collective-permute-done.8.refs_6_), channel_id=1, source_target_pairs={{0,1},{1,0},{2,3},{3,2},{4,5},{5,4},{6,7},{7,6},{8,9},{9,8},{10,11... | collective-permute-start | bytes 417800 | tf_op jit(solution)/shard_map/ppermute | solution.py:45
  31.2 9.6 %collective-permute-start.15 = (bf16[512,128]{1,0:T(8,128)(2,1)S(1)}, bf16[512,128]{1,0:T(8,128)(2,1)S(1)}, u32[]{:S(2)}, u32[]{:S(2)}) collective-permute-start(bf16[512,128]{1,0:T(8,128)(2,1)S(1)} %get-tuple-element.74.agg_ref.refs_0_), channel_id=1, source_target_pairs={{0,8},{1,9},{2,10},{3,11},{4,12},{5,13},{6,14},{7,15},{8,0},{9,1},... | collective-permute-start | bytes 393224 | tf_op jit(solution)/shard_map/ppermute | solution.py:45
  33.5 9.6 %collective-permute-start.17 = (bf16[512,128]{1,0:T(8,128)(2,1)S(1)}, bf16[512,128]{1,0:T(8,128)(2,1)S(1)}, u32[]{:S(2)}, u32[]{:S(2)}) collective-permute-start(bf16[512,128]{1,0:T(8,128)(2,1)S(1)} %get-tuple-element.74.agg_ref.refs_0_), channel_id=1, source_target_pairs={{0,2},{1,3},{2,0},{3,1},{4,6},{5,7},{6,4},{7,5},{8,10},{9,11},{10,... | collective-permute-start | bytes 393224 | tf_op jit(solution)/shard_map/ppermute | solution.py:45
  35.1 10.2 %collective-permute-start.18 = (bf16[512,128]{1,0:T(8,128)(2,1)S(1)}, bf16[512,128]{1,0:T(8,128)(2,1)S(1)}, u32[]{:S(2)}, u32[]{:S(2)}) collective-permute-start(bf16[512,128]{1,0:T(8,128)(2,1)S(1)} %get-tuple-element.74.agg_ref.refs_0_), channel_id=1, source_target_pairs={{0,4},{1,5},{2,6},{3,7},{4,0},{5,1},{6,2},{7,3},{8,12},{9,13},{10,... | collective-permute-start | bytes 393224 | tf_op jit(solution)/shard_map/ppermute | solution.py:45
  36.9 9.3 %collective-permute-start.19 = (bf16[512,128]{1,0:T(8,128)(2,1)S(1)}, bf16[512,128]{1,0:T(8,128)(2,1)S(1)}, u32[]{:S(2)}, u32[]{:S(2)}) collective-permute-start(bf16[512,128]{1,0:T(8,128)(2,1)S(1)} %get-tuple-element.74.agg_ref.refs_0_), channel_id=1, source_target_pairs={{0,6},{1,7},{2,4},{3,5},{4,2},{5,3},{6,0},{7,1},{8,14},{9,15},{10,... | collective-permute-start | bytes 393224 | tf_op jit(solution)/shard_map/ppermute | solution.py:45
  40.8 9.9 %collective-permute-start.20 = (bf16[512,128]{1,0:T(8,128)(2,1)S(1)}, bf16[512,128]{1,0:T(8,128)(2,1)S(1)}, u32[]{:S(2)}, u32[]{:S(2)}) collective-permute-start(bf16[512,128]{1,0:T(8,128)(2,1)S(1)} %collective-permute-done.15.refs_0_), channel_id=1, source_target_pairs={{0,2},{1,3},{2,0},{3,1},{4,6},{5,7},{6,4},{7,5},{8,10},{9,11},{10,... | collective-permute-start | bytes 393224 | tf_op jit(solution)/shard_map/ppermute | solution.py:45
  42.4 9.5 %collective-permute-start.16 = (bf16[512,128]{1,0:T(8,128)(2,1)S(1)}, bf16[512,128]{1,0:T(8,128)(2,1)S(1)}, u32[]{:S(2)}, u32[]{:S(2)}) collective-permute-start(bf16[512,128]{1,0:T(8,128)(2,1)S(1)} %collective-permute-done.15.refs_0_), channel_id=1, source_target_pairs={{0,6},{1,7},{2,4},{3,5},{4,2},{5,3},{6,0},{7,1},{8,14},{9,15},{10,... | collective-permute-start | bytes 393224 | tf_op jit(solution)/shard_map/ppermute | solution.py:45
  43.2 8.7 %collective-permute-start.21 = (bf16[512,128]{1,0:T(8,128)(2,1)S(1)}, bf16[512,128]{1,0:T(8,128)(2,1)S(1)}, u32[]{:S(2)}, u32[]{:S(2)}) collective-permute-start(bf16[512,128]{1,0:T(8,128)(2,1)S(1)} %collective-permute-done.15.refs_0_), channel_id=1, source_target_pairs={{0,4},{1,5},{2,6},{3,7},{4,0},{5,1},{6,2},{7,3},{8,12},{9,13},{10,... | collective-permute-start | bytes 393224 | tf_op jit(solution)/shard_map/ppermute | solution.py:45
  53.5 1.3 %collective-permute-start.22 = (f32[176,128]{1,0:T(8,128)S(1)}, f32[176,128]{1,0:T(8,128)S(1)}, u32[]{:S(2)}, u32[]{:S(2)}) collective-permute-start(f32[176,128]{1,0:T(8,128)S(1)} %get-tuple-element.117.refs_15_), channel_id=1, source_target_pairs={{0,1},{1,0},{2,3},{3,2},{4,5},{5,4},{6,7},{7,6},{8,9},{9,8},{10,11... | collective-permute-start | bytes 270344 | tf_op jit(solution)/shard_map/ppermute | solution.py:45
  57.6 1.8 %collective-permute-start.23 = (f32[432,256]{1,0:T(8,128)S(1)}, f32[432,256]{1,0:T(8,128)S(1)}, u32[]{:S(2)}, u32[]{:S(2)}) collective-permute-start(f32[432,256]{1,0:T(8,128)S(1)} %get-tuple-element.118.mine_ref), channel_id=1, source_target_pairs={{0,1},{1,0},{2,3},{3,2},{4,5},{5,4},{6,7},{7,6},{8,9},{9,8},{10,11... | collective-permute-start | bytes 1327112 | tf_op jit(solution)/shard_map/ppermute | solution.py:45

commit v5 on v4

--- a/solution.py
+++ b/solution.py
@@ -172,28 +172,15 @@
     )(*inputs)
 
 
-def turn_kernel(first, adj_ref, turned_ref, adj, sems):
+def _turn(adj, turned_ref, arrived=None):
     tiles, neigh = turned_ref.shape[0:2]
-    pieces = sems.shape[1]
-    part = TILE // pieces
-    copies = [
-        [
-            pltpu.make_async_copy(
-                adj_ref.at[pl.ds((first + t) * TILE + i * part, part)], adj.at[t, pl.ds(i * part, part)], sems.at[t, i]
-            )
-            for i in range(pieces)
-        ]
-        for t in range(tiles)
-    ]
-    for copy in sum(copies, []):
-        copy.start()
     side = SUB * SUB
     row = _iota((side, side), 0)
     move = ((row % SUB) * SUB + row // SUB == _iota((side, side), 1)).astype(BF16)
     for t in range(tiles):
         for b in range(TILE // SUB):
-            if b * SUB % part == 0:
-                copies[t][b * SUB // part].wait()
+            if arrived:
+                arrived(t, b)
             for j in range(neigh // (2 * SUB)):
                 halves = [
                     adj[t, SUB * b : SUB * (b + 1), SUB * k : SUB * (k + 1), :].reshape(side, TILE)
@@ -207,19 +194,68 @@
                     ].reshape(SUB, SUB, TILE)
 
 
-def turn(adjacency, first, tiles):
-    _, neigh, tile = adjacency.shape
+def turn_kernel(adj_ref, turned_ref, rest_ref, adj, sems, rest_sem):
+    tiles = turned_ref.shape[0]
+    pieces = sems.shape[1]
+    part = TILE // pieces
+    copies = [
+        [
+            pltpu.make_async_copy(
+                adj_ref.at[pl.ds(t * TILE + i * part, part)], adj.at[t, pl.ds(i * part, part)], sems.at[t, i]
+            )
+            for i in range(pieces)
+        ]
+        for t in range(tiles)
+    ]
+    rest = pltpu.make_async_copy(adj_ref.at[pl.ds(tiles * TILE, rest_ref.shape[0])], rest_ref, rest_sem)
+    for copy in sum(copies, []):
+        copy.start()
+    rest.start()
+
+    def arrived(t, b):
+        if b * SUB % part == 0:
+            copies[t][b * SUB // part].wait()
+
+    _turn(adj, turned_ref, arrived)
+    rest.wait()
+
+
+def turn(adjacency):
+    rows, neigh, tile = adjacency.shape
+    tiles = rows // tile // 2
     pieces = 2
     return pl.pallas_call(
-        lambda *refs: turn_kernel(first, *refs),
+        turn_kernel,
         in_specs=[pl.BlockSpec(memory_space=pltpu.HBM)],
-        out_specs=pl.BlockSpec(memory_space=pltpu.VMEM),
-        out_shape=jax.ShapeDtypeStruct((tiles, neigh, tile, tile), BF16),
-        scratch_shapes=[pltpu.VMEM((tiles, tile, neigh, tile), BF16), pltpu.SemaphoreType.DMA((tiles, pieces))],
-        cost_estimate=pl.CostEstimate(flops=tiles << 29, bytes_accessed=tiles << 21, transcendentals=0),
+        out_specs=[pl.BlockSpec(memory_space=pltpu.VMEM)] * 2,
+        out_shape=[
+            jax.ShapeDtypeStruct((tiles, neigh, tile, tile), BF16),
+            jax.ShapeDtypeStruct((rows - tiles * tile, neigh, tile), BF16),
+        ],
+        scratch_shapes=[
+            pltpu.VMEM((tiles, tile, neigh, tile), BF16),
+            pltpu.SemaphoreType.DMA((tiles, pieces)),
+            pltpu.SemaphoreType.DMA,
+        ],
+        cost_estimate=pl.CostEstimate(flops=tiles << 29, bytes_accessed=tiles << 22, transcendentals=0),
         compiler_params=_params(16),
         name="turn_adjacency",
     )(_stay(adjacency))
+
+
+def turn_rest(rest):
+    rows, neigh, tile = rest.shape
+    shape = (rows // tile, neigh, tile, tile)
+    vmem = pl.BlockSpec(memory_space=pltpu.VMEM)
+    return pl.pallas_call(
+        _turn,
+        in_specs=[vmem],
+        out_specs=vmem,
+        out_shape=jax.ShapeDtypeStruct(shape, BF16),
+        cost_estimate=pl.CostEstimate(flops=shape[0] << 29, bytes_accessed=shape[0] << 21, transcendentals=0),
+        compiler_params=_params(12),
+        name="turn_rest",
+    )(rest.reshape(rows // tile, tile, neigh, tile))
 
 
 def _place(ms, blocks, prior, px_ref, labels_ref, got):
@@ -311,34 +347,85 @@
     return [kinds == held[j : j + 1, :].astype(jnp.int32) for j in range(QUAD)]
 
 
+def _rows(owner, px_ref, rows):
+    return px_ref[pl.ds(pl.multiple_of(owner * rows, rows), rows), :]
+
+
 def _inputs(pair, px_ref, agg_ref):
     rows = agg_ref.shape[0] // 2
-    x = [px_ref[pl.ds(pl.multiple_of(_owner(pair, o) * rows, rows), rows), :] for o in range(2)]
+    x = [_rows(_owner(pair, o), px_ref, rows) for o in range(2)]
     return jnp.concatenate([jnp.concatenate(x, axis=0), agg_ref[...]], axis=1)
 
 
-def _forward(c, blocks, px_ref, labels_ref, in_t_ref, out_t_ref, bias_ref, agg_ref, hid_ref, slope_ref, loss_ref, count_ref):
+def _forward(owners, inputs, labels_ref, in_t_ref, out_t_ref, bias_ref, keep):
+    hidden = jnp.maximum(_dot(in_t_ref[...], inputs, NT), 0.0).astype(BF16)
+    logits = _dot(out_t_ref[...], hidden) + jnp.concatenate([bias_ref[...]] * (hidden.shape[1] // LANES), axis=1)
+    logits -= jnp.log(jnp.sum(jnp.exp(logits), axis=0, keepdims=True))
+    probs = jnp.exp(logits)
+    kinds = _iota(bias_ref.shape, 0)
+    loss = count = jnp.zeros(bias_ref.shape, F32)
+    lane = 0
+    for owner in owners:
+        for hot in _hot(kinds, labels_ref, owner):
+            cut = slice(lane, lane + LANES)
+            one = hot.astype(F32)
+            loss -= jnp.where(hot, logits[:, cut], 0.0)
+            count += one
+            keep(cut, probs[:, cut] - one)
+            lane += LANES
+    return hidden, loss, count
+
+
+def pair_kernel(c, *refs):
+    blocks, (px_ref, *shared), outs = refs[0:2], refs[2:7], refs[7:12]
+    agg_ref, hid_ref, slope_ref, loss_ref, count_ref = outs
     me = lax.axis_index("nodes")
     pair = (me // QUAD) ^ c
     rows = blocks[0].shape[0]
     for o, block in enumerate(blocks):
         at = ((me // 2 % 2) ^ o) * rows
         agg_ref[pl.ds(pl.multiple_of(at, rows), rows), :] = block[...]
-    hidden = jnp.maximum(_dot(in_t_ref[...], _inputs(pair, px_ref, agg_ref), NT), 0.0).astype(BF16)
-    hid_ref[...] = hidden
-    logits = _dot(out_t_ref[...], hidden) + jnp.concatenate([bias_ref[...]] * (2 * rows // LANES), axis=1)
-    logits -= jnp.log(jnp.sum(jnp.exp(logits), axis=0, keepdims=True))
-    probs = jnp.exp(logits)
-    kinds = _iota(bias_ref.shape, 0)
-    loss = count = jnp.zeros(bias_ref.shape, F32)
-    for o in range(2):
-        for j, hot in enumerate(_hot(kinds, labels_ref, _owner(pair, o))):
-            cut = slice(o * rows + j * LANES, o * rows + (j + 1) * LANES)
-            one = hot.astype(F32)
-            loss -= jnp.where(hot, logits[:, cut], 0.0)
-            count += one
-            slope_ref[:, cut] = probs[:, cut] - one
-    loss_ref[...], count_ref[...] = loss, count
+
+    def keep(cut, x):
+        slope_ref[:, cut] = x
+
+    owners = [_owner(pair, o) for o in range(2)]
+    hid_ref[...], loss_ref[...], count_ref[...] = _forward(owners, _inputs(pair, px_ref, agg_ref), *shared, keep)
+
+
+def one_kernel(m, *refs):
+    block, (px_ref, *shared), (hid_ref, slope_ref, loss_ref, count_ref) = refs[0], refs[1:6], refs[6:10]
+    owner = lax.axis_index("nodes") ^ m
+    inputs = jnp.concatenate([_rows(owner, px_ref, block.shape[0]), block[...]], axis=1)
+
+    def keep(cut, x):
+        slope_ref[:, cut] = x
+
+    hid_ref[...], loss_ref[...], count_ref[...] = _forward([owner], inputs, *shared, keep)
+
+
+def last_kernel(m, *refs):
+    blocks, (px_ref, *shared), partner, prior = refs[0:2], refs[2:7], refs[7:11], refs[11:17]
+    agg_ref, hid_ref, slope_ref, stats_ref, part, losses, counts = refs[17:]
+    me = lax.axis_index("nodes")
+    rows = blocks[0].shape[0]
+    at = [pl.ds(pl.multiple_of(((me // 2 % 2) ^ o) * rows, rows), rows) for o in range(2)]
+    for o, block in enumerate(blocks):
+        agg_ref[at[o], :] = block[...]
+    hid_ref[:, at[0]], slope_ref[:, at[0]] = partner[0][...], partner[1][...]
+
+    def keep(cut, x):
+        part[:, cut] = x
+
+    inputs = jnp.concatenate([_rows(me ^ m, px_ref, rows), blocks[1][...]], axis=1)
+    hidden, loss, count = _forward([me ^ m], inputs, *shared, keep)
+    hid_ref[:, at[1]], slope_ref[:, at[1]] = hidden, part[...]
+    mine = me // QUAD
+    for c in range(QUAD - 1):
+        losses[mine ^ c], counts[mine ^ c] = prior[2 * c][...], prior[2 * c + 1][...]
+    losses[mine ^ (QUAD - 1)], counts[mine ^ (QUAD - 1)] = loss + partner[2][...], count + partner[3][...]
+    loss, count = (jnp.sum(sum(x[q] for q in range(QUAD)), axis=1, keepdims=True) for x in (losses, counts))
+    stats_ref[...] = jnp.where(_iota(stats_ref.shape, 1) == 0, loss, count)
 
 
 def own_kernel(px_ref, agg_ref, in_t_ref, hidden_ref):
@@ -361,46 +448,44 @@
     )(part_x, agg, in_t)
 
 
-def forward_kernel(c, before, *refs):
-    blocks, shared, refs = refs[0:2], refs[2:7], refs[7:]
-    prior, outs = refs[: 2 * before], refs[2 * before :]
-    _forward(c, blocks, *shared, *outs[0:5])
-    if before:
-        losses, counts = outs[6:8]
-        mine = lax.axis_index("nodes") // QUAD
-        for i in range(before):
-            losses[mine ^ i], counts[mine ^ i] = prior[2 * i][...], prior[2 * i + 1][...]
-        losses[mine ^ c], counts[mine ^ c] = outs[3][...], outs[4][...]
-        loss, count = (jnp.sum(sum(x[q] for q in range(QUAD)), axis=1, keepdims=True) for x in (losses, counts))
-        outs[5][...] = jnp.where(_iota(outs[5].shape, 1) == 0, loss, count)
-
-
-def forward(have, c, shared, prior=()):
+def _call(kernel, name, shapes, operands, scratch=()):
+    vmem = pl.BlockSpec(memory_space=pltpu.VMEM)
+    return pl.pallas_call(
+        kernel,
+        in_specs=[vmem] * len(operands),
+        out_specs=[vmem] * len(shapes),
+        out_shape=[jax.ShapeDtypeStruct(*x) for x in shapes],
+        scratch_shapes=[pltpu.VMEM(*x) for x in scratch],
+        cost_estimate=pl.CostEstimate(flops=1 << 29, bytes_accessed=1 << 21, transcendentals=1 << 18),
+        compiler_params=_params(12),
+        name=name,
+    )(*operands)
+
+
+def forward_pair(have, c, shared):
     rows, width = have[0].shape
     units, padded = shared[2].shape[0], shared[4].shape[0]
-    vmem = pl.BlockSpec(memory_space=pltpu.VMEM)
-    shapes = [
-        jax.ShapeDtypeStruct((2 * rows, width), BF16),
-        jax.ShapeDtypeStruct((units, 2 * rows), BF16),
-        jax.ShapeDtypeStruct((padded, 2 * rows), F32),
-        jax.ShapeDtypeStruct((padded, LANES), F32),
-        jax.ShapeDtypeStruct((padded, LANES), F32),
-    ]
-    scratch = []
-    if prior:
-        shapes.append(jax.ShapeDtypeStruct((padded, LANES), F32))
-        scratch = [pltpu.VMEM((QUAD, padded, LANES), F32)] * 2
+    stat = ((padded, LANES), F32)
+    shapes = [((2 * rows, width), BF16), ((units, 2 * rows), BF16), ((padded, 2 * rows), F32), stat, stat]
+    return _call(lambda *refs: pair_kernel(c, *refs), "forward_pair", shapes, [have[4 * c], have[4 * c + 2], *shared])
+
+
+def forward_one(have, m, shared):
+    rows, units, padded = have[0].shape[0], shared[2].shape[0], shared[4].shape[0]
+    stat = ((padded, LANES), F32)
+    shapes = [((units, rows), BF16), ((padded, rows), F32), stat, stat]
+    return _call(lambda *refs: one_kernel(m, *refs), "forward_one", shapes, [have[m], *shared])
+
+
+def forward_last(have, m, shared, partner, prior):
+    rows, width = have[0].shape
+    units, padded = shared[2].shape[0], shared[4].shape[0]
+    stat = ((padded, LANES), F32)
+    shapes = [((2 * rows, width), BF16), ((units, 2 * rows), BF16), ((padded, 2 * rows), F32), stat]
     stats = [x for held in prior for x in held[3:5]]
-    return pl.pallas_call(
-        lambda *refs: forward_kernel(c, len(prior), *refs),
-        in_specs=[vmem] * (7 + len(stats)),
-        out_specs=[vmem] * len(shapes),
-        out_shape=shapes,
-        scratch_shapes=scratch,
-        cost_estimate=pl.CostEstimate(flops=1 << 29, bytes_accessed=1 << 21, transcendentals=1 << 18),
-        compiler_params=_params(12),
-        name="forward",
-    )(have[4 * c], have[4 * c + 2], *shared, *stats)
+    scratch = [((padded, rows), F32)] + [((QUAD, padded, LANES), F32)] * 2
+    operands = [have[m - 2], have[m], *shared, *partner, *stats]
+    return _call(lambda *refs: last_kernel(m, *refs), "forward_last", shapes, operands, scratch)
 
 
 def backward_kernel(classes, *refs):
@@ -484,12 +569,13 @@
 ):
     packed = pack(features, cluster, slot, labels, DEVICES)
     early, late = tuple(range(0, 8)), tuple(range(8, 16))
-    half = features.shape[0] // TILE // 2
-    have, near, (prior, far) = gather_rows(
-        packed,
-        lambda have: turn(adjacency, 0, half),
-        lambda have: (place(have, early), turn(adjacency, half, half)),
-    )
+    raw = []
+
+    def first(have):
+        raw.extend(turn(adjacency))
+        return raw
+
+    have, (near, _), (prior, far) = gather_rows(packed, first, lambda have: (place(have, early), turn_rest(raw[1])))
     part_x, all_labels, agg = aggregate(have, late, prior, (near, far), halo_tiles, tile_slots)
     weighed = []
 
@@ -499,12 +585,13 @@
 
     def ahead(have):
         in_t, out_t, _, bias = weighed
-        return [forward(have, c, (part_x, all_labels, in_t, out_t, bias)) for c in range(QUAD - 1)]
-
-    have, (_, hidden), held = gather_plane(agg, first, ahead)
+        shared = (part_x, all_labels, in_t, out_t, bias)
+        return [forward_pair(have, c, shared) for c in range(QUAD - 1)], forward_one(have, DEVICES - QUAD, shared)
+
+    have, (_, hidden), (held, partner) = gather_plane(agg, first, ahead)
     in_t, out_t, out_p, bias = weighed
     shared = (part_x, all_labels, in_t, out_t, bias)
-    *last, mine = forward(have, QUAD - 1, shared, held)
+    *last, mine = forward_last(have, DEVICES - 2, shared, partner, held)
     classes = w_out.shape[1]
     sums, class_weight = backward([*held, last], part_x, all_labels, out_p, mine, swap(mine, 1), classes)
     grad_self, grad_neigh, grad_out = total(sums, swap(sums, 1), *w_self.shape, classes)

time: 60.5 us -> 58 us (0.959)
  Pallas kernels: 23.6 us -> 22.1 us
  waiting for transfers between devices: 13.1 us -> 12.4 us
    pallas_call x6 -> x7, Pallas kernels: 10.6 us -> 9.17 us  [the longest x5 4.4 us: _call(): pl.pallas_call(kernel, in_specs=[vmem] * len(operands), out_specs=[vmem]...]
    ppermute x24, waiting for transfers between devices: 13.1 us -> 12.4 us  [swap(): return lax.ppermute(x, 'nodes', [(i, i ^ m) for i in range(DEVICES)])]
  transfers between devices with their start and end apart: 24 -> 24, of which waited for: 10 -> 10; matrix products, arithmetic and copies ran while one was open for 0% -> 0% of each run, Pallas kernels for 21% -> 20%
where the time goes in v5:
time: 58 us; the launch traced here: 57.8 us
  starting transfers between devices  22.5 us (39%)
  Pallas kernels  22.1 us (38%)
  waiting for transfers between devices  12.4 us (21%)
  between operations  0.81 us (1%)
    ppermute x24, starting transfers between devices, swap(): return lax.ppermute(x, 'nodes', [(i, i ^ m) for i in range(DEVICES)])  22.5 us
    ppermute x24, waiting for transfers between devices, swap(): return lax.ppermute(x, 'nodes', [(i, i ^ m) for i in range(DEVICES)])  12.4 us
    pallas_call x5, Pallas kernels, _call(): pl.pallas_call(kernel, in_specs=[vmem] * len(operands), out_specs=[vmem]...  4.4 us
    pallas_call x1, Pallas kernels, aggregate(): pl.pallas_call(lambda *refs: aggregate_kernel(ms, len(turned), *refs), in...  4.33 us
    pallas_call x1, Pallas kernels, turn(): pl.pallas_call(turn_kernel, in_specs=[pl.BlockSpec(memory_space=pltpu.HBM...  3.52 us
    pallas_call x1, Pallas kernels, backward(): pl.pallas_call(lambda *refs: backward_kernel(classes, *refs), in_specs=[v...  2.81 us
    pallas_call x1, Pallas kernels, pack(): pl.pallas_call(lambda *refs: pack_kernel(devices, *refs), in_specs=[pl.Bl...  1.45 us
    pallas_call x1, Pallas kernels, place(): pl.pallas_call(lambda *refs: _place(ms, refs[:len(ms)], None, *refs[len(m...  1.34 us
  transfers between devices with their start and end apart: 24, of which 10 were waited for; matrix products, arithmetic and copies ran while one was open for 0% of the time, Pallas kernels for 20%

profile of v5, /device:TPU:0, one launch (start us, length us, event | category | flops | bytes accessed | tf_op | source)
XLA Modules:
  0.0 57.8 jit_solution(4587118939919377753)
XLA Ops:
  0.6 1.5 %pack_rows.1.refs_0_ = bf16[17,32,128]{2,1,0:T(8,128)(2,1)S(1)} custom-call(bf16[512,128]{1,0:T(8,128)(2,1)} %refs_0_.2, s32[1,512]{1,0:T(1,128)} %bitcast.10, s32[1,512]{1,0:T(1,128)} %bitcast.11, s32[4,128]{1,0:T(4,128)} %bitcast.12), custom_call_target="tpu_custom_call" | custom-call | tf_op jit(solution)/shard_map/pack_rows/pallas_call | solution.py:121
  2.1 4.1 %collective-permute-start = (bf16[17,32,128]{2,1,0:T(8,128)(2,1)S(1)}, bf16[17,32,128]{2,1,0:T(8,128)(2,1)S(1)}, u32[]{:S(2)}, u32[]{:S(2)}) collective-permute-start(bf16[17,32,128]{2,1,0:T(8,128)(2,1)S(1)} %pack_rows.1.refs_0_), channel_id=1, source_target_pairs={{0,8},{1,9},{2,10},{3,11},{4,12},{5,13},{6,14},{7,15},{8,0},{9,1},... | collective-permute-start | bytes 417800 | tf_op jit(solution)/shard_map/ppermute | solution.py:45
  6.2 1.6 %collective-permute-start.1 = (bf16[17,32,128]{2,1,0:T(8,128)(2,1)S(1)}, bf16[17,32,128]{2,1,0:T(8,128)(2,1)S(1)}, u32[]{:S(2)}, u32[]{:S(2)}) collective-permute-start(bf16[17,32,128]{2,1,0:T(8,128)(2,1)S(1)} %pack_rows.1.refs_0_), channel_id=1, source_target_pairs={{0,4},{1,5},{2,6},{3,7},{4,0},{5,1},{6,2},{7,3},{8,12},{9,13},{10,... | collective-permute-start | bytes 417800 | tf_op jit(solution)/shard_map/ppermute | solution.py:45
  7.8 1.5 %collective-permute-start.2 = (bf16[17,32,128]{2,1,0:T(8,128)(2,1)S(1)}, bf16[17,32,128]{2,1,0:T(8,128)(2,1)S(1)}, u32[]{:S(2)}, u32[]{:S(2)}) collective-permute-start(bf16[17,32,128]{2,1,0:T(8,128)(2,1)S(1)} %pack_rows.1.refs_0_), channel_id=1, source_target_pairs={{0,2},{1,3},{2,0},{3,1},{4,6},{5,7},{6,4},{7,5},{8,10},{9,11},{10,... | collective-permute-start | bytes 417800 | tf_op jit(solution)/shard_map/ppermute | solution.py:45
  9.3 3.5 %turn_adjacency.1 = (bf16[2,64,128,128]{3,2,1,0:T(8,128)(2,1)S(1)}, bf16[256,64,128]{2,1,0:T(8,128)(2,1)S(1)}) custom-call(bf16[512,64,128]{2,1,0:T(8,128)(2,1)} %adj_ref.1), custom_call_target="tpu_custom_call" | custom-call | flops 1073741824 | bytes 8388608 | tf_op jit(solution)/shard_map/turn_adjacency/pallas_call | solution.py:227
  12.8 0.1 collective-permute-done.refs_0_
  13.0 0.2 collective-permute-done.1.refs_4_
  13.1 0.0 collective-permute-done.2.refs_2_
  13.2 1.6 %collective-permute-start.12 = (bf16[17,32,128]{2,1,0:T(8,128)(2,1)S(1)}, bf16[17,32,128]{2,1,0:T(8,128)(2,1)S(1)}, u32[]{:S(2)}, u32[]{:S(2)}) collective-permute-start(bf16[17,32,128]{2,1,0:T(8,128)(2,1)S(1)} %collective-permute-done.1.refs_4_), channel_id=1, source_target_pairs={{0,2},{1,3},{2,0},{3,1},{4,6},{5,7},{6,4},{7,5},{8,10},{9,11},{10,... | collective-permute-start | bytes 417800 | tf_op jit(solution)/shard_map/ppermute | solution.py:45
  14.7 1.4 %collective-permute-start.6 = (bf16[17,32,128]{2,1,0:T(8,128)(2,1)S(1)}, bf16[17,32,128]{2,1,0:T(8,128)(2,1)S(1)}, u32[]{:S(2)}, u32[]{:S(2)}) collective-permute-start(bf16[17,32,128]{2,1,0:T(8,128)(2,1)S(1)} %collective-permute-done.refs_0_), channel_id=1, source_target_pairs={{0,4},{1,5},{2,6},{3,7},{4,0},{5,1},{6,2},{7,3},{8,12},{9,13},{10,... | collective-permute-start | bytes 417800 | tf_op jit(solution)/shard_map/ppermute | solution.py:45
  16.1 0.5 collective-permute-start.10
  16.7 0.0 collective-permute-done.9.refs_1_
  16.7 0.5 collective-permute-start.4
  17.2 1.8 %collective-permute-done.12.refs_6_ = bf16[17,32,128]{2,1,0:T(8,128)(2,1)S(1)} collective-permute-done((bf16[17,32,128]{2,1,0:T(8,128)(2,1)S(1)}, bf16[17,32,128]{2,1,0:T(8,128)(2,1)S(1)}, u32[]{:S(2)}, u32[]{:S(2)}) %collective-permute-start.12) | collective-permute-done | bytes 139296 | tf_op jit(solution)/shard_map/ppermute | solution.py:45
  19.0 0.0 collective-permute-start.13
  19.0 0.8 %collective-permute-done.6.refs_4_ = bf16[17,32,128]{2,1,0:T(8,128)(2,1)S(1)} collective-permute-done((bf16[17,32,128]{2,1,0:T(8,128)(2,1)S(1)}, bf16[17,32,128]{2,1,0:T(8,128)(2,1)S(1)}, u32[]{:S(2)}, u32[]{:S(2)}) %collective-permute-start.6) | collective-permute-done | bytes 139296 | tf_op jit(solution)/shard_map/ppermute | solution.py:45
  19.8 1.0 %collective-permute-start.8 = (bf16[17,32,128]{2,1,0:T(8,128)(2,1)S(1)}, bf16[17,32,128]{2,1,0:T(8,128)(2,1)S(1)}, u32[]{:S(2)}, u32[]{:S(2)}) collective-permute-start(bf16[17,32,128]{2,1,0:T(8,128)(2,1)S(1)} %collective-permute-done.6.refs_4_), channel_id=1, source_target_pairs={{0,2},{1,3},{2,0},{3,1},{4,6},{5,7},{6,4},{7,5},{8,10},{9,11},{10,... | collective-permute-start | bytes 417800 | tf_op jit(solution)/shard_map/ppermute | solution.py:45
  20.7 1.3 %turn_rest.1.refs_11_ = bf16[2,64,128,128]{3,2,1,0:T(8,128)(2,1)S(1)} custom-call(bf16[2,128,64,128]{3,2,1,0:T(8,128)(2,1)S(1)} %bitcast.8), custom_call_target="tpu_custom_call" | custom-call | flops 1073741824 | bytes 4194304 | tf_op jit(solution)/shard_map/turn_rest/pallas_call | solution.py:250
  22.0 0.0 collective-permute-done.11.refs_5_
  22.0 0.1 collective-permute-start.3
  22.1 0.5 collective-permute-start.7
  22.6 0.0 collective-permute-done.4.refs_2_
  22.6 0.1 collective-permute-start.5
  22.7 1.3 %place.1 = (bf16[8192,128]{1,0:T(8,128)(2,1)S(1)}, bf16[16,16,128]{2,1,0:T(8,128)(2,1)S(1)}) custom-call(bf16[17,32,128]{2,1,0:T(8,128)(2,1)S(1)} %pack_rows.1.refs_0_, bf16[17,32,128]{2,1,0:T(8,128)(2,1)S(1)} %collective-permute-done.9.refs_1_, bf16[17,32,128]{2,1,0:T(8,128)(2,1)S(1)} %collective-permute-done.2.refs_2_, ...), custom_call_target="tpu_custom_call" | custom-call | flops 1073741824 | bytes 4194304 | tf_op jit(solution)/shard_map/place/pallas_call | solution.py:296
  24.0 1.2 %collective-permute-done.8.refs_6_ = bf16[17,32,128]{2,1,0:T(8,128)(2,1)S(1)} collective-permute-done((bf16[17,32,128]{2,1,0:T(8,128)(2,1)S(1)}, bf16[17,32,128]{2,1,0:T(8,128)(2,1)S(1)}, u32[]{:S(2)}, u32[]{:S(2)}) %collective-permute-start.8) | collective-permute-done | bytes 139296 | tf_op jit(solution)/shard_map/ppermute | solution.py:45
  25.2 1.3 %collective-permute-done.14.refs_7_ = bf16[17,32,128]{2,1,0:T(8,128)(2,1)S(1)} collective-permute-done((bf16[17,32,128]{2,1,0:T(8,128)(2,1)S(1)}, bf16[17,32,128]{2,1,0:T(8,128)(2,1)S(1)}, u32[]{:S(2)}, u32[]{:S(2)}) %collective-permute-start.14) | collective-permute-done | bytes 139296 | tf_op jit(solution)/shard_map/ppermute | solution.py:45
  26.6 4.3 %aggregate.1 = (bf16[8192,128]{1,0:T(8,128)(2,1)S(1)}, bf16[16,16,128]{2,1,0:T(8,128)(2,1)S(1)}, bf16[512,128]{1,0:T(8,128)(2,1)S(1)}) custom-call(bf16[17,32,128]{2,1,0:T(8,128)(2,1)S(1)} %collective-permute-done.refs_0_, bf16[17,32,128]{2,1,0:T(8,128)(2,1)S(1)} %collective-permute-done.3.refs_1_, bf16[17,32,128]{2,1,0:T(8,128)(2,1)S(1)} %collective-permute-done.4.refs_2_, ...), custom_call_target="tpu_custom_call" | custom-call | tf_op jit(solution)/shard_map/aggregate/pallas_call | solution.py:330
  30.9 2.4 %collective-permute-start.15 = (bf16[512,128]{1,0:T(8,128)(2,1)S(1)}, bf16[512,128]{1,0:T(8,128)(2,1)S(1)}, u32[]{:S(2)}, u32[]{:S(2)}) collective-permute-start(bf16[512,128]{1,0:T(8,128)(2,1)S(1)} %get-tuple-element.86.agg_ref.refs_0_), channel_id=1, source_target_pairs={{0,8},{1,9},{2,10},{3,11},{4,12},{5,13},{6,14},{7,15},{8,0},{9,1},... | collective-permute-start | bytes 393224 | tf_op jit(solution)/shard_map/ppermute | solution.py:45
  33.3 0.5 collective-permute-start.17
  33.8 3.0 %collective-permute-start.18 = (bf16[512,128]{1,0:T(8,128)(2,1)S(1)}, bf16[512,128]{1,0:T(8,128)(2,1)S(1)}, u32[]{:S(2)}, u32[]{:S(2)}) collective-permute-start(bf16[512,128]{1,0:T(8,128)(2,1)S(1)} %get-tuple-element.86.agg_ref.refs_0_), channel_id=1, source_target_pairs={{0,4},{1,5},{2,6},{3,7},{4,0},{5,1},{6,2},{7,3},{8,12},{9,13},{10,... | collective-permute-start | bytes 393224 | tf_op jit(solution)/shard_map/ppermute | solution.py:45
  36.9 1.2 %weights.1 = (bf16[256,256]{1,0:T(8,128)(2,1)S(1)}, bf16[176,256]{1,0:T(8,128)(2,1)S(1)}, bf16[256,176]{1,0:T(8,128)(2,1)S(1)}, f32[176,128]{1,0:T(8,128)S(1)}) custom-call(bf16[128,256]{1,0:T(8,128)(2,1)} %refs_0_.3, bf16[128,256]{1,0:T(8,128)(2,1)} %refs_1_.1, bf16[172,256]{1,0:T(8,128)(2,1)} %bitcast.9, f32[1,172]{1,0:T(1,128)} %bitcast.13), custom_call_target="tpu_custom_call" | custom-call | bytes 2097152 | tf_op jit(solution)/shard_map/weights/pallas_call | solution.py:153
  38.1 1.0 %own.1 = bf16[512,256]{1,0:T(8,128)(2,1)} custom-call(bf16[8192,128]{1,0:T(8,128)(2,1)S(1)} %get-tuple-element.91.px_ref.refs_2_.refs_1_.refs_12_, bf16[512,128]{1,0:T(8,128)(2,1)S(1)} %get-tuple-element.86.agg_ref.refs_0_, bf16[256,256]{1,0:T(8,128)(2,1)S(1)} %get-tuple-element.87.in_t_ref.refs_4_.refs_3_), custom_call_target="tpu_custom_call" | custom-call | flops 67108864 | bytes 262144 | tf_op jit(solution)/shard_map/own/pallas_call | solution.py:440
  39.0 1.3 %collective-permute-done.15.refs_0_ = bf16[512,128]{1,0:T(8,128)(2,1)S(1)} collective-permute-done((bf16[512,128]{1,0:T(8,128)(2,1)S(1)}, bf16[512,128]{1,0:T(8,128)(2,1)S(1)}, u32[]{:S(2)}, u32[]{:S(2)}) %collective-permute-start.15) | collective-permute-done | bytes 131104 | tf_op jit(solution)/shard_map/ppermute | solution.py:45
  40.4 0.6 %collective-permute-start.21 = (bf16[512,128]{1,0:T(8,128)(2,1)S(1)}, bf16[512,128]{1,0:T(8,128)(2,1)S(1)}, u32[]{:S(2)}, u32[]{:S(2)}) collective-permute-start(bf16[512,128]{1,0:T(8,128)(2,1)S(1)} %collective-permute-done.15.refs_0_), channel_id=1, source_target_pairs={{0,4},{1,5},{2,6},{3,7},{4,0},{5,1},{6,2},{7,3},{8,12},{9,13},{10,... | collective-permute-start | bytes 393224 | tf_op jit(solution)/shard_map/ppermute | solution.py:45
  41.0 1.5 %collective-permute-start.20 = (bf16[512,128]{1,0:T(8,128)(2,1)S(1)}, bf16[512,128]{1,0:T(8,128)(2,1)S(1)}, u32[]{:S(2)}, u32[]{:S(2)}) collective-permute-start(bf16[512,128]{1,0:T(8,128)(2,1)S(1)} %collective-permute-done.15.refs_0_), channel_id=1, source_target_pairs={{0,2},{1,3},{2,0},{3,1},{4,6},{5,7},{6,4},{7,5},{8,10},{9,11},{10,... | collective-permute-start | bytes 393224 | tf_op jit(solution)/shard_map/ppermute | solution.py:45
  42.5 1.3 %collective-permute-start.16 = (bf16[512,128]{1,0:T(8,128)(2,1)S(1)}, bf16[512,128]{1,0:T(8,128)(2,1)S(1)}, u32[]{:S(2)}, u32[]{:S(2)}) collective-permute-start(bf16[512,128]{1,0:T(8,128)(2,1)S(1)} %collective-permute-done.15.refs_0_), channel_id=1, source_target_pairs={{0,6},{1,7},{2,4},{3,5},{4,2},{5,3},{6,0},{7,1},{8,14},{9,15},{10,... | collective-permute-start | bytes 393224 | tf_op jit(solution)/shard_map/ppermute | solution.py:45
  43.9 0.9 %forward_pair.3 = (bf16[1024,128]{1,0:T(8,128)(2,1)S(1)}, bf16[256,1024]{1,0:T(8,128)(2,1)S(1)}, f32[176,1024]{1,0:T(8,128)S(1)}, f32[176,128]{1,0:T(8,128)S(1)}, f32[176,128]{1,0:T(8,128)S(1)}) custom-call(bf16[512,128]{1,0:T(8,128)(2,1)S(1)} %get-tuple-element.86.agg_ref.refs_0_, bf16[512,128]{1,0:T(8,128)(2,1)S(1)} %collective-permute-done.17.refs_1_, ...), custom_call_target="tpu_custom_call" | custom-call | flops 536870912 | bytes 2097152 | tf_op jit(solution)/shard_map/forward_pair/pallas_call | solution.py:453
  44.8 0.9 %forward_pair.4 = (bf16[1024,128]{1,0:T(8,128)(2,1)S(1)}, bf16[256,1024]{1,0:T(8,128)(2,1)S(1)}, f32[176,1024]{1,0:T(8,128)S(1)}, f32[176,128]{1,0:T(8,128)S(1)}, f32[176,128]{1,0:T(8,128)S(1)}) custom-call(bf16[512,128]{1,0:T(8,128)(2,1)S(1)} %collective-permute-done.18.refs_0_, bf16[512,128]{1,0:T(8,128)(2,1)S(1)} %collective-permute-done.19.refs_1_, ...), custom_call_target="tpu_custom_call" | custom-call | flops 536870912 | bytes 2097152 | tf_op jit(solution)/shard_map/forward_pair/pallas_call | solution.py:453
  45.7 2.6 %collective-permute-done.21.refs_0_ = bf16[512,128]{1,0:T(8,128)(2,1)S(1)} collective-permute-done((bf16[512,128]{1,0:T(8,128)(2,1)S(1)}, bf16[512,128]{1,0:T(8,128)(2,1)S(1)}, u32[]{:S(2)}, u32[]{:S(2)}) %collective-permute-start.21) | collective-permute-done | bytes 131104 | tf_op jit(solution)/shard_map/ppermute | solution.py:45
  48.3 0.8 %forward_one.1 = (bf16[256,512]{1,0:T(8,128)(2,1)S(1)}, f32[176,512]{1,0:T(8,128)S(1)}, f32[176,128]{1,0:T(8,128)S(1)}, f32[176,128]{1,0:T(8,128)S(1)}) custom-call(bf16[512,128]{1,0:T(8,128)(2,1)S(1)} %collective-permute-done.21.refs_0_, bf16[8192,128]{1,0:T(8,128)(2,1)S(1)} %get-tuple-element.91.px_ref.refs_2_.refs_1_.refs_12_, ...), custom_call_target="tpu_custom_call" | custom-call | flops 536870912 | bytes 2097152 | tf_op jit(solution)/shard_map/forward_one/pallas_call | solution.py:453
  49.1 0.9 %forward_pair.5 = (bf16[1024,128]{1,0:T(8,128)(2,1)S(1)}, bf16[256,1024]{1,0:T(8,128)(2,1)S(1)}, f32[176,1024]{1,0:T(8,128)S(1)}, f32[176,128]{1,0:T(8,128)S(1)}, f32[176,128]{1,0:T(8,128)S(1)}) custom-call(bf16[512,128]{1,0:T(8,128)(2,1)S(1)} %collective-permute-done.15.refs_0_, bf16[512,128]{1,0:T(8,128)(2,1)S(1)} %collective-permute-done.20.refs_1_, ...), custom_call_target="tpu_custom_call" | custom-call | flops 536870912 | bytes 2097152 | tf_op jit(solution)/shard_map/forward_pair/pallas_call | solution.py:453
  50.1 0.9 %forward_last.1 = (bf16[1024,128]{1,0:T(8,128)(2,1)S(1)}, bf16[256,1024]{1,0:T(8,128)(2,1)S(1)}, f32[176,1024]{1,0:T(8,128)S(1)}, f32[176,128]{1,0:T(8,128)S(1)}) custom-call(bf16[512,128]{1,0:T(8,128)(2,1)S(1)} %collective-permute-done.21.refs_0_, bf16[512,128]{1,0:T(8,128)(2,1)S(1)} %collective-permute-done.16.refs_1_, ...), custom_call_target="tpu_custom_call" | custom-call | flops 536870912 | bytes 2097152 | tf_op jit(solution)/shard_map/forward_last/pallas_call | solution.py:453
  50.9 0.1 collective-permute-start.22
  51.0 1.3 %collective-permute-done.22.refs_16_ = f32[176,128]{1,0:T(8,128)S(1)} collective-permute-done((f32[176,128]{1,0:T(8,128)S(1)}, f32[176,128]{1,0:T(8,128)S(1)}, u32[]{:S(2)}, u32[]{:S(2)}) %collective-permute-start.22) | collective-permute-done | bytes 90144 | tf_op jit(solution)/shard_map/ppermute | solution.py:45
  52.3 2.8 %backward.1 = (f32[432,256]{1,0:T(8,128)S(1)}, f32[1,172]{1,0:T(1,128)}) custom-call(bf16[1024,128]{1,0:T(8,128)(2,1)S(1)} %get-tuple-element.114.refs_0_, bf16[256,1024]{1,0:T(8,128)(2,1)S(1)} %get-tuple-element.115.refs_1_, f32[176,1024]{1,0:T(8,128)S(1)} %get-tuple-element.116.refs_2_, bf16[1024,128]{1,0:T(8,128)(2,1)S(1)} %get-tuple-element.117.refs_3_, ...), custom_call_target="tpu_custom_call" | custom-call | tf_op jit(solution)/shard_map/backward/pallas_call | solution.py:528
  55.1 0.2 collective-permute-start.23
  55.3 1.6 %collective-permute-done.23.other_ref = f32[432,256]{1,0:T(8,128)S(1)} collective-permute-done((f32[432,256]{1,0:T(8,128)S(1)}, f32[432,256]{1,0:T(8,128)S(1)}, u32[]{:S(2)}, u32[]{:S(2)}) %collective-permute-start.23) | collective-permute-done | bytes 442400 | tf_op jit(solution)/shard_map/ppermute | solution.py:45
  56.9 0.9 %total.1 = (f32[128,256]{1,0:T(8,128)}, f32[128,256]{1,0:T(8,128)}, f32[172,256]{1,0:T(8,128)}) custom-call(f32[432,256]{1,0:T(8,128)S(1)} %get-tuple-element.138.mine_ref, f32[432,256]{1,0:T(8,128)S(1)} %collective-permute-done.23.other_ref), custom_call_target="tpu_custom_call" | custom-call | tf_op jit(solution)/shard_map/total/pallas_call | solution.py:553
  (18 shorter events, 0.0 us)
Async XLA Ops:
  2.1 10.9 %collective-permute-start = (bf16[17,32,128]{2,1,0:T(8,128)(2,1)S(1)}, bf16[17,32,128]{2,1,0:T(8,128)(2,1)S(1)}, u32[]{:S(2)}, u32[]{:S(2)}) collective-permute-start(bf16[17,32,128]{2,1,0:T(8,128)(2,1)S(1)} %pack_rows.1.refs_0_), channel_id=1, source_target_pairs={{0,8},{1,9},{2,10},{3,11},{4,12},{5,13},{6,14},{7,15},{8,0},{9,1},... | collective-permute-start | bytes 417800 | tf_op jit(solution)/shard_map/ppermute | solution.py:45
  6.2 7.0 %collective-permute-start.1 = (bf16[17,32,128]{2,1,0:T(8,128)(2,1)S(1)}, bf16[17,32,128]{2,1,0:T(8,128)(2,1)S(1)}, u32[]{:S(2)}, u32[]{:S(2)}) collective-permute-start(bf16[17,32,128]{2,1,0:T(8,128)(2,1)S(1)} %pack_rows.1.refs_0_), channel_id=1, source_target_pairs={{0,4},{1,5},{2,6},{3,7},{4,0},{5,1},{6,2},{7,3},{8,12},{9,13},{10,... | collective-permute-start | bytes 417800 | tf_op jit(solution)/shard_map/ppermute | solution.py:45
  7.8 5.4 %collective-permute-start.2 = (bf16[17,32,128]{2,1,0:T(8,128)(2,1)S(1)}, bf16[17,32,128]{2,1,0:T(8,128)(2,1)S(1)}, u32[]{:S(2)}, u32[]{:S(2)}) collective-permute-start(bf16[17,32,128]{2,1,0:T(8,128)(2,1)S(1)} %pack_rows.1.refs_0_), channel_id=1, source_target_pairs={{0,2},{1,3},{2,0},{3,1},{4,6},{5,7},{6,4},{7,5},{8,10},{9,11},{10,... | collective-permute-start | bytes 417800 | tf_op jit(solution)/shard_map/ppermute | solution.py:45
  9.3 7.4 %collective-permute-start.9 = (bf16[17,32,128]{2,1,0:T(8,128)(2,1)S(1)}, bf16[17,32,128]{2,1,0:T(8,128)(2,1)S(1)}, u32[]{:S(2)}, u32[]{:S(2)}) collective-permute-start(bf16[17,32,128]{2,1,0:T(8,128)(2,1)S(1)} %pack_rows.1.refs_0_), channel_id=1, source_target_pairs={{0,1},{1,0},{2,3},{3,2},{4,5},{5,4},{6,7},{7,6},{8,9},{9,8},{10,11... | collective-permute-start | bytes 417800 | tf_op jit(solution)/shard_map/ppermute | solution.py:45
  13.2 5.8 %collective-permute-start.12 = (bf16[17,32,128]{2,1,0:T(8,128)(2,1)S(1)}, bf16[17,32,128]{2,1,0:T(8,128)(2,1)S(1)}, u32[]{:S(2)}, u32[]{:S(2)}) collective-permute-start(bf16[17,32,128]{2,1,0:T(8,128)(2,1)S(1)} %collective-permute-done.1.refs_4_), channel_id=1, source_target_pairs={{0,2},{1,3},{2,0},{3,1},{4,6},{5,7},{6,4},{7,5},{8,10},{9,11},{10,... | collective-permute-start | bytes 417800 | tf_op jit(solution)/shard_map/ppermute | solution.py:45
  14.7 5.1 %collective-permute-start.6 = (bf16[17,32,128]{2,1,0:T(8,128)(2,1)S(1)}, bf16[17,32,128]{2,1,0:T(8,128)(2,1)S(1)}, u32[]{:S(2)}, u32[]{:S(2)}) collective-permute-start(bf16[17,32,128]{2,1,0:T(8,128)(2,1)S(1)} %collective-permute-done.refs_0_), channel_id=1, source_target_pairs={{0,4},{1,5},{2,6},{3,7},{4,0},{5,1},{6,2},{7,3},{8,12},{9,13},{10,... | collective-permute-start | bytes 417800 | tf_op jit(solution)/shard_map/ppermute | solution.py:45
  16.1 5.9 %collective-permute-start.11 = (bf16[17,32,128]{2,1,0:T(8,128)(2,1)S(1)}, bf16[17,32,128]{2,1,0:T(8,128)(2,1)S(1)}, u32[]{:S(2)}, u32[]{:S(2)}) collective-permute-start(bf16[17,32,128]{2,1,0:T(8,128)(2,1)S(1)} %collective-permute-done.1.refs_4_), channel_id=1, source_target_pairs={{0,1},{1,0},{2,3},{3,2},{4,5},{5,4},{6,7},{7,6},{8,9},{9,8},{10,11... | collective-permute-start | bytes 417800 | tf_op jit(solution)/shard_map/ppermute | solution.py:45
  16.1 6.0 %collective-permute-start.10 = (bf16[17,32,128]{2,1,0:T(8,128)(2,1)S(1)}, bf16[17,32,128]{2,1,0:T(8,128)(2,1)S(1)}, u32[]{:S(2)}, u32[]{:S(2)}) collective-permute-start(bf16[17,32,128]{2,1,0:T(8,128)(2,1)S(1)} %collective-permute-done.2.refs_2_), channel_id=1, source_target_pairs={{0,1},{1,0},{2,3},{3,2},{4,5},{5,4},{6,7},{7,6},{8,9},{9,8},{10,11... | collective-permute-start | bytes 417800 | tf_op jit(solution)/shard_map/ppermute | solution.py:45
  16.7 6.0 %collective-permute-start.4 = (bf16[17,32,128]{2,1,0:T(8,128)(2,1)S(1)}, bf16[17,32,128]{2,1,0:T(8,128)(2,1)S(1)}, u32[]{:S(2)}, u32[]{:S(2)}) collective-permute-start(bf16[17,32,128]{2,1,0:T(8,128)(2,1)S(1)} %collective-permute-done.refs_0_), channel_id=1, source_target_pairs={{0,2},{1,3},{2,0},{3,1},{4,6},{5,7},{6,4},{7,5},{8,10},{9,11},{10,... | collective-permute-start | bytes 417800 | tf_op jit(solution)/shard_map/ppermute | solution.py:45
  19.0 3.7 %collective-permute-start.13 = (bf16[17,32,128]{2,1,0:T(8,128)(2,1)S(1)}, bf16[17,32,128]{2,1,0:T(8,128)(2,1)S(1)}, u32[]{:S(2)}, u32[]{:S(2)}) collective-permute-start(bf16[17,32,128]{2,1,0:T(8,128)(2,1)S(1)} %collective-permute-done.12.refs_6_), channel_id=1, source_target_pairs={{0,1},{1,0},{2,3},{3,2},{4,5},{5,4},{6,7},{7,6},{8,9},{9,8},{10,11... | collective-permute-start | bytes 417800 | tf_op jit(solution)/shard_map/ppermute | solution.py:45
  19.8 5.4 %collective-permute-start.8 = (bf16[17,32,128]{2,1,0:T(8,128)(2,1)S(1)}, bf16[17,32,128]{2,1,0:T(8,128)(2,1)S(1)}, u32[]{:S(2)}, u32[]{:S(2)}) collective-permute-start(bf16[17,32,128]{2,1,0:T(8,128)(2,1)S(1)} %collective-permute-done.6.refs_4_), channel_id=1, source_target_pairs={{0,2},{1,3},{2,0},{3,1},{4,6},{5,7},{6,4},{7,5},{8,10},{9,11},{10,... | collective-permute-start | bytes 417800 | tf_op jit(solution)/shard_map/ppermute | solution.py:45
  20.7 5.8 %copy-start = (s32[4,64]{1,0:T(4,128)S(1)}, s32[4,64]{1,0:T(4,128)}, u32[]{:S(2)}) copy-start(s32[4,64]{1,0:T(4,128)} %refs_13_.1) | copy-start | bytes 3076
  20.7 5.8 %copy-start.1 = (s32[1,64]{1,0:T(1,128)S(1)}, s32[1,64]{1,0:T(1,128)}, u32[]{:S(2)}) copy-start(s32[1,64]{1,0:T(1,128)} %refs_12_.1) | copy-start | bytes 772
  22.0 3.2 %collective-permute-start.3 = (bf16[17,32,128]{2,1,0:T(8,128)(2,1)S(1)}, bf16[17,32,128]{2,1,0:T(8,128)(2,1)S(1)}, u32[]{:S(2)}, u32[]{:S(2)}) collective-permute-start(bf16[17,32,128]{2,1,0:T(8,128)(2,1)S(1)} %collective-permute-done.refs_0_), channel_id=1, source_target_pairs={{0,1},{1,0},{2,3},{3,2},{4,5},{5,4},{6,7},{7,6},{8,9},{9,8},{10,11... | collective-permute-start | bytes 417800 | tf_op jit(solution)/shard_map/ppermute | solution.py:45
  22.1 3.1 %collective-permute-start.7 = (bf16[17,32,128]{2,1,0:T(8,128)(2,1)S(1)}, bf16[17,32,128]{2,1,0:T(8,128)(2,1)S(1)}, u32[]{:S(2)}, u32[]{:S(2)}) collective-permute-start(bf16[17,32,128]{2,1,0:T(8,128)(2,1)S(1)} %collective-permute-done.6.refs_4_), channel_id=1, source_target_pairs={{0,1},{1,0},{2,3},{3,2},{4,5},{5,4},{6,7},{7,6},{8,9},{9,8},{10,11... | collective-permute-start | bytes 417800 | tf_op jit(solution)/shard_map/ppermute | solution.py:45
  22.6 2.6 %collective-permute-start.5 = (bf16[17,32,128]{2,1,0:T(8,128)(2,1)S(1)}, bf16[17,32,128]{2,1,0:T(8,128)(2,1)S(1)}, u32[]{:S(2)}, u32[]{:S(2)}) collective-permute-start(bf16[17,32,128]{2,1,0:T(8,128)(2,1)S(1)} %collective-permute-done.4.refs_2_), channel_id=1, source_target_pairs={{0,1},{1,0},{2,3},{3,2},{4,5},{5,4},{6,7},{7,6},{8,9},{9,8},{10,11... | collective-permute-start | bytes 417800 | tf_op jit(solution)/shard_map/ppermute | solution.py:45
  25.2 1.4 %collective-permute-start.14 = (bf16[17,32,128]{2,1,0:T(8,128)(2,1)S(1)}, bf16[17,32,128]{2,1,0:T(8,128)(2,1)S(1)}, u32[]{:S(2)}, u32[]{:S(2)}) collective-permute-start(bf16[17,32,128]{2,1,0:T(8,128)(2,1)S(1)} %collective-permute-done.8.refs_6_), channel_id=1, source_target_pairs={{0,1},{1,0},{2,3},{3,2},{4,5},{5,4},{6,7},{7,6},{8,9},{9,8},{10,11... | collective-permute-start | bytes 417800 | tf_op jit(solution)/shard_map/ppermute | solution.py:45
  30.9 9.4 %collective-permute-start.15 = (bf16[512,128]{1,0:T(8,128)(2,1)S(1)}, bf16[512,128]{1,0:T(8,128)(2,1)S(1)}, u32[]{:S(2)}, u32[]{:S(2)}) collective-permute-start(bf16[512,128]{1,0:T(8,128)(2,1)S(1)} %get-tuple-element.86.agg_ref.refs_0_), channel_id=1, source_target_pairs={{0,8},{1,9},{2,10},{3,11},{4,12},{5,13},{6,14},{7,15},{8,0},{9,1},... | collective-permute-start | bytes 393224 | tf_op jit(solution)/shard_map/ppermute | solution.py:45
  33.3 9.2 %collective-permute-start.17 = (bf16[512,128]{1,0:T(8,128)(2,1)S(1)}, bf16[512,128]{1,0:T(8,128)(2,1)S(1)}, u32[]{:S(2)}, u32[]{:S(2)}) collective-permute-start(bf16[512,128]{1,0:T(8,128)(2,1)S(1)} %get-tuple-element.86.agg_ref.refs_0_), channel_id=1, source_target_pairs={{0,2},{1,3},{2,0},{3,1},{4,6},{5,7},{6,4},{7,5},{8,10},{9,11},{10,... | collective-permute-start | bytes 393224 | tf_op jit(solution)/shard_map/ppermute | solution.py:45
  33.8 10.9 %collective-permute-start.18 = (bf16[512,128]{1,0:T(8,128)(2,1)S(1)}, bf16[512,128]{1,0:T(8,128)(2,1)S(1)}, u32[]{:S(2)}, u32[]{:S(2)}) collective-permute-start(bf16[512,128]{1,0:T(8,128)(2,1)S(1)} %get-tuple-element.86.agg_ref.refs_0_), channel_id=1, source_target_pairs={{0,4},{1,5},{2,6},{3,7},{4,0},{5,1},{6,2},{7,3},{8,12},{9,13},{10,... | collective-permute-start | bytes 393224 | tf_op jit(solution)/shard_map/ppermute | solution.py:45
  36.9 7.9 %collective-permute-start.19 = (bf16[512,128]{1,0:T(8,128)(2,1)S(1)}, bf16[512,128]{1,0:T(8,128)(2,1)S(1)}, u32[]{:S(2)}, u32[]{:S(2)}) collective-permute-start(bf16[512,128]{1,0:T(8,128)(2,1)S(1)} %get-tuple-element.86.agg_ref.refs_0_), channel_id=1, source_target_pairs={{0,6},{1,7},{2,4},{3,5},{4,2},{5,3},{6,0},{7,1},{8,14},{9,15},{10,... | collective-permute-start | bytes 393224 | tf_op jit(solution)/shard_map/ppermute | solution.py:45
  40.4 8.0 %collective-permute-start.21 = (bf16[512,128]{1,0:T(8,128)(2,1)S(1)}, bf16[512,128]{1,0:T(8,128)(2,1)S(1)}, u32[]{:S(2)}, u32[]{:S(2)}) collective-permute-start(bf16[512,128]{1,0:T(8,128)(2,1)S(1)} %collective-permute-done.15.refs_0_), channel_id=1, source_target_pairs={{0,4},{1,5},{2,6},{3,7},{4,0},{5,1},{6,2},{7,3},{8,12},{9,13},{10,... | collective-permute-start | bytes 393224 | tf_op jit(solution)/shard_map/ppermute | solution.py:45
  41.0 8.1 %collective-permute-start.20 = (bf16[512,128]{1,0:T(8,128)(2,1)S(1)}, bf16[512,128]{1,0:T(8,128)(2,1)S(1)}, u32[]{:S(2)}, u32[]{:S(2)}) collective-permute-start(bf16[512,128]{1,0:T(8,128)(2,1)S(1)} %collective-permute-done.15.refs_0_), channel_id=1, source_target_pairs={{0,2},{1,3},{2,0},{3,1},{4,6},{5,7},{6,4},{7,5},{8,10},{9,11},{10,... | collective-permute-start | bytes 393224 | tf_op jit(solution)/shard_map/ppermute | solution.py:45
  42.5 7.5 %collective-permute-start.16 = (bf16[512,128]{1,0:T(8,128)(2,1)S(1)}, bf16[512,128]{1,0:T(8,128)(2,1)S(1)}, u32[]{:S(2)}, u32[]{:S(2)}) collective-permute-start(bf16[512,128]{1,0:T(8,128)(2,1)S(1)} %collective-permute-done.15.refs_0_), channel_id=1, source_target_pairs={{0,6},{1,7},{2,4},{3,5},{4,2},{5,3},{6,0},{7,1},{8,14},{9,15},{10,... | collective-permute-start | bytes 393224 | tf_op jit(solution)/shard_map/ppermute | solution.py:45
  50.9 1.4 %collective-permute-start.22 = (f32[176,128]{1,0:T(8,128)S(1)}, f32[176,128]{1,0:T(8,128)S(1)}, u32[]{:S(2)}, u32[]{:S(2)}) collective-permute-start(f32[176,128]{1,0:T(8,128)S(1)} %get-tuple-element.137.refs_15_), channel_id=1, source_target_pairs={{0,1},{1,0},{2,3},{3,2},{4,5},{5,4},{6,7},{7,6},{8,9},{9,8},{10,11... | collective-permute-start | bytes 270344 | tf_op jit(solution)/shard_map/ppermute | solution.py:45
  55.1 1.8 %collective-permute-start.23 = (f32[432,256]{1,0:T(8,128)S(1)}, f32[432,256]{1,0:T(8,128)S(1)}, u32[]{:S(2)}, u32[]{:S(2)}) collective-permute-start(f32[432,256]{1,0:T(8,128)S(1)} %get-tuple-element.138.mine_ref), channel_id=1, source_target_pairs={{0,1},{1,0},{2,3},{3,2},{4,5},{5,4},{6,7},{7,6},{8,9},{9,8},{10,11... | collective-permute-start | bytes 1327112 | tf_op jit(solution)/shard_map/ppermute | solution.py:45

commit v6 on v5

--- a/solution.py
+++ b/solution.py
@@ -71,16 +71,17 @@
     return have, done
 
 
-def gather_plane(block, first, second):
+def gather_plane(block, first, second, third):
     have = {0: block}
     have[8], have[4], have[2], have[6] = (swap(block, m) for m in (8, 4, 2, 6))
     have[8], one = lax.optimization_barrier((have[8], first(have)))
     have[12], have[10], have[14] = swap(have[8], 4), swap(have[8], 2), swap(have[8], 6)
-    have[14], two = lax.optimization_barrier((have[14], second(have)))
-    return have, one, two
-
-
-def gather_rows(block, first, second):
+    have[10], two = lax.optimization_barrier((have[10], second(have)))
+    have[12], three = lax.optimization_barrier((have[12], third(have)))
+    return have, one, two, three
+
+
+def gather_rows(block, first, second, third):
     have = {0: block}
     have[8], have[4], have[2] = (swap(block, m) for m in (8, 4, 2))
     (have[8], have[4], have[2]), one = lax.optimization_barrier(((have[8], have[4], have[2]), first(have)))
@@ -90,7 +91,8 @@
     have[11], have[13] = swap(have[10], 1), swap(have[12], 1)
     have[14], two = lax.optimization_barrier((have[14], second(have)))
     have[15] = swap(have[14], 1)
-    return have, one, two
+    have[15], three = lax.optimization_barrier((have[15], third(have, two)))
+    return have, one, two, three
 
 
 def pack_kernel(devices, *refs):
@@ -290,19 +292,20 @@
     ]
 
 
-def place(have, ms):
+def place(have, ms, prior=()):
     per, width = have[0].shape[1:]
     vmem = pl.BlockSpec(memory_space=pltpu.VMEM)
-    return pl.pallas_call(
-        lambda *refs: _place(ms, refs[: len(ms)], None, *refs[len(ms) :]),
-        in_specs=[vmem] * len(ms),
+    n = len(ms) + len(prior)
+    return pl.pallas_call(
+        lambda *refs: _place(ms, refs[: len(ms)], refs[len(ms) : n], *refs[n:]),
+        in_specs=[vmem] * n,
         out_specs=[vmem] * 2,
         out_shape=_placed(per, width),
         scratch_shapes=[pltpu.VMEM((DEVICES, len(ms) * per, width), BF16)],
         cost_estimate=pl.CostEstimate(flops=1 << 30, bytes_accessed=1 << 22, transcendentals=0),
         compiler_params=_params(16),
         name="place",
-    )(*[have[m] for m in ms])
+    )(*[have[m] for m in ms], *prior)
 
 
 def aggregate_kernel(ms, parts, *refs):
@@ -568,14 +571,19 @@
     features, cluster, slot, halo_tiles, tile_slots, adjacency, labels, w_self, w_neigh, w_out, b_out
 ):
     packed = pack(features, cluster, slot, labels, DEVICES)
-    early, late = tuple(range(0, 8)), tuple(range(8, 16))
     raw = []
 
     def first(have):
         raw.extend(turn(adjacency))
         return raw
 
-    have, (near, _), (prior, far) = gather_rows(packed, first, lambda have: (place(have, early), turn_rest(raw[1])))
+    have, (near, _), (_, far), prior = gather_rows(
+        packed,
+        first,
+        lambda have: (place(have, range(0, 8)), turn_rest(raw[1])),
+        lambda have, done: place(have, range(8, 12), done[0]),
+    )
+    late = range(12, 16)
     part_x, all_labels, agg = aggregate(have, late, prior, (near, far), halo_tiles, tile_slots)
     weighed = []
 
@@ -583,14 +591,18 @@
         weighed.extend(weights(w_self, w_neigh, w_out, b_out))
         return weighed, own(part_x, agg, weighed[0])
 
-    def ahead(have):
-        in_t, out_t, _, bias = weighed
-        shared = (part_x, all_labels, in_t, out_t, bias)
-        return [forward_pair(have, c, shared) for c in range(QUAD - 1)], forward_one(have, DEVICES - QUAD, shared)
-
-    have, (_, hidden), (held, partner) = gather_plane(agg, first, ahead)
+    def ahead(cs):
+        def work(have):
+            in_t, out_t, _, bias = weighed
+            return [forward_pair(have, c, (part_x, all_labels, in_t, out_t, bias)) for c in cs]
+
+        return work
+
+    have, (_, hidden), two, three = gather_plane(agg, first, ahead((0, 1)), ahead((2,)))
+    held = [*two, *three]
     in_t, out_t, out_p, bias = weighed
     shared = (part_x, all_labels, in_t, out_t, bias)
+    partner = forward_one(have, DEVICES - QUAD, shared)
     *last, mine = forward_last(have, DEVICES - 2, shared, partner, held)
     classes = w_out.shape[1]
     sums, class_weight = backward([*held, last], part_x, all_labels, out_p, mine, swap(mine, 1), classes)

time: 58 us -> 57.2 us (0.986)
  waiting for transfers between devices: 12.4 us -> 11.4 us
    ppermute x24, waiting for transfers between devices: 12.4 us -> 11.4 us  [swap(): return lax.ppermute(x, 'nodes', [(i, i ^ m) for i in range(DEVICES)])]
    pallas_call x1 -> x2, Pallas kernels: 1.34 us -> 2.09 us  [place(): pl.pallas_call(lambda *refs: _place(ms, refs[:len(ms)], refs[len(ms):n],...]
    pallas_call x1, Pallas kernels: 4.33 us -> 3.75 us  [aggregate(): pl.pallas_call(lambda *refs: aggregate_kernel(ms, len(turned), *refs), in...]
  transfers between devices with their start and end apart: 24 -> 24, of which waited for: 10 -> 12; matrix products, arithmetic and copies ran while one was open for 0% -> 0% of each run, Pallas kernels for 20% -> 22%
where the time goes in v6:
time: 57.2 us; the launch traced here: 57 us
  starting transfers between devices  22.5 us (39%)
  Pallas kernels  22.3 us (39%)
  waiting for transfers between devices  11.4 us (20%)
  between operations  0.82 us (1%)
    ppermute x24, starting transfers between devices, swap(): return lax.ppermute(x, 'nodes', [(i, i ^ m) for i in range(DEVICES)])  22.5 us
    ppermute x24, waiting for transfers between devices, swap(): return lax.ppermute(x, 'nodes', [(i, i ^ m) for i in range(DEVICES)])  11.4 us
    pallas_call x5, Pallas kernels, _call(): pl.pallas_call(kernel, in_specs=[vmem] * len(operands), out_specs=[vmem]...  4.41 us
    pallas_call x1, Pallas kernels, aggregate(): pl.pallas_call(lambda *refs: aggregate_kernel(ms, len(turned), *refs), in...  3.75 us
    pallas_call x1, Pallas kernels, turn(): pl.pallas_call(turn_kernel, in_specs=[pl.BlockSpec(memory_space=pltpu.HBM...  3.52 us
    pallas_call x1, Pallas kernels, backward(): pl.pallas_call(lambda *refs: backward_kernel(classes, *refs), in_specs=[v...  2.81 us
    pallas_call x2, Pallas kernels, place(): pl.pallas_call(lambda *refs: _place(ms, refs[:len(ms)], refs[len(ms):n],...  2.09 us
    pallas_call x1, Pallas kernels, pack(): pl.pallas_call(lambda *refs: pack_kernel(devices, *refs), in_specs=[pl.Bl...  1.45 us
  transfers between devices with their start and end apart: 24, of which 12 were waited for; matrix products, arithmetic and copies ran while one was open for 0% of the time, Pallas kernels for 22%

profile of v6, /device:TPU:0, one launch (start us, length us, event | category | flops | bytes accessed | tf_op | source)
XLA Modules:
  0.0 57.0 jit_solution(5176962865189895108)
XLA Ops:
  0.6 1.5 %pack_rows.1.refs_0_ = bf16[17,32,128]{2,1,0:T(8,128)(2,1)S(1)} custom-call(bf16[512,128]{1,0:T(8,128)(2,1)} %refs_0_.2, s32[1,512]{1,0:T(1,128)} %bitcast.10, s32[1,512]{1,0:T(1,128)} %bitcast.11, s32[4,128]{1,0:T(4,128)} %bitcast.12), custom_call_target="tpu_custom_call" | custom-call | tf_op jit(solution)/shard_map/pack_rows/pallas_call | solution.py:123
  2.1 4.1 %collective-permute-start = (bf16[17,32,128]{2,1,0:T(8,128)(2,1)S(1)}, bf16[17,32,128]{2,1,0:T(8,128)(2,1)S(1)}, u32[]{:S(2)}, u32[]{:S(2)}) collective-permute-start(bf16[17,32,128]{2,1,0:T(8,128)(2,1)S(1)} %pack_rows.1.refs_0_), channel_id=1, source_target_pairs={{0,8},{1,9},{2,10},{3,11},{4,12},{5,13},{6,14},{7,15},{8,0},{9,1},... | collective-permute-start | bytes 417800 | tf_op jit(solution)/shard_map/ppermute | solution.py:45
  6.2 1.6 %collective-permute-start.1 = (bf16[17,32,128]{2,1,0:T(8,128)(2,1)S(1)}, bf16[17,32,128]{2,1,0:T(8,128)(2,1)S(1)}, u32[]{:S(2)}, u32[]{:S(2)}) collective-permute-start(bf16[17,32,128]{2,1,0:T(8,128)(2,1)S(1)} %pack_rows.1.refs_0_), channel_id=1, source_target_pairs={{0,4},{1,5},{2,6},{3,7},{4,0},{5,1},{6,2},{7,3},{8,12},{9,13},{10,... | collective-permute-start | bytes 417800 | tf_op jit(solution)/shard_map/ppermute | solution.py:45
  7.8 1.5 %collective-permute-start.2 = (bf16[17,32,128]{2,1,0:T(8,128)(2,1)S(1)}, bf16[17,32,128]{2,1,0:T(8,128)(2,1)S(1)}, u32[]{:S(2)}, u32[]{:S(2)}) collective-permute-start(bf16[17,32,128]{2,1,0:T(8,128)(2,1)S(1)} %pack_rows.1.refs_0_), channel_id=1, source_target_pairs={{0,2},{1,3},{2,0},{3,1},{4,6},{5,7},{6,4},{7,5},{8,10},{9,11},{10,... | collective-permute-start | bytes 417800 | tf_op jit(solution)/shard_map/ppermute | solution.py:45
  9.3 3.5 %turn_adjacency.1 = (bf16[2,64,128,128]{3,2,1,0:T(8,128)(2,1)S(1)}, bf16[256,64,128]{2,1,0:T(8,128)(2,1)S(1)}) custom-call(bf16[512,64,128]{2,1,0:T(8,128)(2,1)} %adj_ref.1), custom_call_target="tpu_custom_call" | custom-call | flops 1073741824 | bytes 8388608 | tf_op jit(solution)/shard_map/turn_adjacency/pallas_call | solution.py:229
  12.8 0.1 collective-permute-done.refs_0_
  13.0 0.2 collective-permute-done.1.refs_4_
  13.2 1.6 %collective-permute-start.9 = (bf16[17,32,128]{2,1,0:T(8,128)(2,1)S(1)}, bf16[17,32,128]{2,1,0:T(8,128)(2,1)S(1)}, u32[]{:S(2)}, u32[]{:S(2)}) collective-permute-start(bf16[17,32,128]{2,1,0:T(8,128)(2,1)S(1)} %collective-permute-done.1.refs_4_), channel_id=1, source_target_pairs={{0,2},{1,3},{2,0},{3,1},{4,6},{5,7},{6,4},{7,5},{8,10},{9,11},{10,... | collective-permute-start | bytes 417800 | tf_op jit(solution)/shard_map/ppermute | solution.py:45
  14.7 1.4 %collective-permute-start.3 = (bf16[17,32,128]{2,1,0:T(8,128)(2,1)S(1)}, bf16[17,32,128]{2,1,0:T(8,128)(2,1)S(1)}, u32[]{:S(2)}, u32[]{:S(2)}) collective-permute-start(bf16[17,32,128]{2,1,0:T(8,128)(2,1)S(1)} %collective-permute-done.refs_0_), channel_id=1, source_target_pairs={{0,4},{1,5},{2,6},{3,7},{4,0},{5,1},{6,2},{7,3},{8,12},{9,13},{10,... | collective-permute-start | bytes 417800 | tf_op jit(solution)/shard_map/ppermute | solution.py:45
  16.1 0.5 collective-permute-start.13
  16.7 0.2 collective-permute-start.7
  16.9 2.1 %collective-permute-done.9.refs_6_ = bf16[17,32,128]{2,1,0:T(8,128)(2,1)S(1)} collective-permute-done((bf16[17,32,128]{2,1,0:T(8,128)(2,1)S(1)}, bf16[17,32,128]{2,1,0:T(8,128)(2,1)S(1)}, u32[]{:S(2)}, u32[]{:S(2)}) %collective-permute-start.9) | collective-permute-done | bytes 139296 | tf_op jit(solution)/shard_map/ppermute | solution.py:45
  19.0 0.8 %collective-permute-done.3.refs_0_ = bf16[17,32,128]{2,1,0:T(8,128)(2,1)S(1)} collective-permute-done((bf16[17,32,128]{2,1,0:T(8,128)(2,1)S(1)}, bf16[17,32,128]{2,1,0:T(8,128)(2,1)S(1)}, u32[]{:S(2)}, u32[]{:S(2)}) %collective-permute-start.3) | collective-permute-done | bytes 139296 | tf_op jit(solution)/shard_map/ppermute | solution.py:45
  19.8 1.0 %collective-permute-start.5 = (bf16[17,32,128]{2,1,0:T(8,128)(2,1)S(1)}, bf16[17,32,128]{2,1,0:T(8,128)(2,1)S(1)}, u32[]{:S(2)}, u32[]{:S(2)}) collective-permute-start(bf16[17,32,128]{2,1,0:T(8,128)(2,1)S(1)} %collective-permute-done.3.refs_0_), channel_id=1, source_target_pairs={{0,2},{1,3},{2,0},{3,1},{4,6},{5,7},{6,4},{7,5},{8,10},{9,11},{10,... | collective-permute-start | bytes 417800 | tf_op jit(solution)/shard_map/ppermute | solution.py:45
  20.7 1.3 %turn_rest.1.refs_7_ = bf16[2,64,128,128]{3,2,1,0:T(8,128)(2,1)S(1)} custom-call(bf16[2,128,64,128]{3,2,1,0:T(8,128)(2,1)S(1)} %bitcast.8), custom_call_target="tpu_custom_call" | custom-call | flops 1073741824 | bytes 4194304 | tf_op jit(solution)/shard_map/turn_rest/pallas_call | solution.py:252
  22.0 0.0 copy-start
  22.0 0.0 copy-start.1
  22.0 0.1 collective-permute-start.12
  22.1 0.2 collective-permute-done.13.refs_2_
  22.3 0.3 collective-permute-start.14
  22.6 1.3 %place.2 = (bf16[8192,128]{1,0:T(8,128)(2,1)S(1)}, bf16[16,16,128]{2,1,0:T(8,128)(2,1)S(1)}) custom-call(bf16[17,32,128]{2,1,0:T(8,128)(2,1)S(1)} %pack_rows.1.refs_0_, bf16[17,32,128]{2,1,0:T(8,128)(2,1)S(1)} %collective-permute-done.6.refs_1_, bf16[17,32,128]{2,1,0:T(8,128)(2,1)S(1)} %collective-permute-done.2.refs_2_, ...), custom_call_target="tpu_custom_call" | custom-call | flops 1073741824 | bytes 4194304 | tf_op jit(solution)/shard_map/place/pallas_call | solution.py:299
  24.0 1.2 %collective-permute-done.5.refs_2_ = bf16[17,32,128]{2,1,0:T(8,128)(2,1)S(1)} collective-permute-done((bf16[17,32,128]{2,1,0:T(8,128)(2,1)S(1)}, bf16[17,32,128]{2,1,0:T(8,128)(2,1)S(1)}, u32[]{:S(2)}, u32[]{:S(2)}) %collective-permute-start.5) | collective-permute-done | bytes 139296 | tf_op jit(solution)/shard_map/ppermute | solution.py:45
  25.2 0.5 collective-permute-start.4
  25.7 0.7 %place.3 = (bf16[8192,128]{1,0:T(8,128)(2,1)S(1)}, bf16[16,16,128]{2,1,0:T(8,128)(2,1)S(1)}) custom-call(bf16[17,32,128]{2,1,0:T(8,128)(2,1)S(1)} %collective-permute-done.refs_0_, bf16[17,32,128]{2,1,0:T(8,128)(2,1)S(1)} %collective-permute-done.12.refs_1_, bf16[17,32,128]{2,1,0:T(8,128)(2,1)S(1)} %collective-permute-done.13.refs_2_, ...), custom_call_target="tpu_custom_call" | custom-call | flops 1073741824 | bytes 4194304 | tf_op jit(solution)/shard_map/place/pallas_call | solution.py:299
  26.5 0.1 collective-permute-done.11.refs_3_
  26.6 0.2 collective-permute-done.4.refs_1_
  26.8 3.8 %aggregate.1 = (bf16[8192,128]{1,0:T(8,128)(2,1)S(1)}, bf16[16,16,128]{2,1,0:T(8,128)(2,1)S(1)}, bf16[512,128]{1,0:T(8,128)(2,1)S(1)}) custom-call(bf16[17,32,128]{2,1,0:T(8,128)(2,1)S(1)} %collective-permute-done.3.refs_0_, bf16[17,32,128]{2,1,0:T(8,128)(2,1)S(1)} %collective-permute-done.4.refs_1_, ...), custom_call_target="tpu_custom_call" | custom-call | tf_op jit(solution)/shard_map/aggregate/pallas_call | solution.py:333
  30.5 2.4 %collective-permute-start.15 = (bf16[512,128]{1,0:T(8,128)(2,1)S(1)}, bf16[512,128]{1,0:T(8,128)(2,1)S(1)}, u32[]{:S(2)}, u32[]{:S(2)}) collective-permute-start(bf16[512,128]{1,0:T(8,128)(2,1)S(1)} %get-tuple-element.93.agg_ref.refs_0_), channel_id=1, source_target_pairs={{0,8},{1,9},{2,10},{3,11},{4,12},{5,13},{6,14},{7,15},{8,0},{9,1},... | collective-permute-start | bytes 393224 | tf_op jit(solution)/shard_map/ppermute | solution.py:45
  32.9 0.5 collective-permute-start.17
  33.4 3.0 %collective-permute-start.18 = (bf16[512,128]{1,0:T(8,128)(2,1)S(1)}, bf16[512,128]{1,0:T(8,128)(2,1)S(1)}, u32[]{:S(2)}, u32[]{:S(2)}) collective-permute-start(bf16[512,128]{1,0:T(8,128)(2,1)S(1)} %get-tuple-element.93.agg_ref.refs_0_), channel_id=1, source_target_pairs={{0,4},{1,5},{2,6},{3,7},{4,0},{5,1},{6,2},{7,3},{8,12},{9,13},{10,... | collective-permute-start | bytes 393224 | tf_op jit(solution)/shard_map/ppermute | solution.py:45
  36.5 1.2 %weights.1 = (bf16[256,256]{1,0:T(8,128)(2,1)S(1)}, bf16[176,256]{1,0:T(8,128)(2,1)S(1)}, bf16[256,176]{1,0:T(8,128)(2,1)S(1)}, f32[176,128]{1,0:T(8,128)S(1)}) custom-call(bf16[128,256]{1,0:T(8,128)(2,1)} %refs_0_.3, bf16[128,256]{1,0:T(8,128)(2,1)} %refs_1_.1, bf16[172,256]{1,0:T(8,128)(2,1)} %bitcast.9, f32[1,172]{1,0:T(1,128)} %bitcast.13), custom_call_target="tpu_custom_call" | custom-call | bytes 2097152 | tf_op jit(solution)/shard_map/weights/pallas_call | solution.py:155
  37.7 1.0 %own.1 = bf16[512,256]{1,0:T(8,128)(2,1)} custom-call(bf16[8192,128]{1,0:T(8,128)(2,1)S(1)} %get-tuple-element.98.px_ref.refs_2_.refs_1_.refs_12_, bf16[512,128]{1,0:T(8,128)(2,1)S(1)} %get-tuple-element.93.agg_ref.refs_0_, bf16[256,256]{1,0:T(8,128)(2,1)S(1)} %get-tuple-element.94.in_t_ref.refs_4_.refs_3_), custom_call_target="tpu_custom_call" | custom-call | flops 67108864 | bytes 262144 | tf_op jit(solution)/shard_map/own/pallas_call | solution.py:443
  38.6 1.5 %collective-permute-done.15.refs_0_ = bf16[512,128]{1,0:T(8,128)(2,1)S(1)} collective-permute-done((bf16[512,128]{1,0:T(8,128)(2,1)S(1)}, bf16[512,128]{1,0:T(8,128)(2,1)S(1)}, u32[]{:S(2)}, u32[]{:S(2)}) %collective-permute-start.15) | collective-permute-done | bytes 131104 | tf_op jit(solution)/shard_map/ppermute | solution.py:45
  40.1 0.7 %collective-permute-start.16 = (bf16[512,128]{1,0:T(8,128)(2,1)S(1)}, bf16[512,128]{1,0:T(8,128)(2,1)S(1)}, u32[]{:S(2)}, u32[]{:S(2)}) collective-permute-start(bf16[512,128]{1,0:T(8,128)(2,1)S(1)} %collective-permute-done.15.refs_0_), channel_id=1, source_target_pairs={{0,2},{1,3},{2,0},{3,1},{4,6},{5,7},{6,4},{7,5},{8,10},{9,11},{10,... | collective-permute-start | bytes 393224 | tf_op jit(solution)/shard_map/ppermute | solution.py:45
  40.8 1.4 %collective-permute-start.20 = (bf16[512,128]{1,0:T(8,128)(2,1)S(1)}, bf16[512,128]{1,0:T(8,128)(2,1)S(1)}, u32[]{:S(2)}, u32[]{:S(2)}) collective-permute-start(bf16[512,128]{1,0:T(8,128)(2,1)S(1)} %collective-permute-done.15.refs_0_), channel_id=1, source_target_pairs={{0,4},{1,5},{2,6},{3,7},{4,0},{5,1},{6,2},{7,3},{8,12},{9,13},{10,... | collective-permute-start | bytes 393224 | tf_op jit(solution)/shard_map/ppermute | solution.py:45
  42.1 1.5 %collective-permute-start.21 = (bf16[512,128]{1,0:T(8,128)(2,1)S(1)}, bf16[512,128]{1,0:T(8,128)(2,1)S(1)}, u32[]{:S(2)}, u32[]{:S(2)}) collective-permute-start(bf16[512,128]{1,0:T(8,128)(2,1)S(1)} %collective-permute-done.15.refs_0_), channel_id=1, source_target_pairs={{0,6},{1,7},{2,4},{3,5},{4,2},{5,3},{6,0},{7,1},{8,14},{9,15},{10,... | collective-permute-start | bytes 393224 | tf_op jit(solution)/shard_map/ppermute | solution.py:45
  43.6 0.9 %forward_pair.3 = (bf16[1024,128]{1,0:T(8,128)(2,1)S(1)}, bf16[256,1024]{1,0:T(8,128)(2,1)S(1)}, f32[176,1024]{1,0:T(8,128)S(1)}, f32[176,128]{1,0:T(8,128)S(1)}, f32[176,128]{1,0:T(8,128)S(1)}) custom-call(bf16[512,128]{1,0:T(8,128)(2,1)S(1)} %get-tuple-element.93.agg_ref.refs_0_, bf16[512,128]{1,0:T(8,128)(2,1)S(1)} %collective-permute-done.17.refs_1_, ...), custom_call_target="tpu_custom_call" | custom-call | flops 536870912 | bytes 2097152 | tf_op jit(solution)/shard_map/forward_pair/pallas_call | solution.py:456
  44.6 0.9 %forward_pair.4 = (bf16[1024,128]{1,0:T(8,128)(2,1)S(1)}, bf16[256,1024]{1,0:T(8,128)(2,1)S(1)}, f32[176,1024]{1,0:T(8,128)S(1)}, f32[176,128]{1,0:T(8,128)S(1)}, f32[176,128]{1,0:T(8,128)S(1)}) custom-call(bf16[512,128]{1,0:T(8,128)(2,1)S(1)} %collective-permute-done.18.refs_0_, bf16[512,128]{1,0:T(8,128)(2,1)S(1)} %collective-permute-done.19.refs_1_, ...), custom_call_target="tpu_custom_call" | custom-call | flops 536870912 | bytes 2097152 | tf_op jit(solution)/shard_map/forward_pair/pallas_call | solution.py:456
  45.5 2.1 %collective-permute-done.16.refs_1_ = bf16[512,128]{1,0:T(8,128)(2,1)S(1)} collective-permute-done((bf16[512,128]{1,0:T(8,128)(2,1)S(1)}, bf16[512,128]{1,0:T(8,128)(2,1)S(1)}, u32[]{:S(2)}, u32[]{:S(2)}) %collective-permute-start.16) | collective-permute-done | bytes 131104 | tf_op jit(solution)/shard_map/ppermute | solution.py:45
  47.5 1.1 %forward_pair.5 = (bf16[1024,128]{1,0:T(8,128)(2,1)S(1)}, bf16[256,1024]{1,0:T(8,128)(2,1)S(1)}, f32[176,1024]{1,0:T(8,128)S(1)}, f32[176,128]{1,0:T(8,128)S(1)}, f32[176,128]{1,0:T(8,128)S(1)}) custom-call(bf16[512,128]{1,0:T(8,128)(2,1)S(1)} %collective-permute-done.15.refs_0_, bf16[512,128]{1,0:T(8,128)(2,1)S(1)} %collective-permute-done.16.refs_1_, ...), custom_call_target="tpu_custom_call" | custom-call | flops 536870912 | bytes 2097152 | tf_op jit(solution)/shard_map/forward_pair/pallas_call | solution.py:456
  48.6 0.6 %forward_one.1 = (bf16[256,512]{1,0:T(8,128)(2,1)S(1)}, f32[176,512]{1,0:T(8,128)S(1)}, f32[176,128]{1,0:T(8,128)S(1)}, f32[176,128]{1,0:T(8,128)S(1)}) custom-call(bf16[512,128]{1,0:T(8,128)(2,1)S(1)} %collective-permute-done.20.refs_0_, bf16[8192,128]{1,0:T(8,128)(2,1)S(1)} %get-tuple-element.98.px_ref.refs_2_.refs_1_.refs_12_, ...), custom_call_target="tpu_custom_call" | custom-call | flops 536870912 | bytes 2097152 | tf_op jit(solution)/shard_map/forward_one/pallas_call | solution.py:456
  49.3 0.9 %forward_last.1 = (bf16[1024,128]{1,0:T(8,128)(2,1)S(1)}, bf16[256,1024]{1,0:T(8,128)(2,1)S(1)}, f32[176,1024]{1,0:T(8,128)S(1)}, f32[176,128]{1,0:T(8,128)S(1)}) custom-call(bf16[512,128]{1,0:T(8,128)(2,1)S(1)} %collective-permute-done.20.refs_0_, bf16[512,128]{1,0:T(8,128)(2,1)S(1)} %collective-permute-done.21.refs_1_, ...), custom_call_target="tpu_custom_call" | custom-call | flops 536870912 | bytes 2097152 | tf_op jit(solution)/shard_map/forward_last/pallas_call | solution.py:456
  50.2 0.1 collective-permute-start.22
  50.2 1.3 %collective-permute-done.22.refs_16_ = f32[176,128]{1,0:T(8,128)S(1)} collective-permute-done((f32[176,128]{1,0:T(8,128)S(1)}, f32[176,128]{1,0:T(8,128)S(1)}, u32[]{:S(2)}, u32[]{:S(2)}) %collective-permute-start.22) | collective-permute-done | bytes 90144 | tf_op jit(solution)/shard_map/ppermute | solution.py:45
  51.5 2.8 %backward.1 = (f32[432,256]{1,0:T(8,128)S(1)}, f32[1,172]{1,0:T(1,128)}) custom-call(bf16[1024,128]{1,0:T(8,128)(2,1)S(1)} %get-tuple-element.112.refs_0_, bf16[256,1024]{1,0:T(8,128)(2,1)S(1)} %get-tuple-element.113.refs_1_, f32[176,1024]{1,0:T(8,128)S(1)} %get-tuple-element.114.refs_2_, bf16[1024,128]{1,0:T(8,128)(2,1)S(1)} %get-tuple-element.115.refs_3_, ...), custom_call_target="tpu_custom_call" | custom-call | tf_op jit(solution)/shard_map/backward/pallas_call | solution.py:531
  54.3 0.2 collective-permute-start.23
  54.5 1.6 %collective-permute-done.23.other_ref = f32[432,256]{1,0:T(8,128)S(1)} collective-permute-done((f32[432,256]{1,0:T(8,128)S(1)}, f32[432,256]{1,0:T(8,128)S(1)}, u32[]{:S(2)}, u32[]{:S(2)}) %collective-permute-start.23) | collective-permute-done | bytes 442400 | tf_op jit(solution)/shard_map/ppermute | solution.py:45
  56.1 0.9 %total.1 = (f32[128,256]{1,0:T(8,128)}, f32[128,256]{1,0:T(8,128)}, f32[172,256]{1,0:T(8,128)}) custom-call(f32[432,256]{1,0:T(8,128)S(1)} %get-tuple-element.142.mine_ref, f32[432,256]{1,0:T(8,128)S(1)} %collective-permute-done.23.other_ref), custom_call_target="tpu_custom_call" | custom-call | tf_op jit(solution)/shard_map/total/pallas_call | solution.py:556
  (19 shorter events, 0.0 us)
Async XLA Ops:
  2.1 10.9 %collective-permute-start = (bf16[17,32,128]{2,1,0:T(8,128)(2,1)S(1)}, bf16[17,32,128]{2,1,0:T(8,128)(2,1)S(1)}, u32[]{:S(2)}, u32[]{:S(2)}) collective-permute-start(bf16[17,32,128]{2,1,0:T(8,128)(2,1)S(1)} %pack_rows.1.refs_0_), channel_id=1, source_target_pairs={{0,8},{1,9},{2,10},{3,11},{4,12},{5,13},{6,14},{7,15},{8,0},{9,1},... | collective-permute-start | bytes 417800 | tf_op jit(solution)/shard_map/ppermute | solution.py:45
  6.2 7.0 %collective-permute-start.1 = (bf16[17,32,128]{2,1,0:T(8,128)(2,1)S(1)}, bf16[17,32,128]{2,1,0:T(8,128)(2,1)S(1)}, u32[]{:S(2)}, u32[]{:S(2)}) collective-permute-start(bf16[17,32,128]{2,1,0:T(8,128)(2,1)S(1)} %pack_rows.1.refs_0_), channel_id=1, source_target_pairs={{0,4},{1,5},{2,6},{3,7},{4,0},{5,1},{6,2},{7,3},{8,12},{9,13},{10,... | collective-permute-start | bytes 417800 | tf_op jit(solution)/shard_map/ppermute | solution.py:45
  7.8 5.4 %collective-permute-start.2 = (bf16[17,32,128]{2,1,0:T(8,128)(2,1)S(1)}, bf16[17,32,128]{2,1,0:T(8,128)(2,1)S(1)}, u32[]{:S(2)}, u32[]{:S(2)}) collective-permute-start(bf16[17,32,128]{2,1,0:T(8,128)(2,1)S(1)} %pack_rows.1.refs_0_), channel_id=1, source_target_pairs={{0,2},{1,3},{2,0},{3,1},{4,6},{5,7},{6,4},{7,5},{8,10},{9,11},{10,... | collective-permute-start | bytes 417800 | tf_op jit(solution)/shard_map/ppermute | solution.py:45
  9.3 7.4 %collective-permute-start.6 = (bf16[17,32,128]{2,1,0:T(8,128)(2,1)S(1)}, bf16[17,32,128]{2,1,0:T(8,128)(2,1)S(1)}, u32[]{:S(2)}, u32[]{:S(2)}) collective-permute-start(bf16[17,32,128]{2,1,0:T(8,128)(2,1)S(1)} %pack_rows.1.refs_0_), channel_id=1, source_target_pairs={{0,1},{1,0},{2,3},{3,2},{4,5},{5,4},{6,7},{7,6},{8,9},{9,8},{10,11... | collective-permute-start | bytes 417800 | tf_op jit(solution)/shard_map/ppermute | solution.py:45
  13.2 5.8 %collective-permute-start.9 = (bf16[17,32,128]{2,1,0:T(8,128)(2,1)S(1)}, bf16[17,32,128]{2,1,0:T(8,128)(2,1)S(1)}, u32[]{:S(2)}, u32[]{:S(2)}) collective-permute-start(bf16[17,32,128]{2,1,0:T(8,128)(2,1)S(1)} %collective-permute-done.1.refs_4_), channel_id=1, source_target_pairs={{0,2},{1,3},{2,0},{3,1},{4,6},{5,7},{6,4},{7,5},{8,10},{9,11},{10,... | collective-permute-start | bytes 417800 | tf_op jit(solution)/shard_map/ppermute | solution.py:45
  14.7 5.1 %collective-permute-start.3 = (bf16[17,32,128]{2,1,0:T(8,128)(2,1)S(1)}, bf16[17,32,128]{2,1,0:T(8,128)(2,1)S(1)}, u32[]{:S(2)}, u32[]{:S(2)}) collective-permute-start(bf16[17,32,128]{2,1,0:T(8,128)(2,1)S(1)} %collective-permute-done.refs_0_), channel_id=1, source_target_pairs={{0,4},{1,5},{2,6},{3,7},{4,0},{5,1},{6,2},{7,3},{8,12},{9,13},{10,... | collective-permute-start | bytes 417800 | tf_op jit(solution)/shard_map/ppermute | solution.py:45
  16.1 5.9 %collective-permute-start.8 = (bf16[17,32,128]{2,1,0:T(8,128)(2,1)S(1)}, bf16[17,32,128]{2,1,0:T(8,128)(2,1)S(1)}, u32[]{:S(2)}, u32[]{:S(2)}) collective-permute-start(bf16[17,32,128]{2,1,0:T(8,128)(2,1)S(1)} %collective-permute-done.1.refs_4_), channel_id=1, source_target_pairs={{0,1},{1,0},{2,3},{3,2},{4,5},{5,4},{6,7},{7,6},{8,9},{9,8},{10,11... | collective-permute-start | bytes 417800 | tf_op jit(solution)/shard_map/ppermute | solution.py:45
  16.1 6.1 %collective-permute-start.13 = (bf16[17,32,128]{2,1,0:T(8,128)(2,1)S(1)}, bf16[17,32,128]{2,1,0:T(8,128)(2,1)S(1)}, u32[]{:S(2)}, u32[]{:S(2)}) collective-permute-start(bf16[17,32,128]{2,1,0:T(8,128)(2,1)S(1)} %collective-permute-done.refs_0_), channel_id=1, source_target_pairs={{0,2},{1,3},{2,0},{3,1},{4,6},{5,7},{6,4},{7,5},{8,10},{9,11},{10,... | collective-permute-start | bytes 417800 | tf_op jit(solution)/shard_map/ppermute | solution.py:45
  16.7 6.0 %collective-permute-start.7 = (bf16[17,32,128]{2,1,0:T(8,128)(2,1)S(1)}, bf16[17,32,128]{2,1,0:T(8,128)(2,1)S(1)}, u32[]{:S(2)}, u32[]{:S(2)}) collective-permute-start(bf16[17,32,128]{2,1,0:T(8,128)(2,1)S(1)} %collective-permute-done.2.refs_2_), channel_id=1, source_target_pairs={{0,1},{1,0},{2,3},{3,2},{4,5},{5,4},{6,7},{7,6},{8,9},{9,8},{10,11... | collective-permute-start | bytes 417800 | tf_op jit(solution)/shard_map/ppermute | solution.py:45
  19.0 3.6 %collective-permute-start.10 = (bf16[17,32,128]{2,1,0:T(8,128)(2,1)S(1)}, bf16[17,32,128]{2,1,0:T(8,128)(2,1)S(1)}, u32[]{:S(2)}, u32[]{:S(2)}) collective-permute-start(bf16[17,32,128]{2,1,0:T(8,128)(2,1)S(1)} %collective-permute-done.9.refs_6_), channel_id=1, source_target_pairs={{0,1},{1,0},{2,3},{3,2},{4,5},{5,4},{6,7},{7,6},{8,9},{9,8},{10,11... | collective-permute-start | bytes 417800 | tf_op jit(solution)/shard_map/ppermute | solution.py:45
  19.8 5.4 %collective-permute-start.5 = (bf16[17,32,128]{2,1,0:T(8,128)(2,1)S(1)}, bf16[17,32,128]{2,1,0:T(8,128)(2,1)S(1)}, u32[]{:S(2)}, u32[]{:S(2)}) collective-permute-start(bf16[17,32,128]{2,1,0:T(8,128)(2,1)S(1)} %collective-permute-done.3.refs_0_), channel_id=1, source_target_pairs={{0,2},{1,3},{2,0},{3,1},{4,6},{5,7},{6,4},{7,5},{8,10},{9,11},{10,... | collective-permute-start | bytes 417800 | tf_op jit(solution)/shard_map/ppermute | solution.py:45
  22.0 4.8 %copy-start = (s32[4,64]{1,0:T(4,128)S(1)}, s32[4,64]{1,0:T(4,128)}, u32[]{:S(2)}) copy-start(s32[4,64]{1,0:T(4,128)} %refs_9_.1) | copy-start | bytes 3076
  22.0 4.8 %copy-start.1 = (s32[1,64]{1,0:T(1,128)S(1)}, s32[1,64]{1,0:T(1,128)}, u32[]{:S(2)}) copy-start(s32[1,64]{1,0:T(1,128)} %refs_8_.1) | copy-start | bytes 772
  22.0 3.7 %collective-permute-start.12 = (bf16[17,32,128]{2,1,0:T(8,128)(2,1)S(1)}, bf16[17,32,128]{2,1,0:T(8,128)(2,1)S(1)}, u32[]{:S(2)}, u32[]{:S(2)}) collective-permute-start(bf16[17,32,128]{2,1,0:T(8,128)(2,1)S(1)} %collective-permute-done.refs_0_), channel_id=1, source_target_pairs={{0,1},{1,0},{2,3},{3,2},{4,5},{5,4},{6,7},{7,6},{8,9},{9,8},{10,11... | collective-permute-start | bytes 417800 | tf_op jit(solution)/shard_map/ppermute | solution.py:45
  22.3 3.4 %collective-permute-start.14 = (bf16[17,32,128]{2,1,0:T(8,128)(2,1)S(1)}, bf16[17,32,128]{2,1,0:T(8,128)(2,1)S(1)}, u32[]{:S(2)}, u32[]{:S(2)}) collective-permute-start(bf16[17,32,128]{2,1,0:T(8,128)(2,1)S(1)} %collective-permute-done.13.refs_2_), channel_id=1, source_target_pairs={{0,1},{1,0},{2,3},{3,2},{4,5},{5,4},{6,7},{7,6},{8,9},{9,8},{10,11... | collective-permute-start | bytes 417800 | tf_op jit(solution)/shard_map/ppermute | solution.py:45
  25.2 1.4 %collective-permute-start.11 = (bf16[17,32,128]{2,1,0:T(8,128)(2,1)S(1)}, bf16[17,32,128]{2,1,0:T(8,128)(2,1)S(1)}, u32[]{:S(2)}, u32[]{:S(2)}) collective-permute-start(bf16[17,32,128]{2,1,0:T(8,128)(2,1)S(1)} %collective-permute-done.5.refs_2_), channel_id=1, source_target_pairs={{0,1},{1,0},{2,3},{3,2},{4,5},{5,4},{6,7},{7,6},{8,9},{9,8},{10,11... | collective-permute-start | bytes 417800 | tf_op jit(solution)/shard_map/ppermute | solution.py:45
  25.2 1.6 %collective-permute-start.4 = (bf16[17,32,128]{2,1,0:T(8,128)(2,1)S(1)}, bf16[17,32,128]{2,1,0:T(8,128)(2,1)S(1)}, u32[]{:S(2)}, u32[]{:S(2)}) collective-permute-start(bf16[17,32,128]{2,1,0:T(8,128)(2,1)S(1)} %collective-permute-done.3.refs_0_), channel_id=1, source_target_pairs={{0,1},{1,0},{2,3},{3,2},{4,5},{5,4},{6,7},{7,6},{8,9},{9,8},{10,11... | collective-permute-start | bytes 417800 | tf_op jit(solution)/shard_map/ppermute | solution.py:45
  30.5 9.6 %collective-permute-start.15 = (bf16[512,128]{1,0:T(8,128)(2,1)S(1)}, bf16[512,128]{1,0:T(8,128)(2,1)S(1)}, u32[]{:S(2)}, u32[]{:S(2)}) collective-permute-start(bf16[512,128]{1,0:T(8,128)(2,1)S(1)} %get-tuple-element.93.agg_ref.refs_0_), channel_id=1, source_target_pairs={{0,8},{1,9},{2,10},{3,11},{4,12},{5,13},{6,14},{7,15},{8,0},{9,1},... | collective-permute-start | bytes 393224 | tf_op jit(solution)/shard_map/ppermute | solution.py:45
  32.9 9.2 %collective-permute-start.17 = (bf16[512,128]{1,0:T(8,128)(2,1)S(1)}, bf16[512,128]{1,0:T(8,128)(2,1)S(1)}, u32[]{:S(2)}, u32[]{:S(2)}) collective-permute-start(bf16[512,128]{1,0:T(8,128)(2,1)S(1)} %get-tuple-element.93.agg_ref.refs_0_), channel_id=1, source_target_pairs={{0,2},{1,3},{2,0},{3,1},{4,6},{5,7},{6,4},{7,5},{8,10},{9,11},{10,... | collective-permute-start | bytes 393224 | tf_op jit(solution)/shard_map/ppermute | solution.py:45
  33.4 11.1 %collective-permute-start.18 = (bf16[512,128]{1,0:T(8,128)(2,1)S(1)}, bf16[512,128]{1,0:T(8,128)(2,1)S(1)}, u32[]{:S(2)}, u32[]{:S(2)}) collective-permute-start(bf16[512,128]{1,0:T(8,128)(2,1)S(1)} %get-tuple-element.93.agg_ref.refs_0_), channel_id=1, source_target_pairs={{0,4},{1,5},{2,6},{3,7},{4,0},{5,1},{6,2},{7,3},{8,12},{9,13},{10,... | collective-permute-start | bytes 393224 | tf_op jit(solution)/shard_map/ppermute | solution.py:45
  36.5 8.1 %collective-permute-start.19 = (bf16[512,128]{1,0:T(8,128)(2,1)S(1)}, bf16[512,128]{1,0:T(8,128)(2,1)S(1)}, u32[]{:S(2)}, u32[]{:S(2)}) collective-permute-start(bf16[512,128]{1,0:T(8,128)(2,1)S(1)} %get-tuple-element.93.agg_ref.refs_0_), channel_id=1, source_target_pairs={{0,6},{1,7},{2,4},{3,5},{4,2},{5,3},{6,0},{7,1},{8,14},{9,15},{10,... | collective-permute-start | bytes 393224 | tf_op jit(solution)/shard_map/ppermute | solution.py:45
  40.1 7.4 %collective-permute-start.16 = (bf16[512,128]{1,0:T(8,128)(2,1)S(1)}, bf16[512,128]{1,0:T(8,128)(2,1)S(1)}, u32[]{:S(2)}, u32[]{:S(2)}) collective-permute-start(bf16[512,128]{1,0:T(8,128)(2,1)S(1)} %collective-permute-done.15.refs_0_), channel_id=1, source_target_pairs={{0,2},{1,3},{2,0},{3,1},{4,6},{5,7},{6,4},{7,5},{8,10},{9,11},{10,... | collective-permute-start | bytes 393224 | tf_op jit(solution)/shard_map/ppermute | solution.py:45
  40.8 7.9 %collective-permute-start.20 = (bf16[512,128]{1,0:T(8,128)(2,1)S(1)}, bf16[512,128]{1,0:T(8,128)(2,1)S(1)}, u32[]{:S(2)}, u32[]{:S(2)}) collective-permute-start(bf16[512,128]{1,0:T(8,128)(2,1)S(1)} %collective-permute-done.15.refs_0_), channel_id=1, source_target_pairs={{0,4},{1,5},{2,6},{3,7},{4,0},{5,1},{6,2},{7,3},{8,12},{9,13},{10,... | collective-permute-start | bytes 393224 | tf_op jit(solution)/shard_map/ppermute | solution.py:45
  42.1 7.1 %collective-permute-start.21 = (bf16[512,128]{1,0:T(8,128)(2,1)S(1)}, bf16[512,128]{1,0:T(8,128)(2,1)S(1)}, u32[]{:S(2)}, u32[]{:S(2)}) collective-permute-start(bf16[512,128]{1,0:T(8,128)(2,1)S(1)} %collective-permute-done.15.refs_0_), channel_id=1, source_target_pairs={{0,6},{1,7},{2,4},{3,5},{4,2},{5,3},{6,0},{7,1},{8,14},{9,15},{10,... | collective-permute-start | bytes 393224 | tf_op jit(solution)/shard_map/ppermute | solution.py:45
  50.2 1.4 %collective-permute-start.22 = (f32[176,128]{1,0:T(8,128)S(1)}, f32[176,128]{1,0:T(8,128)S(1)}, u32[]{:S(2)}, u32[]{:S(2)}) collective-permute-start(f32[176,128]{1,0:T(8,128)S(1)} %get-tuple-element.141.refs_15_), channel_id=1, source_target_pairs={{0,1},{1,0},{2,3},{3,2},{4,5},{5,4},{6,7},{7,6},{8,9},{9,8},{10,11... | collective-permute-start | bytes 270344 | tf_op jit(solution)/shard_map/ppermute | solution.py:45
  54.3 1.8 %collective-permute-start.23 = (f32[432,256]{1,0:T(8,128)S(1)}, f32[432,256]{1,0:T(8,128)S(1)}, u32[]{:S(2)}, u32[]{:S(2)}) collective-permute-start(f32[432,256]{1,0:T(8,128)S(1)} %get-tuple-element.142.mine_ref), channel_id=1, source_target_pairs={{0,1},{1,0},{2,3},{3,2},{4,5},{5,4},{6,7},{7,6},{8,9},{9,8},{10,11... | collective-permute-start | bytes 1327112 | tf_op jit(solution)/shard_map/ppermute | solution.py:45

commit v7 on v6

--- a/solution.py
+++ b/solution.py
@@ -132,10 +132,10 @@
 
 
 def weights_kernel(*refs):
-    sources, (in_t_ref, out_t_ref, out_ref, bias_ref), targets = refs[0:4], refs[4:8], refs[8:12]
-    wide, line, sems = refs[12:15]
+    sources, w_out_ref, (in_t_ref, out_t_ref, out_ref, bias_ref), targets = refs[0:3], refs[3], refs[4:8], refs[8:11]
+    wide, line, sems = refs[11:14]
     _fetch(sources, targets, sems)
-    self_ref, neigh_ref, w_out_ref, b_ref = targets
+    self_ref, neigh_ref, b_ref = targets
     classes = w_out_ref.shape[0]
     in_t_ref[...] = jnp.transpose(jnp.concatenate([self_ref[...], neigh_ref[...]], axis=0).astype(F32)).astype(BF16)
     wide[...] = jnp.zeros_like(wide)
@@ -151,10 +151,10 @@
     width, units = w_self.shape
     classes = w_out.shape[1]
     padded = -(-classes // SUB) * SUB
-    inputs = [_stay(x) for x in (w_self, w_neigh, w_out.T, b_out.reshape(1, classes))]
+    inputs = [_stay(x) for x in (w_self, w_neigh, b_out.reshape(1, classes))]
     return pl.pallas_call(
         weights_kernel,
-        in_specs=[pl.BlockSpec(memory_space=pltpu.HBM)] * 4,
+        in_specs=[pl.BlockSpec(memory_space=pltpu.HBM)] * 3 + [pl.BlockSpec(memory_space=pltpu.VMEM)],
         out_specs=[pl.BlockSpec(memory_space=pltpu.VMEM)] * 4,
         out_shape=[
             jax.ShapeDtypeStruct((units, 2 * width), BF16),
@@ -166,12 +166,12 @@
             *[pltpu.VMEM(x.shape, x.dtype) for x in inputs],
             pltpu.VMEM((padded, units), F32),
             pltpu.VMEM((1, 2 * LANES), F32),
-            pltpu.SemaphoreType.DMA((4,)),
+            pltpu.SemaphoreType.DMA((3,)),
         ],
         cost_estimate=pl.CostEstimate(flops=0, bytes_accessed=1 << 21, transcendentals=0),
         compiler_params=_params(8),
         name="weights",
-    )(*inputs)
+    )(*inputs, w_out.T)
 
 
 def _turn(adj, turned_ref, arrived=None):

time: 57.2 us -> 57.2 us (level)
  no operation moved by 1% of the time
where the time goes in v7:
time: 57.2 us; the launch traced here: 57 us
  starting transfers between devices  22.5 us (39%)
  Pallas kernels  22.2 us (39%)
  waiting for transfers between devices  11.5 us (20%)
  between operations  0.82 us (1%)
    ppermute x24, starting transfers between devices, swap(): return lax.ppermute(x, 'nodes', [(i, i ^ m) for i in range(DEVICES)])  22.5 us
    ppermute x24, waiting for transfers between devices, swap(): return lax.ppermute(x, 'nodes', [(i, i ^ m) for i in range(DEVICES)])  11.5 us
    pallas_call x5, Pallas kernels, _call(): pl.pallas_call(kernel, in_specs=[vmem] * len(operands), out_specs=[vmem]...  4.4 us
    pallas_call x1, Pallas kernels, aggregate(): pl.pallas_call(lambda *refs: aggregate_kernel(ms, len(turned), *refs), in...  3.75 us
    pallas_call x1, Pallas kernels, turn(): pl.pallas_call(turn_kernel, in_specs=[pl.BlockSpec(memory_space=pltpu.HBM...  3.52 us
    pallas_call x1, Pallas kernels, backward(): pl.pallas_call(lambda *refs: backward_kernel(classes, *refs), in_specs=[v...  2.81 us
    pallas_call x2, Pallas kernels, place(): pl.pallas_call(lambda *refs: _place(ms, refs[:len(ms)], refs[len(ms):n],...  2.09 us
    pallas_call x1, Pallas kernels, pack(): pl.pallas_call(lambda *refs: pack_kernel(devices, *refs), in_specs=[pl.Bl...  1.45 us
  transfers between devices with their start and end apart: 24, of which 12 were waited for; matrix products, arithmetic and copies ran while one was open for 0% of the time, Pallas kernels for 22%

profile of v7, /device:TPU:0, one launch (start us, length us, event | category | flops | bytes accessed | tf_op | source)
XLA Modules:
  0.0 57.0 jit_solution(831944811278018846)
XLA Ops:
  0.6 1.5 %pack_rows.1.refs_0_ = bf16[17,32,128]{2,1,0:T(8,128)(2,1)S(1)} custom-call(bf16[512,128]{1,0:T(8,128)(2,1)} %refs_0_.2, s32[1,512]{1,0:T(1,128)} %bitcast.10, s32[1,512]{1,0:T(1,128)} %bitcast.11, s32[4,128]{1,0:T(4,128)} %bitcast.12), custom_call_target="tpu_custom_call" | custom-call | tf_op jit(solution)/shard_map/pack_rows/pallas_call | solution.py:123
  2.1 4.1 %collective-permute-start = (bf16[17,32,128]{2,1,0:T(8,128)(2,1)S(1)}, bf16[17,32,128]{2,1,0:T(8,128)(2,1)S(1)}, u32[]{:S(2)}, u32[]{:S(2)}) collective-permute-start(bf16[17,32,128]{2,1,0:T(8,128)(2,1)S(1)} %pack_rows.1.refs_0_), channel_id=1, source_target_pairs={{0,8},{1,9},{2,10},{3,11},{4,12},{5,13},{6,14},{7,15},{8,0},{9,1},... | collective-permute-start | bytes 417800 | tf_op jit(solution)/shard_map/ppermute | solution.py:45
  6.2 1.6 %collective-permute-start.1 = (bf16[17,32,128]{2,1,0:T(8,128)(2,1)S(1)}, bf16[17,32,128]{2,1,0:T(8,128)(2,1)S(1)}, u32[]{:S(2)}, u32[]{:S(2)}) collective-permute-start(bf16[17,32,128]{2,1,0:T(8,128)(2,1)S(1)} %pack_rows.1.refs_0_), channel_id=1, source_target_pairs={{0,4},{1,5},{2,6},{3,7},{4,0},{5,1},{6,2},{7,3},{8,12},{9,13},{10,... | collective-permute-start | bytes 417800 | tf_op jit(solution)/shard_map/ppermute | solution.py:45
  7.8 1.5 %collective-permute-start.2 = (bf16[17,32,128]{2,1,0:T(8,128)(2,1)S(1)}, bf16[17,32,128]{2,1,0:T(8,128)(2,1)S(1)}, u32[]{:S(2)}, u32[]{:S(2)}) collective-permute-start(bf16[17,32,128]{2,1,0:T(8,128)(2,1)S(1)} %pack_rows.1.refs_0_), channel_id=1, source_target_pairs={{0,2},{1,3},{2,0},{3,1},{4,6},{5,7},{6,4},{7,5},{8,10},{9,11},{10,... | collective-permute-start | bytes 417800 | tf_op jit(solution)/shard_map/ppermute | solution.py:45
  9.3 3.5 %turn_adjacency.1 = (bf16[2,64,128,128]{3,2,1,0:T(8,128)(2,1)S(1)}, bf16[256,64,128]{2,1,0:T(8,128)(2,1)S(1)}) custom-call(bf16[512,64,128]{2,1,0:T(8,128)(2,1)} %adj_ref.1), custom_call_target="tpu_custom_call" | custom-call | flops 1073741824 | bytes 8388608 | tf_op jit(solution)/shard_map/turn_adjacency/pallas_call | solution.py:229
  12.8 0.1 collective-permute-done.refs_0_
  13.0 0.2 collective-permute-done.1.refs_4_
  13.2 1.6 %collective-permute-start.9 = (bf16[17,32,128]{2,1,0:T(8,128)(2,1)S(1)}, bf16[17,32,128]{2,1,0:T(8,128)(2,1)S(1)}, u32[]{:S(2)}, u32[]{:S(2)}) collective-permute-start(bf16[17,32,128]{2,1,0:T(8,128)(2,1)S(1)} %collective-permute-done.1.refs_4_), channel_id=1, source_target_pairs={{0,2},{1,3},{2,0},{3,1},{4,6},{5,7},{6,4},{7,5},{8,10},{9,11},{10,... | collective-permute-start | bytes 417800 | tf_op jit(solution)/shard_map/ppermute | solution.py:45
  14.7 1.4 %collective-permute-start.3 = (bf16[17,32,128]{2,1,0:T(8,128)(2,1)S(1)}, bf16[17,32,128]{2,1,0:T(8,128)(2,1)S(1)}, u32[]{:S(2)}, u32[]{:S(2)}) collective-permute-start(bf16[17,32,128]{2,1,0:T(8,128)(2,1)S(1)} %collective-permute-done.refs_0_), channel_id=1, source_target_pairs={{0,4},{1,5},{2,6},{3,7},{4,0},{5,1},{6,2},{7,3},{8,12},{9,13},{10,... | collective-permute-start | bytes 417800 | tf_op jit(solution)/shard_map/ppermute | solution.py:45
  16.1 0.5 collective-permute-start.13
  16.7 0.2 collective-permute-start.7
  16.9 2.1 %collective-permute-done.9.refs_6_ = bf16[17,32,128]{2,1,0:T(8,128)(2,1)S(1)} collective-permute-done((bf16[17,32,128]{2,1,0:T(8,128)(2,1)S(1)}, bf16[17,32,128]{2,1,0:T(8,128)(2,1)S(1)}, u32[]{:S(2)}, u32[]{:S(2)}) %collective-permute-start.9) | collective-permute-done | bytes 139296 | tf_op jit(solution)/shard_map/ppermute | solution.py:45
  19.0 0.8 %collective-permute-done.3.refs_0_ = bf16[17,32,128]{2,1,0:T(8,128)(2,1)S(1)} collective-permute-done((bf16[17,32,128]{2,1,0:T(8,128)(2,1)S(1)}, bf16[17,32,128]{2,1,0:T(8,128)(2,1)S(1)}, u32[]{:S(2)}, u32[]{:S(2)}) %collective-permute-start.3) | collective-permute-done | bytes 139296 | tf_op jit(solution)/shard_map/ppermute | solution.py:45
  19.8 1.0 %collective-permute-start.5 = (bf16[17,32,128]{2,1,0:T(8,128)(2,1)S(1)}, bf16[17,32,128]{2,1,0:T(8,128)(2,1)S(1)}, u32[]{:S(2)}, u32[]{:S(2)}) collective-permute-start(bf16[17,32,128]{2,1,0:T(8,128)(2,1)S(1)} %collective-permute-done.3.refs_0_), channel_id=1, source_target_pairs={{0,2},{1,3},{2,0},{3,1},{4,6},{5,7},{6,4},{7,5},{8,10},{9,11},{10,... | collective-permute-start | bytes 417800 | tf_op jit(solution)/shard_map/ppermute | solution.py:45
  20.7 1.3 %turn_rest.1.refs_7_ = bf16[2,64,128,128]{3,2,1,0:T(8,128)(2,1)S(1)} custom-call(bf16[2,128,64,128]{3,2,1,0:T(8,128)(2,1)S(1)} %bitcast.8), custom_call_target="tpu_custom_call" | custom-call | flops 1073741824 | bytes 4194304 | tf_op jit(solution)/shard_map/turn_rest/pallas_call | solution.py:252
  22.0 0.0 copy-start.1
  22.0 0.0 copy-start.2
  22.0 0.1 collective-permute-start.12
  22.1 0.2 collective-permute-done.13.refs_2_
  22.3 0.3 collective-permute-start.14
  22.6 1.3 %place.2 = (bf16[8192,128]{1,0:T(8,128)(2,1)S(1)}, bf16[16,16,128]{2,1,0:T(8,128)(2,1)S(1)}) custom-call(bf16[17,32,128]{2,1,0:T(8,128)(2,1)S(1)} %pack_rows.1.refs_0_, bf16[17,32,128]{2,1,0:T(8,128)(2,1)S(1)} %collective-permute-done.6.refs_1_, bf16[17,32,128]{2,1,0:T(8,128)(2,1)S(1)} %collective-permute-done.2.refs_2_, ...), custom_call_target="tpu_custom_call" | custom-call | flops 1073741824 | bytes 4194304 | tf_op jit(solution)/shard_map/place/pallas_call | solution.py:299
  24.0 1.2 %collective-permute-done.5.refs_2_ = bf16[17,32,128]{2,1,0:T(8,128)(2,1)S(1)} collective-permute-done((bf16[17,32,128]{2,1,0:T(8,128)(2,1)S(1)}, bf16[17,32,128]{2,1,0:T(8,128)(2,1)S(1)}, u32[]{:S(2)}, u32[]{:S(2)}) %collective-permute-start.5) | collective-permute-done | bytes 139296 | tf_op jit(solution)/shard_map/ppermute | solution.py:45
  25.2 0.5 collective-permute-start.4
  25.7 0.7 %place.3 = (bf16[8192,128]{1,0:T(8,128)(2,1)S(1)}, bf16[16,16,128]{2,1,0:T(8,128)(2,1)S(1)}) custom-call(bf16[17,32,128]{2,1,0:T(8,128)(2,1)S(1)} %collective-permute-done.refs_0_, bf16[17,32,128]{2,1,0:T(8,128)(2,1)S(1)} %collective-permute-done.12.refs_1_, bf16[17,32,128]{2,1,0:T(8,128)(2,1)S(1)} %collective-permute-done.13.refs_2_, ...), custom_call_target="tpu_custom_call" | custom-call | flops 1073741824 | bytes 4194304 | tf_op jit(solution)/shard_map/place/pallas_call | solution.py:299
  26.5 0.1 collective-permute-done.11.refs_3_
  26.6 0.2 collective-permute-done.4.refs_1_
  26.8 3.8 %aggregate.1 = (bf16[8192,128]{1,0:T(8,128)(2,1)S(1)}, bf16[16,16,128]{2,1,0:T(8,128)(2,1)S(1)}, bf16[512,128]{1,0:T(8,128)(2,1)S(1)}) custom-call(bf16[17,32,128]{2,1,0:T(8,128)(2,1)S(1)} %collective-permute-done.3.refs_0_, bf16[17,32,128]{2,1,0:T(8,128)(2,1)S(1)} %collective-permute-done.4.refs_1_, ...), custom_call_target="tpu_custom_call" | custom-call | tf_op jit(solution)/shard_map/aggregate/pallas_call | solution.py:333
  30.5 2.4 %collective-permute-start.15 = (bf16[512,128]{1,0:T(8,128)(2,1)S(1)}, bf16[512,128]{1,0:T(8,128)(2,1)S(1)}, u32[]{:S(2)}, u32[]{:S(2)}) collective-permute-start(bf16[512,128]{1,0:T(8,128)(2,1)S(1)} %get-tuple-element.93.agg_ref.refs_0_), channel_id=1, source_target_pairs={{0,8},{1,9},{2,10},{3,11},{4,12},{5,13},{6,14},{7,15},{8,0},{9,1},... | collective-permute-start | bytes 393224 | tf_op jit(solution)/shard_map/ppermute | solution.py:45
  32.9 0.5 collective-permute-start.17
  33.4 3.0 %collective-permute-start.18 = (bf16[512,128]{1,0:T(8,128)(2,1)S(1)}, bf16[512,128]{1,0:T(8,128)(2,1)S(1)}, u32[]{:S(2)}, u32[]{:S(2)}) collective-permute-start(bf16[512,128]{1,0:T(8,128)(2,1)S(1)} %get-tuple-element.93.agg_ref.refs_0_), channel_id=1, source_target_pairs={{0,4},{1,5},{2,6},{3,7},{4,0},{5,1},{6,2},{7,3},{8,12},{9,13},{10,... | collective-permute-start | bytes 393224 | tf_op jit(solution)/shard_map/ppermute | solution.py:45
  36.5 1.1 %weights.1 = (bf16[256,256]{1,0:T(8,128)(2,1)S(1)}, bf16[176,256]{1,0:T(8,128)(2,1)S(1)}, bf16[256,176]{1,0:T(8,128)(2,1)S(1)}, f32[176,128]{1,0:T(8,128)S(1)}) custom-call(bf16[128,256]{1,0:T(8,128)(2,1)} %refs_0_.3, bf16[128,256]{1,0:T(8,128)(2,1)} %refs_1_.1, f32[1,172]{1,0:T(1,128)} %bitcast.13, bf16[172,256]{1,0:T(8,128)(2,1)S(1)} %bitcast.9), custom_call_target="tpu_custom_call" | custom-call | bytes 2097152 | tf_op jit(solution)/shard_map/weights/pallas_call | solution.py:155
  37.6 1.0 %own.1 = bf16[512,256]{1,0:T(8,128)(2,1)} custom-call(bf16[8192,128]{1,0:T(8,128)(2,1)S(1)} %get-tuple-element.98.px_ref.refs_2_.refs_1_.refs_12_, bf16[512,128]{1,0:T(8,128)(2,1)S(1)} %get-tuple-element.93.agg_ref.refs_0_, bf16[256,256]{1,0:T(8,128)(2,1)S(1)} %get-tuple-element.94.in_t_ref.refs_4_.refs_3_), custom_call_target="tpu_custom_call" | custom-call | flops 67108864 | bytes 262144 | tf_op jit(solution)/shard_map/own/pallas_call | solution.py:443
  38.5 1.6 %collective-permute-done.15.refs_0_ = bf16[512,128]{1,0:T(8,128)(2,1)S(1)} collective-permute-done((bf16[512,128]{1,0:T(8,128)(2,1)S(1)}, bf16[512,128]{1,0:T(8,128)(2,1)S(1)}, u32[]{:S(2)}, u32[]{:S(2)}) %collective-permute-start.15) | collective-permute-done | bytes 131104 | tf_op jit(solution)/shard_map/ppermute | solution.py:45
  40.1 0.7 %collective-permute-start.16 = (bf16[512,128]{1,0:T(8,128)(2,1)S(1)}, bf16[512,128]{1,0:T(8,128)(2,1)S(1)}, u32[]{:S(2)}, u32[]{:S(2)}) collective-permute-start(bf16[512,128]{1,0:T(8,128)(2,1)S(1)} %collective-permute-done.15.refs_0_), channel_id=1, source_target_pairs={{0,2},{1,3},{2,0},{3,1},{4,6},{5,7},{6,4},{7,5},{8,10},{9,11},{10,... | collective-permute-start | bytes 393224 | tf_op jit(solution)/shard_map/ppermute | solution.py:45
  40.8 1.3 %collective-permute-start.20 = (bf16[512,128]{1,0:T(8,128)(2,1)S(1)}, bf16[512,128]{1,0:T(8,128)(2,1)S(1)}, u32[]{:S(2)}, u32[]{:S(2)}) collective-permute-start(bf16[512,128]{1,0:T(8,128)(2,1)S(1)} %collective-permute-done.15.refs_0_), channel_id=1, source_target_pairs={{0,4},{1,5},{2,6},{3,7},{4,0},{5,1},{6,2},{7,3},{8,12},{9,13},{10,... | collective-permute-start | bytes 393224 | tf_op jit(solution)/shard_map/ppermute | solution.py:45
  42.0 1.6 %collective-permute-start.21 = (bf16[512,128]{1,0:T(8,128)(2,1)S(1)}, bf16[512,128]{1,0:T(8,128)(2,1)S(1)}, u32[]{:S(2)}, u32[]{:S(2)}) collective-permute-start(bf16[512,128]{1,0:T(8,128)(2,1)S(1)} %collective-permute-done.15.refs_0_), channel_id=1, source_target_pairs={{0,6},{1,7},{2,4},{3,5},{4,2},{5,3},{6,0},{7,1},{8,14},{9,15},{10,... | collective-permute-start | bytes 393224 | tf_op jit(solution)/shard_map/ppermute | solution.py:45
  43.6 0.9 %forward_pair.3 = (bf16[1024,128]{1,0:T(8,128)(2,1)S(1)}, bf16[256,1024]{1,0:T(8,128)(2,1)S(1)}, f32[176,1024]{1,0:T(8,128)S(1)}, f32[176,128]{1,0:T(8,128)S(1)}, f32[176,128]{1,0:T(8,128)S(1)}) custom-call(bf16[512,128]{1,0:T(8,128)(2,1)S(1)} %get-tuple-element.93.agg_ref.refs_0_, bf16[512,128]{1,0:T(8,128)(2,1)S(1)} %collective-permute-done.17.refs_1_, ...), custom_call_target="tpu_custom_call" | custom-call | flops 536870912 | bytes 2097152 | tf_op jit(solution)/shard_map/forward_pair/pallas_call | solution.py:456
  44.6 0.9 %forward_pair.4 = (bf16[1024,128]{1,0:T(8,128)(2,1)S(1)}, bf16[256,1024]{1,0:T(8,128)(2,1)S(1)}, f32[176,1024]{1,0:T(8,128)S(1)}, f32[176,128]{1,0:T(8,128)S(1)}, f32[176,128]{1,0:T(8,128)S(1)}) custom-call(bf16[512,128]{1,0:T(8,128)(2,1)S(1)} %collective-permute-done.18.refs_0_, bf16[512,128]{1,0:T(8,128)(2,1)S(1)} %collective-permute-done.19.refs_1_, ...), custom_call_target="tpu_custom_call" | custom-call | flops 536870912 | bytes 2097152 | tf_op jit(solution)/shard_map/forward_pair/pallas_call | solution.py:456
  45.5 2.1 %collective-permute-done.16.refs_1_ = bf16[512,128]{1,0:T(8,128)(2,1)S(1)} collective-permute-done((bf16[512,128]{1,0:T(8,128)(2,1)S(1)}, bf16[512,128]{1,0:T(8,128)(2,1)S(1)}, u32[]{:S(2)}, u32[]{:S(2)}) %collective-permute-start.16) | collective-permute-done | bytes 131104 | tf_op jit(solution)/shard_map/ppermute | solution.py:45
  47.5 1.1 %forward_pair.5 = (bf16[1024,128]{1,0:T(8,128)(2,1)S(1)}, bf16[256,1024]{1,0:T(8,128)(2,1)S(1)}, f32[176,1024]{1,0:T(8,128)S(1)}, f32[176,128]{1,0:T(8,128)S(1)}, f32[176,128]{1,0:T(8,128)S(1)}) custom-call(bf16[512,128]{1,0:T(8,128)(2,1)S(1)} %collective-permute-done.15.refs_0_, bf16[512,128]{1,0:T(8,128)(2,1)S(1)} %collective-permute-done.16.refs_1_, ...), custom_call_target="tpu_custom_call" | custom-call | flops 536870912 | bytes 2097152 | tf_op jit(solution)/shard_map/forward_pair/pallas_call | solution.py:456
  48.6 0.6 %forward_one.1 = (bf16[256,512]{1,0:T(8,128)(2,1)S(1)}, f32[176,512]{1,0:T(8,128)S(1)}, f32[176,128]{1,0:T(8,128)S(1)}, f32[176,128]{1,0:T(8,128)S(1)}) custom-call(bf16[512,128]{1,0:T(8,128)(2,1)S(1)} %collective-permute-done.20.refs_0_, bf16[8192,128]{1,0:T(8,128)(2,1)S(1)} %get-tuple-element.98.px_ref.refs_2_.refs_1_.refs_12_, ...), custom_call_target="tpu_custom_call" | custom-call | flops 536870912 | bytes 2097152 | tf_op jit(solution)/shard_map/forward_one/pallas_call | solution.py:456
  49.3 0.9 %forward_last.1 = (bf16[1024,128]{1,0:T(8,128)(2,1)S(1)}, bf16[256,1024]{1,0:T(8,128)(2,1)S(1)}, f32[176,1024]{1,0:T(8,128)S(1)}, f32[176,128]{1,0:T(8,128)S(1)}) custom-call(bf16[512,128]{1,0:T(8,128)(2,1)S(1)} %collective-permute-done.20.refs_0_, bf16[512,128]{1,0:T(8,128)(2,1)S(1)} %collective-permute-done.21.refs_1_, ...), custom_call_target="tpu_custom_call" | custom-call | flops 536870912 | bytes 2097152 | tf_op jit(solution)/shard_map/forward_last/pallas_call | solution.py:456
  50.2 0.1 collective-permute-start.22
  50.2 1.3 %collective-permute-done.22.refs_16_ = f32[176,128]{1,0:T(8,128)S(1)} collective-permute-done((f32[176,128]{1,0:T(8,128)S(1)}, f32[176,128]{1,0:T(8,128)S(1)}, u32[]{:S(2)}, u32[]{:S(2)}) %collective-permute-start.22) | collective-permute-done | bytes 90144 | tf_op jit(solution)/shard_map/ppermute | solution.py:45
  51.5 2.8 %backward.1 = (f32[432,256]{1,0:T(8,128)S(1)}, f32[1,172]{1,0:T(1,128)}) custom-call(bf16[1024,128]{1,0:T(8,128)(2,1)S(1)} %get-tuple-element.112.refs_0_, bf16[256,1024]{1,0:T(8,128)(2,1)S(1)} %get-tuple-element.113.refs_1_, f32[176,1024]{1,0:T(8,128)S(1)} %get-tuple-element.114.refs_2_, bf16[1024,128]{1,0:T(8,128)(2,1)S(1)} %get-tuple-element.115.refs_3_, ...), custom_call_target="tpu_custom_call" | custom-call | tf_op jit(solution)/shard_map/backward/pallas_call | solution.py:531
  54.3 0.2 collective-permute-start.23
  54.5 1.6 %collective-permute-done.23.other_ref = f32[432,256]{1,0:T(8,128)S(1)} collective-permute-done((f32[432,256]{1,0:T(8,128)S(1)}, f32[432,256]{1,0:T(8,128)S(1)}, u32[]{:S(2)}, u32[]{:S(2)}) %collective-permute-start.23) | collective-permute-done | bytes 442400 | tf_op jit(solution)/shard_map/ppermute | solution.py:45
  56.1 0.9 %total.1 = (f32[128,256]{1,0:T(8,128)}, f32[128,256]{1,0:T(8,128)}, f32[172,256]{1,0:T(8,128)}) custom-call(f32[432,256]{1,0:T(8,128)S(1)} %get-tuple-element.142.mine_ref, f32[432,256]{1,0:T(8,128)S(1)} %collective-permute-done.23.other_ref), custom_call_target="tpu_custom_call" | custom-call | tf_op jit(solution)/shard_map/total/pallas_call | solution.py:556
  (21 shorter events, 0.1 us)
Async XLA Ops:
  2.1 10.9 %collective-permute-start = (bf16[17,32,128]{2,1,0:T(8,128)(2,1)S(1)}, bf16[17,32,128]{2,1,0:T(8,128)(2,1)S(1)}, u32[]{:S(2)}, u32[]{:S(2)}) collective-permute-start(bf16[17,32,128]{2,1,0:T(8,128)(2,1)S(1)} %pack_rows.1.refs_0_), channel_id=1, source_target_pairs={{0,8},{1,9},{2,10},{3,11},{4,12},{5,13},{6,14},{7,15},{8,0},{9,1},... | collective-permute-start | bytes 417800 | tf_op jit(solution)/shard_map/ppermute | solution.py:45
  6.2 7.0 %collective-permute-start.1 = (bf16[17,32,128]{2,1,0:T(8,128)(2,1)S(1)}, bf16[17,32,128]{2,1,0:T(8,128)(2,1)S(1)}, u32[]{:S(2)}, u32[]{:S(2)}) collective-permute-start(bf16[17,32,128]{2,1,0:T(8,128)(2,1)S(1)} %pack_rows.1.refs_0_), channel_id=1, source_target_pairs={{0,4},{1,5},{2,6},{3,7},{4,0},{5,1},{6,2},{7,3},{8,12},{9,13},{10,... | collective-permute-start | bytes 417800 | tf_op jit(solution)/shard_map/ppermute | solution.py:45
  7.8 5.4 %collective-permute-start.2 = (bf16[17,32,128]{2,1,0:T(8,128)(2,1)S(1)}, bf16[17,32,128]{2,1,0:T(8,128)(2,1)S(1)}, u32[]{:S(2)}, u32[]{:S(2)}) collective-permute-start(bf16[17,32,128]{2,1,0:T(8,128)(2,1)S(1)} %pack_rows.1.refs_0_), channel_id=1, source_target_pairs={{0,2},{1,3},{2,0},{3,1},{4,6},{5,7},{6,4},{7,5},{8,10},{9,11},{10,... | collective-permute-start | bytes 417800 | tf_op jit(solution)/shard_map/ppermute | solution.py:45
  9.3 7.4 %collective-permute-start.6 = (bf16[17,32,128]{2,1,0:T(8,128)(2,1)S(1)}, bf16[17,32,128]{2,1,0:T(8,128)(2,1)S(1)}, u32[]{:S(2)}, u32[]{:S(2)}) collective-permute-start(bf16[17,32,128]{2,1,0:T(8,128)(2,1)S(1)} %pack_rows.1.refs_0_), channel_id=1, source_target_pairs={{0,1},{1,0},{2,3},{3,2},{4,5},{5,4},{6,7},{7,6},{8,9},{9,8},{10,11... | collective-permute-start | bytes 417800 | tf_op jit(solution)/shard_map/ppermute | solution.py:45
  13.2 5.8 %collective-permute-start.9 = (bf16[17,32,128]{2,1,0:T(8,128)(2,1)S(1)}, bf16[17,32,128]{2,1,0:T(8,128)(2,1)S(1)}, u32[]{:S(2)}, u32[]{:S(2)}) collective-permute-start(bf16[17,32,128]{2,1,0:T(8,128)(2,1)S(1)} %collective-permute-done.1.refs_4_), channel_id=1, source_target_pairs={{0,2},{1,3},{2,0},{3,1},{4,6},{5,7},{6,4},{7,5},{8,10},{9,11},{10,... | collective-permute-start | bytes 417800 | tf_op jit(solution)/shard_map/ppermute | solution.py:45
  14.7 5.1 %collective-permute-start.3 = (bf16[17,32,128]{2,1,0:T(8,128)(2,1)S(1)}, bf16[17,32,128]{2,1,0:T(8,128)(2,1)S(1)}, u32[]{:S(2)}, u32[]{:S(2)}) collective-permute-start(bf16[17,32,128]{2,1,0:T(8,128)(2,1)S(1)} %collective-permute-done.refs_0_), channel_id=1, source_target_pairs={{0,4},{1,5},{2,6},{3,7},{4,0},{5,1},{6,2},{7,3},{8,12},{9,13},{10,... | collective-permute-start | bytes 417800 | tf_op jit(solution)/shard_map/ppermute | solution.py:45
  16.1 5.9 %collective-permute-start.8 = (bf16[17,32,128]{2,1,0:T(8,128)(2,1)S(1)}, bf16[17,32,128]{2,1,0:T(8,128)(2,1)S(1)}, u32[]{:S(2)}, u32[]{:S(2)}) collective-permute-start(bf16[17,32,128]{2,1,0:T(8,128)(2,1)S(1)} %collective-permute-done.1.refs_4_), channel_id=1, source_target_pairs={{0,1},{1,0},{2,3},{3,2},{4,5},{5,4},{6,7},{7,6},{8,9},{9,8},{10,11... | collective-permute-start | bytes 417800 | tf_op jit(solution)/shard_map/ppermute | solution.py:45
  16.1 6.1 %collective-permute-start.13 = (bf16[17,32,128]{2,1,0:T(8,128)(2,1)S(1)}, bf16[17,32,128]{2,1,0:T(8,128)(2,1)S(1)}, u32[]{:S(2)}, u32[]{:S(2)}) collective-permute-start(bf16[17,32,128]{2,1,0:T(8,128)(2,1)S(1)} %collective-permute-done.refs_0_), channel_id=1, source_target_pairs={{0,2},{1,3},{2,0},{3,1},{4,6},{5,7},{6,4},{7,5},{8,10},{9,11},{10,... | collective-permute-start | bytes 417800 | tf_op jit(solution)/shard_map/ppermute | solution.py:45
  16.7 6.0 %collective-permute-start.7 = (bf16[17,32,128]{2,1,0:T(8,128)(2,1)S(1)}, bf16[17,32,128]{2,1,0:T(8,128)(2,1)S(1)}, u32[]{:S(2)}, u32[]{:S(2)}) collective-permute-start(bf16[17,32,128]{2,1,0:T(8,128)(2,1)S(1)} %collective-permute-done.2.refs_2_), channel_id=1, source_target_pairs={{0,1},{1,0},{2,3},{3,2},{4,5},{5,4},{6,7},{7,6},{8,9},{9,8},{10,11... | collective-permute-start | bytes 417800 | tf_op jit(solution)/shard_map/ppermute | solution.py:45
  19.0 3.6 %collective-permute-start.10 = (bf16[17,32,128]{2,1,0:T(8,128)(2,1)S(1)}, bf16[17,32,128]{2,1,0:T(8,128)(2,1)S(1)}, u32[]{:S(2)}, u32[]{:S(2)}) collective-permute-start(bf16[17,32,128]{2,1,0:T(8,128)(2,1)S(1)} %collective-permute-done.9.refs_6_), channel_id=1, source_target_pairs={{0,1},{1,0},{2,3},{3,2},{4,5},{5,4},{6,7},{7,6},{8,9},{9,8},{10,11... | collective-permute-start | bytes 417800 | tf_op jit(solution)/shard_map/ppermute | solution.py:45
  19.8 5.4 %collective-permute-start.5 = (bf16[17,32,128]{2,1,0:T(8,128)(2,1)S(1)}, bf16[17,32,128]{2,1,0:T(8,128)(2,1)S(1)}, u32[]{:S(2)}, u32[]{:S(2)}) collective-permute-start(bf16[17,32,128]{2,1,0:T(8,128)(2,1)S(1)} %collective-permute-done.3.refs_0_), channel_id=1, source_target_pairs={{0,2},{1,3},{2,0},{3,1},{4,6},{5,7},{6,4},{7,5},{8,10},{9,11},{10,... | collective-permute-start | bytes 417800 | tf_op jit(solution)/shard_map/ppermute | solution.py:45
  22.0 4.8 %copy-start.1 = (s32[4,64]{1,0:T(4,128)S(1)}, s32[4,64]{1,0:T(4,128)}, u32[]{:S(2)}) copy-start(s32[4,64]{1,0:T(4,128)} %refs_9_.1) | copy-start | bytes 3076
  22.0 4.8 %copy-start.2 = (s32[1,64]{1,0:T(1,128)S(1)}, s32[1,64]{1,0:T(1,128)}, u32[]{:S(2)}) copy-start(s32[1,64]{1,0:T(1,128)} %refs_8_.1) | copy-start | bytes 772
  22.0 3.7 %collective-permute-start.12 = (bf16[17,32,128]{2,1,0:T(8,128)(2,1)S(1)}, bf16[17,32,128]{2,1,0:T(8,128)(2,1)S(1)}, u32[]{:S(2)}, u32[]{:S(2)}) collective-permute-start(bf16[17,32,128]{2,1,0:T(8,128)(2,1)S(1)} %collective-permute-done.refs_0_), channel_id=1, source_target_pairs={{0,1},{1,0},{2,3},{3,2},{4,5},{5,4},{6,7},{7,6},{8,9},{9,8},{10,11... | collective-permute-start | bytes 417800 | tf_op jit(solution)/shard_map/ppermute | solution.py:45
  22.3 3.4 %collective-permute-start.14 = (bf16[17,32,128]{2,1,0:T(8,128)(2,1)S(1)}, bf16[17,32,128]{2,1,0:T(8,128)(2,1)S(1)}, u32[]{:S(2)}, u32[]{:S(2)}) collective-permute-start(bf16[17,32,128]{2,1,0:T(8,128)(2,1)S(1)} %collective-permute-done.13.refs_2_), channel_id=1, source_target_pairs={{0,1},{1,0},{2,3},{3,2},{4,5},{5,4},{6,7},{7,6},{8,9},{9,8},{10,11... | collective-permute-start | bytes 417800 | tf_op jit(solution)/shard_map/ppermute | solution.py:45
  25.2 1.4 %collective-permute-start.11 = (bf16[17,32,128]{2,1,0:T(8,128)(2,1)S(1)}, bf16[17,32,128]{2,1,0:T(8,128)(2,1)S(1)}, u32[]{:S(2)}, u32[]{:S(2)}) collective-permute-start(bf16[17,32,128]{2,1,0:T(8,128)(2,1)S(1)} %collective-permute-done.5.refs_2_), channel_id=1, source_target_pairs={{0,1},{1,0},{2,3},{3,2},{4,5},{5,4},{6,7},{7,6},{8,9},{9,8},{10,11... | collective-permute-start | bytes 417800 | tf_op jit(solution)/shard_map/ppermute | solution.py:45
  25.2 1.6 %collective-permute-start.4 = (bf16[17,32,128]{2,1,0:T(8,128)(2,1)S(1)}, bf16[17,32,128]{2,1,0:T(8,128)(2,1)S(1)}, u32[]{:S(2)}, u32[]{:S(2)}) collective-permute-start(bf16[17,32,128]{2,1,0:T(8,128)(2,1)S(1)} %collective-permute-done.3.refs_0_), channel_id=1, source_target_pairs={{0,1},{1,0},{2,3},{3,2},{4,5},{5,4},{6,7},{7,6},{8,9},{9,8},{10,11... | collective-permute-start | bytes 417800 | tf_op jit(solution)/shard_map/ppermute | solution.py:45
  26.6 9.9 %copy-start = (bf16[256,172]{0,1:T(8,128)(2,1)S(1)}, bf16[256,172]{0,1:T(8,128)(2,1)}, u32[]{:S(2)}) copy-start(bf16[256,172]{0,1:T(8,128)(2,1)} %param.20) | copy-start | bytes 264196
  30.5 9.6 %collective-permute-start.15 = (bf16[512,128]{1,0:T(8,128)(2,1)S(1)}, bf16[512,128]{1,0:T(8,128)(2,1)S(1)}, u32[]{:S(2)}, u32[]{:S(2)}) collective-permute-start(bf16[512,128]{1,0:T(8,128)(2,1)S(1)} %get-tuple-element.93.agg_ref.refs_0_), channel_id=1, source_target_pairs={{0,8},{1,9},{2,10},{3,11},{4,12},{5,13},{6,14},{7,15},{8,0},{9,1},... | collective-permute-start | bytes 393224 | tf_op jit(solution)/shard_map/ppermute | solution.py:45
  32.9 9.1 %collective-permute-start.17 = (bf16[512,128]{1,0:T(8,128)(2,1)S(1)}, bf16[512,128]{1,0:T(8,128)(2,1)S(1)}, u32[]{:S(2)}, u32[]{:S(2)}) collective-permute-start(bf16[512,128]{1,0:T(8,128)(2,1)S(1)} %get-tuple-element.93.agg_ref.refs_0_), channel_id=1, source_target_pairs={{0,2},{1,3},{2,0},{3,1},{4,6},{5,7},{6,4},{7,5},{8,10},{9,11},{10,... | collective-permute-start | bytes 393224 | tf_op jit(solution)/shard_map/ppermute | solution.py:45
  33.4 11.1 %collective-permute-start.18 = (bf16[512,128]{1,0:T(8,128)(2,1)S(1)}, bf16[512,128]{1,0:T(8,128)(2,1)S(1)}, u32[]{:S(2)}, u32[]{:S(2)}) collective-permute-start(bf16[512,128]{1,0:T(8,128)(2,1)S(1)} %get-tuple-element.93.agg_ref.refs_0_), channel_id=1, source_target_pairs={{0,4},{1,5},{2,6},{3,7},{4,0},{5,1},{6,2},{7,3},{8,12},{9,13},{10,... | collective-permute-start | bytes 393224 | tf_op jit(solution)/shard_map/ppermute | solution.py:45
  36.5 8.1 %collective-permute-start.19 = (bf16[512,128]{1,0:T(8,128)(2,1)S(1)}, bf16[512,128]{1,0:T(8,128)(2,1)S(1)}, u32[]{:S(2)}, u32[]{:S(2)}) collective-permute-start(bf16[512,128]{1,0:T(8,128)(2,1)S(1)} %get-tuple-element.93.agg_ref.refs_0_), channel_id=1, source_target_pairs={{0,6},{1,7},{2,4},{3,5},{4,2},{5,3},{6,0},{7,1},{8,14},{9,15},{10,... | collective-permute-start | bytes 393224 | tf_op jit(solution)/shard_map/ppermute | solution.py:45
  40.1 7.4 %collective-permute-start.16 = (bf16[512,128]{1,0:T(8,128)(2,1)S(1)}, bf16[512,128]{1,0:T(8,128)(2,1)S(1)}, u32[]{:S(2)}, u32[]{:S(2)}) collective-permute-start(bf16[512,128]{1,0:T(8,128)(2,1)S(1)} %collective-permute-done.15.refs_0_), channel_id=1, source_target_pairs={{0,2},{1,3},{2,0},{3,1},{4,6},{5,7},{6,4},{7,5},{8,10},{9,11},{10,... | collective-permute-start | bytes 393224 | tf_op jit(solution)/shard_map/ppermute | solution.py:45
  40.8 7.9 %collective-permute-start.20 = (bf16[512,128]{1,0:T(8,128)(2,1)S(1)}, bf16[512,128]{1,0:T(8,128)(2,1)S(1)}, u32[]{:S(2)}, u32[]{:S(2)}) collective-permute-start(bf16[512,128]{1,0:T(8,128)(2,1)S(1)} %collective-permute-done.15.refs_0_), channel_id=1, source_target_pairs={{0,4},{1,5},{2,6},{3,7},{4,0},{5,1},{6,2},{7,3},{8,12},{9,13},{10,... | collective-permute-start | bytes 393224 | tf_op jit(solution)/shard_map/ppermute | solution.py:45
  42.0 7.2 %collective-permute-start.21 = (bf16[512,128]{1,0:T(8,128)(2,1)S(1)}, bf16[512,128]{1,0:T(8,128)(2,1)S(1)}, u32[]{:S(2)}, u32[]{:S(2)}) collective-permute-start(bf16[512,128]{1,0:T(8,128)(2,1)S(1)} %collective-permute-done.15.refs_0_), channel_id=1, source_target_pairs={{0,6},{1,7},{2,4},{3,5},{4,2},{5,3},{6,0},{7,1},{8,14},{9,15},{10,... | collective-permute-start | bytes 393224 | tf_op jit(solution)/shard_map/ppermute | solution.py:45
  50.2 1.4 %collective-permute-start.22 = (f32[176,128]{1,0:T(8,128)S(1)}, f32[176,128]{1,0:T(8,128)S(1)}, u32[]{:S(2)}, u32[]{:S(2)}) collective-permute-start(f32[176,128]{1,0:T(8,128)S(1)} %get-tuple-element.141.refs_15_), channel_id=1, source_target_pairs={{0,1},{1,0},{2,3},{3,2},{4,5},{5,4},{6,7},{7,6},{8,9},{9,8},{10,11... | collective-permute-start | bytes 270344 | tf_op jit(solution)/shard_map/ppermute | solution.py:45
  54.3 1.8 %collective-permute-start.23 = (f32[432,256]{1,0:T(8,128)S(1)}, f32[432,256]{1,0:T(8,128)S(1)}, u32[]{:S(2)}, u32[]{:S(2)}) collective-permute-start(f32[432,256]{1,0:T(8,128)S(1)} %get-tuple-element.142.mine_ref), channel_id=1, source_target_pairs={{0,1},{1,0},{2,3},{3,2},{4,5},{5,4},{6,7},{7,6},{8,9},{9,8},{10,11... | collective-permute-start | bytes 1327112 | tf_op jit(solution)/shard_map/ppermute | solution.py:45

commit v8 on v7

--- a/solution.py
+++ b/solution.py
@@ -77,7 +77,7 @@
     have[8], one = lax.optimization_barrier((have[8], first(have)))
     have[12], have[10], have[14] = swap(have[8], 4), swap(have[8], 2), swap(have[8], 6)
     have[10], two = lax.optimization_barrier((have[10], second(have)))
-    have[12], three = lax.optimization_barrier((have[12], third(have)))
+    have[12], three = lax.optimization_barrier((have[12], third(have, two)))
     return have, one, two, three
 
 
@@ -407,9 +407,9 @@
     hid_ref[...], loss_ref[...], count_ref[...] = _forward([owner], inputs, *shared, keep)
 
 
-def last_kernel(m, *refs):
-    blocks, (px_ref, *shared), partner, prior = refs[0:2], refs[2:7], refs[7:11], refs[11:17]
-    agg_ref, hid_ref, slope_ref, stats_ref, part, losses, counts = refs[17:]
+def rest_kernel(m, *refs):
+    blocks, (px_ref, *shared), partner, outs = refs[0:2], refs[2:7], refs[7:11], refs[11:]
+    agg_ref, hid_ref, slope_ref, loss_ref, count_ref, part = outs
     me = lax.axis_index("nodes")
     rows = blocks[0].shape[0]
     at = [pl.ds(pl.multiple_of(((me // 2 % 2) ^ o) * rows, rows), rows) for o in range(2)]
@@ -423,10 +423,17 @@
     inputs = jnp.concatenate([_rows(me ^ m, px_ref, rows), blocks[1][...]], axis=1)
     hidden, loss, count = _forward([me ^ m], inputs, *shared, keep)
     hid_ref[:, at[1]], slope_ref[:, at[1]] = hidden, part[...]
-    mine = me // QUAD
+    loss_ref[...], count_ref[...] = loss + partner[2][...], count + partner[3][...]
+
+
+def last_kernel(m, *refs):
+    prior, refs = refs[11:17], refs[:11] + refs[17:]
+    stats_ref, part, loss_ref, count_ref, losses, counts = refs[14:]
+    rest_kernel(m, *refs[:14], loss_ref, count_ref, part)
+    mine = lax.axis_index("nodes") // QUAD
     for c in range(QUAD - 1):
         losses[mine ^ c], counts[mine ^ c] = prior[2 * c][...], prior[2 * c + 1][...]
-    losses[mine ^ (QUAD - 1)], counts[mine ^ (QUAD - 1)] = loss + partner[2][...], count + partner[3][...]
+    losses[mine ^ (QUAD - 1)], counts[mine ^ (QUAD - 1)] = loss_ref[...], count_ref[...]
     loss, count = (jnp.sum(sum(x[q] for q in range(QUAD)), axis=1, keepdims=True) for x in (losses, counts))
     stats_ref[...] = jnp.where(_iota(stats_ref.shape, 1) == 0, loss, count)
 
@@ -480,14 +487,17 @@
     return _call(lambda *refs: one_kernel(m, *refs), "forward_one", shapes, [have[m], *shared])
 
 
-def forward_last(have, m, shared, partner, prior):
+def forward_rest(have, m, shared, partner, prior=()):
     rows, width = have[0].shape
     units, padded = shared[2].shape[0], shared[4].shape[0]
     stat = ((padded, LANES), F32)
     shapes = [((2 * rows, width), BF16), ((units, 2 * rows), BF16), ((padded, 2 * rows), F32), stat]
-    stats = [x for held in prior for x in held[3:5]]
-    scratch = [((padded, rows), F32)] + [((QUAD, padded, LANES), F32)] * 2
-    operands = [have[m - 2], have[m], *shared, *partner, *stats]
+    scratch = [((padded, rows), F32)]
+    operands = [have[m - 2], have[m], *shared, *partner]
+    if not prior:
+        return _call(lambda *refs: rest_kernel(m, *refs), "forward_rest", [*shapes, stat], operands, scratch)
+    operands += [x for held in prior for x in held[3:5]]
+    scratch += [stat] * 2 + [((QUAD, padded, LANES), F32)] * 2
     return _call(lambda *refs: last_kernel(m, *refs), "forward_last", shapes, operands, scratch)
 
 
@@ -591,19 +601,21 @@
         weighed.extend(weights(w_self, w_neigh, w_out, b_out))
         return weighed, own(part_x, agg, weighed[0])
 
-    def ahead(cs):
-        def work(have):
-            in_t, out_t, _, bias = weighed
-            return [forward_pair(have, c, (part_x, all_labels, in_t, out_t, bias)) for c in cs]
-
-        return work
-
-    have, (_, hidden), two, three = gather_plane(agg, first, ahead((0, 1)), ahead((2,)))
-    held = [*two, *three]
-    in_t, out_t, out_p, bias = weighed
-    shared = (part_x, all_labels, in_t, out_t, bias)
-    partner = forward_one(have, DEVICES - QUAD, shared)
-    *last, mine = forward_last(have, DEVICES - 2, shared, partner, held)
+    def shared():
+        in_t, out_t, _, bias = weighed
+        return part_x, all_labels, in_t, out_t, bias
+
+    def second(have):
+        return [forward_pair(have, c, shared()) for c in (0, 1)]
+
+    def third(have, done):
+        return forward_rest(have, 10, shared(), forward_one(have, 8, shared()))
+
+    have, (_, hidden), held, more = gather_plane(agg, first, second, third)
+    held = [*held, more]
+    out_p = weighed[2]
+    partner = forward_one(have, 12, shared())
+    *last, mine = forward_rest(have, 14, shared(), partner, held)
     classes = w_out.shape[1]
     sums, class_weight = backward([*held, last], part_x, all_labels, out_p, mine, swap(mine, 1), classes)
     grad_self, grad_neigh, grad_out = total(sums, swap(sums, 1), *w_self.shape, classes)

time: 57.2 us -> 57 us (level)
  waiting for transfers between devices: 11.5 us -> 10.8 us
    ppermute x24, waiting for transfers between devices: 11.5 us -> 10.8 us  [swap(): return lax.ppermute(x, 'nodes', [(i, i ^ m) for i in range(DEVICES)])]
    pallas_call x5 -> x6, Pallas kernels: 4.4 us -> 4.78 us  [_call(): pl.pallas_call(kernel, in_specs=[vmem] * len(operands), out_specs=[vmem]...]
  transfers between devices with their start and end apart: 24 -> 24, of which waited for: 12 -> 13; matrix products, arithmetic and copies ran while one was open for 0% -> 0% of each run, Pallas kernels for 22% -> 23%
where the time goes in v8:
time: 57 us; the launch traced here: 56.8 us
  Pallas kernels  22.6 us (40%)
  starting transfers between devices  22.5 us (39%)
  waiting for transfers between devices  10.8 us (19%)
  between operations  0.83 us (1%)
    ppermute x24, starting transfers between devices, swap(): return lax.ppermute(x, 'nodes', [(i, i ^ m) for i in range(DEVICES)])  22.5 us
    ppermute x24, waiting for transfers between devices, swap(): return lax.ppermute(x, 'nodes', [(i, i ^ m) for i in range(DEVICES)])  10.8 us
    pallas_call x6, Pallas kernels, _call(): pl.pallas_call(kernel, in_specs=[vmem] * len(operands), out_specs=[vmem]...  4.78 us
    pallas_call x1, Pallas kernels, aggregate(): pl.pallas_call(lambda *refs: aggregate_kernel(ms, len(turned), *refs), in...  3.75 us
    pallas_call x1, Pallas kernels, turn(): pl.pallas_call(turn_kernel, in_specs=[pl.BlockSpec(memory_space=pltpu.HBM...  3.52 us
    pallas_call x1, Pallas kernels, backward(): pl.pallas_call(lambda *refs: backward_kernel(classes, *refs), in_specs=[v...  2.81 us
    pallas_call x2, Pallas kernels, place(): pl.pallas_call(lambda *refs: _place(ms, refs[:len(ms)], refs[len(ms):n],...  2.09 us
    pallas_call x1, Pallas kernels, pack(): pl.pallas_call(lambda *refs: pack_kernel(devices, *refs), in_specs=[pl.Bl...  1.45 us
  transfers between devices with their start and end apart: 24, of which 13 were waited for; matrix products, arithmetic and copies ran while one was open for 0% of the time, Pallas kernels for 23%

profile of v8, /device:TPU:0, one launch (start us, length us, event | category | flops | bytes accessed | tf_op | source)
XLA Modules:
  0.0 56.8 jit_solution(2137099019110059023)
XLA Ops:
  0.6 1.5 %pack_rows.1.refs_0_ = bf16[17,32,128]{2,1,0:T(8,128)(2,1)S(1)} custom-call(bf16[512,128]{1,0:T(8,128)(2,1)} %refs_0_.2, s32[1,512]{1,0:T(1,128)} %bitcast.10, s32[1,512]{1,0:T(1,128)} %bitcast.11, s32[4,128]{1,0:T(4,128)} %bitcast.12), custom_call_target="tpu_custom_call" | custom-call | tf_op jit(solution)/shard_map/pack_rows/pallas_call | solution.py:123
  2.1 4.1 %collective-permute-start = (bf16[17,32,128]{2,1,0:T(8,128)(2,1)S(1)}, bf16[17,32,128]{2,1,0:T(8,128)(2,1)S(1)}, u32[]{:S(2)}, u32[]{:S(2)}) collective-permute-start(bf16[17,32,128]{2,1,0:T(8,128)(2,1)S(1)} %pack_rows.1.refs_0_), channel_id=1, source_target_pairs={{0,8},{1,9},{2,10},{3,11},{4,12},{5,13},{6,14},{7,15},{8,0},{9,1},... | collective-permute-start | bytes 417800 | tf_op jit(solution)/shard_map/ppermute | solution.py:45
  6.2 1.6 %collective-permute-start.1 = (bf16[17,32,128]{2,1,0:T(8,128)(2,1)S(1)}, bf16[17,32,128]{2,1,0:T(8,128)(2,1)S(1)}, u32[]{:S(2)}, u32[]{:S(2)}) collective-permute-start(bf16[17,32,128]{2,1,0:T(8,128)(2,1)S(1)} %pack_rows.1.refs_0_), channel_id=1, source_target_pairs={{0,4},{1,5},{2,6},{3,7},{4,0},{5,1},{6,2},{7,3},{8,12},{9,13},{10,... | collective-permute-start | bytes 417800 | tf_op jit(solution)/shard_map/ppermute | solution.py:45
  7.8 1.5 %collective-permute-start.2 = (bf16[17,32,128]{2,1,0:T(8,128)(2,1)S(1)}, bf16[17,32,128]{2,1,0:T(8,128)(2,1)S(1)}, u32[]{:S(2)}, u32[]{:S(2)}) collective-permute-start(bf16[17,32,128]{2,1,0:T(8,128)(2,1)S(1)} %pack_rows.1.refs_0_), channel_id=1, source_target_pairs={{0,2},{1,3},{2,0},{3,1},{4,6},{5,7},{6,4},{7,5},{8,10},{9,11},{10,... | collective-permute-start | bytes 417800 | tf_op jit(solution)/shard_map/ppermute | solution.py:45
  9.3 3.5 %turn_adjacency.1 = (bf16[2,64,128,128]{3,2,1,0:T(8,128)(2,1)S(1)}, bf16[256,64,128]{2,1,0:T(8,128)(2,1)S(1)}) custom-call(bf16[512,64,128]{2,1,0:T(8,128)(2,1)} %adj_ref.1), custom_call_target="tpu_custom_call" | custom-call | flops 1073741824 | bytes 8388608 | tf_op jit(solution)/shard_map/turn_adjacency/pallas_call | solution.py:229
  12.8 0.1 collective-permute-done.refs_0_
  13.0 0.2 collective-permute-done.1.refs_4_
  13.2 1.6 %collective-permute-start.9 = (bf16[17,32,128]{2,1,0:T(8,128)(2,1)S(1)}, bf16[17,32,128]{2,1,0:T(8,128)(2,1)S(1)}, u32[]{:S(2)}, u32[]{:S(2)}) collective-permute-start(bf16[17,32,128]{2,1,0:T(8,128)(2,1)S(1)} %collective-permute-done.1.refs_4_), channel_id=1, source_target_pairs={{0,2},{1,3},{2,0},{3,1},{4,6},{5,7},{6,4},{7,5},{8,10},{9,11},{10,... | collective-permute-start | bytes 417800 | tf_op jit(solution)/shard_map/ppermute | solution.py:45
  14.7 1.4 %collective-permute-start.3 = (bf16[17,32,128]{2,1,0:T(8,128)(2,1)S(1)}, bf16[17,32,128]{2,1,0:T(8,128)(2,1)S(1)}, u32[]{:S(2)}, u32[]{:S(2)}) collective-permute-start(bf16[17,32,128]{2,1,0:T(8,128)(2,1)S(1)} %collective-permute-done.refs_0_), channel_id=1, source_target_pairs={{0,4},{1,5},{2,6},{3,7},{4,0},{5,1},{6,2},{7,3},{8,12},{9,13},{10,... | collective-permute-start | bytes 417800 | tf_op jit(solution)/shard_map/ppermute | solution.py:45
  16.1 0.5 collective-permute-start.13
  16.7 0.2 collective-permute-start.7
  16.9 2.1 %collective-permute-done.9.refs_6_ = bf16[17,32,128]{2,1,0:T(8,128)(2,1)S(1)} collective-permute-done((bf16[17,32,128]{2,1,0:T(8,128)(2,1)S(1)}, bf16[17,32,128]{2,1,0:T(8,128)(2,1)S(1)}, u32[]{:S(2)}, u32[]{:S(2)}) %collective-permute-start.9) | collective-permute-done | bytes 139296 | tf_op jit(solution)/shard_map/ppermute | solution.py:45
  19.0 0.8 %collective-permute-done.3.refs_0_ = bf16[17,32,128]{2,1,0:T(8,128)(2,1)S(1)} collective-permute-done((bf16[17,32,128]{2,1,0:T(8,128)(2,1)S(1)}, bf16[17,32,128]{2,1,0:T(8,128)(2,1)S(1)}, u32[]{:S(2)}, u32[]{:S(2)}) %collective-permute-start.3) | collective-permute-done | bytes 139296 | tf_op jit(solution)/shard_map/ppermute | solution.py:45
  19.8 1.0 %collective-permute-start.5 = (bf16[17,32,128]{2,1,0:T(8,128)(2,1)S(1)}, bf16[17,32,128]{2,1,0:T(8,128)(2,1)S(1)}, u32[]{:S(2)}, u32[]{:S(2)}) collective-permute-start(bf16[17,32,128]{2,1,0:T(8,128)(2,1)S(1)} %collective-permute-done.3.refs_0_), channel_id=1, source_target_pairs={{0,2},{1,3},{2,0},{3,1},{4,6},{5,7},{6,4},{7,5},{8,10},{9,11},{10,... | collective-permute-start | bytes 417800 | tf_op jit(solution)/shard_map/ppermute | solution.py:45
  20.7 1.3 %turn_rest.1.refs_7_ = bf16[2,64,128,128]{3,2,1,0:T(8,128)(2,1)S(1)} custom-call(bf16[2,128,64,128]{3,2,1,0:T(8,128)(2,1)S(1)} %bitcast.8), custom_call_target="tpu_custom_call" | custom-call | flops 1073741824 | bytes 4194304 | tf_op jit(solution)/shard_map/turn_rest/pallas_call | solution.py:252
  22.0 0.1 collective-permute-start.12
  22.1 0.2 collective-permute-done.13.refs_2_
  22.3 0.3 collective-permute-start.14
  22.6 1.3 %place.2 = (bf16[8192,128]{1,0:T(8,128)(2,1)S(1)}, bf16[16,16,128]{2,1,0:T(8,128)(2,1)S(1)}) custom-call(bf16[17,32,128]{2,1,0:T(8,128)(2,1)S(1)} %pack_rows.1.refs_0_, bf16[17,32,128]{2,1,0:T(8,128)(2,1)S(1)} %collective-permute-done.6.refs_1_, bf16[17,32,128]{2,1,0:T(8,128)(2,1)S(1)} %collective-permute-done.2.refs_2_, ...), custom_call_target="tpu_custom_call" | custom-call | flops 1073741824 | bytes 4194304 | tf_op jit(solution)/shard_map/place/pallas_call | solution.py:299
  24.0 1.2 %collective-permute-done.5.refs_2_ = bf16[17,32,128]{2,1,0:T(8,128)(2,1)S(1)} collective-permute-done((bf16[17,32,128]{2,1,0:T(8,128)(2,1)S(1)}, bf16[17,32,128]{2,1,0:T(8,128)(2,1)S(1)}, u32[]{:S(2)}, u32[]{:S(2)}) %collective-permute-start.5) | collective-permute-done | bytes 139296 | tf_op jit(solution)/shard_map/ppermute | solution.py:45
  25.2 0.5 collective-permute-start.4
  25.7 0.7 %place.3 = (bf16[8192,128]{1,0:T(8,128)(2,1)S(1)}, bf16[16,16,128]{2,1,0:T(8,128)(2,1)S(1)}) custom-call(bf16[17,32,128]{2,1,0:T(8,128)(2,1)S(1)} %collective-permute-done.refs_0_, bf16[17,32,128]{2,1,0:T(8,128)(2,1)S(1)} %collective-permute-done.12.refs_1_, bf16[17,32,128]{2,1,0:T(8,128)(2,1)S(1)} %collective-permute-done.13.refs_2_, ...), custom_call_target="tpu_custom_call" | custom-call | flops 1073741824 | bytes 4194304 | tf_op jit(solution)/shard_map/place/pallas_call | solution.py:299
  26.5 0.1 collective-permute-done.11.refs_3_
  26.6 0.2 collective-permute-done.4.refs_1_
  26.8 3.8 %aggregate.1 = (bf16[8192,128]{1,0:T(8,128)(2,1)S(1)}, bf16[16,16,128]{2,1,0:T(8,128)(2,1)S(1)}, bf16[512,128]{1,0:T(8,128)(2,1)S(1)}) custom-call(bf16[17,32,128]{2,1,0:T(8,128)(2,1)S(1)} %collective-permute-done.3.refs_0_, bf16[17,32,128]{2,1,0:T(8,128)(2,1)S(1)} %collective-permute-done.4.refs_1_, ...), custom_call_target="tpu_custom_call" | custom-call | tf_op jit(solution)/shard_map/aggregate/pallas_call | solution.py:333
  30.5 2.4 %collective-permute-start.15 = (bf16[512,128]{1,0:T(8,128)(2,1)S(1)}, bf16[512,128]{1,0:T(8,128)(2,1)S(1)}, u32[]{:S(2)}, u32[]{:S(2)}) collective-permute-start(bf16[512,128]{1,0:T(8,128)(2,1)S(1)} %get-tuple-element.97.agg_ref.refs_0_), channel_id=1, source_target_pairs={{0,8},{1,9},{2,10},{3,11},{4,12},{5,13},{6,14},{7,15},{8,0},{9,1},... | collective-permute-start | bytes 393224 | tf_op jit(solution)/shard_map/ppermute | solution.py:45
  32.9 0.5 collective-permute-start.17
  33.4 3.0 %collective-permute-start.18 = (bf16[512,128]{1,0:T(8,128)(2,1)S(1)}, bf16[512,128]{1,0:T(8,128)(2,1)S(1)}, u32[]{:S(2)}, u32[]{:S(2)}) collective-permute-start(bf16[512,128]{1,0:T(8,128)(2,1)S(1)} %get-tuple-element.97.agg_ref.refs_0_), channel_id=1, source_target_pairs={{0,4},{1,5},{2,6},{3,7},{4,0},{5,1},{6,2},{7,3},{8,12},{9,13},{10,... | collective-permute-start | bytes 393224 | tf_op jit(solution)/shard_map/ppermute | solution.py:45
  36.5 1.1 %weights.1 = (bf16[256,256]{1,0:T(8,128)(2,1)S(1)}, bf16[176,256]{1,0:T(8,128)(2,1)S(1)}, bf16[256,176]{1,0:T(8,128)(2,1)S(1)}, f32[176,128]{1,0:T(8,128)S(1)}) custom-call(bf16[128,256]{1,0:T(8,128)(2,1)} %refs_0_.3, bf16[128,256]{1,0:T(8,128)(2,1)} %refs_1_.1, f32[1,172]{1,0:T(1,128)} %bitcast.13, bf16[172,256]{1,0:T(8,128)(2,1)S(1)} %bitcast.9), custom_call_target="tpu_custom_call" | custom-call | bytes 2097152 | tf_op jit(solution)/shard_map/weights/pallas_call | solution.py:155
  37.6 1.0 %own.1 = bf16[512,256]{1,0:T(8,128)(2,1)} custom-call(bf16[8192,128]{1,0:T(8,128)(2,1)S(1)} %get-tuple-element.102.px_ref.refs_2_.refs_1_.refs_12_, bf16[512,128]{1,0:T(8,128)(2,1)S(1)} %get-tuple-element.97.agg_ref.refs_0_, bf16[256,256]{1,0:T(8,128)(2,1)S(1)} %get-tuple-element.98.in_t_ref.refs_4_.refs_3_), custom_call_target="tpu_custom_call" | custom-call | flops 67108864 | bytes 262144 | tf_op jit(solution)/shard_map/own/pallas_call | solution.py:450
  38.5 1.6 %collective-permute-done.15.refs_0_ = bf16[512,128]{1,0:T(8,128)(2,1)S(1)} collective-permute-done((bf16[512,128]{1,0:T(8,128)(2,1)S(1)}, bf16[512,128]{1,0:T(8,128)(2,1)S(1)}, u32[]{:S(2)}, u32[]{:S(2)}) %collective-permute-start.15) | collective-permute-done | bytes 131104 | tf_op jit(solution)/shard_map/ppermute | solution.py:45
  40.1 0.7 %collective-permute-start.16 = (bf16[512,128]{1,0:T(8,128)(2,1)S(1)}, bf16[512,128]{1,0:T(8,128)(2,1)S(1)}, u32[]{:S(2)}, u32[]{:S(2)}) collective-permute-start(bf16[512,128]{1,0:T(8,128)(2,1)S(1)} %collective-permute-done.15.refs_0_), channel_id=1, source_target_pairs={{0,2},{1,3},{2,0},{3,1},{4,6},{5,7},{6,4},{7,5},{8,10},{9,11},{10,... | collective-permute-start | bytes 393224 | tf_op jit(solution)/shard_map/ppermute | solution.py:45
  40.8 1.3 %collective-permute-start.20 = (bf16[512,128]{1,0:T(8,128)(2,1)S(1)}, bf16[512,128]{1,0:T(8,128)(2,1)S(1)}, u32[]{:S(2)}, u32[]{:S(2)}) collective-permute-start(bf16[512,128]{1,0:T(8,128)(2,1)S(1)} %collective-permute-done.15.refs_0_), channel_id=1, source_target_pairs={{0,4},{1,5},{2,6},{3,7},{4,0},{5,1},{6,2},{7,3},{8,12},{9,13},{10,... | collective-permute-start | bytes 393224 | tf_op jit(solution)/shard_map/ppermute | solution.py:45
  42.0 0.6 %forward_one.2 = (bf16[256,512]{1,0:T(8,128)(2,1)S(1)}, f32[176,512]{1,0:T(8,128)S(1)}, f32[176,128]{1,0:T(8,128)S(1)}, f32[176,128]{1,0:T(8,128)S(1)}) custom-call(bf16[512,128]{1,0:T(8,128)(2,1)S(1)} %collective-permute-done.15.refs_0_, bf16[8192,128]{1,0:T(8,128)(2,1)S(1)} %get-tuple-element.102.px_ref.refs_2_.refs_1_.refs_12_, ...), custom_call_target="tpu_custom_call" | custom-call | flops 536870912 | bytes 2097152 | tf_op jit(solution)/shard_map/forward_one/pallas_call | solution.py:463
  42.7 1.6 %collective-permute-start.21 = (bf16[512,128]{1,0:T(8,128)(2,1)S(1)}, bf16[512,128]{1,0:T(8,128)(2,1)S(1)}, u32[]{:S(2)}, u32[]{:S(2)}) collective-permute-start(bf16[512,128]{1,0:T(8,128)(2,1)S(1)} %collective-permute-done.15.refs_0_), channel_id=1, source_target_pairs={{0,6},{1,7},{2,4},{3,5},{4,2},{5,3},{6,0},{7,1},{8,14},{9,15},{10,... | collective-permute-start | bytes 393224 | tf_op jit(solution)/shard_map/ppermute | solution.py:45
  44.3 0.9 %forward_pair.2 = (bf16[1024,128]{1,0:T(8,128)(2,1)S(1)}, bf16[256,1024]{1,0:T(8,128)(2,1)S(1)}, f32[176,1024]{1,0:T(8,128)S(1)}, f32[176,128]{1,0:T(8,128)S(1)}, f32[176,128]{1,0:T(8,128)S(1)}) custom-call(bf16[512,128]{1,0:T(8,128)(2,1)S(1)} %get-tuple-element.97.agg_ref.refs_0_, bf16[512,128]{1,0:T(8,128)(2,1)S(1)} %collective-permute-done.17.refs_1_, ...), custom_call_target="tpu_custom_call" | custom-call | flops 536870912 | bytes 2097152 | tf_op jit(solution)/shard_map/forward_pair/pallas_call | solution.py:463
  45.3 1.1 %forward_pair.3 = (bf16[1024,128]{1,0:T(8,128)(2,1)S(1)}, bf16[256,1024]{1,0:T(8,128)(2,1)S(1)}, f32[176,1024]{1,0:T(8,128)S(1)}, f32[176,128]{1,0:T(8,128)S(1)}, f32[176,128]{1,0:T(8,128)S(1)}) custom-call(bf16[512,128]{1,0:T(8,128)(2,1)S(1)} %collective-permute-done.18.refs_0_, bf16[512,128]{1,0:T(8,128)(2,1)S(1)} %collective-permute-done.19.refs_1_, ...), custom_call_target="tpu_custom_call" | custom-call | flops 536870912 | bytes 2097152 | tf_op jit(solution)/shard_map/forward_pair/pallas_call | solution.py:463
  46.4 1.2 %collective-permute-done.16.refs_1_ = bf16[512,128]{1,0:T(8,128)(2,1)S(1)} collective-permute-done((bf16[512,128]{1,0:T(8,128)(2,1)S(1)}, bf16[512,128]{1,0:T(8,128)(2,1)S(1)}, u32[]{:S(2)}, u32[]{:S(2)}) %collective-permute-start.16) | collective-permute-done | bytes 131104 | tf_op jit(solution)/shard_map/ppermute | solution.py:45
  47.5 0.7 %forward_rest.1 = (bf16[1024,128]{1,0:T(8,128)(2,1)S(1)}, bf16[256,1024]{1,0:T(8,128)(2,1)S(1)}, f32[176,1024]{1,0:T(8,128)S(1)}, f32[176,128]{1,0:T(8,128)S(1)}, f32[176,128]{1,0:T(8,128)S(1)}) custom-call(bf16[512,128]{1,0:T(8,128)(2,1)S(1)} %collective-permute-done.15.refs_0_, bf16[512,128]{1,0:T(8,128)(2,1)S(1)} %collective-permute-done.16.refs_1_, ...), custom_call_target="tpu_custom_call" | custom-call | flops 536870912 | bytes 2097152 | tf_op jit(solution)/shard_map/forward_rest/pallas_call | solution.py:463
  48.3 0.6 %forward_one.3 = (bf16[256,512]{1,0:T(8,128)(2,1)S(1)}, f32[176,512]{1,0:T(8,128)S(1)}, f32[176,128]{1,0:T(8,128)S(1)}, f32[176,128]{1,0:T(8,128)S(1)}) custom-call(bf16[512,128]{1,0:T(8,128)(2,1)S(1)} %collective-permute-done.20.refs_0_, bf16[8192,128]{1,0:T(8,128)(2,1)S(1)} %get-tuple-element.102.px_ref.refs_2_.refs_1_.refs_12_, ...), custom_call_target="tpu_custom_call" | custom-call | flops 536870912 | bytes 2097152 | tf_op jit(solution)/shard_map/forward_one/pallas_call | solution.py:463
  48.9 0.2 collective-permute-done.21.refs_1_
  49.1 0.8 %forward_last.1 = (bf16[1024,128]{1,0:T(8,128)(2,1)S(1)}, bf16[256,1024]{1,0:T(8,128)(2,1)S(1)}, f32[176,1024]{1,0:T(8,128)S(1)}, f32[176,128]{1,0:T(8,128)S(1)}) custom-call(bf16[512,128]{1,0:T(8,128)(2,1)S(1)} %collective-permute-done.20.refs_0_, bf16[512,128]{1,0:T(8,128)(2,1)S(1)} %collective-permute-done.21.refs_1_, ...), custom_call_target="tpu_custom_call" | custom-call | flops 536870912 | bytes 2097152 | tf_op jit(solution)/shard_map/forward_last/pallas_call | solution.py:463
  49.9 0.1 collective-permute-start.22
  50.0 1.3 %collective-permute-done.22.refs_16_ = f32[176,128]{1,0:T(8,128)S(1)} collective-permute-done((f32[176,128]{1,0:T(8,128)S(1)}, f32[176,128]{1,0:T(8,128)S(1)}, u32[]{:S(2)}, u32[]{:S(2)}) %collective-permute-start.22) | collective-permute-done | bytes 90144 | tf_op jit(solution)/shard_map/ppermute | solution.py:45
  51.3 2.8 %backward.1 = (f32[432,256]{1,0:T(8,128)S(1)}, f32[1,172]{1,0:T(1,128)}) custom-call(bf16[1024,128]{1,0:T(8,128)(2,1)S(1)} %get-tuple-element.116.refs_0_, bf16[256,1024]{1,0:T(8,128)(2,1)S(1)} %get-tuple-element.117.refs_1_, f32[176,1024]{1,0:T(8,128)S(1)} %get-tuple-element.118.refs_2_, bf16[1024,128]{1,0:T(8,128)(2,1)S(1)} %get-tuple-element.119.refs_3_, ...), custom_call_target="tpu_custom_call" | custom-call | tf_op jit(solution)/shard_map/backward/pallas_call | solution.py:541
  54.1 0.2 collective-permute-start.23
  54.3 1.6 %collective-permute-done.23.other_ref = f32[432,256]{1,0:T(8,128)S(1)} collective-permute-done((f32[432,256]{1,0:T(8,128)S(1)}, f32[432,256]{1,0:T(8,128)S(1)}, u32[]{:S(2)}, u32[]{:S(2)}) %collective-permute-start.23) | collective-permute-done | bytes 442400 | tf_op jit(solution)/shard_map/ppermute | solution.py:45
  55.9 0.9 %total.1 = (f32[128,256]{1,0:T(8,128)}, f32[128,256]{1,0:T(8,128)}, f32[172,256]{1,0:T(8,128)}) custom-call(f32[432,256]{1,0:T(8,128)S(1)} %get-tuple-element.150.mine_ref, f32[432,256]{1,0:T(8,128)S(1)} %collective-permute-done.23.other_ref), custom_call_target="tpu_custom_call" | custom-call | tf_op jit(solution)/shard_map/total/pallas_call | solution.py:566
  (22 shorter events, 0.1 us)
Async XLA Ops:
  2.1 10.9 %collective-permute-start = (bf16[17,32,128]{2,1,0:T(8,128)(2,1)S(1)}, bf16[17,32,128]{2,1,0:T(8,128)(2,1)S(1)}, u32[]{:S(2)}, u32[]{:S(2)}) collective-permute-start(bf16[17,32,128]{2,1,0:T(8,128)(2,1)S(1)} %pack_rows.1.refs_0_), channel_id=1, source_target_pairs={{0,8},{1,9},{2,10},{3,11},{4,12},{5,13},{6,14},{7,15},{8,0},{9,1},... | collective-permute-start | bytes 417800 | tf_op jit(solution)/shard_map/ppermute | solution.py:45
  6.2 7.0 %collective-permute-start.1 = (bf16[17,32,128]{2,1,0:T(8,128)(2,1)S(1)}, bf16[17,32,128]{2,1,0:T(8,128)(2,1)S(1)}, u32[]{:S(2)}, u32[]{:S(2)}) collective-permute-start(bf16[17,32,128]{2,1,0:T(8,128)(2,1)S(1)} %pack_rows.1.refs_0_), channel_id=1, source_target_pairs={{0,4},{1,5},{2,6},{3,7},{4,0},{5,1},{6,2},{7,3},{8,12},{9,13},{10,... | collective-permute-start | bytes 417800 | tf_op jit(solution)/shard_map/ppermute | solution.py:45
  7.8 5.4 %collective-permute-start.2 = (bf16[17,32,128]{2,1,0:T(8,128)(2,1)S(1)}, bf16[17,32,128]{2,1,0:T(8,128)(2,1)S(1)}, u32[]{:S(2)}, u32[]{:S(2)}) collective-permute-start(bf16[17,32,128]{2,1,0:T(8,128)(2,1)S(1)} %pack_rows.1.refs_0_), channel_id=1, source_target_pairs={{0,2},{1,3},{2,0},{3,1},{4,6},{5,7},{6,4},{7,5},{8,10},{9,11},{10,... | collective-permute-start | bytes 417800 | tf_op jit(solution)/shard_map/ppermute | solution.py:45
  9.3 7.4 %collective-permute-start.6 = (bf16[17,32,128]{2,1,0:T(8,128)(2,1)S(1)}, bf16[17,32,128]{2,1,0:T(8,128)(2,1)S(1)}, u32[]{:S(2)}, u32[]{:S(2)}) collective-permute-start(bf16[17,32,128]{2,1,0:T(8,128)(2,1)S(1)} %pack_rows.1.refs_0_), channel_id=1, source_target_pairs={{0,1},{1,0},{2,3},{3,2},{4,5},{5,4},{6,7},{7,6},{8,9},{9,8},{10,11... | collective-permute-start | bytes 417800 | tf_op jit(solution)/shard_map/ppermute | solution.py:45
  13.2 5.8 %collective-permute-start.9 = (bf16[17,32,128]{2,1,0:T(8,128)(2,1)S(1)}, bf16[17,32,128]{2,1,0:T(8,128)(2,1)S(1)}, u32[]{:S(2)}, u32[]{:S(2)}) collective-permute-start(bf16[17,32,128]{2,1,0:T(8,128)(2,1)S(1)} %collective-permute-done.1.refs_4_), channel_id=1, source_target_pairs={{0,2},{1,3},{2,0},{3,1},{4,6},{5,7},{6,4},{7,5},{8,10},{9,11},{10,... | collective-permute-start | bytes 417800 | tf_op jit(solution)/shard_map/ppermute | solution.py:45
  14.7 5.1 %collective-permute-start.3 = (bf16[17,32,128]{2,1,0:T(8,128)(2,1)S(1)}, bf16[17,32,128]{2,1,0:T(8,128)(2,1)S(1)}, u32[]{:S(2)}, u32[]{:S(2)}) collective-permute-start(bf16[17,32,128]{2,1,0:T(8,128)(2,1)S(1)} %collective-permute-done.refs_0_), channel_id=1, source_target_pairs={{0,4},{1,5},{2,6},{3,7},{4,0},{5,1},{6,2},{7,3},{8,12},{9,13},{10,... | collective-permute-start | bytes 417800 | tf_op jit(solution)/shard_map/ppermute | solution.py:45
  16.1 5.9 %collective-permute-start.8 = (bf16[17,32,128]{2,1,0:T(8,128)(2,1)S(1)}, bf16[17,32,128]{2,1,0:T(8,128)(2,1)S(1)}, u32[]{:S(2)}, u32[]{:S(2)}) collective-permute-start(bf16[17,32,128]{2,1,0:T(8,128)(2,1)S(1)} %collective-permute-done.1.refs_4_), channel_id=1, source_target_pairs={{0,1},{1,0},{2,3},{3,2},{4,5},{5,4},{6,7},{7,6},{8,9},{9,8},{10,11... | collective-permute-start | bytes 417800 | tf_op jit(solution)/shard_map/ppermute | solution.py:45
  16.1 6.1 %collective-permute-start.13 = (bf16[17,32,128]{2,1,0:T(8,128)(2,1)S(1)}, bf16[17,32,128]{2,1,0:T(8,128)(2,1)S(1)}, u32[]{:S(2)}, u32[]{:S(2)}) collective-permute-start(bf16[17,32,128]{2,1,0:T(8,128)(2,1)S(1)} %collective-permute-done.refs_0_), channel_id=1, source_target_pairs={{0,2},{1,3},{2,0},{3,1},{4,6},{5,7},{6,4},{7,5},{8,10},{9,11},{10,... | collective-permute-start | bytes 417800 | tf_op jit(solution)/shard_map/ppermute | solution.py:45
  16.7 6.0 %collective-permute-start.7 = (bf16[17,32,128]{2,1,0:T(8,128)(2,1)S(1)}, bf16[17,32,128]{2,1,0:T(8,128)(2,1)S(1)}, u32[]{:S(2)}, u32[]{:S(2)}) collective-permute-start(bf16[17,32,128]{2,1,0:T(8,128)(2,1)S(1)} %collective-permute-done.2.refs_2_), channel_id=1, source_target_pairs={{0,1},{1,0},{2,3},{3,2},{4,5},{5,4},{6,7},{7,6},{8,9},{9,8},{10,11... | collective-permute-start | bytes 417800 | tf_op jit(solution)/shard_map/ppermute | solution.py:45
  19.0 3.6 %collective-permute-start.10 = (bf16[17,32,128]{2,1,0:T(8,128)(2,1)S(1)}, bf16[17,32,128]{2,1,0:T(8,128)(2,1)S(1)}, u32[]{:S(2)}, u32[]{:S(2)}) collective-permute-start(bf16[17,32,128]{2,1,0:T(8,128)(2,1)S(1)} %collective-permute-done.9.refs_6_), channel_id=1, source_target_pairs={{0,1},{1,0},{2,3},{3,2},{4,5},{5,4},{6,7},{7,6},{8,9},{9,8},{10,11... | collective-permute-start | bytes 417800 | tf_op jit(solution)/shard_map/ppermute | solution.py:45
  19.8 5.4 %collective-permute-start.5 = (bf16[17,32,128]{2,1,0:T(8,128)(2,1)S(1)}, bf16[17,32,128]{2,1,0:T(8,128)(2,1)S(1)}, u32[]{:S(2)}, u32[]{:S(2)}) collective-permute-start(bf16[17,32,128]{2,1,0:T(8,128)(2,1)S(1)} %collective-permute-done.3.refs_0_), channel_id=1, source_target_pairs={{0,2},{1,3},{2,0},{3,1},{4,6},{5,7},{6,4},{7,5},{8,10},{9,11},{10,... | collective-permute-start | bytes 417800 | tf_op jit(solution)/shard_map/ppermute | solution.py:45
  22.0 4.8 %copy-start.1 = (s32[4,64]{1,0:T(4,128)S(1)}, s32[4,64]{1,0:T(4,128)}, u32[]{:S(2)}) copy-start(s32[4,64]{1,0:T(4,128)} %refs_9_.1) | copy-start | bytes 3076
  22.0 4.8 %copy-start.2 = (s32[1,64]{1,0:T(1,128)S(1)}, s32[1,64]{1,0:T(1,128)}, u32[]{:S(2)}) copy-start(s32[1,64]{1,0:T(1,128)} %refs_8_.1) | copy-start | bytes 772
  22.0 3.7 %collective-permute-start.12 = (bf16[17,32,128]{2,1,0:T(8,128)(2,1)S(1)}, bf16[17,32,128]{2,1,0:T(8,128)(2,1)S(1)}, u32[]{:S(2)}, u32[]{:S(2)}) collective-permute-start(bf16[17,32,128]{2,1,0:T(8,128)(2,1)S(1)} %collective-permute-done.refs_0_), channel_id=1, source_target_pairs={{0,1},{1,0},{2,3},{3,2},{4,5},{5,4},{6,7},{7,6},{8,9},{9,8},{10,11... | collective-permute-start | bytes 417800 | tf_op jit(solution)/shard_map/ppermute | solution.py:45
  22.3 3.4 %collective-permute-start.14 = (bf16[17,32,128]{2,1,0:T(8,128)(2,1)S(1)}, bf16[17,32,128]{2,1,0:T(8,128)(2,1)S(1)}, u32[]{:S(2)}, u32[]{:S(2)}) collective-permute-start(bf16[17,32,128]{2,1,0:T(8,128)(2,1)S(1)} %collective-permute-done.13.refs_2_), channel_id=1, source_target_pairs={{0,1},{1,0},{2,3},{3,2},{4,5},{5,4},{6,7},{7,6},{8,9},{9,8},{10,11... | collective-permute-start | bytes 417800 | tf_op jit(solution)/shard_map/ppermute | solution.py:45
  25.2 1.4 %collective-permute-start.11 = (bf16[17,32,128]{2,1,0:T(8,128)(2,1)S(1)}, bf16[17,32,128]{2,1,0:T(8,128)(2,1)S(1)}, u32[]{:S(2)}, u32[]{:S(2)}) collective-permute-start(bf16[17,32,128]{2,1,0:T(8,128)(2,1)S(1)} %collective-permute-done.5.refs_2_), channel_id=1, source_target_pairs={{0,1},{1,0},{2,3},{3,2},{4,5},{5,4},{6,7},{7,6},{8,9},{9,8},{10,11... | collective-permute-start | bytes 417800 | tf_op jit(solution)/shard_map/ppermute | solution.py:45
  25.2 1.6 %collective-permute-start.4 = (bf16[17,32,128]{2,1,0:T(8,128)(2,1)S(1)}, bf16[17,32,128]{2,1,0:T(8,128)(2,1)S(1)}, u32[]{:S(2)}, u32[]{:S(2)}) collective-permute-start(bf16[17,32,128]{2,1,0:T(8,128)(2,1)S(1)} %collective-permute-done.3.refs_0_), channel_id=1, source_target_pairs={{0,1},{1,0},{2,3},{3,2},{4,5},{5,4},{6,7},{7,6},{8,9},{9,8},{10,11... | collective-permute-start | bytes 417800 | tf_op jit(solution)/shard_map/ppermute | solution.py:45
  26.6 9.9 %copy-start = (bf16[256,172]{0,1:T(8,128)(2,1)S(1)}, bf16[256,172]{0,1:T(8,128)(2,1)}, u32[]{:S(2)}) copy-start(bf16[256,172]{0,1:T(8,128)(2,1)} %param.20) | copy-start | bytes 264196
  30.5 9.6 %collective-permute-start.15 = (bf16[512,128]{1,0:T(8,128)(2,1)S(1)}, bf16[512,128]{1,0:T(8,128)(2,1)S(1)}, u32[]{:S(2)}, u32[]{:S(2)}) collective-permute-start(bf16[512,128]{1,0:T(8,128)(2,1)S(1)} %get-tuple-element.97.agg_ref.refs_0_), channel_id=1, source_target_pairs={{0,8},{1,9},{2,10},{3,11},{4,12},{5,13},{6,14},{7,15},{8,0},{9,1},... | collective-permute-start | bytes 393224 | tf_op jit(solution)/shard_map/ppermute | solution.py:45
  32.9 9.7 %collective-permute-start.17 = (bf16[512,128]{1,0:T(8,128)(2,1)S(1)}, bf16[512,128]{1,0:T(8,128)(2,1)S(1)}, u32[]{:S(2)}, u32[]{:S(2)}) collective-permute-start(bf16[512,128]{1,0:T(8,128)(2,1)S(1)} %get-tuple-element.97.agg_ref.refs_0_), channel_id=1, source_target_pairs={{0,2},{1,3},{2,0},{3,1},{4,6},{5,7},{6,4},{7,5},{8,10},{9,11},{10,... | collective-permute-start | bytes 393224 | tf_op jit(solution)/shard_map/ppermute | solution.py:45
  33.4 11.8 %collective-permute-start.18 = (bf16[512,128]{1,0:T(8,128)(2,1)S(1)}, bf16[512,128]{1,0:T(8,128)(2,1)S(1)}, u32[]{:S(2)}, u32[]{:S(2)}) collective-permute-start(bf16[512,128]{1,0:T(8,128)(2,1)S(1)} %get-tuple-element.97.agg_ref.refs_0_), channel_id=1, source_target_pairs={{0,4},{1,5},{2,6},{3,7},{4,0},{5,1},{6,2},{7,3},{8,12},{9,13},{10,... | collective-permute-start | bytes 393224 | tf_op jit(solution)/shard_map/ppermute | solution.py:45
  36.5 8.8 %collective-permute-start.19 = (bf16[512,128]{1,0:T(8,128)(2,1)S(1)}, bf16[512,128]{1,0:T(8,128)(2,1)S(1)}, u32[]{:S(2)}, u32[]{:S(2)}) collective-permute-start(bf16[512,128]{1,0:T(8,128)(2,1)S(1)} %get-tuple-element.97.agg_ref.refs_0_), channel_id=1, source_target_pairs={{0,6},{1,7},{2,4},{3,5},{4,2},{5,3},{6,0},{7,1},{8,14},{9,15},{10,... | collective-permute-start | bytes 393224 | tf_op jit(solution)/shard_map/ppermute | solution.py:45
  40.1 7.4 %collective-permute-start.16 = (bf16[512,128]{1,0:T(8,128)(2,1)S(1)}, bf16[512,128]{1,0:T(8,128)(2,1)S(1)}, u32[]{:S(2)}, u32[]{:S(2)}) collective-permute-start(bf16[512,128]{1,0:T(8,128)(2,1)S(1)} %collective-permute-done.15.refs_0_), channel_id=1, source_target_pairs={{0,2},{1,3},{2,0},{3,1},{4,6},{5,7},{6,4},{7,5},{8,10},{9,11},{10,... | collective-permute-start | bytes 393224 | tf_op jit(solution)/shard_map/ppermute | solution.py:45
  40.8 7.5 %collective-permute-start.20 = (bf16[512,128]{1,0:T(8,128)(2,1)S(1)}, bf16[512,128]{1,0:T(8,128)(2,1)S(1)}, u32[]{:S(2)}, u32[]{:S(2)}) collective-permute-start(bf16[512,128]{1,0:T(8,128)(2,1)S(1)} %collective-permute-done.15.refs_0_), channel_id=1, source_target_pairs={{0,4},{1,5},{2,6},{3,7},{4,0},{5,1},{6,2},{7,3},{8,12},{9,13},{10,... | collective-permute-start | bytes 393224 | tf_op jit(solution)/shard_map/ppermute | solution.py:45
  42.7 6.4 %collective-permute-start.21 = (bf16[512,128]{1,0:T(8,128)(2,1)S(1)}, bf16[512,128]{1,0:T(8,128)(2,1)S(1)}, u32[]{:S(2)}, u32[]{:S(2)}) collective-permute-start(bf16[512,128]{1,0:T(8,128)(2,1)S(1)} %collective-permute-done.15.refs_0_), channel_id=1, source_target_pairs={{0,6},{1,7},{2,4},{3,5},{4,2},{5,3},{6,0},{7,1},{8,14},{9,15},{10,... | collective-permute-start | bytes 393224 | tf_op jit(solution)/shard_map/ppermute | solution.py:45
  49.9 1.4 %collective-permute-start.22 = (f32[176,128]{1,0:T(8,128)S(1)}, f32[176,128]{1,0:T(8,128)S(1)}, u32[]{:S(2)}, u32[]{:S(2)}) collective-permute-start(f32[176,128]{1,0:T(8,128)S(1)} %get-tuple-element.149.refs_15_), channel_id=1, source_target_pairs={{0,1},{1,0},{2,3},{3,2},{4,5},{5,4},{6,7},{7,6},{8,9},{9,8},{10,11... | collective-permute-start | bytes 270344 | tf_op jit(solution)/shard_map/ppermute | solution.py:45
  54.1 1.8 %collective-permute-start.23 = (f32[432,256]{1,0:T(8,128)S(1)}, f32[432,256]{1,0:T(8,128)S(1)}, u32[]{:S(2)}, u32[]{:S(2)}) collective-permute-start(f32[432,256]{1,0:T(8,128)S(1)} %get-tuple-element.150.mine_ref), channel_id=1, source_target_pairs={{0,1},{1,0},{2,3},{3,2},{4,5},{5,4},{6,7},{7,6},{8,9},{9,8},{10,11... | collective-permute-start | bytes 1327112 | tf_op jit(solution)/shard_map/ppermute | solution.py:45
